TPU v7x, 512 devices: a whole 4x8x8 slice. The times are simulated.
512 devices in a mesh: tile: 128 (over z_hi, x, y), rep: 4 (over z_lo, core).
Axes of the slice: x: 4, y: 8, z: 8 (z_hi: 4, z_lo: 2; z = z_hi * 2 + z_lo), core: 2. Of those that a mesh axis runs over, the one named last changes fastest.
Arguments:
- features: bfloat16 [4, 8, 4096, 384], P('rep', None, 'tile'), may hold values from -6 to 6
- cotangent: bfloat16 [4, 8, 4096, 384], P('rep', None, 'tile'), may hold values from -6 to 6
- kernel: float32 [7, 7, 384], replicated, may hold values from -0.875 to 0.875
- conv_bias: float32 [384], replicated, may hold values from -3 to 3
- ln_gain: float32 [384], replicated, may hold values from 0.5 to 2
- ln_bias: float32 [384], replicated, may hold values from -3 to 3
- w_in: bfloat16 [384, 1536], replicated, may hold values from -0.3125 to 0.3125
- b_in: float32 [1536], replicated, may hold values from -3 to 3
- w_out: bfloat16 [1536, 384], replicated, may hold values from -0.15625 to 0.15625
- layer_scale: float32 [384], replicated, may hold values from 0.5 to 2
- tissue: int32 [4, 512], P('rep', 'tile'), may hold values from 0 to 1, as said below
Outputs:
- grad_features: bfloat16 [4, 8, 4096, 384], P('rep', None, 'tile')
- grad_w_in: float32 [1536, 384], P(('tile', 'rep'))
- grad_w_out: bfloat16 [1536, 384], replicated
Inputs may be any that keep to these rules, and one draw needn't show every extreme that they name: Within each band, among the 4 tiles of one index of tile (aligned blocks along the second dimension), at least 1 and at most 3 are tissue, and in every band some index has exactly 3.
All inputs are finite; a program needn't handle non-finite values.
Results may differ from a plain program's by a relative error of at most 0.0069.
Values may be sent and summed in bfloat16 or wider, within the bound.
No kernel may reach another device: no remote copies, remote signals or barrier semaphores. Data moves between devices by JAX's collectives and lax.ppermute only.
A program may use at most 64 MiB of HBM per device.

v0:
```python
import math

import jax
import jax.numpy as jnp
from jax import lax
from jax.sharding import PartitionSpec as P

TILE_SIDE = 8


EPSILON = 1e-06


def extended(block, sides, width):
    for axis, dim in sides:
        count = lax.axis_size(axis)
        forward = [(i, i + 1) for i in range(count - 1)]
        backward = [(target, source) for source, target in forward]
        low = lax.ppermute(
            lax.slice_in_dim(block, block.shape[dim] - width, None, axis=dim), axis, forward
        )
        high = lax.ppermute(lax.slice_in_dim(block, 0, width, axis=dim), axis, backward)
        block = jnp.concatenate([low, block, high], axis=dim)
    return block


def depthwise(padded, kernel, height, breadth):
    total = jnp.zeros((height, breadth, padded.shape[-1]), jnp.float32)
    for a in range(7):
        for e in range(7):
            total = (
                total + padded[a : a + height, e : e + breadth].astype(jnp.float32) * kernel[a, e]
            )
    return total


def transposed(padded, kernel, height, breadth):
    total = jnp.zeros((height, breadth, padded.shape[-1]), jnp.float32)
    for a in range(7):
        for e in range(7):
            total = total + padded[6 - a : 6 - a + height, 6 - e : 6 - e + breadth] * kernel[a, e]
    return total


def gelu_slope(preact):
    normal_cdf = 0.5 * (1.0 + lax.erf(preact * 0.7071067811865476))
    density = jnp.exp(-0.5 * preact * preact) * 0.3989422804014327
    return normal_cdf + preact * density


def contract(left, right):
    return lax.dot_general(
        left, right, (((0,), (0,)), ((), ())), preferred_element_type=jnp.float32
    )


def branch_back(conv_rows, grad_rows, gate_rows, ln_gain, ln_bias, w_in, b_in, w_out, layer_scale):
    centre = conv_rows - jnp.mean(conv_rows, axis=-1, keepdims=True)
    inverse = lax.rsqrt(jnp.mean(centre * centre, axis=-1, keepdims=True) + EPSILON)
    standard = centre * inverse
    normed = (standard * ln_gain + ln_bias).astype(jnp.bfloat16)
    preact = jnp.dot(normed, w_in, preferred_element_type=jnp.float32) + b_in
    hidden = jax.nn.gelu(preact, approximate=False).astype(jnp.bfloat16)
    out_grad = (grad_rows.astype(jnp.float32) * layer_scale * gate_rows).astype(jnp.bfloat16)
    back_hidden = lax.dot_general(
        out_grad, w_out, (((1,), (1,)), ((), ())), preferred_element_type=jnp.float32
    )
    grad_pre = (back_hidden * gelu_slope(preact)).astype(jnp.bfloat16)
    grad_std = (
        lax.dot_general(
            grad_pre, w_in, (((1,), (1,)), ((), ())), preferred_element_type=jnp.float32
        )
        * ln_gain
    )
    grad_conv = inverse * (
        grad_std
        - jnp.mean(grad_std, axis=-1, keepdims=True)
        - standard * jnp.mean(grad_std * standard, axis=-1, keepdims=True)
    )
    return (normed, hidden, out_grad, grad_pre, grad_conv)


def body(
    features, cotangent, kernel, conv_bias, ln_gain, ln_bias, w_in, b_in, w_out, layer_scale, tissue
):
    image = features[0]
    upstream = cotangent[0]
    flags = tissue[0]
    height, breadth, channels = image.shape
    tiles = flags.shape[0]
    padded = extended(image, (("tile", 1),), 3)
    padded = jnp.pad(padded, ((3, 3), (0, 0), (0, 0)))
    conv_out = depthwise(padded, kernel, height, breadth) + conv_bias
    column_gate = jnp.broadcast_to(flags.astype(jnp.float32)[:, None], (tiles, TILE_SIDE)).reshape(
        breadth
    )
    gate_rows = jnp.broadcast_to(column_gate[None, :], (height, breadth)).reshape(-1, 1)
    normed, hidden, out_grad, grad_pre, grad_conv = branch_back(
        conv_out.reshape(-1, channels),
        upstream.reshape(-1, channels),
        gate_rows,
        ln_gain,
        ln_bias,
        w_in,
        b_in,
        w_out,
        layer_scale,
    )
    grad_band = grad_conv.reshape(height, breadth, channels)
    positions = height * breadth * lax.axis_size("tile") * lax.axis_size("rep")
    scale = 1.0 / math.sqrt(positions)
    out_total = lax.psum(contract(hidden, out_grad), ("tile", "rep"))
    grad_w_out = (out_total * scale).astype(jnp.bfloat16)
    grad_w_in = lax.psum_scatter(
        contract(grad_pre, normed) * scale, ("tile", "rep"), scatter_dimension=0, tiled=True
    )
    grad_pad = extended(grad_band, (("tile", 1),), 3)
    grad_pad = jnp.pad(grad_pad, ((3, 3), (0, 0), (0, 0)))
    grad_image = (
        upstream.astype(jnp.float32) + transposed(grad_pad, kernel, height, breadth)
    ).astype(jnp.bfloat16)
    return (grad_image[None], grad_w_in, grad_w_out)


def solution(mesh):
    placed = (
        P("rep", None, "tile", None),
        P("rep", None, "tile", None),
        P(),
        P(),
        P(),
        P(),
        P(),
        P(),
        P(),
        P(),
        P("rep", "tile"),
    )
    return jax.shard_map(
        body,
        mesh=mesh,
        in_specs=placed,
        out_specs=(P("rep", None, "tile", None), P(("tile", "rep"), None), P()),
        check_vma=False,
    )
```

profile of v0, /device:TPU:1, one launch (start us, length us, event | category | flops | bytes accessed | tf_op | source)
XLA Modules:
  0.0 339.8 jit_solution(16033583256207704197)
XLA Ops:
  7.2 0.0 all-reduce.6.cloned.1.call-start
  7.2 1.0 fusion.124
  8.2 1.3 collective-permute-start.1
  9.5 4.7 %collective-permute-start = (bf16[8,3,384]{2,1,0:T(4,128)(2,1)S(1)}, bf16[8,3,384]{2,1,0:T(4,128)(2,1)S(1)}, u32[]{:S(2)}, u32[]{:S(2)}) collective-permute-start(bf16[8,3,384]{2,1,0:T(4,128)(2,1)S(1)} %get-tuple-element.60), channel_id=1, source_target_pairs={{0,4},{4,8},{8,12},{12,16},{16,20},{20,24},{24,28},{28,32},{32,36}... | collective-permute-start | bytes 55304 | tf_op jit(solution)/shard_map/ppermute | solution.py:19
  14.2 1.2 slice_reduce_fusion.48
  15.4 1.1 slice_reduce_fusion.47
  16.5 0.7 convert_bitcast_fusion
  17.2 0.1 broadcast_in_dim.8
  17.3 0.1 broadcast_in_dim.9
  17.4 0.1 mul.1038
  17.4 1.0 fusion.85
  18.5 1.0 slice_reduce_fusion.46
  19.5 1.0 fusion.22
  20.6 4.1 %fusion.122 = (f32[8,32]{1,0:T(8,128)S(1)}, f32[8,32,384]{2,1,0:T(8,128)S(1)}) fusion(f32[384]{0:T(512)} %param.14, f32[384]{0:T(512)S(1)} %get-tuple-element.52, bf16[14,38,384]{2,1,0:T(8,128)(2,1)S(1)} %fusion.22, f32[384]{0:T(512)S(1)} %get-tuple-element.53, f32[384]{0:T(512)S(1)} %get-tuple-element.6, f32[384]{0:T(512)S(1)} %get-tuple-element.7, ...), kind=kLoop, calls=%fused_computation.264 | loop fusion | flops 16318208 | bytes 8962048 | tf_op jit(solution)/shard_map/reduce_sum | solution.py:58
  24.7 0.1 div.16
  24.8 0.2 multiply_reduce_fusion.1
  25.0 0.1 rsqrt.12
  25.1 0.2 add_convert_fusion
  25.2 0.6 convolution_add_fusion
  25.8 5.0 %fusion.16 = f32[1536,384]{1,0:T(8,128)} fusion(bf16[256,384]{1,0:T(8,128)(2,1)S(1)} %fusion.85, f32[256,1536]{1,0:T(8,128)S(1)} %convolution_add_fusion), kind=kOutput, calls=%fused_computation.35 | convolution fusion | flops 327548928 | bytes 4128768 | tf_op jit(solution)/shard_map/dot_general | solution.py:52
  30.8 0.9 fusion
  31.7 2.1 convolution_multiply_fusion
  33.8 0.7 fusion.121
  34.5 0.2 subtract_multiply_fusion
  34.8 1.3 collective-permute-start.3
  36.1 4.0 %collective-permute-start.2 = (f32[8,3,384]{2,1,0:T(4,128)S(1)}, f32[8,3,384]{2,1,0:T(4,128)S(1)}, u32[]{:S(2)}, u32[]{:S(2)}) collective-permute-start(f32[8,3,384]{2,1,0:T(4,128)S(1)} %get-tuple-element.58), channel_id=1, source_target_pairs={{0,4},{4,8},{8,12},{12,16},{16,20},{20,24},{24,28},{28,32},{32,36}... | collective-permute-start | bytes 110600 | tf_op jit(solution)/shard_map/ppermute | solution.py:19
  40.1 1.1 collective-permute-done.2
  41.2 0.1 select_maximum_fusion
  41.3 3.6 %fusion.90 = bf16[1,8,32,384]{3,2,1,0:T(8,128)(2,1)} fusion(f32[384]{0:T(512)S(1)} %get-tuple-element.52, f32[14,38,384]{2,1,0:T(8,128)S(1)} %select_maximum_fusion, f32[384]{0:T(512)S(1)} %get-tuple-element.53, f32[384]{0:T(512)S(1)} %get-tuple-element.6, f32[384]{0:T(512)S(1)} %get-tuple-element.7, f32[384]{0:T(512)S(1)} %get-tuple-element.8, ...), kind=kLoop, calls=%fused_computation.177 | loop fusion | flops 10420224 | bytes 17450496 | tf_op jit(solution)/shard_map/broadcast_in_dim | solution.py:122
  44.9 283.8 %all-reduce.6.cloned.1.call-done = (f32[1536,384]{1,0:T(8,128)}, f32[1536,384]{1,0:T(8,128)}) async-done(((f32[1536,384]{1,0:T(8,128)}, f32[1536,384]{1,0:T(8,128)}), (f32[1536,384]{1,0:T(8,128)}, f32[1536,384]{1,0:T(8,128)})) %all-reduce.6.cloned.1.call-update) | async-done | bytes 4718608
  328.7 2.9 multiply_convert_fusion
  331.6 1.3 constant_dynamic-slice_fusion
  (23 shorter events, 0.1 us)
Async XLA Ops:
  7.2 18.1 %copy-start = (bf16[384,1536]{1,0:T(8,128)(2,1)S(1)}, bf16[384,1536]{1,0:T(8,128)(2,1)}, u32[]{:S(2)}) copy-start(bf16[384,1536]{1,0:T(8,128)(2,1)} %param.17) | copy-start | bytes 3538948
  7.2 13.3 %copy-start.1 = (bf16[1,8,32,384]{3,2,1,0:T(8,128)(2,1)S(1)}, bf16[1,8,32,384]{3,2,1,0:T(8,128)(2,1)}, u32[]{:S(2)}) copy-start(bf16[1,8,32,384]{3,2,1,0:T(8,128)(2,1)} %param.11) | copy-start | bytes 589828
  7.2 321.5 %all-reduce.6.cloned.1.call-start = ((), (), s32[]{:S(2)}) async-start(), calls=%async_computation | async-start | bytes 9437184
  8.2 11.2 %collective-permute-start.1 = (bf16[8,3,384]{2,1,0:T(4,128)(2,1)S(1)}, bf16[8,3,384]{2,1,0:T(4,128)(2,1)S(1)}, u32[]{:S(2)}, u32[]{:S(2)}) collective-permute-start(bf16[8,3,384]{2,1,0:T(4,128)(2,1)S(1)} %get-tuple-element.61), channel_id=1, source_target_pairs={{4,0},{8,4},{12,8},{16,12},{20,16},{24,20},{28,24},{32,28},{36,32}... | collective-permute-start | bytes 55304 | tf_op jit(solution)/shard_map/ppermute | solution.py:22
  9.5 10.0 %collective-permute-start = (bf16[8,3,384]{2,1,0:T(4,128)(2,1)S(1)}, bf16[8,3,384]{2,1,0:T(4,128)(2,1)S(1)}, u32[]{:S(2)}, u32[]{:S(2)}) collective-permute-start(bf16[8,3,384]{2,1,0:T(4,128)(2,1)S(1)} %get-tuple-element.60), channel_id=1, source_target_pairs={{0,4},{4,8},{8,12},{12,16},{16,20},{20,24},{24,28},{28,32},{32,36}... | collective-permute-start | bytes 55304 | tf_op jit(solution)/shard_map/ppermute | solution.py:19
  20.5 4.5 %copy-start.4 = (f32[384]{0:T(512)S(1)}, f32[384]{0:T(512)}, u32[]{:S(2)}) copy-start(f32[384]{0:T(512)} %param.15) | copy-start | bytes 4612
  20.5 4.5 %copy-start.5 = (f32[384]{0:T(512)S(1)}, f32[384]{0:T(512)}, u32[]{:S(2)}) copy-start(f32[384]{0:T(512)} %param.16) | copy-start | bytes 4612
  20.5 4.7 %copy-start.3 = (f32[1536]{0:T(1024)S(1)}, f32[1536]{0:T(1024)}, u32[]{:S(2)}) copy-start(f32[1536]{0:T(1024)} %param.18) | copy-start | bytes 18436
  25.8 5.0 %copy-start.6 = (bf16[1536,384]{1,0:T(8,128)(2,1)S(1)}, bf16[1536,384]{1,0:T(8,128)(2,1)}, u32[]{:S(2)}) copy-start(bf16[1536,384]{1,0:T(8,128)(2,1)} %param.19) | copy-start | bytes 3538948
  34.5 6.8 %copy-start.2 = (bf16[1,8,32,384]{3,2,1,0:T(8,128)(2,1)S(1)}, bf16[1,8,32,384]{3,2,1,0:T(8,128)(2,1)}, u32[]{:S(2)}) copy-start(bf16[1,8,32,384]{3,2,1,0:T(8,128)(2,1)} %param.12) | copy-start | bytes 589828
  34.8 5.3 %collective-permute-start.3 = (f32[8,3,384]{2,1,0:T(4,128)S(1)}, f32[8,3,384]{2,1,0:T(4,128)S(1)}, u32[]{:S(2)}, u32[]{:S(2)}) collective-permute-start(f32[8,3,384]{2,1,0:T(4,128)S(1)} %get-tuple-element.59), channel_id=1, source_target_pairs={{4,0},{8,4},{12,8},{16,12},{20,16},{24,20},{28,24},{32,28},{36,32}... | collective-permute-start | bytes 110600 | tf_op jit(solution)/shard_map/ppermute | solution.py:22
  36.1 5.2 %collective-permute-start.2 = (f32[8,3,384]{2,1,0:T(4,128)S(1)}, f32[8,3,384]{2,1,0:T(4,128)S(1)}, u32[]{:S(2)}, u32[]{:S(2)}) collective-permute-start(f32[8,3,384]{2,1,0:T(4,128)S(1)} %get-tuple-element.58), channel_id=1, source_target_pairs={{0,4},{4,8},{8,12},{12,16},{16,20},{20,24},{24,28},{28,32},{32,36}... | collective-permute-start | bytes 110600 | tf_op jit(solution)/shard_map/ppermute | solution.py:19
Sparse Core Ops, SparseCore 0:
  33.9 294.7 all-reduce.5
where the time goes:
time: 341 us; the launch traced here: 340 us
  waiting for transfers between devices  285 us (84%)
  between operations  14.3 us (4%)
  other arithmetic  14 us (4%)
  starting transfers between devices  11.3 us (3%)
  matrix products  9.2 us (3%)
  local copies, waits for them, and re-layouts  6.08 us (2%)
    unnamed x2, waiting for transfers between devices  284 us
    ppermute x2, starting transfers between devices, extended(): lax.ppermute(lax.slice_in_dim(block, block.shape[dim] - width, None, axis...  8.65 us
    dot_general x2, matrix products, contract(): lax.dot_general(left, right, (((0,), (0,)), ((), ())), preferred_element_...  7.05 us
  transfers between devices with their start and end apart: 5, of which 2 were waited for; matrix products, arithmetic and copies ran while one was open for 3% of the time, Pallas kernels for 0%

commit v1 on v0

--- a/solution.py
+++ b/solution.py
@@ -80,6 +80,54 @@
     return (normed, hidden, out_grad, grad_pre, grad_conv)
 
 
+TILE = ("zh", "x", "y")
+RING = ("zh", "y", "zl")
+EVERY = ("zh", "x", "y", "zl", "c")
+SWAP = [(0, 1), (1, 0)]
+
+
+def from_core(total):
+    core = lax.axis_index("c")
+    half = total.shape[0] // 2
+    sent = lax.dynamic_slice_in_dim(total, (1 - core) * half, half).astype(jnp.bfloat16)
+    kept = lax.dynamic_slice_in_dim(total, core * half, half)
+    return kept + lax.ppermute(sent, "c", SWAP).astype(jnp.float32)
+
+
+def scatter_sum(total, axes, count):
+    rows = total.shape[0] // count
+    blocks = total.astype(jnp.bfloat16).reshape(count, rows, total.shape[1])
+    blocks = lax.all_to_all(blocks, axes, split_axis=0, concat_axis=0, tiled=True)
+    return jnp.sum(blocks.astype(jnp.float32), axis=0)
+
+
+def gather(block, axes, count):
+    blocks = jnp.broadcast_to(block[None], (count,) + block.shape)
+    blocks = lax.all_to_all(blocks, axes, split_axis=0, concat_axis=0, tiled=True)
+    return blocks.reshape(count * block.shape[0], block.shape[1])
+
+
+def both_cores(half):
+    core = lax.axis_index("c")
+    rows = half.shape[0]
+    other = lax.ppermute(half, "c", SWAP)
+    whole = jnp.zeros((2 * rows, half.shape[1]), half.dtype)
+    whole = lax.dynamic_update_slice_in_dim(whole, half, core * rows, 0)
+    return lax.dynamic_update_slice_in_dim(whole, other, (1 - core) * rows, 0)
+
+
+def owners(sizes):
+    zh_n, x_n, y_n, zl_n, c_n = sizes
+    pairs = []
+    for source in range(zh_n * x_n * y_n * zl_n * c_n):
+        rest, c = divmod(source, c_n)
+        rest, zl = divmod(rest, zl_n)
+        rest, y = divmod(rest, y_n)
+        zh, x = divmod(rest, x_n)
+        pairs.append((source, (((c * x_n + x) * zh_n + zh) * y_n + y) * zl_n + zl))
+    return pairs
+
+
 def body(
     features, cotangent, kernel, conv_bias, ln_gain, ln_bias, w_in, b_in, w_out, layer_scale, tissue
 ):
@@ -88,7 +136,7 @@
     flags = tissue[0]
     height, breadth, channels = image.shape
     tiles = flags.shape[0]
-    padded = extended(image, (("tile", 1),), 3)
+    padded = extended(image, ((TILE, 1),), 3)
     padded = jnp.pad(padded, ((3, 3), (0, 0), (0, 0)))
     conv_out = depthwise(padded, kernel, height, breadth) + conv_bias
     column_gate = jnp.broadcast_to(flags.astype(jnp.float32)[:, None], (tiles, TILE_SIDE)).reshape(
@@ -107,14 +155,17 @@
         layer_scale,
     )
     grad_band = grad_conv.reshape(height, breadth, channels)
-    positions = height * breadth * lax.axis_size("tile") * lax.axis_size("rep")
-    scale = 1.0 / math.sqrt(positions)
-    out_total = lax.psum(contract(hidden, out_grad), ("tile", "rep"))
-    grad_w_out = (out_total * scale).astype(jnp.bfloat16)
-    grad_w_in = lax.psum_scatter(
-        contract(grad_pre, normed) * scale, ("tile", "rep"), scatter_dimension=0, tiled=True
-    )
-    grad_pad = extended(grad_band, (("tile", 1),), 3)
+    sizes = [lax.axis_size(axis) for axis in EVERY]
+    ring = sizes[0] * sizes[2] * sizes[3]
+    scale = 1.0 / math.sqrt(height * breadth * math.prod(sizes))
+    out_total = scatter_sum(from_core(contract(hidden, out_grad)), "x", sizes[1])
+    out_total = scatter_sum(out_total, RING, ring)
+    grad_w_out = gather((out_total * scale).astype(jnp.bfloat16), RING, ring)
+    grad_w_out = both_cores(gather(grad_w_out, "x", sizes[1]))
+    in_total = scatter_sum(from_core(contract(grad_pre, normed)), "x", sizes[1])
+    in_total = scatter_sum(in_total, RING, ring)
+    grad_w_in = lax.ppermute(in_total * scale, EVERY, owners(sizes))
+    grad_pad = extended(grad_band, ((TILE, 1),), 3)
     grad_pad = jnp.pad(grad_pad, ((3, 3), (0, 0), (0, 0)))
     grad_image = (
         upstream.astype(jnp.float32) + transposed(grad_pad, kernel, height, breadth)
@@ -123,23 +174,14 @@
 
 
 def solution(mesh):
-    placed = (
-        P("rep", None, "tile", None),
-        P("rep", None, "tile", None),
-        P(),
-        P(),
-        P(),
-        P(),
-        P(),
-        P(),
-        P(),
-        P(),
-        P("rep", "tile"),
-    )
+    devices = mesh.devices.reshape(4, 4, 8, 2, 2)
+    fine = jax.sharding.Mesh(devices, EVERY)
+    band = P(("zl", "c"), None, TILE, None)
+    placed = (band, band) + (P(),) * 8 + (P(("zl", "c"), TILE),)
     return jax.shard_map(
         body,
-        mesh=mesh,
+        mesh=fine,
         in_specs=placed,
-        out_specs=(P("rep", None, "tile", None), P(("tile", "rep"), None), P()),
+        out_specs=(band, P(EVERY, None), P()),
         check_vma=False,
     )

time: 341 us -> 152 us (0.45)
  waiting for transfers between devices: 285 us -> 29.7 us
  starting transfers between devices: 11.3 us -> 71.3 us
  between operations: 14.3 us -> 1.73 us
  blocking collectives: 0 us -> 12 us
  local copies, waits for them, and re-layouts: 6.08 us -> 13.5 us
    unnamed x2 -> x0, waiting for transfers between devices: 284 us -> none
    all_to_all x0 -> x5, starting transfers between devices: none -> 31.7 us  [the longest x3 22.8 us: scatter_sum(): lax.all_to_all(blocks, axes, split_axis=0, concat_axis=0, tiled=True)]
    all_to_all x0 -> x5, waiting for transfers between devices: none -> 29.6 us  [the longest x3 20 us: scatter_sum(): lax.all_to_all(blocks, axes, split_axis=0, concat_axis=0, tiled=True)]
    ppermute x0 -> x4, starting transfers between devices: none -> 28.3 us  [the longest x1 15.8 us: body(): grad_w_in = lax.ppermute(in_total * scale, EVERY, owners(sizes))]
    all_to_all x0 -> x1, blocking collectives: none -> 12 us  [scatter_sum(): lax.all_to_all(blocks, axes, split_axis=0, concat_axis=0, tiled=True)]
  transfers between devices with their start and end apart: 5 -> 13, of which waited for: 2 -> 4; matrix products, arithmetic and copies ran while one was open for 3% -> 14% of each run, Pallas kernels for 0% -> 0%
where the time goes in v1:
time: 152 us; the launch traced here: 151 us
  starting transfers between devices  71.3 us (47%)
  waiting for transfers between devices  29.7 us (20%)
  other arithmetic  15.5 us (10%)
  local copies, waits for them, and re-layouts  13.5 us (9%)
  blocking collectives  12 us (8%)
  matrix products  7.05 us (5%)
  between operations  1.73 us (1%)
    all_to_all x3, starting transfers between devices, scatter_sum(): lax.all_to_all(blocks, axes, split_axis=0, concat_axis=0, tiled=True)  22.8 us
    all_to_all x3, waiting for transfers between devices, scatter_sum(): lax.all_to_all(blocks, axes, split_axis=0, concat_axis=0, tiled=True)  20 us
    ppermute x1, starting transfers between devices, body(): grad_w_in = lax.ppermute(in_total * scale, EVERY, owners(sizes))  15.8 us
    all_to_all x1, blocking collectives, scatter_sum(): lax.all_to_all(blocks, axes, split_axis=0, concat_axis=0, tiled=True)  12 us
    ppermute x2, starting transfers between devices, from_core(): return kept + lax.ppermute(sent, 'c', SWAP).astype(jnp.float32)  10.6 us
    all_to_all x2, waiting for transfers between devices, gather(): lax.all_to_all(blocks, axes, split_axis=0, concat_axis=0, tiled=True)  9.64 us
    all_to_all x2, starting transfers between devices, gather(): lax.all_to_all(blocks, axes, split_axis=0, concat_axis=0, tiled=True)  8.92 us
    ppermute x2, starting transfers between devices, extended(): lax.ppermute(lax.slice_in_dim(block, block.shape[dim] - width, None, axis...  8.65 us
  transfers between devices with their start and end apart: 13, of which 4 were waited for; matrix products, arithmetic and copies ran while one was open for 14% of the time, Pallas kernels for 0%

profile of v1, /device:TPU:1, one launch (start us, length us, event | category | flops | bytes accessed | tf_op | source)
XLA Modules:
  0.0 150.7 jit_solution(17266645119449453012)
XLA Ops:
  0.7 1.0 fusion.124
  1.6 1.3 collective-permute-start.1
  2.9 4.7 %collective-permute-start = (bf16[8,3,384]{2,1,0:T(4,128)(2,1)S(1)}, bf16[8,3,384]{2,1,0:T(4,128)(2,1)S(1)}, u32[]{:S(2)}, u32[]{:S(2)}) collective-permute-start(bf16[8,3,384]{2,1,0:T(4,128)(2,1)S(1)} %get-tuple-element.58), channel_id=1, source_target_pairs={{0,4},{4,8},{8,12},{12,16},{16,20},{20,24},{24,28},{28,32},{32,36}... | collective-permute-start | bytes 55304 | tf_op jit(solution)/shard_map/ppermute | solution.py:19
  7.6 1.3 slice_reduce_fusion.48
  9.0 1.3 slice_reduce_fusion.47
  11.4 1.0 fusion.85
  12.4 1.6 %slice_reduce_fusion.46 = (f32[384]{0:T(512)S(1)}, f32[384]{0:T(512)S(1)}, f32[384]{0:T(512)S(1)}, f32[384]{0:T(512)S(1)}, f32[384]{0:T(512)S(1)}, /*index=5*/f3...) fusion(f32[7,7,384]{2,1,0:T(8,128)} %param.13), kind=kLoop, calls=%fused_computation.234 | loop fusion | bytes 33792 | tf_op jit(solution)/shard_map/slice | solution.py:32
  14.0 1.0 fusion.22
  15.1 4.0 %fusion.122 = (f32[8,32]{1,0:T(8,128)S(1)}, f32[8,32,384]{2,1,0:T(8,128)S(1)}) fusion(f32[384]{0:T(512)} %param.14, f32[384]{0:T(512)} %get-tuple-element.52, bf16[14,38,384]{2,1,0:T(8,128)(2,1)S(1)} %fusion.22, f32[384]{0:T(512)} %get-tuple-element.53, f32[384]{0:T(512)S(1)} %get-tuple-element.6, f32[384]{0:T(512)S(1)} %get-tuple-element.7, ...), kind=kLoop, calls=%fused_computation.271 | loop fusion | flops 16318208 | bytes 8962048 | tf_op jit(solution)/shard_map/reduce_sum | solution.py:58
  20.7 4.3 %fusion.16 = f32[1536,384]{1,0:T(8,128)S(1)} fusion(bf16[256,384]{1,0:T(8,128)(2,1)S(1)} %fusion.85, f32[256,1536]{1,0:T(8,128)S(1)} %convolution_add_fusion), kind=kOutput, calls=%fused_computation.37 | convolution fusion | flops 327548928 | bytes 4128768 | tf_op jit(solution)/shard_map/dot_general | solution.py:52
  25.1 8.7 %collective-permute-start.6 = (bf16[768,384]{1,0:T(8,128)(2,1)S(1)}, bf16[768,384]{1,0:T(8,128)(2,1)S(1)}, u32[]{:S(2)}, u32[]{:S(2)}) collective-permute-start(bf16[768,384]{1,0:T(8,128)(2,1)S(1)} %dynamic-slice_convert_fusion), channel_id=1, source_target_pairs={{0,1},{1,0},{2,3},{3,2},{4,5},{5,4},{6,7},{7,6},{8,9},{9,8},{10,11... | collective-permute-start | bytes 1769480 | tf_op jit(solution)/shard_map/ppermute | solution.py:94
  35.2 1.4 copy-done.1
  36.7 0.9 dynamic-slice_convert_fusion.1
  37.5 1.9 %collective-permute-start.4 = (bf16[768,384]{1,0:T(8,128)(2,1)}, bf16[768,384]{1,0:T(8,128)(2,1)}, u32[]{:S(2)}, u32[]{:S(2)}) collective-permute-start(bf16[768,384]{1,0:T(8,128)(2,1)} %dynamic-slice_convert_fusion.1), channel_id=1, source_target_pairs={{0,1},{1,0},{2,3},{3,2},{4,5},{5,4},{6,7},{7,6},{8,9},{9,8},{10,11... | collective-permute-start | bytes 1769480 | tf_op jit(solution)/shard_map/ppermute | solution.py:94
  39.6 12.0 %all_to_all.30 = bf16[4,192,384]{2,1,0:T(8,128)(2,1)S(1)} all-to-all(bf16[4,192,384]{2,1,0:T(8,128)(2,1)S(1)} %bitcast.41), channel_id=1, replica_groups=mesh['zh'=4,'x'=4,'y'=8,'zl'=2,'c'=2] {'x'}, dimensions={0} | all-to-all | bytes 1179648 | tf_op jit(solution)/shard_map/all_to_all | solution.py:100
  52.4 14.7 %all-to-all-start.3 = ((bf16[64,3,384]{2,1,0:T(4,128)(2,1)}), bf16[64,3,384]{2,1,0:T(4,128)(2,1)S(1)}, u32[]{:S(2)}, u32[]{:S(2)}) async-start(bf16[64,3,384]{2,1,0:T(4,128)(2,1)} %reshape.95), calls=%async_computation.3 | async-start | bytes 393216 | tf_op jit(solution)/shard_map/all_to_all | solution.py:100
  67.2 2.4 %add_convert_fusion.1 = bf16[768,384]{1,0:T(8,128)(2,1)} fusion(bf16[768,384]{1,0:T(8,128)(2,1)} %collective-permute-done.4, f32[1536,384]{1,0:T(8,128)} %copy-done.1, s32[]{:T(128)S(6)} %select_n.4), kind=kLoop, calls=%fused_computation.32 | loop fusion | flops 884736 | bytes 2359300 | tf_op jit(solution)/shard_map/convert_element_type | solution.py:99
  69.6 8.9 %all-to-all-done.3 = bf16[64,3,384]{2,1,0:T(4,128)(2,1)S(1)} async-done(((bf16[64,3,384]{2,1,0:T(4,128)(2,1)}), bf16[64,3,384]{2,1,0:T(4,128)(2,1)S(1)}, u32[]{:S(2)}, u32[]{:S(2)}) %all-to-all-start.3) | async-done | bytes 147488 | tf_op jit(solution)/shard_map/all_to_all | solution.py:100
  78.5 3.5 %all-to-all-start = ((bf16[4,192,384]{2,1,0:T(8,128)(2,1)}), bf16[4,192,384]{2,1,0:T(8,128)(2,1)S(1)}, u32[]{:S(2)}, u32[]{:S(2)}) async-start(bf16[4,192,384]{2,1,0:T(8,128)(2,1)} %bitcast.7), calls=%async_computation | async-start | bytes 1179648 | tf_op jit(solution)/shard_map/all_to_all | solution.py:100
  82.1 7.1 %all-to-all-done = bf16[4,192,384]{2,1,0:T(8,128)(2,1)S(1)} async-done(((bf16[4,192,384]{2,1,0:T(8,128)(2,1)}), bf16[4,192,384]{2,1,0:T(8,128)(2,1)S(1)}, u32[]{:S(2)}, u32[]{:S(2)}) %all-to-all-start) | async-done | bytes 589856 | tf_op jit(solution)/shard_map/all_to_all | solution.py:100
  89.9 5.4 %all-to-all-start.4 = ((bf16[64,3,384]{2,1,0:T(4,128)(2,1)}), bf16[64,3,384]{2,1,0:T(4,128)(2,1)}, u32[]{:S(2)}, u32[]{:S(2)}) async-start(bf16[64,3,384]{2,1,0:T(4,128)(2,1)} %broadcast_in_dim.21), calls=%async_computation.4 | async-start | bytes 393216 | tf_op jit(solution)/shard_map/all_to_all | solution.py:106
  97.0 9.6 %all-to-all-done.4 = bf16[64,3,384]{2,1,0:T(4,128)(2,1)} async-done(((bf16[64,3,384]{2,1,0:T(4,128)(2,1)}), bf16[64,3,384]{2,1,0:T(4,128)(2,1)}, u32[]{:S(2)}, u32[]{:S(2)}) %all-to-all-start.4) | async-done | bytes 147488 | tf_op jit(solution)/shard_map/all_to_all | solution.py:106
  106.6 4.6 %all-to-all-start.1 = ((bf16[64,3,384]{2,1,0:T(4,128)(2,1)}), bf16[64,3,384]{2,1,0:T(4,128)(2,1)S(1)}, u32[]{:S(2)}, u32[]{:S(2)}) async-start(bf16[64,3,384]{2,1,0:T(4,128)(2,1)} %reshape.93), calls=%async_computation.1 | async-start | bytes 393216 | tf_op jit(solution)/shard_map/all_to_all | solution.py:100
  111.3 0.9 subtract_multiply_fusion
  112.2 1.3 collective-permute-start.3
  113.5 4.0 %collective-permute-start.2 = (f32[8,3,384]{2,1,0:T(4,128)S(1)}, f32[8,3,384]{2,1,0:T(4,128)S(1)}, u32[]{:S(2)}, u32[]{:S(2)}) collective-permute-start(f32[8,3,384]{2,1,0:T(4,128)S(1)} %get-tuple-element.56), channel_id=1, source_target_pairs={{0,4},{4,8},{8,12},{12,16},{16,20},{20,24},{24,28},{28,32},{32,36}... | collective-permute-start | bytes 110600 | tf_op jit(solution)/shard_map/ppermute | solution.py:19
  117.5 1.1 broadcast_in_dim.22
  118.6 3.9 %all-to-all-done.1 = bf16[64,3,384]{2,1,0:T(4,128)(2,1)S(1)} async-done(((bf16[64,3,384]{2,1,0:T(4,128)(2,1)}), bf16[64,3,384]{2,1,0:T(4,128)(2,1)S(1)}, u32[]{:S(2)}, u32[]{:S(2)}) %all-to-all-start.1) | async-done | bytes 147488 | tf_op jit(solution)/shard_map/all_to_all | solution.py:100
  123.4 3.5 %all-to-all-start.5 = ((bf16[4,192,384]{2,1,0:T(8,128)(2,1)}), bf16[4,192,384]{2,1,0:T(8,128)(2,1)S(1)}, u32[]{:S(2)}, u32[]{:S(2)}) async-start(bf16[4,192,384]{2,1,0:T(8,128)(2,1)} %broadcast_in_dim.23), calls=%async_computation.5 | async-start | bytes 1179648 | tf_op jit(solution)/shard_map/all_to_all | solution.py:106
  127.1 15.8 %collective-permute-start.5 = (f32[3,384]{1,0:T(4,128)S(1)}, f32[3,384]{1,0:T(4,128)S(1)}, u32[]{:S(2)}, u32[]{:S(2)}) collective-permute-start(f32[3,384]{1,0:T(4,128)S(1)} %broadcast_multiply_fusion), channel_id=1, source_target_pairs={{0,0},{1,256},{2,1},{3,257},{4,2},{5,258},{6,3},{7,259},{8,4},{9,2... | collective-permute-start | bytes 13832 | tf_op jit(solution)/shard_map/ppermute | solution.py:167
  142.9 1.9 %collective-permute-start.7 = (bf16[768,384]{1,0:T(8,128)(2,1)S(1)}, bf16[768,384]{1,0:T(8,128)(2,1)S(1)}, u32[]{:S(2)}, u32[]{:S(2)}) collective-permute-start(bf16[768,384]{1,0:T(8,128)(2,1)S(1)} %bitcast.42), channel_id=1, source_target_pairs={{0,1},{1,0},{2,3},{3,2},{4,5},{5,4},{6,7},{7,6},{8,9},{9,8},{10,11... | collective-permute-start | bytes 1769480 | tf_op jit(solution)/shard_map/ppermute | solution.py:113
  144.9 4.4 %fusion.90 = bf16[1,8,32,384]{3,2,1,0:T(8,128)(2,1)} fusion(f32[384]{0:T(512)} %get-tuple-element.52, f32[14,38,384]{2,1,0:T(8,128)S(1)} %select_maximum_fusion, f32[384]{0:T(512)} %get-tuple-element.53, f32[384]{0:T(512)S(1)} %get-tuple-element.6, f32[384]{0:T(512)S(1)} %get-tuple-element.7, f32[384]{0:T(512)S(1)} %get-tuple-element.8, ...), kind=kLoop, calls=%fused_computation.181 | loop fusion | flops 10420224 | bytes 17450496 | tf_op jit(solution)/shard_map/broadcast_in_dim | solution.py:173
  (150 shorter events, 9.6 us)
Async XLA Ops:
  0.6 19.4 %copy-start = (bf16[384,1536]{1,0:T(8,128)(2,1)S(1)}, bf16[384,1536]{1,0:T(8,128)(2,1)}, u32[]{:S(2)}) copy-start(bf16[384,1536]{1,0:T(8,128)(2,1)} %param.17) | copy-start | bytes 3538948
  0.6 14.4 %copy-start.3 = (bf16[1,8,32,384]{3,2,1,0:T(8,128)(2,1)S(1)}, bf16[1,8,32,384]{3,2,1,0:T(8,128)(2,1)}, u32[]{:S(2)}) copy-start(bf16[1,8,32,384]{3,2,1,0:T(8,128)(2,1)} %param.11) | copy-start | bytes 589828
  1.6 12.4 %collective-permute-start.1 = (bf16[8,3,384]{2,1,0:T(4,128)(2,1)S(1)}, bf16[8,3,384]{2,1,0:T(4,128)(2,1)S(1)}, u32[]{:S(2)}, u32[]{:S(2)}) collective-permute-start(bf16[8,3,384]{2,1,0:T(4,128)(2,1)S(1)} %get-tuple-element.59), channel_id=1, source_target_pairs={{4,0},{8,4},{12,8},{16,12},{20,16},{24,20},{28,24},{32,28},{36,32}... | collective-permute-start | bytes 55304 | tf_op jit(solution)/shard_map/ppermute | solution.py:22
  2.9 11.1 %collective-permute-start = (bf16[8,3,384]{2,1,0:T(4,128)(2,1)S(1)}, bf16[8,3,384]{2,1,0:T(4,128)(2,1)S(1)}, u32[]{:S(2)}, u32[]{:S(2)}) collective-permute-start(bf16[8,3,384]{2,1,0:T(4,128)(2,1)S(1)} %get-tuple-element.58), channel_id=1, source_target_pairs={{0,4},{4,8},{8,12},{12,16},{16,20},{20,24},{24,28},{28,32},{32,36}... | collective-permute-start | bytes 55304 | tf_op jit(solution)/shard_map/ppermute | solution.py:19
  8.9 10.3 %copy-start.5 = (f32[384]{0:T(512)}, f32[384]{0:T(512)S(1)}, u32[]{:S(2)}) copy-start(f32[384]{0:T(512)S(1)} %get-tuple-element.9) | copy-start | bytes 4612
  8.9 10.3 %copy-start.7 = (f32[384]{0:T(512)}, f32[384]{0:T(512)S(1)}, u32[]{:S(2)}) copy-start(f32[384]{0:T(512)S(1)} %get-tuple-element.10) | copy-start | bytes 4612
  8.9 10.3 %copy-start.9 = (f32[384]{0:T(512)}, f32[384]{0:T(512)S(1)}, u32[]{:S(2)}) copy-start(f32[384]{0:T(512)S(1)} %get-tuple-element.11) | copy-start | bytes 4612
  8.9 10.3 %copy-start.11 = (f32[384]{0:T(512)}, f32[384]{0:T(512)S(1)}, u32[]{:S(2)}) copy-start(f32[384]{0:T(512)S(1)} %get-tuple-element.12) | copy-start | bytes 4612
  8.9 10.3 %copy-start.13 = (f32[384]{0:T(512)}, f32[384]{0:T(512)S(1)}, u32[]{:S(2)}) copy-start(f32[384]{0:T(512)S(1)} %get-tuple-element.13) | copy-start | bytes 4612
  8.9 10.3 %copy-start.14 = (f32[384]{0:T(512)}, f32[384]{0:T(512)S(1)}, u32[]{:S(2)}) copy-start(f32[384]{0:T(512)S(1)} %get-tuple-element.14) | copy-start | bytes 4612
  8.9 10.3 %copy-start.15 = (f32[384]{0:T(512)}, f32[384]{0:T(512)S(1)}, u32[]{:S(2)}) copy-start(f32[384]{0:T(512)S(1)} %get-tuple-element.15) | copy-start | bytes 4612
  8.9 10.3 %copy-start.16 = (f32[384]{0:T(512)}, f32[384]{0:T(512)S(1)}, u32[]{:S(2)}) copy-start(f32[384]{0:T(512)S(1)} %get-tuple-element.16) | copy-start | bytes 4612
  8.9 10.3 %copy-start.17 = (f32[384]{0:T(512)}, f32[384]{0:T(512)S(1)}, u32[]{:S(2)}) copy-start(f32[384]{0:T(512)S(1)} %get-tuple-element.17) | copy-start | bytes 4612
  19.6 75.8 %copy-start.48 = (f32[256]{0:T(256)}, f32[256]{0:T(256)S(1)}, u32[]{:S(2)}) copy-start(f32[256]{0:T(256)S(1)} %div.16) | copy-start | bytes 3076
  19.9 75.5 %copy-start.49 = (f32[256]{0:T(256)}, f32[256]{0:T(256)S(1)}, u32[]{:S(2)}) copy-start(f32[256]{0:T(256)S(1)} %rsqrt.12) | copy-start | bytes 3076
  20.7 13.1 %copy-start.53 = (bf16[1536,384]{1,0:T(8,128)(2,1)S(1)}, bf16[1536,384]{1,0:T(8,128)(2,1)}, u32[]{:S(2)}) copy-start(bf16[1536,384]{1,0:T(8,128)(2,1)} %param.19) | copy-start | bytes 3538948
  25.1 14.4 %collective-permute-start.6 = (bf16[768,384]{1,0:T(8,128)(2,1)S(1)}, bf16[768,384]{1,0:T(8,128)(2,1)S(1)}, u32[]{:S(2)}, u32[]{:S(2)}) collective-permute-start(bf16[768,384]{1,0:T(8,128)(2,1)S(1)} %dynamic-slice_convert_fusion), channel_id=1, source_target_pairs={{0,1},{1,0},{2,3},{3,2},{4,5},{5,4},{6,7},{7,6},{8,9},{9,8},{10,11... | collective-permute-start | bytes 1769480 | tf_op jit(solution)/shard_map/ppermute | solution.py:94
  37.5 29.6 %collective-permute-start.4 = (bf16[768,384]{1,0:T(8,128)(2,1)}, bf16[768,384]{1,0:T(8,128)(2,1)}, u32[]{:S(2)}, u32[]{:S(2)}) collective-permute-start(bf16[768,384]{1,0:T(8,128)(2,1)} %dynamic-slice_convert_fusion.1), channel_id=1, source_target_pairs={{0,1},{1,0},{2,3},{3,2},{4,5},{5,4},{6,7},{7,6},{8,9},{9,8},{10,11... | collective-permute-start | bytes 1769480 | tf_op jit(solution)/shard_map/ppermute | solution.py:94
  52.4 26.1 %all-to-all-start.3 = ((bf16[64,3,384]{2,1,0:T(4,128)(2,1)}), bf16[64,3,384]{2,1,0:T(4,128)(2,1)S(1)}, u32[]{:S(2)}, u32[]{:S(2)}) async-start(bf16[64,3,384]{2,1,0:T(4,128)(2,1)} %reshape.95), calls=%async_computation.3 | async-start | bytes 393216 | tf_op jit(solution)/shard_map/all_to_all | solution.py:100
  78.5 10.7 %all-to-all-start = ((bf16[4,192,384]{2,1,0:T(8,128)(2,1)}), bf16[4,192,384]{2,1,0:T(8,128)(2,1)S(1)}, u32[]{:S(2)}, u32[]{:S(2)}) async-start(bf16[4,192,384]{2,1,0:T(8,128)(2,1)} %bitcast.7), calls=%async_computation | async-start | bytes 1179648 | tf_op jit(solution)/shard_map/all_to_all | solution.py:100
  89.9 16.7 %all-to-all-start.4 = ((bf16[64,3,384]{2,1,0:T(4,128)(2,1)}), bf16[64,3,384]{2,1,0:T(4,128)(2,1)}, u32[]{:S(2)}, u32[]{:S(2)}) async-start(bf16[64,3,384]{2,1,0:T(4,128)(2,1)} %broadcast_in_dim.21), calls=%async_computation.4 | async-start | bytes 393216 | tf_op jit(solution)/shard_map/all_to_all | solution.py:106
  106.6 15.9 %all-to-all-start.1 = ((bf16[64,3,384]{2,1,0:T(4,128)(2,1)}), bf16[64,3,384]{2,1,0:T(4,128)(2,1)S(1)}, u32[]{:S(2)}, u32[]{:S(2)}) async-start(bf16[64,3,384]{2,1,0:T(4,128)(2,1)} %reshape.93), calls=%async_computation.1 | async-start | bytes 393216 | tf_op jit(solution)/shard_map/all_to_all | solution.py:100
  112.2 14.7 %collective-permute-start.3 = (f32[8,3,384]{2,1,0:T(4,128)S(1)}, f32[8,3,384]{2,1,0:T(4,128)S(1)}, u32[]{:S(2)}, u32[]{:S(2)}) collective-permute-start(f32[8,3,384]{2,1,0:T(4,128)S(1)} %get-tuple-element.57), channel_id=1, source_target_pairs={{4,0},{8,4},{12,8},{16,12},{20,16},{24,20},{28,24},{32,28},{36,32}... | collective-permute-start | bytes 110600 | tf_op jit(solution)/shard_map/ppermute | solution.py:22
  113.5 13.4 %collective-permute-start.2 = (f32[8,3,384]{2,1,0:T(4,128)S(1)}, f32[8,3,384]{2,1,0:T(4,128)S(1)}, u32[]{:S(2)}, u32[]{:S(2)}) collective-permute-start(f32[8,3,384]{2,1,0:T(4,128)S(1)} %get-tuple-element.56), channel_id=1, source_target_pairs={{0,4},{4,8},{8,12},{12,16},{16,20},{20,24},{24,28},{28,32},{32,36}... | collective-permute-start | bytes 110600 | tf_op jit(solution)/shard_map/ppermute | solution.py:19
  118.6 26.3 %copy-start.4 = (bf16[1,8,32,384]{3,2,1,0:T(8,128)(2,1)S(1)}, bf16[1,8,32,384]{3,2,1,0:T(8,128)(2,1)}, u32[]{:S(2)}) copy-start(bf16[1,8,32,384]{3,2,1,0:T(8,128)(2,1)} %param.12) | copy-start | bytes 589828
  118.6 26.3 %copy-start.6 = (f32[384]{0:T(512)S(1)}, f32[384]{0:T(512)}, u32[]{:S(2)}) copy-start(f32[384]{0:T(512)} %copy-done.5) | copy-start | bytes 4612
  118.6 26.3 %copy-start.8 = (f32[384]{0:T(512)S(1)}, f32[384]{0:T(512)}, u32[]{:S(2)}) copy-start(f32[384]{0:T(512)} %copy-done.7) | copy-start | bytes 4612
  118.6 26.3 %copy-start.10 = (f32[384]{0:T(512)S(1)}, f32[384]{0:T(512)}, u32[]{:S(2)}) copy-start(f32[384]{0:T(512)} %copy-done.9) | copy-start | bytes 4612
  118.6 26.3 %copy-start.12 = (f32[384]{0:T(512)S(1)}, f32[384]{0:T(512)}, u32[]{:S(2)}) copy-start(f32[384]{0:T(512)} %copy-done.11) | copy-start | bytes 4612
  123.4 19.5 %all-to-all-start.5 = ((bf16[4,192,384]{2,1,0:T(8,128)(2,1)}), bf16[4,192,384]{2,1,0:T(8,128)(2,1)S(1)}, u32[]{:S(2)}, u32[]{:S(2)}) async-start(bf16[4,192,384]{2,1,0:T(8,128)(2,1)} %broadcast_in_dim.23), calls=%async_computation.5 | async-start | bytes 1179648 | tf_op jit(solution)/shard_map/all_to_all | solution.py:106
  127.1 22.2 %collective-permute-start.5 = (f32[3,384]{1,0:T(4,128)S(1)}, f32[3,384]{1,0:T(4,128)S(1)}, u32[]{:S(2)}, u32[]{:S(2)}) collective-permute-start(f32[3,384]{1,0:T(4,128)S(1)} %broadcast_multiply_fusion), channel_id=1, source_target_pairs={{0,0},{1,256},{2,1},{3,257},{4,2},{5,258},{6,3},{7,259},{8,4},{9,2... | collective-permute-start | bytes 13832 | tf_op jit(solution)/shard_map/ppermute | solution.py:167
  142.9 6.6 %collective-permute-start.7 = (bf16[768,384]{1,0:T(8,128)(2,1)S(1)}, bf16[768,384]{1,0:T(8,128)(2,1)S(1)}, u32[]{:S(2)}, u32[]{:S(2)}) collective-permute-start(bf16[768,384]{1,0:T(8,128)(2,1)S(1)} %bitcast.42), channel_id=1, source_target_pairs={{0,1},{1,0},{2,3},{3,2},{4,5},{5,4},{6,7},{7,6},{8,9},{9,8},{10,11... | collective-permute-start | bytes 1769480 | tf_op jit(solution)/shard_map/ppermute | solution.py:113
  (35 other events, 276.9 us)

commit v2 on v1

v2 whole, which is shorter than its diff:
```python
import functools
import math

import jax
import jax.numpy as jnp
from jax import lax
from jax.experimental import pallas as pl
from jax.experimental.pallas import tpu as pltpu
from jax.sharding import PartitionSpec as P

SIDE = 8
HALO = 3
TAPS = 7
COLS = 32
LANES = 128
CHUNK = 32
EPSILON = 1e-06
VMEM_LIMIT = 48 * 1024 * 1024
NT = (((1,), (1,)), ((), ()))

TILE = ("zh", "x", "y")
RING = ("zh", "y", "zl")
EVERY = ("zh", "x", "y", "zl", "c")
SWAP = [(0, 1), (1, 0)]


def matmul(left, right, dims=(((1,), (0,)), ((), ()))):
    return lax.dot_general(left, right, dims, preferred_element_type=jnp.float32)


def shifted(column, a):
    move = a - HALO
    if move == 0:
        return column
    row = lax.broadcasted_iota(jnp.int32, column.shape, 0)
    inside = (row + move >= 0) & (row + move < SIDE)
    return jnp.where(inside, pltpu.roll(column, (-move) % SIDE, 0), 0.0)


def convolve(columns, taps, lanes, flip):
    count = len(columns) - 2 * HALO
    totals = [None] * count
    for a in range(TAPS):
        sums = [None] * count
        for e in range(TAPS):
            place = (TAPS - 1 - a) * TAPS + TAPS - 1 - e if flip else a * TAPS + e
            tap = taps[place : place + 1, lanes]
            for j in range(count):
                if columns[j + e] is None:
                    continue
                term = columns[j + e] * tap
                sums[j] = term if sums[j] is None else sums[j] + term
        for j in range(count):
            if sums[j] is None:
                continue
            moved = shifted(sums[j], a)
            totals[j] = moved if totals[j] is None else totals[j] + moved
    return totals


def lane_blocks(width):
    return [slice(start, start + LANES) for start in range(0, width, LANES)]


def widen(source, wide):
    for k, lanes in enumerate(lane_blocks(source.shape[1])):
        wide[k] = source[:, lanes].astype(jnp.float32)


def first_kernel(
    flags, features, cotangent, w_out, w_in, b_in, taps, scale,
    conv, out_grad, back, w_in_t, b_cols, wide
):
    width = features.shape[1]
    widen(cotangent, wide)
    rows = SIDE * SIDE
    for k, lanes in enumerate(lane_blocks(width)):
        for t in range(COLS // SIDE):
            gate = flags[t].astype(jnp.float32)
            tile = jnp.concatenate(
                [wide[k, pl.ds(t * SIDE + j, SIDE, stride=COLS), :] for j in range(SIDE)], axis=0
            )
            tile = (tile * scale[:, lanes] * gate).astype(jnp.bfloat16)
            out_grad[t * rows : (t + 1) * rows, lanes] = tile
    back[...] = matmul(w_out[...], out_grad[...], NT)
    widen(features, wide)
    for k, lanes in enumerate(lane_blocks(width)):
        for t in range(COLS // SIDE):
            columns = []
            for j in range(t * SIDE - HALO, (t + 1) * SIDE + HALO):
                inside = 0 <= j < COLS
                columns.append(wide[k, pl.ds(j, SIDE, stride=COLS), :] if inside else None)
            for j, total in enumerate(convolve(columns, taps, lanes, False)):
                start = (t * SIDE + j) * SIDE
                conv[start : start + SIDE, lanes] = total
    hidden = w_in.shape[1]
    for start in range(0, hidden, LANES):
        w_in_t[start : start + LANES, :] = w_in[:, start : start + LANES].T
        b_cols[start : start + LANES, :] = jnp.broadcast_to(
            b_in[:, start : start + LANES], (LANES, LANES)
        ).T


def second_kernel(
    core, conv, low, high, taps, conv_bias, gain, bias, w_in_t, b_cols, out_grad,
    kept, sent, standard, inverse, normed, preact, cdf, rows, low_wide, high_wide, hidden
):
    width = conv.shape[1]
    rows[...] = conv[...]
    widen(low, low_wide)
    widen(high, high_wide)
    for k, lanes in enumerate(lane_blocks(width)):
        near = [low_wide[k, pl.ds(j, SIDE, stride=HALO), :] for j in range(HALO)]
        for j, total in enumerate(convolve(near + [None] * (2 * HALO), taps, lanes, False)):
            rows[j * SIDE : (j + 1) * SIDE, lanes] += total
        near = [high_wide[k, pl.ds(j, SIDE, stride=HALO), :] for j in range(HALO)]
        for j, total in enumerate(convolve([None] * (2 * HALO) + near, taps, lanes, False)):
            start = (COLS - HALO + j) * SIDE
            rows[start : start + SIDE, lanes] += total
    conv_out = rows[...] + conv_bias[...]
    centre = conv_out - jnp.mean(conv_out, axis=-1, keepdims=True)
    scale = lax.rsqrt(jnp.mean(centre * centre, axis=-1, keepdims=True) + EPSILON)
    inverse[...] = jnp.broadcast_to(scale, inverse.shape)
    standard[...] = centre * scale
    normed[...] = (standard[...] * gain[...] + bias[...]).astype(jnp.bfloat16)
    preact[...] = matmul(w_in_t[...], normed[...], NT)

    def step(i, carry):
        part = pl.ds(pl.multiple_of(i * CHUNK, CHUNK), CHUNK)
        for lanes in lane_blocks(preact.shape[1]):
            z = preact[part, lanes] + b_cols[part, :]
            below = 0.5 * (1.0 + lax.erf(z * 0.7071067811865476))
            preact[part, lanes] = z
            cdf[part, lanes] = below
            hidden[part, lanes] = (z * below).astype(jnp.bfloat16)
        return carry

    lax.fori_loop(0, preact.shape[0] // CHUNK, step, 0, unroll=2)
    half = hidden.shape[0] // 2
    other = pl.ds(pl.multiple_of((1 - core[0]) * half, half), half)
    own = pl.ds(pl.multiple_of(core[0] * half, half), half)
    sent[...] = matmul(hidden[other, :], out_grad[...]).astype(jnp.bfloat16)
    kept[...] = matmul(hidden[own, :], out_grad[...])


def third_kernel(
    core, back, preact, cdf, w_in, normed, standard, inverse, gain,
    kept, sent, grad_conv, low, high, grad_pre
):
    def step(i, carry):
        part = pl.ds(pl.multiple_of(i * CHUNK, CHUNK), CHUNK)
        for lanes in lane_blocks(preact.shape[1]):
            z = preact[part, lanes]
            density = jnp.exp(-0.5 * z * z) * 0.3989422804014327
            slope = cdf[part, lanes] + z * density
            grad_pre[part, lanes] = (back[part, lanes] * slope).astype(jnp.bfloat16)
        return carry

    lax.fori_loop(0, preact.shape[0] // CHUNK, step, 0, unroll=2)
    half = grad_pre.shape[0] // 2
    other = pl.ds(pl.multiple_of((1 - core[0]) * half, half), half)
    own = pl.ds(pl.multiple_of(core[0] * half, half), half)
    grad_std = matmul(w_in[...], grad_pre[...]).T * gain[...]
    sent[...] = matmul(grad_pre[other, :], normed[...]).astype(jnp.bfloat16)
    kept[...] = matmul(grad_pre[own, :], normed[...])
    norm = standard[...]
    mean = jnp.mean(grad_std, axis=-1, keepdims=True)
    along = jnp.mean(grad_std * norm, axis=-1, keepdims=True)
    result = inverse[:, :1] * (grad_std - mean - norm * along)
    grad_conv[...] = result
    edge = HALO * SIDE
    low[...] = result[:edge, :]
    high[...] = result[result.shape[0] - edge :, :]


def last_kernel(grad_conv, low, high, taps, cotangent, grad_features, wide):
    for k, lanes in enumerate(lane_blocks(grad_conv.shape[1])):
        for t in range(COLS // SIDE):
            columns = []
            for j in range(t * SIDE - HALO, (t + 1) * SIDE + HALO):
                if j < 0:
                    source, place = low, j + HALO
                elif j >= COLS:
                    source, place = high, j - COLS
                else:
                    source, place = grad_conv, j
                columns.append(source[place * SIDE : (place + 1) * SIDE, lanes])
            for j, total in enumerate(convolve(columns, taps, lanes, True)):
                wide[k, pl.ds(t * SIDE + j, SIDE, stride=COLS), :] = total
        result = cotangent[:, lanes].astype(jnp.float32) + wide[k]
        grad_features[:, lanes] = result.astype(jnp.bfloat16)


def call(kernel, outs, scratch, scalars, arrays, flops, nbytes):
    in_specs = [pl.BlockSpec(memory_space=pltpu.SMEM)] * len(scalars)
    in_specs += [pl.BlockSpec(memory_space=pltpu.VMEM)] * len(arrays)
    return pl.pallas_call(
        kernel,
        out_shape=[jax.ShapeDtypeStruct(shape, kind) for shape, kind in outs],
        in_specs=in_specs,
        out_specs=[pl.BlockSpec(memory_space=pltpu.VMEM)] * len(outs),
        scratch_shapes=[pltpu.VMEM(shape, kind) for shape, kind in scratch],
        compiler_params=pltpu.CompilerParams(vmem_limit_bytes=VMEM_LIMIT),
        cost_estimate=pl.CostEstimate(flops=flops, bytes_accessed=nbytes, transcendentals=0),
    )(*scalars, *arrays)


def before_halos(flags, features, cotangent, w_out, w_in, b_in, taps, layer_scale):
    rows, width = features.shape
    hidden = w_out.shape[0]
    f32, b16 = jnp.float32, jnp.bfloat16
    return call(
        first_kernel,
        [((rows, width), f32), ((rows, width), b16), ((hidden, rows), f32), ((hidden, width), b16), ((hidden, LANES), f32)],
        [((width // LANES, rows, LANES), f32)],
        [flags],
        [features, cotangent, w_out, w_in, b_in[None], taps, layer_scale[None]],
        2 * rows * width * hidden, 8 * 1024 * 1024,
    )


def forward(core, conv, low, high, taps, conv_bias, gain, bias, w_in_t, b_cols, out_grad):
    rows, width = conv.shape
    hidden = w_in_t.shape[0]
    f32, b16 = jnp.float32, jnp.bfloat16
    return call(
        second_kernel,
        [((hidden // 2, width), f32), ((hidden // 2, width), b16), ((rows, width), f32), ((rows, LANES), f32),
         ((rows, width), b16), ((hidden, rows), f32), ((hidden, rows), f32)],
        [((rows, width), f32), ((width // LANES, HALO * SIDE, LANES), f32), ((width // LANES, HALO * SIDE, LANES), f32),
         ((hidden, rows), b16)],
        [core],
        [conv, low, high, taps, conv_bias[None], gain[None], bias[None], w_in_t, b_cols, out_grad],
        4 * rows * width * hidden, 8 * 1024 * 1024,
    )


def backward(core, back, preact, cdf, w_in, normed, standard, inverse, gain):
    rows, width = standard.shape
    hidden = back.shape[0]
    f32, b16 = jnp.float32, jnp.bfloat16
    return call(
        third_kernel,
        [((hidden // 2, width), f32), ((hidden // 2, width), b16), ((rows, width), f32),
         ((HALO * SIDE, width), f32), ((HALO * SIDE, width), f32)],
        [((hidden, rows), b16)],
        [core],
        [back, preact, cdf, w_in, normed, standard, inverse, gain[None]],
        4 * rows * width * hidden, 8 * 1024 * 1024,
    )


def to_features(grad_conv, low, high, taps, cotangent):
    rows, width = grad_conv.shape
    return call(
        last_kernel,
        [((rows, width), jnp.bfloat16)],
        [((width // LANES, rows, LANES), jnp.float32)],
        [],
        [grad_conv, low, high, taps, cotangent],
        2 * 49 * rows * width, 2 * 1024 * 1024,
    )[0]


def from_left(block):
    count = lax.axis_size(TILE)
    return lax.ppermute(block, TILE, [(i, i + 1) for i in range(count - 1)])


def from_right(block):
    count = lax.axis_size(TILE)
    return lax.ppermute(block, TILE, [(i + 1, i) for i in range(count - 1)])


def core_sum(kept, sent):
    return kept + lax.ppermute(sent, "c", SWAP).astype(jnp.float32)


def exchange(blocks, axes):
    return lax.all_to_all(blocks, axes, split_axis=0, concat_axis=0, tiled=True)


def in_blocks(total, count):
    rows, width = total.shape
    return total.astype(jnp.bfloat16).reshape(count, rows // count, width)


def added(blocks):
    return jnp.sum(blocks.astype(jnp.float32), axis=0)


def copies(block, count):
    return jnp.broadcast_to(block[None], (count,) + block.shape)


def joined(blocks):
    return blocks.reshape(-1, blocks.shape[-1])


def both_cores(half):
    core = lax.axis_index("c")
    rows, width = half.shape
    other = lax.ppermute(half, "c", SWAP)
    whole = jnp.zeros((2 * rows, width), half.dtype)
    whole = lax.dynamic_update_slice_in_dim(whole, half, core * rows, 0)
    return lax.dynamic_update_slice_in_dim(whole, other, (1 - core) * rows, 0)


def owners(sizes):
    zh_n, x_n, y_n, zl_n, c_n = sizes
    pairs = []
    for source in range(zh_n * x_n * y_n * zl_n * c_n):
        rest, c = divmod(source, c_n)
        rest, zl = divmod(rest, zl_n)
        rest, y = divmod(rest, y_n)
        zh, x = divmod(rest, x_n)
        pairs.append((source, (((c * x_n + x) * zh_n + zh) * y_n + y) * zl_n + zl))
    return pairs


def body(
    features, cotangent, kernel, conv_bias, ln_gain, ln_bias, w_in, b_in, w_out, layer_scale, tissue
):
    image = features[0]
    height, breadth, channels = image.shape
    low = from_left(image[:, breadth - HALO :]).reshape(-1, channels)
    high = from_right(image[:, :HALO]).reshape(-1, channels)
    rows = image.reshape(-1, channels)
    upstream = cotangent[0].reshape(-1, channels)
    taps = kernel.reshape(-1, channels)
    core = lax.axis_index("c").astype(jnp.int32).reshape(1)
    sizes = [lax.axis_size(axis) for axis in EVERY]
    lines, ring = sizes[1], sizes[0] * sizes[2] * sizes[3]
    scale = 1.0 / math.sqrt(height * breadth * math.prod(sizes))

    conv, out_grad, back, w_in_t, b_cols = before_halos(
        tissue[0], rows, upstream, w_out, w_in, b_in, taps, layer_scale
    )
    kept, sent, standard, inverse, normed, preact, cdf = forward(
        core, conv, low, high, taps, conv_bias, ln_gain, ln_bias, w_in_t, b_cols, out_grad
    )
    out_total = core_sum(kept, sent)
    kept, sent, grad_conv, low, high = backward(
        core, back, preact, cdf, w_in, normed, standard, inverse, ln_gain
    )
    in_total = core_sum(kept, sent)
    low, high = from_left(high), from_right(low)

    out_total = added(exchange(in_blocks(out_total, lines), "x"))
    in_total = added(exchange(in_blocks(in_total, lines), "x"))
    out_total = added(exchange(in_blocks(out_total, ring), RING))
    own = copies((out_total * scale).astype(jnp.bfloat16), ring)
    mixed = exchange(jnp.stack([own, in_blocks(in_total, ring)], axis=1), RING)
    grad_w_out = joined(mixed[:, 0])
    grad_w_in = lax.ppermute(added(mixed[:, 1]) * scale, EVERY, owners(sizes))
    grad_w_out = both_cores(joined(exchange(copies(grad_w_out, lines), "x")))
    grad_image = to_features(grad_conv, low, high, taps, upstream)
    return (grad_image.reshape(1, height, breadth, channels), grad_w_in, grad_w_out)


def solution(mesh):
    fine = jax.sharding.Mesh(mesh.devices.reshape(4, 4, 8, 2, 2), EVERY)
    band = P(("zl", "c"), None, TILE, None)
    placed = (band, band) + (P(),) * 8 + (P(("zl", "c"), TILE),)
    return jax.shard_map(
        body,
        mesh=fine,
        in_specs=placed,
        out_specs=(band, P(EVERY, None), P()),
        check_vma=False,
    )
```

time: 152 us -> 149 us (0.980)
  Pallas kernels: 0 us -> 14.4 us
  blocking collectives: 12 us -> 25.7 us
  other arithmetic: 15.5 us -> 2.94 us
  starting transfers between devices: 71.3 us -> 60.7 us
  matrix products: 7.05 us -> 0 us
  local copies, waits for them, and re-layouts: 13.5 us -> 16.8 us
  waiting for transfers between devices: 29.7 us -> 27.1 us
    pallas_call x0 -> x4, Pallas kernels: none -> 14.4 us  [call(): pl.pallas_call(kernel, out_shape=[jax.ShapeDtypeStruct(shape, kind) for s...]
    all_to_all x1 -> x2, blocking collectives: 12 us -> 25.7 us  [exchange(): return lax.all_to_all(blocks, axes, split_axis=0, concat_axis=0, tiled=True)]
    all_to_all x5 -> x3, starting transfers between devices: 31.7 us -> 22.3 us  [exchange(): return lax.all_to_all(blocks, axes, split_axis=0, concat_axis=0, tiled=True)]
    ppermute x7, starting transfers between devices: 37.6 us -> 29.8 us  [the longest x1 11.8 us: body(): grad_w_in = lax.ppermute(added(mixed[:, 1]) * scale, EVERY, owners(sizes))]
    dot_general x5 -> x0, matrix products: 7.05 us -> none  [the longest x2 4.91 us: contract(): lax.dot_general(left, right, (((0,), (0,)), ((), ())), preferred_element_...]
    ppermute x1, starting transfers between devices: 1.92 us -> 8.67 us  [both_cores(): other = lax.ppermute(half, 'c', SWAP)]
    unnamed x109 -> x23, local copies, waits for them, and re-layouts: 2.65 us -> 8.08 us
    broadcast_in_dim x1 -> x0, other arithmetic: 4.4 us -> none  [body(): return (grad_image[None], grad_w_in, grad_w_out)]
  transfers between devices with their start and end apart: 13 -> 11, of which waited for: 4 -> 3; matrix products, arithmetic and copies ran while one was open for 14% -> 6% of each run, Pallas kernels for 0% -> 7%
where the time goes in v2:
time: 149 us
  starting transfers between devices  60.7 us (41%)
  waiting for transfers between devices  27.1 us (18%)
  blocking collectives  25.7 us (17%)
  local copies, waits for them, and re-layouts  16.8 us (11%)
  Pallas kernels  14.4 us (10%)
  other arithmetic  2.94 us (2%)
    all_to_all x3, waiting for transfers between devices, exchange(): return lax.all_to_all(blocks, axes, split_axis=0, concat_axis=0, tiled=True)  27.1 us
    all_to_all x2, blocking collectives, exchange(): return lax.all_to_all(blocks, axes, split_axis=0, concat_axis=0, tiled=True)  25.7 us
    all_to_all x3, starting transfers between devices, exchange(): return lax.all_to_all(blocks, axes, split_axis=0, concat_axis=0, tiled=True)  22.3 us
    pallas_call x4, Pallas kernels, call(): pl.pallas_call(kernel, out_shape=[jax.ShapeDtypeStruct(shape, kind) for s...  14.4 us
    ppermute x1, starting transfers between devices, body(): grad_w_in = lax.ppermute(added(mixed[:, 1]) * scale, EVERY, owners(sizes))  11.8 us
    ppermute x1, starting transfers between devices, both_cores(): other = lax.ppermute(half, 'c', SWAP)  8.67 us
    unnamed x23, local copies, waits for them, and re-layouts  8.08 us
    ppermute x2, starting transfers between devices, core_sum(): return kept + lax.ppermute(sent, 'c', SWAP).astype(jnp.float32)  7.94 us
  transfers between devices with their start and end apart: 11, of which 3 were waited for; matrix products, arithmetic and copies ran while one was open for 6% of the time, Pallas kernels for 7%

profile of v2, /device:TPU:1, one launch (start us, length us, event | category | flops | bytes accessed | tf_op | source)
XLA Modules:
  0.0 148.5 jit_solution(1224898388658044194)
XLA Ops:
  0.6 0.8 fusion.1
  1.5 4.6 %collective-permute-start = (bf16[8,3,384]{2,1,0:T(4,128)(2,1)S(1)}, bf16[8,3,384]{2,1,0:T(4,128)(2,1)}, u32[]{:S(2)}, u32[]{:S(2)}) collective-permute-start(bf16[8,3,384]{2,1,0:T(4,128)(2,1)S(1)} %get-tuple-element.38), channel_id=1, source_target_pairs={{0,4},{4,8},{8,12},{12,16},{16,20},{20,24},{24,28},{28,32},{32,36}... | collective-permute-start | bytes 55304 | tf_op jit(solution)/shard_map/ppermute | solution.py:267
  6.1 1.3 collective-permute-start.1
  8.1 0.9 reshape.36.taps
  11.8 1.3 copy-done
  13.0 1.3 copy-done.3
  14.3 0.9 copy-done.6
  15.2 0.9 copy-done.8
  16.8 4.0 %shard_map.130 = (f32[256,384]{1,0:T(8,128)S(1)}, bf16[256,384]{1,0:T(8,128)(2,1)S(1)}, f32[1536,256]{1,0:T(8,128)}, bf16[1536,384]{1,0:T(8,128)(2,1)S(1)}, f32[1536,128]{1,0:T(8,128)S(1)}) custom-call(s32[4]{0:T(128)S(1)} %bitcast.13, bf16[256,384]{1,0:T(8,128)(2,1)S(1)} %bitcast.12, bf16[256,384]{1,0:T(8,128)(2,1)S(1)} %bitcast.9, ...), custom_call_target="tpu_custom_call" | custom-call | flops 301989888 | bytes 8388608 | tf_op jit(solution)/shard_map/pallas_call | solution.py:197
  20.8 0.9 copy-done.4
  21.7 0.9 reshape.37.low
  22.6 1.1 copy-done.5
  23.8 3.9 %shard_map.131 = (f32[768,384]{1,0:T(8,128)S(1)}, bf16[768,384]{1,0:T(8,128)(2,1)S(1)}, f32[256,384]{1,0:T(8,128)S(1)}, f32[256,128]{1,0:T(8,128)S(1)}, bf16[256...) custom-call(s32[1]{0:T(128)} %bitcast.core, f32[256,384]{1,0:T(8,128)S(1)} %get-tuple-element.21.conv, ...), custom_call_target="tpu_custom_call" | custom-call | flops 603979776 | bytes 8388608 | tf_op jit(solution)/shard_map/pallas_call | solution.py:197
  27.6 6.0 %collective-permute-start.4 = (bf16[768,384]{1,0:T(8,128)(2,1)S(1)}, bf16[768,384]{1,0:T(8,128)(2,1)S(1)}, u32[]{:S(2)}, u32[]{:S(2)}) collective-permute-start(bf16[768,384]{1,0:T(8,128)(2,1)S(1)} %get-tuple-element.34), channel_id=1, source_target_pairs={{0,1},{1,0},{2,3},{3,2},{4,5},{5,4},{6,7},{7,6},{8,9},{9,8},{10,11... | collective-permute-start | bytes 1769480 | tf_op jit(solution)/shard_map/ppermute | solution.py:276
  33.7 4.2 %shard_map.132 = (f32[768,384]{1,0:T(8,128)S(1)}, bf16[768,384]{1,0:T(8,128)(2,1)}, f32[256,384]{1,0:T(8,128)S(1)}, f32[24,384]{1,0:T(8,128)S(1)}, f32[24,384]{1,0:T(8,128)S(1)}) custom-call(s32[1]{0:T(128)} %bitcast.core, f32[1536,256]{1,0:T(8,128)S(1)} %copy-done.2, f32[1536,256]{1,0:T(8,128)} %get-tuple-element.25.preact, ...), custom_call_target="tpu_custom_call" | custom-call | flops 603979776 | bytes 8388608 | tf_op jit(solution)/shard_map/pallas_call | solution.py:197
  37.9 1.9 %collective-permute-start.5 = (bf16[768,384]{1,0:T(8,128)(2,1)}, bf16[768,384]{1,0:T(8,128)(2,1)S(1)}, u32[]{:S(2)}, u32[]{:S(2)}) collective-permute-start(bf16[768,384]{1,0:T(8,128)(2,1)} %get-tuple-element.36), channel_id=1, source_target_pairs={{0,1},{1,0},{2,3},{3,2},{4,5},{5,4},{6,7},{7,6},{8,9},{9,8},{10,11... | collective-permute-start | bytes 1769480 | tf_op jit(solution)/shard_map/ppermute | solution.py:276
  39.8 1.0 add_convert_fusion.1
  40.8 3.5 %all-to-all-start = ((bf16[4,192,384]{2,1,0:T(8,128)(2,1)}), bf16[4,192,384]{2,1,0:T(8,128)(2,1)S(1)}, u32[]{:S(2)}, u32[]{:S(2)}) async-start(bf16[4,192,384]{2,1,0:T(8,128)(2,1)} %bitcast.6), calls=%async_computation | async-start | bytes 1179648 | tf_op jit(solution)/shard_map/all_to_all | solution.py:280
  44.3 1.0 add_convert_fusion
  45.3 8.5 %all-to-all-done = bf16[4,192,384]{2,1,0:T(8,128)(2,1)S(1)} async-done(((bf16[4,192,384]{2,1,0:T(8,128)(2,1)}), bf16[4,192,384]{2,1,0:T(8,128)(2,1)S(1)}, u32[]{:S(2)}, u32[]{:S(2)}) %all-to-all-start) | async-done | bytes 589856 | tf_op jit(solution)/shard_map/all_to_all | solution.py:280
  53.8 3.5 %all-to-all-start.2 = ((bf16[4,192,384]{2,1,0:T(8,128)(2,1)}), bf16[4,192,384]{2,1,0:T(8,128)(2,1)S(1)}, u32[]{:S(2)}, u32[]{:S(2)}) async-start(bf16[4,192,384]{2,1,0:T(8,128)(2,1)} %bitcast.16), calls=%async_computation.2 | async-start | bytes 1179648 | tf_op jit(solution)/shard_map/all_to_all | solution.py:280
  58.1 7.4 %all-to-all-done.2 = bf16[4,192,384]{2,1,0:T(8,128)(2,1)S(1)} async-done(((bf16[4,192,384]{2,1,0:T(8,128)(2,1)}), bf16[4,192,384]{2,1,0:T(8,128)(2,1)S(1)}, u32[]{:S(2)}, u32[]{:S(2)}) %all-to-all-start.2) | async-done | bytes 589856 | tf_op jit(solution)/shard_map/all_to_all | solution.py:280
  65.5 15.3 %all-to-all-start.1 = ((bf16[64,3,384]{2,1,0:T(4,128)(2,1)}), bf16[64,3,384]{2,1,0:T(4,128)(2,1)S(1)}, u32[]{:S(2)}, u32[]{:S(2)}) async-start(bf16[64,3,384]{2,1,0:T(4,128)(2,1)} %reshape.41), calls=%async_computation.1 | async-start | bytes 393216 | tf_op jit(solution)/shard_map/all_to_all | solution.py:280
  81.0 11.2 %all-to-all-done.1 = bf16[64,3,384]{2,1,0:T(4,128)(2,1)S(1)} async-done(((bf16[64,3,384]{2,1,0:T(4,128)(2,1)}), bf16[64,3,384]{2,1,0:T(4,128)(2,1)S(1)}, u32[]{:S(2)}, u32[]{:S(2)}) %all-to-all-start.1) | async-done | bytes 147488 | tf_op jit(solution)/shard_map/all_to_all | solution.py:280
  93.0 15.9 %all_to_all.25 = bf16[64,2,3,384]{3,1,2,0:T(2,128)(2,1)S(1)} all-to-all(bf16[64,2,3,384]{3,1,2,0:T(2,128)(2,1)S(1)} %copy.14), channel_id=1, replica_groups=mesh['zh'=4,'x'=4,'y'=8,'zl'=2,'c'=2] {'zh','y','zl'}, dimensions={0} | all-to-all | bytes 589824 | tf_op jit(solution)/shard_map/all_to_all | solution.py:280
  108.9 0.9 slice_reduce_fusion
  110.0 9.8 %all_to_all.26 = bf16[4,192,384]{2,1,0:T(8,128)(2,1)S(1)} all-to-all(bf16[4,192,384]{2,1,0:T(8,128)(2,1)S(1)} %broadcast_in_dim.34), channel_id=1, replica_groups=mesh['zh'=4,'x'=4,'y'=8,'zl'=2,'c'=2] {'x'}, dimensions={0} | all-to-all | bytes 1179648 | tf_op jit(solution)/shard_map/all_to_all | solution.py:280
  119.8 8.7 %collective-permute-start.7 = (bf16[768,384]{1,0:T(8,128)(2,1)S(1)}, bf16[768,384]{1,0:T(8,128)(2,1)S(1)}, u32[]{:S(2)}, u32[]{:S(2)}) collective-permute-start(bf16[768,384]{1,0:T(8,128)(2,1)S(1)} %bitcast.14), channel_id=1, source_target_pairs={{0,1},{1,0},{2,3},{3,2},{4,5},{5,4},{6,7},{7,6},{8,9},{9,8},{10,11... | collective-permute-start | bytes 1769480 | tf_op jit(solution)/shard_map/ppermute | solution.py:303
  128.5 2.8 %collective-permute-start.2 = (f32[24,384]{1,0:T(8,128)S(1)}, f32[24,384]{1,0:T(8,128)S(1)}, u32[]{:S(2)}, u32[]{:S(2)}) collective-permute-start(f32[24,384]{1,0:T(8,128)S(1)} %get-tuple-element.31), channel_id=1, source_target_pairs={{0,4},{4,8},{8,12},{12,16},{16,20},{20,24},{24,28},{28,32},{32,36}... | collective-permute-start | bytes 110600 | tf_op jit(solution)/shard_map/ppermute | solution.py:267
  131.3 1.3 collective-permute-start.3
  133.0 11.8 %collective-permute-start.6 = (f32[3,384]{1,0:T(4,128)S(1)}, f32[3,384]{1,0:T(4,128)S(1)}, u32[]{:S(2)}, u32[]{:S(2)}) collective-permute-start(f32[3,384]{1,0:T(4,128)S(1)} %broadcast_multiply_fusion), channel_id=1, source_target_pairs={{0,0},{1,256},{2,1},{3,257},{4,2},{5,258},{6,3},{7,259},{8,4},{9,2... | collective-permute-start | bytes 13832 | tf_op jit(solution)/shard_map/ppermute | solution.py:355
  144.9 2.3 %shard_map.133 = bf16[256,384]{1,0:T(8,128)(2,1)} custom-call(f32[256,384]{1,0:T(8,128)S(1)} %get-tuple-element.30.grad_conv, f32[24,384]{1,0:T(8,128)S(1)} %collective-permute-done.2.low, f32[24,384]{1,0:T(8,128)S(1)} %collective-permute-done.3.high, f32[49,384]{1,0:T(8,128)S(1)} %reshape.36.taps, bf16[256,384]{1,0:T(8,128)(2,1)S(1)} %bitcast.10), custom_call_target="tpu_custom_call" | custom-call | flops 9633792 | bytes 2097152 | tf_op jit(solution)/shard_map/pallas_call | solution.py:197
  (47 shorter events, 7.9 us)
Async XLA Ops:
  1.5 20.2 %collective-permute-start = (bf16[8,3,384]{2,1,0:T(4,128)(2,1)S(1)}, bf16[8,3,384]{2,1,0:T(4,128)(2,1)}, u32[]{:S(2)}, u32[]{:S(2)}) collective-permute-start(bf16[8,3,384]{2,1,0:T(4,128)(2,1)S(1)} %get-tuple-element.38), channel_id=1, source_target_pairs={{0,4},{4,8},{8,12},{12,16},{16,20},{20,24},{24,28},{28,32},{32,36}... | collective-permute-start | bytes 55304 | tf_op jit(solution)/shard_map/ppermute | solution.py:267
  6.1 16.5 %collective-permute-start.1 = (bf16[8,3,384]{2,1,0:T(4,128)(2,1)S(1)}, bf16[8,3,384]{2,1,0:T(4,128)(2,1)S(1)}, u32[]{:S(2)}, u32[]{:S(2)}) collective-permute-start(bf16[8,3,384]{2,1,0:T(4,128)(2,1)S(1)} %get-tuple-element.37), channel_id=1, source_target_pairs={{4,0},{8,4},{12,8},{16,12},{20,16},{24,20},{28,24},{32,28},{36,32}... | collective-permute-start | bytes 55304 | tf_op jit(solution)/shard_map/ppermute | solution.py:272
  11.8 1.3 copy-start
  13.0 1.3 copy-start.3
  14.3 0.9 copy-start.6
  15.2 0.9 copy-start.8
  16.2 0.7 copy-start.9
  20.8 0.9 copy-start.4
  21.7 12.0 %copy-start.2 = (f32[1536,256]{1,0:T(8,128)S(1)}, f32[1536,256]{1,0:T(8,128)}, u32[]{:S(2)}) copy-start(f32[1536,256]{1,0:T(8,128)} %get-tuple-element.20.back) | copy-start | bytes 4718596
  22.6 1.1 copy-start.5
  23.8 9.9 %copy-start.1 = (bf16[384,1536]{1,0:T(8,128)(2,1)S(1)}, bf16[384,1536]{1,0:T(8,128)(2,1)}, u32[]{:S(2)}) copy-start(bf16[384,1536]{1,0:T(8,128)(2,1)} %w_in.3) | copy-start | bytes 3538948
  27.6 12.2 %collective-permute-start.4 = (bf16[768,384]{1,0:T(8,128)(2,1)S(1)}, bf16[768,384]{1,0:T(8,128)(2,1)S(1)}, u32[]{:S(2)}, u32[]{:S(2)}) collective-permute-start(bf16[768,384]{1,0:T(8,128)(2,1)S(1)} %get-tuple-element.34), channel_id=1, source_target_pairs={{0,1},{1,0},{2,3},{3,2},{4,5},{5,4},{6,7},{7,6},{8,9},{9,8},{10,11... | collective-permute-start | bytes 1769480 | tf_op jit(solution)/shard_map/ppermute | solution.py:276
  37.9 6.4 %collective-permute-start.5 = (bf16[768,384]{1,0:T(8,128)(2,1)}, bf16[768,384]{1,0:T(8,128)(2,1)S(1)}, u32[]{:S(2)}, u32[]{:S(2)}) collective-permute-start(bf16[768,384]{1,0:T(8,128)(2,1)} %get-tuple-element.36), channel_id=1, source_target_pairs={{0,1},{1,0},{2,3},{3,2},{4,5},{5,4},{6,7},{7,6},{8,9},{9,8},{10,11... | collective-permute-start | bytes 1769480 | tf_op jit(solution)/shard_map/ppermute | solution.py:276
  40.8 13.0 %all-to-all-start = ((bf16[4,192,384]{2,1,0:T(8,128)(2,1)}), bf16[4,192,384]{2,1,0:T(8,128)(2,1)S(1)}, u32[]{:S(2)}, u32[]{:S(2)}) async-start(bf16[4,192,384]{2,1,0:T(8,128)(2,1)} %bitcast.6), calls=%async_computation | async-start | bytes 1179648 | tf_op jit(solution)/shard_map/all_to_all | solution.py:280
  53.8 11.7 %all-to-all-start.2 = ((bf16[4,192,384]{2,1,0:T(8,128)(2,1)}), bf16[4,192,384]{2,1,0:T(8,128)(2,1)S(1)}, u32[]{:S(2)}, u32[]{:S(2)}) async-start(bf16[4,192,384]{2,1,0:T(8,128)(2,1)} %bitcast.16), calls=%async_computation.2 | async-start | bytes 1179648 | tf_op jit(solution)/shard_map/all_to_all | solution.py:280
  65.5 26.7 %all-to-all-start.1 = ((bf16[64,3,384]{2,1,0:T(4,128)(2,1)}), bf16[64,3,384]{2,1,0:T(4,128)(2,1)S(1)}, u32[]{:S(2)}, u32[]{:S(2)}) async-start(bf16[64,3,384]{2,1,0:T(4,128)(2,1)} %reshape.41), calls=%async_computation.1 | async-start | bytes 393216 | tf_op jit(solution)/shard_map/all_to_all | solution.py:280
  109.9 35.0 %copy-start.7 = (bf16[1,8,32,384]{3,2,1,0:T(8,128)(2,1)S(1)}, bf16[1,8,32,384]{3,2,1,0:T(8,128)(2,1)}, u32[]{:S(2)}) copy-start(bf16[1,8,32,384]{3,2,1,0:T(8,128)(2,1)} %param.12) | copy-start | bytes 589828
  119.8 27.6 %collective-permute-start.7 = (bf16[768,384]{1,0:T(8,128)(2,1)S(1)}, bf16[768,384]{1,0:T(8,128)(2,1)S(1)}, u32[]{:S(2)}, u32[]{:S(2)}) collective-permute-start(bf16[768,384]{1,0:T(8,128)(2,1)S(1)} %bitcast.14), channel_id=1, source_target_pairs={{0,1},{1,0},{2,3},{3,2},{4,5},{5,4},{6,7},{7,6},{8,9},{9,8},{10,11... | collective-permute-start | bytes 1769480 | tf_op jit(solution)/shard_map/ppermute | solution.py:303
  128.5 16.4 %collective-permute-start.2 = (f32[24,384]{1,0:T(8,128)S(1)}, f32[24,384]{1,0:T(8,128)S(1)}, u32[]{:S(2)}, u32[]{:S(2)}) collective-permute-start(f32[24,384]{1,0:T(8,128)S(1)} %get-tuple-element.31), channel_id=1, source_target_pairs={{0,4},{4,8},{8,12},{12,16},{16,20},{20,24},{24,28},{28,32},{32,36}... | collective-permute-start | bytes 110600 | tf_op jit(solution)/shard_map/ppermute | solution.py:267
  131.3 13.5 %collective-permute-start.3 = (f32[24,384]{1,0:T(8,128)S(1)}, f32[24,384]{1,0:T(8,128)S(1)}, u32[]{:S(2)}, u32[]{:S(2)}) collective-permute-start(f32[24,384]{1,0:T(8,128)S(1)} %get-tuple-element.32), channel_id=1, source_target_pairs={{4,0},{8,4},{12,8},{16,12},{20,16},{24,20},{28,24},{32,28},{36,32}... | collective-permute-start | bytes 110600 | tf_op jit(solution)/shard_map/ppermute | solution.py:272
  133.0 14.1 %collective-permute-start.6 = (f32[3,384]{1,0:T(4,128)S(1)}, f32[3,384]{1,0:T(4,128)S(1)}, u32[]{:S(2)}, u32[]{:S(2)}) collective-permute-start(f32[3,384]{1,0:T(4,128)S(1)} %broadcast_multiply_fusion), channel_id=1, source_target_pairs={{0,0},{1,256},{2,1},{3,257},{4,2},{5,258},{6,3},{7,259},{8,4},{9,2... | collective-permute-start | bytes 13832 | tf_op jit(solution)/shard_map/ppermute | solution.py:355
  147.5 1.0 copy-start.10

commit v3 on v2

v3 whole, which is shorter than its diff:
```python
import functools
import math

import jax
import jax.numpy as jnp
from jax import lax
from jax.experimental import pallas as pl
from jax.experimental.pallas import tpu as pltpu
from jax.sharding import PartitionSpec as P

SIDE = 8
HALO = 3
TAPS = 7
COLS = 32
LANES = 128
CHUNK = 32
ROWS = 3
PLACES = 32
EPSILON = 1e-06
VMEM_LIMIT = 48 * 1024 * 1024
NT = (((1,), (1,)), ((), ()))

TILE = ("zh", "x", "y")
RING = ("zh", "y", "zl")
EVERY = ("zh", "x", "y", "zl", "c")
SWAP = [(0, 1), (1, 0)]


def matmul(left, right, dims=(((1,), (0,)), ((), ()))):
    return lax.dot_general(left, right, dims, preferred_element_type=jnp.float32)


def shifted(column, a):
    move = a - HALO
    if move == 0:
        return column
    row = lax.broadcasted_iota(jnp.int32, column.shape, 0)
    inside = (row + move >= 0) & (row + move < SIDE)
    return jnp.where(inside, pltpu.roll(column, (-move) % SIDE, 0), 0.0)


def convolve(columns, taps, lanes, flip):
    count = len(columns) - 2 * HALO
    totals = [None] * count
    for a in range(TAPS):
        sums = [None] * count
        for e in range(TAPS):
            row, place = (TAPS - 1 - a, TAPS - 1 - e) if flip else (a, e)
            tap = taps[row, place : place + 1, lanes]
            for j in range(count):
                if columns[j + e] is None:
                    continue
                term = columns[j + e] * tap
                sums[j] = term if sums[j] is None else sums[j] + term
        for j in range(count):
            if sums[j] is None:
                continue
            moved = shifted(sums[j], a)
            totals[j] = moved if totals[j] is None else totals[j] + moved
    return totals


def lane_blocks(width):
    return [slice(start, start + LANES) for start in range(0, width, LANES)]


def widen(source, wide):
    for k, lanes in enumerate(lane_blocks(source.shape[1])):
        wide[k] = source[:, lanes].astype(jnp.float32)


def first_kernel(
    flags, features, cotangent, w_out, w_in, b_in, taps, scale, conv_bias, gain, bias,
    conv, out_grad, back, w_in_t, b_cols, w_in_here, taps_here, vectors,
    wide, flags_here, image, upstream, w_out_here, b_here, scale_here, conv_bias_here, gain_here, bias_here, sems
):
    width = features.shape[1]
    pairs = [
        (flags, flags_here), (cotangent, upstream), (scale, scale_here), (w_out, w_out_here),
        (features, image), (taps, taps_here), (w_in, w_in_here), (b_in, b_here),
        (conv_bias, conv_bias_here), (gain, gain_here), (bias, bias_here),
    ]
    copies = [pltpu.make_async_copy(src, dst, sems.at[i]) for i, (src, dst) in enumerate(pairs)]
    for copy in copies:
        copy.start()
    for copy in copies[:3]:
        copy.wait()
    widen(upstream, wide)
    rows = SIDE * SIDE
    by_lane = scale_here[...].reshape(1, width)
    for k, lanes in enumerate(lane_blocks(width)):
        for t in range(COLS // SIDE):
            gate = flags_here[0, t].astype(jnp.float32)
            tile = jnp.concatenate(
                [wide[k, pl.ds(t * SIDE + j, SIDE, stride=COLS), :] for j in range(SIDE)], axis=0
            )
            tile = (tile * by_lane[:, lanes] * gate).astype(jnp.bfloat16)
            out_grad[t * rows : (t + 1) * rows, lanes] = tile
    copies[3].wait()
    back[...] = matmul(w_out_here[...], out_grad[...], NT)
    copies[4].wait()
    copies[5].wait()
    widen(image, wide)
    for k, lanes in enumerate(lane_blocks(width)):
        for t in range(COLS // SIDE):
            columns = []
            for j in range(t * SIDE - HALO, (t + 1) * SIDE + HALO):
                inside = 0 <= j < COLS
                columns.append(wide[k, pl.ds(j, SIDE, stride=COLS), :] if inside else None)
            for j, total in enumerate(convolve(columns, taps_here, lanes, False)):
                start = (t * SIDE + j) * SIDE
                conv[start : start + SIDE, lanes] = total
    for copy in copies[6:]:
        copy.wait()
    hidden = w_in.shape[1]
    for start in range(0, hidden, LANES):
        w_in_t[start : start + LANES, :] = w_in_here[:, start : start + LANES].T
        b_cols[start : start + LANES, :] = jnp.broadcast_to(
            b_here[start : start + LANES].reshape(1, LANES), (LANES, LANES)
        ).T
    for i, vector in enumerate((conv_bias_here, gain_here, bias_here)):
        vectors[i * SIDE : (i + 1) * SIDE, :] = jnp.broadcast_to(
            vector[...].reshape(1, width), (SIDE, width)
        )


def second_kernel(
    core, conv, low, high, taps, vectors, w_in_t, b_cols, out_grad,
    kept, sent, standard, inverse, normed, preact, cdf, rows, low_wide, high_wide, hidden
):
    width = conv.shape[1]
    rows[...] = conv[...]
    widen(low, low_wide)
    widen(high, high_wide)
    for k, lanes in enumerate(lane_blocks(width)):
        near = [low_wide[k, pl.ds(j, SIDE, stride=HALO), :] for j in range(HALO)]
        for j, total in enumerate(convolve(near + [None] * (2 * HALO), taps, lanes, False)):
            rows[j * SIDE : (j + 1) * SIDE, lanes] += total
        near = [high_wide[k, pl.ds(j, SIDE, stride=HALO), :] for j in range(HALO)]
        for j, total in enumerate(convolve([None] * (2 * HALO) + near, taps, lanes, False)):
            start = (COLS - HALO + j) * SIDE
            rows[start : start + SIDE, lanes] += total
    conv_out = rows[...] + vectors[:1, :]
    centre = conv_out - jnp.mean(conv_out, axis=-1, keepdims=True)
    scale = lax.rsqrt(jnp.mean(centre * centre, axis=-1, keepdims=True) + EPSILON)
    inverse[...] = jnp.broadcast_to(scale, inverse.shape)
    standard[...] = centre * scale
    normed[...] = (standard[...] * vectors[SIDE : SIDE + 1, :] + vectors[2 * SIDE : 2 * SIDE + 1, :]).astype(jnp.bfloat16)
    preact[...] = matmul(w_in_t[...], normed[...], NT)

    def step(i, carry):
        part = pl.ds(pl.multiple_of(i * CHUNK, CHUNK), CHUNK)
        for lanes in lane_blocks(preact.shape[1]):
            z = preact[part, lanes] + b_cols[part, :]
            below = 0.5 * (1.0 + lax.erf(z * 0.7071067811865476))
            preact[part, lanes] = z
            cdf[part, lanes] = below
            hidden[part, lanes] = (z * below).astype(jnp.bfloat16)
        return carry

    lax.fori_loop(0, preact.shape[0] // CHUNK, step, 0, unroll=2)
    half = hidden.shape[0] // 2
    other = pl.ds(pl.multiple_of((1 - core[0]) * half, half), half)
    own = pl.ds(pl.multiple_of(core[0] * half, half), half)
    sent[...] = matmul(hidden[other, :], out_grad[...]).astype(jnp.bfloat16)
    kept[...] = matmul(hidden[own, :], out_grad[...])


def slope_kernel(back, preact, cdf, grad_pre):
    def step(i, carry):
        part = pl.ds(pl.multiple_of(i * CHUNK, CHUNK), CHUNK)
        for lanes in lane_blocks(preact.shape[1]):
            z = preact[part, lanes]
            density = jnp.exp(-0.5 * z * z) * 0.3989422804014327
            slope = cdf[part, lanes] + z * density
            grad_pre[part, lanes] = (back[part, lanes] * slope).astype(jnp.bfloat16)
        return carry

    lax.fori_loop(0, preact.shape[0] // CHUNK, step, 0, unroll=2)


def third_kernel(
    core, grad_pre, w_in, normed, standard, inverse, vectors,
    kept, sent, grad_conv, low, high
):
    grad_std = matmul(w_in[...], grad_pre[...]).T * vectors[SIDE : SIDE + 1, :]
    half = grad_pre.shape[0] // 2
    other = pl.ds(pl.multiple_of((1 - core[0]) * half, half), half)
    own = pl.ds(pl.multiple_of(core[0] * half, half), half)
    sent[...] = matmul(grad_pre[other, :], normed[...]).astype(jnp.bfloat16)
    kept[...] = matmul(grad_pre[own, :], normed[...])
    norm = standard[...]
    mean = jnp.mean(grad_std, axis=-1, keepdims=True)
    along = jnp.mean(grad_std * norm, axis=-1, keepdims=True)
    result = inverse[:, :1] * (grad_std - mean - norm * along)
    grad_conv[...] = result
    edge = HALO * SIDE
    low[...] = result[:edge, :]
    high[...] = result[result.shape[0] - edge :, :]


def last_kernel(grad_conv, low, high, taps, cotangent, grad_features, wide):
    for k, lanes in enumerate(lane_blocks(grad_conv.shape[1])):
        for t in range(COLS // SIDE):
            columns = []
            for j in range(t * SIDE - HALO, (t + 1) * SIDE + HALO):
                if j < 0:
                    source, place = low, j + HALO
                elif j >= COLS:
                    source, place = high, j - COLS
                else:
                    source, place = grad_conv, j
                columns.append(source[place * SIDE : (place + 1) * SIDE, lanes])
            for j, total in enumerate(convolve(columns, taps, lanes, True)):
                wide[k, pl.ds(t * SIDE + j, SIDE, stride=COLS), :] = total
        result = cotangent[:, lanes].astype(jnp.float32) + wide[k]
        grad_features[:, lanes] = result.astype(jnp.bfloat16)


def pack_kernel(out_blocks, kept, received, first, second, spread, total):
    members, places, _ = first.shape
    width = kept.shape[1]
    for k, lanes in enumerate(lane_blocks(width)):
        total[k] = kept[:, lanes] + received[:, lanes].astype(jnp.float32)
    blocks = len(lane_blocks(width))
    for message in (first, second):
        spread[...] = jnp.zeros_like(spread)
        if message is first:
            for r in range(ROWS):
                part = slice(r * members, (r + 1) * members)
                for k, lanes in enumerate(lane_blocks(width)):
                    summed = out_blocks[0, part, lanes].astype(jnp.float32)
                    for i in range(1, out_blocks.shape[0]):
                        summed += out_blocks[i, part, lanes].astype(jnp.float32)
                    spread[pl.ds(r * blocks + k, members, stride=places), :] = summed
        offset = 0 if message is first else 2
        for b in range(2):
            for r in range(ROWS):
                start = (offset + b) * ROWS * members + r
                for k in range(blocks):
                    place = ((1 + b) * ROWS + r) * blocks + k
                    spread[pl.ds(place, members, stride=places), :] = total[
                        k, pl.ds(start, members, stride=ROWS), :
                    ]
        message[...] = spread[...].reshape(message.shape).astype(jnp.bfloat16)


def add_members(received):
    summed = received[0].astype(jnp.float32)
    for i in range(1, received.shape[0]):
        summed += received[i].astype(jnp.float32)
    return summed


def turn_kernel(scale, received, second, message, kept_sums):
    summed = add_members(received)
    kept_sums[...] = summed
    finished = (summed * scale).astype(jnp.bfloat16)
    place = lax.broadcasted_iota(jnp.int32, finished.shape, 0)
    of_out = place < ROWS * ROWS
    for m in range(message.shape[0]):
        message[m] = jnp.where(of_out, finished, second[m])


def unpack_kernel(kept_sums, received, message, spread):
    members, places, _ = received.shape
    lines, rows, width = message.shape
    count = ROWS * members
    spread[...] = received[...].astype(jnp.float32).reshape(spread.shape)
    blocks = len(lane_blocks(width))
    for r in range(ROWS):
        for k, lanes in enumerate(lane_blocks(width)):
            part = spread[pl.ds(r * blocks + k, members, stride=places), :].astype(jnp.bfloat16)
            for i in range(lines):
                message[i, r * members : (r + 1) * members, lanes] = part
    last_sums = add_members(received)
    size = ROWS * blocks
    for i in range(lines):
        sums = kept_sums[...] if i < 2 else last_sums
        start = size * (1 + i % 2)
        part = jnp.concatenate([sums[start : start + size, :], jnp.zeros((rows - count - size, LANES), jnp.float32)], axis=0)
        message[i, count:, :LANES] = part.astype(jnp.bfloat16)
        message[i, count:, LANES:] = jnp.zeros((rows - count, width - LANES), jnp.bfloat16)


def line_kernel(scale, received, grad_w_in, spread):
    count = received.shape[1] - 16
    spread[...] = received[0, count:, :LANES].astype(jnp.float32)
    for i in range(1, received.shape[0]):
        spread[...] += received[i, count:, :LANES].astype(jnp.float32)
    blocks = grad_w_in.shape[1] // LANES
    for k in range(blocks):
        grad_w_in[:, k * LANES : (k + 1) * LANES] = (
            spread[pl.ds(k, ROWS, stride=blocks), :] * scale
        )


def join_kernel(core, own, other, grad_w_out):
    lines, rows, _ = own.shape
    rows -= 16
    half = lines * rows
    for place, source in ((core[0], own), (1 - core[0], other)):
        for i in range(lines):
            start = pl.multiple_of(place * half + i * rows, rows)
            grad_w_out[pl.ds(start, rows), :] = source[i, :rows, :]


def call(kernel, outs, scratch, scalars, arrays, flops, nbytes, space=pltpu.VMEM):
    in_specs = [pl.BlockSpec(memory_space=pltpu.SMEM)] * len(scalars)
    in_specs += [pl.BlockSpec(memory_space=space)] * len(arrays)
    return pl.pallas_call(
        kernel,
        out_shape=[jax.ShapeDtypeStruct(shape, kind) for shape, kind in outs],
        in_specs=in_specs,
        out_specs=[pl.BlockSpec(memory_space=pltpu.VMEM)] * len(outs),
        scratch_shapes=scratch,
        compiler_params=pltpu.CompilerParams(vmem_limit_bytes=VMEM_LIMIT),
        cost_estimate=pl.CostEstimate(flops=flops, bytes_accessed=nbytes, transcendentals=0),
    )(*scalars, *arrays)


F32, B16 = jnp.float32, jnp.bfloat16


def before_halos(flags, features, cotangent, kernel, conv_bias, gain, bias, w_in, b_in, w_out, layer_scale):
    rows, width = features.shape
    hidden = w_out.shape[0]
    return call(
        first_kernel,
        [((rows, width), F32), ((rows, width), B16), ((hidden, rows), F32), ((hidden, width), B16),
         ((hidden, LANES), F32), (w_in.shape, B16), (kernel.shape, F32), ((3 * SIDE, width), F32)],
        [pltpu.VMEM((width // LANES, rows, LANES), F32), pltpu.SMEM(flags.shape, jnp.int32),
         pltpu.VMEM((rows, width), B16), pltpu.VMEM((rows, width), B16), pltpu.VMEM(w_out.shape, B16),
         pltpu.VMEM(b_in.shape, F32), pltpu.VMEM((width,), F32), pltpu.VMEM((width,), F32),
         pltpu.VMEM((width,), F32), pltpu.VMEM((width,), F32),
         pltpu.SemaphoreType.DMA((11,))],
        [],
        [flags, features, cotangent, w_out, w_in, b_in, kernel, layer_scale, conv_bias, gain, bias],
        2 * rows * width * hidden, 8 * 1024 * 1024, pltpu.HBM,
    )


def forward(core, conv, low, high, taps, vectors, w_in_t, b_cols, out_grad):
    rows, width = conv.shape
    hidden = w_in_t.shape[0]
    halo = pltpu.VMEM((width // LANES, HALO * SIDE, LANES), F32)
    return call(
        second_kernel,
        [((hidden // 2, width), F32), ((hidden // 2, width), B16), ((rows, width), F32), ((rows, LANES), F32),
         ((rows, width), B16), ((hidden, rows), F32), ((hidden, rows), F32)],
        [pltpu.VMEM((rows, width), F32), halo, halo, pltpu.VMEM((hidden, rows), B16)],
        [core],
        [conv, low, high, taps, vectors, w_in_t, b_cols, out_grad],
        4 * rows * width * hidden, 8 * 1024 * 1024,
    )


def slopes(back, preact, cdf):
    return call(slope_kernel, [(back.shape, B16)], [], [], [back, preact, cdf], 10 * back.size, 14 * back.size)[0]


def backward(core, grad_pre, w_in, normed, standard, inverse, vectors):
    rows, width = standard.shape
    hidden = grad_pre.shape[0]
    edge = (HALO * SIDE, width)
    return call(
        third_kernel,
        [((hidden // 2, width), F32), ((hidden // 2, width), B16), ((rows, width), F32), (edge, F32), (edge, F32)],
        [],
        [core],
        [grad_pre, w_in, normed, standard, inverse, vectors],
        4 * rows * width * hidden, 8 * 1024 * 1024,
    )


def to_features(grad_conv, low, high, taps, cotangent):
    rows, width = grad_conv.shape
    return call(
        last_kernel,
        [((rows, width), B16)],
        [pltpu.VMEM((width // LANES, rows, LANES), F32)],
        [],
        [grad_conv, low, high, taps, cotangent],
        2 * 49 * rows * width, 2 * 1024 * 1024,
    )[0]


def pack(out_blocks, kept, received, members):
    width = kept.shape[1]
    message = ((members, PLACES, LANES), B16)
    return call(
        pack_kernel,
        [message, message],
        [pltpu.VMEM((members * PLACES, LANES), F32), pltpu.VMEM((width // LANES,) + kept.shape[:1] + (LANES,), F32)],
        [],
        [out_blocks, kept, received],
        kept.size, 8 * kept.size,
    )


def turn(scale, received, second):
    return call(
        functools.partial(turn_kernel, scale),
        [(received.shape, B16), ((PLACES, LANES), F32)], [], [], [received, second],
        received.size, 6 * received.size,
    )


def unpack(kept_sums, received, lines, rows, width):
    return call(
        unpack_kernel,
        [((lines, rows + 16, width), B16)],
        [pltpu.VMEM((received.shape[0] * received.shape[1], LANES), F32)],
        [],
        [kept_sums, received],
        received.size, 6 * received.size,
    )[0]


def over_lines(scale, received):
    return call(
        functools.partial(line_kernel, scale),
        [((ROWS, received.shape[2]), F32)],
        [pltpu.VMEM((16, LANES), F32)],
        [],
        [received],
        received.size, received.size,
    )[0]


def join(core, own, other):
    lines, rows, width = own.shape
    return call(
        join_kernel, [((2 * lines * (rows - 16), width), B16)], [], [core], [own, other],
        own.size, 8 * own.size,
    )[0]


def from_left(block):
    count = lax.axis_size(TILE)
    return lax.ppermute(block, TILE, [(i, i + 1) for i in range(count - 1)])


def from_right(block):
    count = lax.axis_size(TILE)
    return lax.ppermute(block, TILE, [(i + 1, i) for i in range(count - 1)])


def exchange(blocks, axes):
    return lax.all_to_all(blocks, axes, split_axis=0, concat_axis=0, tiled=True)


def swap(block):
    return lax.ppermute(block, "c", SWAP)


def owners(sizes):
    zh_n, x_n, y_n, zl_n, c_n = sizes
    pairs = []
    for source in range(zh_n * x_n * y_n * zl_n * c_n):
        rest, c = divmod(source, c_n)
        rest, zl = divmod(rest, zl_n)
        rest, y = divmod(rest, y_n)
        zh, x = divmod(rest, x_n)
        pairs.append((source, (((c * x_n + x) * zh_n + zh) * y_n + y) * zl_n + zl))
    return pairs


def body(
    features, cotangent, kernel, conv_bias, ln_gain, ln_bias, w_in, b_in, w_out, layer_scale, tissue
):
    image = features[0]
    height, breadth, channels = image.shape
    low = from_left(image[:, breadth - HALO :]).reshape(-1, channels)
    high = from_right(image[:, :HALO]).reshape(-1, channels)
    rows = image.reshape(-1, channels)
    upstream = cotangent[0].reshape(-1, channels)
    core = lax.axis_index("c").astype(jnp.int32).reshape(1)
    sizes = [lax.axis_size(axis) for axis in EVERY]
    lines, ring = sizes[1], sizes[0] * sizes[2] * sizes[3]
    scale = 1.0 / math.sqrt(height * breadth * math.prod(sizes))

    conv, out_grad, back, w_in_t, b_cols, w_in_here, taps, vectors = before_halos(
        tissue, rows, upstream, kernel, conv_bias, ln_gain, ln_bias, w_in, b_in, w_out, layer_scale
    )
    kept, sent, standard, inverse, normed, preact, cdf = forward(
        core, conv, low, high, taps, vectors, w_in_t, b_cols, out_grad
    )
    grad_pre = slopes(back, preact, cdf)
    total = (kept + swap(sent).astype(F32)).astype(B16).reshape(lines, -1, channels)
    total, grad_pre = lax.optimization_barrier((total, grad_pre))
    out_blocks = exchange(total, "x")
    kept, sent, grad_conv, low, high = backward(
        core, grad_pre, w_in_here, normed, standard, inverse, vectors
    )
    received = swap(sent)
    low, high = from_left(high), from_right(low)
    out_blocks, received, low, high = lax.optimization_barrier((out_blocks, received, low, high))

    first, second = pack(out_blocks, kept, received, ring)
    message, kept_sums = turn(scale, exchange(first, RING), second)
    message = unpack(kept_sums, exchange(message, RING), lines, out_blocks.shape[1], channels)
    own = exchange(message, "x")
    own, low, high = lax.optimization_barrier((own, low, high))
    other = swap(own)
    grad_w_in = lax.ppermute(over_lines(scale, own), EVERY, owners(sizes))
    grad_image = to_features(grad_conv, low, high, taps, upstream)
    grad_w_out = join(core, own, other)
    return (grad_image.reshape(1, height, breadth, channels), grad_w_in, grad_w_out)


def solution(mesh):
    fine = jax.sharding.Mesh(mesh.devices.reshape(4, 4, 8, 2, 2), EVERY)
    band = P(("zl", "c"), None, TILE, None)
    placed = (band, band) + (P(),) * 8 + (P(("zl", "c"), TILE),)
    return jax.shard_map(
        body,
        mesh=fine,
        in_specs=placed,
        out_specs=(band, P(EVERY, None), P()),
        check_vma=False,
    )
```

time: 149 us -> 154 us (1.034)
  the two profiles are of different devices: /device:TPU:1 before, /device:TPU:30 now
where the time goes in v3:
time: 154 us; the launch traced here: 153 us
  blocking collectives  71.5 us (46%)
  starting transfers between devices  28 us (18%)
  local copies, waits for them, and re-layouts  21.6 us (14%)
  Pallas kernels  15.8 us (10%)
  waiting for transfers between devices  14 us (9%)
    all_to_all x3, blocking collectives, exchange(): return lax.all_to_all(blocks, axes, split_axis=0, concat_axis=0, tiled=True)  71.5 us
    unnamed x47, local copies, waits for them, and re-layouts  17.4 us
    pallas_call x10, Pallas kernels, call(): pl.pallas_call(kernel, out_shape=[jax.ShapeDtypeStruct(shape, kind) for s...  15.8 us
    ppermute x1, waiting for transfers between devices, body(): grad_w_in = lax.ppermute(over_lines(scale, own), EVERY, owners(sizes))  9.31 us
    ppermute x2, starting transfers between devices, from_left(): return lax.ppermute(block, TILE, [(i, i + 1) for i in range(count - 1)])  8.17 us
    ppermute x3, starting transfers between devices, swap(): return lax.ppermute(block, 'c', SWAP)  6.23 us
    all_to_all x1, starting transfers between devices, exchange(): return lax.all_to_all(blocks, axes, split_axis=0, concat_axis=0, tiled=True)  4.78 us
    ppermute x2, starting transfers between devices, from_right(): return lax.ppermute(block, TILE, [(i + 1, i) for i in range(count - 1)])  4.7 us
  transfers between devices with their start and end apart: 9, of which 2 were waited for; matrix products, arithmetic and copies ran while one was open for 1% of the time, Pallas kernels for 5%

profile of v3, /device:TPU:30, one launch (start us, length us, event | category | flops | bytes accessed | tf_op | source)
XLA Modules:
  0.0 152.8 jit_solution(364177141975051509)
XLA Ops:
  0.6 1.5 fusion
  2.1 2.3 %collective-permute-start.1 = (bf16[8,3,384]{2,1,0:T(4,128)(2,1)}, bf16[8,3,384]{2,1,0:T(4,128)(2,1)}, u32[]{:S(2)}, u32[]{:S(2)}) collective-permute-start(bf16[8,3,384]{2,1,0:T(4,128)(2,1)} %get-tuple-element.69), channel_id=1, source_target_pairs={{4,0},{8,4},{12,8},{16,12},{20,16},{24,20},{28,24},{32,28},{36,32}... | collective-permute-start | bytes 55304 | tf_op jit(solution)/shard_map/ppermute | solution.py:446
  4.5 4.7 %collective-permute-start = (bf16[8,3,384]{2,1,0:T(4,128)(2,1)}, bf16[8,3,384]{2,1,0:T(4,128)(2,1)}, u32[]{:S(2)}, u32[]{:S(2)}) collective-permute-start(bf16[8,3,384]{2,1,0:T(4,128)(2,1)} %get-tuple-element.70), channel_id=1, source_target_pairs={{0,4},{4,8},{8,12},{12,16},{16,20},{20,24},{24,28},{28,32},{32,36}... | collective-permute-start | bytes 55304 | tf_op jit(solution)/shard_map/ppermute | solution.py:441
  9.2 1.3 copy-done.3
  10.4 0.9 copy-done.4
  11.4 0.9 copy-done.9
  12.3 0.9 copy-done.14
  17.3 4.7 %shard_map.130 = (f32[256,384]{1,0:T(8,128)S(1)}, bf16[256,384]{1,0:T(8,128)(2,1)S(1)}, f32[1536,256]{1,0:T(8,128)}, bf16[1536,384]{1,0:T(8,128)(2,1)S(1)}, f32[...) custom-call(s32[1,4]{1,0:T(1,128)S(1)} %copy-done.22, ...), custom_call_target="tpu_custom_call" | custom-call | flops 301989888 | bytes 8388608 | tf_op jit(solution)/shard_map/pallas_call | solution.py:311
  23.9 1.4 reshape.23.high
  25.3 1.4 reshape.22.low
  26.6 0.9 copy-done.7
  27.5 0.9 copy-done.11
  30.7 3.9 %shard_map.131 = (f32[768,384]{1,0:T(8,128)S(1)}, bf16[768,384]{1,0:T(8,128)(2,1)S(1)}, f32[256,384]{1,0:T(8,128)S(1)}, f32[256,128]{1,0:T(8,128)S(1)}, bf16[256...) custom-call(s32[1]{0:T(128)} %bitcast.core, f32[256,384]{1,0:T(8,128)S(1)} %get-tuple-element.36.conv, ...), custom_call_target="tpu_custom_call" | custom-call | flops 603979776 | bytes 8388608 | tf_op jit(solution)/shard_map/pallas_call | solution.py:311
  34.5 1.9 %collective-permute-start.2 = (bf16[768,384]{1,0:T(8,128)(2,1)S(1)}, bf16[768,384]{1,0:T(8,128)(2,1)S(1)}, u32[]{:S(2)}, u32[]{:S(2)}) collective-permute-start(bf16[768,384]{1,0:T(8,128)(2,1)S(1)} %get-tuple-element.43), channel_id=1, source_target_pairs={{0,1},{1,0},{2,3},{3,2},{4,5},{5,4},{6,7},{7,6},{8,9},{9,8},{10,11... | collective-permute-start | bytes 1769480 | tf_op jit(solution)/shard_map/ppermute | solution.py:454
  36.5 1.4 copy-done.1
  37.9 1.4 copy-done.2
  40.0 0.9 add_convert_fusion
  41.0 0.9 shard_map.133
  41.9 2.4 %collective-permute-start.3 = (bf16[768,384]{1,0:T(8,128)(2,1)S(1)}, bf16[768,384]{1,0:T(8,128)(2,1)S(1)}, u32[]{:S(2)}, u32[]{:S(2)}) collective-permute-start(bf16[768,384]{1,0:T(8,128)(2,1)S(1)} %get-tuple-element.54), channel_id=1, source_target_pairs={{0,1},{1,0},{2,3},{3,2},{4,5},{5,4},{6,7},{7,6},{8,9},{9,8},{10,11... | collective-permute-start | bytes 1769480 | tf_op jit(solution)/shard_map/ppermute | solution.py:454
  44.3 4.8 %all-to-all-start = ((bf16[4,192,384]{2,1,0:T(8,128)(2,1)}), bf16[4,192,384]{2,1,0:T(8,128)(2,1)S(1)}, u32[]{:S(2)}, u32[]{:S(2)}) async-start(bf16[4,192,384]{2,1,0:T(8,128)(2,1)} %bitcast.10), calls=%async_computation | async-start | bytes 1179648 | tf_op jit(solution)/shard_map/all_to_all | solution.py:450
  49.0 3.5 %collective-permute-start.4 = (f32[24,384]{1,0:T(8,128)S(1)}, f32[24,384]{1,0:T(8,128)S(1)}, u32[]{:S(2)}, u32[]{:S(2)}) collective-permute-start(f32[24,384]{1,0:T(8,128)S(1)} %get-tuple-element.55), channel_id=1, source_target_pairs={{0,4},{4,8},{8,12},{12,16},{16,20},{20,24},{24,28},{28,32},{32,36}... | collective-permute-start | bytes 110600 | tf_op jit(solution)/shard_map/ppermute | solution.py:441
  52.5 2.4 %collective-permute-start.5 = (f32[24,384]{1,0:T(8,128)S(1)}, f32[24,384]{1,0:T(8,128)S(1)}, u32[]{:S(2)}, u32[]{:S(2)}) collective-permute-start(f32[24,384]{1,0:T(8,128)S(1)} %get-tuple-element.56), channel_id=1, source_target_pairs={{4,0},{8,4},{12,8},{16,12},{20,16},{24,20},{28,24},{32,28},{36,32}... | collective-permute-start | bytes 110600 | tf_op jit(solution)/shard_map/ppermute | solution.py:446
  54.9 4.7 %collective-permute-done.5.high = f32[24,384]{1,0:T(8,128)S(1)} collective-permute-done((f32[24,384]{1,0:T(8,128)S(1)}, f32[24,384]{1,0:T(8,128)S(1)}, u32[]{:S(2)}, u32[]{:S(2)}) %collective-permute-start.5) | collective-permute-done | bytes 36896 | tf_op jit(solution)/shard_map/ppermute | solution.py:446
  59.6 1.7 %shard_map.134 = (bf16[64,32,128]{2,1,0:T(8,128)(2,1)S(1)}, bf16[64,32,128]{2,1,0:T(8,128)(2,1)S(1)}) custom-call(bf16[4,192,384]{2,1,0:T(8,128)(2,1)S(1)} %all-to-all-done.out_blocks, f32[768,384]{1,0:T(8,128)S(1)} %get-tuple-element.58.kept, bf16[768,384]{1,0:T(8,128)(2,1)S(1)} %collective-permute-done.3.received), custom_call_target="tpu_custom_call" | custom-call | flops 294912 | bytes 2359296 | tf_op jit(solution)/shard_map/pallas_call | solution.py:311
  61.3 36.2 %all_to_all.20.received = bf16[64,32,128]{2,1,0:T(8,128)(2,1)S(1)} all-to-all(bf16[64,32,128]{2,1,0:T(8,128)(2,1)S(1)} %get-tuple-element.60), channel_id=1, replica_groups=mesh['zh'=4,'x'=4,'y'=8,'zl'=2,'c'=2] {'zh','y','zl'}, dimensions={0} | all-to-all | bytes 1048576 | tf_op jit(solution)/shard_map/all_to_all | solution.py:450
  97.7 24.3 %all_to_all.21.received = bf16[64,32,128]{2,1,0:T(8,128)(2,1)S(1)} all-to-all(bf16[64,32,128]{2,1,0:T(8,128)(2,1)S(1)} %get-tuple-element.63), channel_id=1, replica_groups=mesh['zh'=4,'x'=4,'y'=8,'zl'=2,'c'=2] {'zh','y','zl'}, dimensions={0} | all-to-all | bytes 1048576 | tf_op jit(solution)/shard_map/all_to_all | solution.py:450
  122.3 11.1 %all_to_all.22.received.own = bf16[4,208,384]{2,1,0:T(8,128)(2,1)S(1)} all-to-all(bf16[4,208,384]{2,1,0:T(8,128)(2,1)S(1)} %shard_map.136), channel_id=1, replica_groups=mesh['zh'=4,'x'=4,'y'=8,'zl'=2,'c'=2] {'x'}, dimensions={0} | all-to-all | bytes 1277952 | tf_op jit(solution)/shard_map/all_to_all | solution.py:450
  133.4 1.9 %collective-permute-start.7 = (bf16[4,208,384]{2,1,0:T(8,128)(2,1)S(1)}, bf16[4,208,384]{2,1,0:T(8,128)(2,1)S(1)}, u32[]{:S(2)}, u32[]{:S(2)}) collective-permute-start(bf16[4,208,384]{2,1,0:T(8,128)(2,1)S(1)} %all_to_all.22.received.own), channel_id=1, source_target_pairs={{0,1},{1,0},{2,3},{3,2},{4,5},{5,4},{6,7},{7,6},{8,9},{9,8},{10,11... | collective-permute-start | bytes 1916936 | tf_op jit(solution)/shard_map/ppermute | solution.py:454
  135.3 4.1 %collective-permute-start.6 = (f32[3,384]{1,0:T(4,128)S(1)}, f32[3,384]{1,0:T(4,128)S(1)}, u32[]{:S(2)}, u32[]{:S(2)}) collective-permute-start(f32[3,384]{1,0:T(4,128)S(1)} %shard_map.138), channel_id=1, source_target_pairs={{0,0},{1,256},{2,1},{3,257},{4,2},{5,258},{6,3},{7,259},{8,4},{9,2... | collective-permute-start | bytes 13832 | tf_op jit(solution)/shard_map/ppermute | solution.py:506
  139.5 2.3 %shard_map.137 = bf16[256,384]{1,0:T(8,128)(2,1)} custom-call(f32[256,384]{1,0:T(8,128)S(1)} %get-tuple-element.52.grad_conv, f32[24,384]{1,0:T(8,128)S(1)} %collective-permute-done.4.low, f32[24,384]{1,0:T(8,128)S(1)} %collective-permute-done.5.high, f32[7,7,384]{2,1,0:T(8,128)S(1)} %copy-done.8, bf16[256,384]{1,0:T(8,128)(2,1)S(1)} %bitcast.7), custom_call_target="tpu_custom_call" | custom-call | flops 9633792 | bytes 2097152 | tf_op jit(solution)/shard_map/pallas_call | solution.py:311
  141.8 9.3 %collective-permute-done.6 = f32[3,384]{1,0:T(4,128)S(1)} collective-permute-done((f32[3,384]{1,0:T(4,128)S(1)}, f32[3,384]{1,0:T(4,128)S(1)}, u32[]{:S(2)}, u32[]{:S(2)}) %collective-permute-start.6) | collective-permute-done | bytes 4640 | tf_op jit(solution)/shard_map/ppermute | solution.py:506
  151.1 1.1 shard_map.139
  (50 shorter events, 10.1 us)
Async XLA Ops:
  2.1 21.8 %collective-permute-start.1 = (bf16[8,3,384]{2,1,0:T(4,128)(2,1)}, bf16[8,3,384]{2,1,0:T(4,128)(2,1)}, u32[]{:S(2)}, u32[]{:S(2)}) collective-permute-start(bf16[8,3,384]{2,1,0:T(4,128)(2,1)} %get-tuple-element.69), channel_id=1, source_target_pairs={{4,0},{8,4},{12,8},{16,12},{20,16},{24,20},{28,24},{32,28},{36,32}... | collective-permute-start | bytes 55304 | tf_op jit(solution)/shard_map/ppermute | solution.py:446
  4.5 20.8 %collective-permute-start = (bf16[8,3,384]{2,1,0:T(4,128)(2,1)}, bf16[8,3,384]{2,1,0:T(4,128)(2,1)}, u32[]{:S(2)}, u32[]{:S(2)}) collective-permute-start(bf16[8,3,384]{2,1,0:T(4,128)(2,1)} %get-tuple-element.70), channel_id=1, source_target_pairs={{0,4},{4,8},{8,12},{12,16},{16,20},{20,24},{24,28},{28,32},{32,36}... | collective-permute-start | bytes 55304 | tf_op jit(solution)/shard_map/ppermute | solution.py:441
  9.2 1.3 copy-start.3
  10.4 0.9 copy-start.4
  11.4 0.9 copy-start.9
  12.3 0.9 copy-start.14
  13.2 0.7 copy-start.17
  13.9 0.7 copy-start.18
  14.6 0.7 copy-start.19
  15.2 0.7 copy-start.20
  15.9 0.7 copy-start.21
  16.6 0.7 copy-start.22
  22.0 0.6 copy-start.6
  22.6 0.7 copy-start.10
  23.3 0.6 copy-start.12
  26.6 0.9 copy-start.7
  27.5 0.9 copy-start.11
  28.4 0.8 copy-start.13
  29.2 0.7 copy-start.15
  29.9 0.7 copy-start.16
  30.7 5.8 %copy-start = (f32[1536,256]{1,0:T(8,128)S(1)}, f32[1536,256]{1,0:T(8,128)}, u32[]{:S(2)}) copy-start(f32[1536,256]{1,0:T(8,128)} %get-tuple-element.44.back) | copy-start | bytes 4718596
  34.5 5.5 %collective-permute-start.2 = (bf16[768,384]{1,0:T(8,128)(2,1)S(1)}, bf16[768,384]{1,0:T(8,128)(2,1)S(1)}, u32[]{:S(2)}, u32[]{:S(2)}) collective-permute-start(bf16[768,384]{1,0:T(8,128)(2,1)S(1)} %get-tuple-element.43), channel_id=1, source_target_pairs={{0,1},{1,0},{2,3},{3,2},{4,5},{5,4},{6,7},{7,6},{8,9},{9,8},{10,11... | collective-permute-start | bytes 1769480 | tf_op jit(solution)/shard_map/ppermute | solution.py:454
  36.5 1.4 copy-start.1
  37.9 1.4 copy-start.2
  41.9 17.7 %collective-permute-start.3 = (bf16[768,384]{1,0:T(8,128)(2,1)S(1)}, bf16[768,384]{1,0:T(8,128)(2,1)S(1)}, u32[]{:S(2)}, u32[]{:S(2)}) collective-permute-start(bf16[768,384]{1,0:T(8,128)(2,1)S(1)} %get-tuple-element.54), channel_id=1, source_target_pairs={{0,1},{1,0},{2,3},{3,2},{4,5},{5,4},{6,7},{7,6},{8,9},{9,8},{10,11... | collective-permute-start | bytes 1769480 | tf_op jit(solution)/shard_map/ppermute | solution.py:454
  44.3 15.3 %all-to-all-start = ((bf16[4,192,384]{2,1,0:T(8,128)(2,1)}), bf16[4,192,384]{2,1,0:T(8,128)(2,1)S(1)}, u32[]{:S(2)}, u32[]{:S(2)}) async-start(bf16[4,192,384]{2,1,0:T(8,128)(2,1)} %bitcast.10), calls=%async_computation | async-start | bytes 1179648 | tf_op jit(solution)/shard_map/all_to_all | solution.py:450
  49.0 5.8 %collective-permute-start.4 = (f32[24,384]{1,0:T(8,128)S(1)}, f32[24,384]{1,0:T(8,128)S(1)}, u32[]{:S(2)}, u32[]{:S(2)}) collective-permute-start(f32[24,384]{1,0:T(8,128)S(1)} %get-tuple-element.55), channel_id=1, source_target_pairs={{0,4},{4,8},{8,12},{12,16},{16,20},{20,24},{24,28},{28,32},{32,36}... | collective-permute-start | bytes 110600 | tf_op jit(solution)/shard_map/ppermute | solution.py:441
  52.5 7.1 %collective-permute-start.5 = (f32[24,384]{1,0:T(8,128)S(1)}, f32[24,384]{1,0:T(8,128)S(1)}, u32[]{:S(2)}, u32[]{:S(2)}) collective-permute-start(f32[24,384]{1,0:T(8,128)S(1)} %get-tuple-element.56), channel_id=1, source_target_pairs={{4,0},{8,4},{12,8},{16,12},{20,16},{24,20},{28,24},{32,28},{36,32}... | collective-permute-start | bytes 110600 | tf_op jit(solution)/shard_map/ppermute | solution.py:446
  122.3 17.2 %copy-start.5 = (bf16[1,8,32,384]{3,2,1,0:T(8,128)(2,1)S(1)}, bf16[1,8,32,384]{3,2,1,0:T(8,128)(2,1)}, u32[]{:S(2)}) copy-start(bf16[1,8,32,384]{3,2,1,0:T(8,128)(2,1)} %param.12) | copy-start | bytes 589828
  122.3 17.2 %copy-start.8 = (f32[7,7,384]{2,1,0:T(8,128)S(1)}, f32[7,7,384]{2,1,0:T(8,128)}, u32[]{:S(2)}) copy-start(f32[7,7,384]{2,1,0:T(8,128)} %copy-done.6) | copy-start | bytes 225796
  133.4 17.7 %collective-permute-start.7 = (bf16[4,208,384]{2,1,0:T(8,128)(2,1)S(1)}, bf16[4,208,384]{2,1,0:T(8,128)(2,1)S(1)}, u32[]{:S(2)}, u32[]{:S(2)}) collective-permute-start(bf16[4,208,384]{2,1,0:T(8,128)(2,1)S(1)} %all_to_all.22.received.own), channel_id=1, source_target_pairs={{0,1},{1,0},{2,3},{3,2},{4,5},{5,4},{6,7},{7,6},{8,9},{9,8},{10,11... | collective-permute-start | bytes 1916936 | tf_op jit(solution)/shard_map/ppermute | solution.py:454
  135.3 15.7 %collective-permute-start.6 = (f32[3,384]{1,0:T(4,128)S(1)}, f32[3,384]{1,0:T(4,128)S(1)}, u32[]{:S(2)}, u32[]{:S(2)}) collective-permute-start(f32[3,384]{1,0:T(4,128)S(1)} %shard_map.138), channel_id=1, source_target_pairs={{0,0},{1,256},{2,1},{3,257},{4,2},{5,258},{6,3},{7,259},{8,4},{9,2... | collective-permute-start | bytes 13832 | tf_op jit(solution)/shard_map/ppermute | solution.py:506

commit v4 on v3

--- a/solution.py
+++ b/solution.py
@@ -15,9 +15,9 @@
 LANES = 128
 CHUNK = 32
 ROWS = 3
-PLACES = 32
+EDGE = 4 * SIDE
 EPSILON = 1e-06
-VMEM_LIMIT = 48 * 1024 * 1024
+VMEM_LIMIT = 24 * 1024 * 1024
 NT = (((1,), (1,)), ((), ()))
 
 TILE = ("zh", "x", "y")
@@ -67,6 +67,18 @@
 def widen(source, wide):
     for k, lanes in enumerate(lane_blocks(source.shape[1])):
         wide[k] = source[:, lanes].astype(jnp.float32)
+
+
+def edge_kernel(features, low, high, image, wide, sem):
+    copy = pltpu.make_async_copy(features, image, sem)
+    copy.start()
+    copy.wait()
+    widen(image, wide)
+    count = EDGE // SIDE
+    for k, lanes in enumerate(lane_blocks(features.shape[1])):
+        for first, edge in ((0, low), (COLS - count, high)):
+            columns = [wide[k, pl.ds(first + j, SIDE, stride=COLS), :] for j in range(count)]
+            edge[:, lanes] = jnp.concatenate(columns, axis=0).astype(jnp.bfloat16)
 
 
 def first_kernel(
@@ -130,13 +142,13 @@
 ):
     width = conv.shape[1]
     rows[...] = conv[...]
-    widen(low, low_wide)
-    widen(high, high_wide)
-    for k, lanes in enumerate(lane_blocks(width)):
-        near = [low_wide[k, pl.ds(j, SIDE, stride=HALO), :] for j in range(HALO)]
+    low_wide[...] = low[...].astype(jnp.float32)
+    high_wide[...] = high[...].astype(jnp.float32)
+    for lanes in lane_blocks(width):
+        near = [low_wide[(j + 1) * SIDE : (j + 2) * SIDE, lanes] for j in range(HALO)]
         for j, total in enumerate(convolve(near + [None] * (2 * HALO), taps, lanes, False)):
             rows[j * SIDE : (j + 1) * SIDE, lanes] += total
-        near = [high_wide[k, pl.ds(j, SIDE, stride=HALO), :] for j in range(HALO)]
+        near = [high_wide[j * SIDE : (j + 1) * SIDE, lanes] for j in range(HALO)]
         for j, total in enumerate(convolve([None] * (2 * HALO) + near, taps, lanes, False)):
             start = (COLS - HALO + j) * SIDE
             rows[start : start + SIDE, lanes] += total
@@ -217,32 +229,18 @@
         grad_features[:, lanes] = result.astype(jnp.bfloat16)
 
 
-def pack_kernel(out_blocks, kept, received, first, second, spread, total):
-    members, places, _ = first.shape
-    width = kept.shape[1]
-    for k, lanes in enumerate(lane_blocks(width)):
-        total[k] = kept[:, lanes] + received[:, lanes].astype(jnp.float32)
-    blocks = len(lane_blocks(width))
-    for message in (first, second):
-        spread[...] = jnp.zeros_like(spread)
-        if message is first:
-            for r in range(ROWS):
-                part = slice(r * members, (r + 1) * members)
-                for k, lanes in enumerate(lane_blocks(width)):
-                    summed = out_blocks[0, part, lanes].astype(jnp.float32)
-                    for i in range(1, out_blocks.shape[0]):
-                        summed += out_blocks[i, part, lanes].astype(jnp.float32)
-                    spread[pl.ds(r * blocks + k, members, stride=places), :] = summed
-        offset = 0 if message is first else 2
-        for b in range(2):
-            for r in range(ROWS):
-                start = (offset + b) * ROWS * members + r
-                for k in range(blocks):
-                    place = ((1 + b) * ROWS + r) * blocks + k
-                    spread[pl.ds(place, members, stride=places), :] = total[
-                        k, pl.ds(start, members, stride=ROWS), :
-                    ]
-        message[...] = spread[...].reshape(message.shape).astype(jnp.bfloat16)
+def pack_kernel(out_blocks, message, spread):
+    members, places, _ = message.shape
+    blocks = lane_blocks(out_blocks.shape[2])
+    spread[...] = jnp.zeros_like(spread)
+    for r in range(ROWS):
+        part = slice(r * members, (r + 1) * members)
+        for k, lanes in enumerate(blocks):
+            summed = out_blocks[0, part, lanes].astype(jnp.float32)
+            for i in range(1, out_blocks.shape[0]):
+                summed += out_blocks[i, part, lanes].astype(jnp.float32)
+            spread[pl.ds(r * len(blocks) + k, members, stride=places), :] = summed
+    message[...] = spread[...].reshape(message.shape).astype(jnp.bfloat16)
 
 
 def add_members(received):
@@ -252,60 +250,50 @@
     return summed
 
 
-def turn_kernel(scale, received, second, message, kept_sums):
-    summed = add_members(received)
-    kept_sums[...] = summed
-    finished = (summed * scale).astype(jnp.bfloat16)
-    place = lax.broadcasted_iota(jnp.int32, finished.shape, 0)
-    of_out = place < ROWS * ROWS
-    for m in range(message.shape[0]):
-        message[m] = jnp.where(of_out, finished, second[m])
-
-
-def unpack_kernel(kept_sums, received, message, spread):
+def turn_kernel(scale, received, in_rows, message, spread, total):
+    members, places, _ = message.shape
+    blocks = lane_blocks(in_rows.shape[1])
+    summed = add_members(received) * scale
+    spread[...] = jnp.zeros_like(spread)
+    size = ROWS * len(blocks)
+    for place in range(size):
+        row = jnp.broadcast_to(summed[place : place + 1, :], (members, LANES))
+        spread[pl.ds(place, members, stride=places), :] = row
+    for k, lanes in enumerate(blocks):
+        total[k] = in_rows[:, lanes]
+        for r in range(ROWS):
+            place = size + r * len(blocks) + k
+            part = total[k, pl.ds(r, members, stride=ROWS), :]
+            spread[pl.ds(place, members, stride=places), :] = part
+    message[...] = spread[...].reshape(message.shape).astype(jnp.bfloat16)
+
+
+def unpack_kernel(scale, received, message, grad_w_in, spread, sums):
     members, places, _ = received.shape
-    lines, rows, width = message.shape
-    count = ROWS * members
+    blocks = lane_blocks(message.shape[2])
     spread[...] = received[...].astype(jnp.float32).reshape(spread.shape)
-    blocks = len(lane_blocks(width))
     for r in range(ROWS):
-        for k, lanes in enumerate(lane_blocks(width)):
-            part = spread[pl.ds(r * blocks + k, members, stride=places), :].astype(jnp.bfloat16)
-            for i in range(lines):
+        for k, lanes in enumerate(blocks):
+            part = spread[pl.ds(r * len(blocks) + k, members, stride=places), :]
+            part = part.astype(jnp.bfloat16)
+            for i in range(message.shape[0]):
                 message[i, r * members : (r + 1) * members, lanes] = part
-    last_sums = add_members(received)
-    size = ROWS * blocks
-    for i in range(lines):
-        sums = kept_sums[...] if i < 2 else last_sums
-        start = size * (1 + i % 2)
-        part = jnp.concatenate([sums[start : start + size, :], jnp.zeros((rows - count - size, LANES), jnp.float32)], axis=0)
-        message[i, count:, :LANES] = part.astype(jnp.bfloat16)
-        message[i, count:, LANES:] = jnp.zeros((rows - count, width - LANES), jnp.bfloat16)
-
-
-def line_kernel(scale, received, grad_w_in, spread):
-    count = received.shape[1] - 16
-    spread[...] = received[0, count:, :LANES].astype(jnp.float32)
-    for i in range(1, received.shape[0]):
-        spread[...] += received[i, count:, :LANES].astype(jnp.float32)
-    blocks = grad_w_in.shape[1] // LANES
-    for k in range(blocks):
-        grad_w_in[:, k * LANES : (k + 1) * LANES] = (
-            spread[pl.ds(k, ROWS, stride=blocks), :] * scale
-        )
-
-
-def join_kernel(core, own, other, grad_w_out):
-    lines, rows, _ = own.shape
-    rows -= 16
-    half = lines * rows
-    for place, source in ((core[0], own), (1 - core[0], other)):
-        for i in range(lines):
-            start = pl.multiple_of(place * half + i * rows, rows)
-            grad_w_out[pl.ds(start, rows), :] = source[i, :rows, :]
+    sums[...] = add_members(received)
+    size = ROWS * len(blocks)
+    for k, lanes in enumerate(blocks):
+        grad_w_in[:, lanes] = sums[pl.ds(size + k, ROWS, stride=len(blocks)), :] * scale
+
+
+def join_kernel(core, own, other, in_rows, grad_w_out, grad_w_in):
+    half = own.shape[0]
+    grad_w_out[pl.ds(pl.multiple_of(core[0] * half, half), half), :] = own[...]
+    grad_w_out[pl.ds(pl.multiple_of((1 - core[0]) * half, half), half), :] = other[...]
+    grad_w_in[...] = in_rows[...]
 
 
 def call(kernel, outs, scratch, scalars, arrays, flops, nbytes, space=pltpu.VMEM):
+    if space == pltpu.HBM:
+        arrays = [pltpu.with_memory_space_constraint(array, pltpu.HBM) for array in arrays]
     in_specs = [pl.BlockSpec(memory_space=pltpu.SMEM)] * len(scalars)
     in_specs += [pl.BlockSpec(memory_space=space)] * len(arrays)
     return pl.pallas_call(
@@ -322,6 +310,18 @@
 F32, B16 = jnp.float32, jnp.bfloat16
 
 
+def edges(features):
+    rows, width = features.shape
+    return call(
+        edge_kernel,
+        [((EDGE, width), B16), ((EDGE, width), B16)],
+        [pltpu.VMEM((rows, width), B16), pltpu.VMEM((width // LANES, rows, LANES), F32), pltpu.SemaphoreType.DMA],
+        [],
+        [features],
+        features.size, 2 * features.size, pltpu.HBM,
+    )
+
+
 def before_halos(flags, features, cotangent, kernel, conv_bias, gain, bias, w_in, b_in, w_out, layer_scale):
     rows, width = features.shape
     hidden = w_out.shape[0]
@@ -343,7 +343,7 @@
 def forward(core, conv, low, high, taps, vectors, w_in_t, b_cols, out_grad):
     rows, width = conv.shape
     hidden = w_in_t.shape[0]
-    halo = pltpu.VMEM((width // LANES, HALO * SIDE, LANES), F32)
+    halo = pltpu.VMEM((EDGE, width), F32)
     return call(
         second_kernel,
         [((hidden // 2, width), F32), ((hidden // 2, width), B16), ((rows, width), F32), ((rows, LANES), F32),
@@ -385,55 +385,47 @@
     )[0]
 
 
-def pack(out_blocks, kept, received, members):
-    width = kept.shape[1]
-    message = ((members, PLACES, LANES), B16)
+def pack(out_blocks, members, places):
     return call(
         pack_kernel,
-        [message, message],
-        [pltpu.VMEM((members * PLACES, LANES), F32), pltpu.VMEM((width // LANES,) + kept.shape[:1] + (LANES,), F32)],
-        [],
-        [out_blocks, kept, received],
-        kept.size, 8 * kept.size,
-    )
-
-
-def turn(scale, received, second):
+        [((members, places, LANES), B16)],
+        [pltpu.VMEM((members * places, LANES), F32)],
+        [],
+        [out_blocks],
+        out_blocks.size, 3 * out_blocks.size,
+    )[0]
+
+
+def turn(scale, received, in_rows, places):
+    members = received.shape[0]
+    rows, width = in_rows.shape
     return call(
         functools.partial(turn_kernel, scale),
-        [(received.shape, B16), ((PLACES, LANES), F32)], [], [], [received, second],
-        received.size, 6 * received.size,
-    )
-
-
-def unpack(kept_sums, received, lines, rows, width):
-    return call(
-        unpack_kernel,
-        [((lines, rows + 16, width), B16)],
-        [pltpu.VMEM((received.shape[0] * received.shape[1], LANES), F32)],
-        [],
-        [kept_sums, received],
+        [((members, places, LANES), B16)],
+        [pltpu.VMEM((members * places, LANES), F32), pltpu.VMEM((width // LANES, rows, LANES), F32)],
+        [],
+        [received, in_rows],
         received.size, 6 * received.size,
     )[0]
 
 
-def over_lines(scale, received):
-    return call(
-        functools.partial(line_kernel, scale),
-        [((ROWS, received.shape[2]), F32)],
-        [pltpu.VMEM((16, LANES), F32)],
+def unpack(scale, received, lines, rows, width):
+    return call(
+        functools.partial(unpack_kernel, scale),
+        [((lines, rows, width), B16), ((ROWS, width), F32)],
+        [pltpu.VMEM((received.shape[0] * received.shape[1], LANES), F32), pltpu.VMEM(received.shape[1:], F32)],
         [],
         [received],
-        received.size, received.size,
-    )[0]
-
-
-def join(core, own, other):
-    lines, rows, width = own.shape
-    return call(
-        join_kernel, [((2 * lines * (rows - 16), width), B16)], [], [core], [own, other],
+        received.size, 6 * received.size,
+    )
+
+
+def join(core, own, other, in_rows):
+    rows, width = own.shape
+    return call(
+        join_kernel, [((2 * rows, width), B16), (in_rows.shape, F32)], [], [core], [own, other, in_rows],
         own.size, 8 * own.size,
-    )[0]
+    )
 
 
 def from_left(block):
@@ -471,9 +463,9 @@
 ):
     image = features[0]
     height, breadth, channels = image.shape
-    low = from_left(image[:, breadth - HALO :]).reshape(-1, channels)
-    high = from_right(image[:, :HALO]).reshape(-1, channels)
     rows = image.reshape(-1, channels)
+    low, high = edges(rows)
+    low, high = from_left(high), from_right(low)
     upstream = cotangent[0].reshape(-1, channels)
     core = lax.axis_index("c").astype(jnp.int32).reshape(1)
     sizes = [lax.axis_size(axis) for axis in EVERY]
@@ -493,19 +485,20 @@
     kept, sent, grad_conv, low, high = backward(
         core, grad_pre, w_in_here, normed, standard, inverse, vectors
     )
-    received = swap(sent)
+    in_total = kept + swap(sent).astype(F32)
     low, high = from_left(high), from_right(low)
-    out_blocks, received, low, high = lax.optimization_barrier((out_blocks, received, low, high))
-
-    first, second = pack(out_blocks, kept, received, ring)
-    message, kept_sums = turn(scale, exchange(first, RING), second)
-    message = unpack(kept_sums, exchange(message, RING), lines, out_blocks.shape[1], channels)
-    own = exchange(message, "x")
-    own, low, high = lax.optimization_barrier((own, low, high))
+    out_blocks, low, high, _ = lax.optimization_barrier((out_blocks, low, high, in_total))
+    in_rows = lax.psum_scatter(in_total, "x", scatter_dimension=0, tiled=True)
+
+    received = exchange(pack(out_blocks, ring, 16), RING)
+    received = exchange(turn(scale, received, in_rows, 24), RING)
+    message, in_rows = unpack(scale, received, lines, out_blocks.shape[1], channels)
+    own = exchange(message, "x").reshape(-1, channels)
+    own, in_rows, low, high = lax.optimization_barrier((own, in_rows, low, high))
     other = swap(own)
-    grad_w_in = lax.ppermute(over_lines(scale, own), EVERY, owners(sizes))
+    in_rows = lax.ppermute(in_rows, EVERY, owners(sizes))
     grad_image = to_features(grad_conv, low, high, taps, upstream)
-    grad_w_out = join(core, own, other)
+    grad_w_out, grad_w_in = join(core, own, other, in_rows)
     return (grad_image.reshape(1, height, breadth, channels), grad_w_in, grad_w_out)
 
 

time: 154 us -> 143 us (0.929)
  local copies, waits for them, and re-layouts: 21.6 us -> 0.97 us
  between operations: 0.84 us -> 14.2 us
  blocking collectives: 71.5 us -> 64.8 us
  waiting for transfers between devices: 14 us -> 18 us
  Pallas kernels: 15.8 us -> 14 us
    unnamed x47 -> x4, local copies, waits for them, and re-layouts: 17.4 us -> 0.97 us
    all_to_all x3, blocking collectives: 71.5 us -> 64.8 us  [exchange(): return lax.all_to_all(blocks, axes, split_axis=0, concat_axis=0, tiled=True)]
    ppermute x3, waiting for transfers between devices: 0.01 us -> 3.08 us  [swap(): return lax.ppermute(block, 'c', SWAP)]
    reshape x2 -> x0, local copies, waits for them, and re-layouts: 2.72 us -> none  [the longest x1 1.37 us: body(): high = from_right(image[:, :HALO]).reshape(-1, channels)]
    pallas_call x10, Pallas kernels: 15.8 us -> 14 us  [call(): pl.pallas_call(kernel, out_shape=[jax.ShapeDtypeStruct(shape, kind) for s...]
  transfers between devices with their start and end apart: 9 -> 10, of which waited for: 2 -> 5; matrix products, arithmetic and copies ran while one was open for 1% -> 0% of each run, Pallas kernels for 5% -> 5%
where the time goes in v4:
time: 143 us; the launch traced here: 142 us
  blocking collectives  64.8 us (45%)
  starting transfers between devices  28.1 us (20%)
  waiting for transfers between devices  18 us (13%)
  between operations  14.2 us (10%)
  Pallas kernels  14 us (10%)
  other arithmetic  2.09 us (1%)
    all_to_all x3, blocking collectives, exchange(): return lax.all_to_all(blocks, axes, split_axis=0, concat_axis=0, tiled=True)  64.8 us
    pallas_call x10, Pallas kernels, call(): pl.pallas_call(kernel, out_shape=[jax.ShapeDtypeStruct(shape, kind) for s...  14 us
    ppermute x2, starting transfers between devices, from_left(): return lax.ppermute(block, TILE, [(i, i + 1) for i in range(count - 1)])  9.24 us
    ppermute x1, waiting for transfers between devices, body(): in_rows = lax.ppermute(in_rows, EVERY, owners(sizes))  9.17 us
    ppermute x3, starting transfers between devices, swap(): return lax.ppermute(block, 'c', SWAP)  5.87 us
    ppermute x2, waiting for transfers between devices, from_right(): return lax.ppermute(block, TILE, [(i + 1, i) for i in range(count - 1)])  5.71 us
    all_to_all x1, starting transfers between devices, exchange(): return lax.all_to_all(blocks, axes, split_axis=0, concat_axis=0, tiled=True)  4.78 us
    ppermute x1, starting transfers between devices, body(): in_rows = lax.ppermute(in_rows, EVERY, owners(sizes))  4.28 us
  transfers between devices with their start and end apart: 10, of which 5 were waited for; matrix products, arithmetic and copies ran while one was open for 0% of the time, Pallas kernels for 5%

profile of v4, /device:TPU:30, one launch (start us, length us, event | category | flops | bytes accessed | tf_op | source)
XLA Modules:
  0.0 142.0 jit_solution(15298905636709016008)
XLA Ops:
  7.2 0.0 reduce-scatter.2.cloned.1.call-start
  7.2 1.0 shard_map.131
  8.2 4.7 %collective-permute-start = (bf16[32,384]{1,0:T(8,128)(2,1)S(1)}, bf16[32,384]{1,0:T(8,128)(2,1)S(1)}, u32[]{:S(2)}, u32[]{:S(2)}) collective-permute-start(bf16[32,384]{1,0:T(8,128)(2,1)S(1)} %get-tuple-element.39), channel_id=1, source_target_pairs={{0,4},{4,8},{8,12},{12,16},{16,20},{20,24},{24,28},{28,32},{32,36}... | collective-permute-start | bytes 73736 | tf_op jit(solution)/shard_map/ppermute | solution.py:433
  12.9 1.9 %collective-permute-start.1 = (bf16[32,384]{1,0:T(8,128)(2,1)S(1)}, bf16[32,384]{1,0:T(8,128)(2,1)S(1)}, u32[]{:S(2)}, u32[]{:S(2)}) collective-permute-start(bf16[32,384]{1,0:T(8,128)(2,1)S(1)} %get-tuple-element.40), channel_id=1, source_target_pairs={{4,0},{8,4},{12,8},{16,12},{20,16},{24,20},{28,24},{32,28},{36,32}... | collective-permute-start | bytes 73736 | tf_op jit(solution)/shard_map/ppermute | solution.py:438
  14.9 4.4 %shard_map.130 = (f32[256,384]{1,0:T(8,128)S(1)}, bf16[256,384]{1,0:T(8,128)(2,1)S(1)}, f32[1536,256]{1,0:T(8,128)S(1)}, bf16[1536,384]{1,0:T(8,128)(2,1)S(1)}, ...) custom-call(s32[1,4]{1,0:T(1,128)} %flags.1, ...), custom_call_target="tpu_custom_call" | custom-call | flops 301989888 | bytes 8388608 | tf_op jit(solution)/shard_map/pallas_call | solution.py:299
  19.3 0.6 collective-permute-done.1.high
  19.9 2.9 %shard_map.132 = (f32[768,384]{1,0:T(8,128)S(1)}, bf16[768,384]{1,0:T(8,128)(2,1)S(1)}, f32[256,384]{1,0:T(8,128)S(1)}, f32[256,128]{1,0:T(8,128)S(1)}, bf16[256...) custom-call(s32[1]{0:T(128)} %bitcast.core, f32[256,384]{1,0:T(8,128)S(1)} %get-tuple-element.38.conv, ...), custom_call_target="tpu_custom_call" | custom-call | flops 603979776 | bytes 8388608 | tf_op jit(solution)/shard_map/pallas_call | solution.py:299
  22.8 1.9 %collective-permute-start.2 = (bf16[768,384]{1,0:T(8,128)(2,1)S(1)}, bf16[768,384]{1,0:T(8,128)(2,1)S(1)}, u32[]{:S(2)}, u32[]{:S(2)}) collective-permute-start(bf16[768,384]{1,0:T(8,128)(2,1)S(1)} %get-tuple-element.47), channel_id=1, source_target_pairs={{0,1},{1,0},{2,3},{3,2},{4,5},{5,4},{6,7},{7,6},{8,9},{9,8},{10,11... | collective-permute-start | bytes 1769480 | tf_op jit(solution)/shard_map/ppermute | solution.py:446
  24.7 0.7 shard_map.133.grad_pre
  25.5 1.2 collective-permute-done.2
  26.7 1.0 add_convert_fusion
  27.7 0.9 shard_map.134
  28.6 2.0 %collective-permute-start.5 = (bf16[768,384]{1,0:T(8,128)(2,1)S(1)}, bf16[768,384]{1,0:T(8,128)(2,1)S(1)}, u32[]{:S(2)}, u32[]{:S(2)}) collective-permute-start(bf16[768,384]{1,0:T(8,128)(2,1)S(1)} %get-tuple-element.61), channel_id=1, source_target_pairs={{0,1},{1,0},{2,3},{3,2},{4,5},{5,4},{6,7},{7,6},{8,9},{9,8},{10,11... | collective-permute-start | bytes 1769480 | tf_op jit(solution)/shard_map/ppermute | solution.py:446
  30.6 1.8 %collective-permute-done.5 = bf16[768,384]{1,0:T(8,128)(2,1)S(1)} collective-permute-done((bf16[768,384]{1,0:T(8,128)(2,1)S(1)}, bf16[768,384]{1,0:T(8,128)(2,1)S(1)}, u32[]{:S(2)}, u32[]{:S(2)}) %collective-permute-start.5) | collective-permute-done | bytes 589856 | tf_op jit(solution)/shard_map/ppermute | solution.py:446
  32.4 1.1 convert_add_fusion
  33.6 0.0 reduce-scatter.2.cloned.1.call-update
  33.6 4.8 %all-to-all-start = ((bf16[4,192,384]{2,1,0:T(8,128)(2,1)}), bf16[4,192,384]{2,1,0:T(8,128)(2,1)S(1)}, u32[]{:S(2)}, u32[]{:S(2)}) async-start(bf16[4,192,384]{2,1,0:T(8,128)(2,1)} %bitcast.3), calls=%async_computation | async-start | bytes 1179648 | tf_op jit(solution)/shard_map/all_to_all | solution.py:442
  38.4 4.5 %collective-permute-start.3 = (f32[24,384]{1,0:T(8,128)S(1)}, f32[24,384]{1,0:T(8,128)S(1)}, u32[]{:S(2)}, u32[]{:S(2)}) collective-permute-start(f32[24,384]{1,0:T(8,128)S(1)} %get-tuple-element.58), channel_id=1, source_target_pairs={{0,4},{4,8},{8,12},{12,16},{16,20},{20,24},{24,28},{28,32},{32,36}... | collective-permute-start | bytes 110600 | tf_op jit(solution)/shard_map/ppermute | solution.py:433
  42.9 1.9 %collective-permute-start.4 = (f32[24,384]{1,0:T(8,128)S(1)}, f32[24,384]{1,0:T(8,128)S(1)}, u32[]{:S(2)}, u32[]{:S(2)}) collective-permute-start(f32[24,384]{1,0:T(8,128)S(1)} %get-tuple-element.59), channel_id=1, source_target_pairs={{4,0},{8,4},{12,8},{16,12},{20,16},{24,20},{28,24},{32,28},{36,32}... | collective-permute-start | bytes 110600 | tf_op jit(solution)/shard_map/ppermute | solution.py:438
  44.9 5.1 %collective-permute-done.4.high = f32[24,384]{1,0:T(8,128)S(1)} collective-permute-done((f32[24,384]{1,0:T(8,128)S(1)}, f32[24,384]{1,0:T(8,128)S(1)}, u32[]{:S(2)}, u32[]{:S(2)}) %collective-permute-start.4) | collective-permute-done | bytes 36896 | tf_op jit(solution)/shard_map/ppermute | solution.py:438
  50.0 0.2 shard_map.135
  50.2 32.5 %all_to_all.20.received = bf16[64,16,128]{2,1,0:T(8,128)(2,1)S(1)} all-to-all(bf16[64,16,128]{2,1,0:T(8,128)(2,1)S(1)} %shard_map.135), channel_id=1, replica_groups=mesh['zh'=4,'x'=4,'y'=8,'zl'=2,'c'=2] {'zh','y','zl'}, dimensions={0} | all-to-all | bytes 524288 | tf_op jit(solution)/shard_map/all_to_all | solution.py:442
  82.7 1.0 copy-done.1
  83.7 0.2 shard_map.136
  83.9 21.5 %all_to_all.21.received = bf16[64,24,128]{2,1,0:T(8,128)(2,1)S(1)} all-to-all(bf16[64,24,128]{2,1,0:T(8,128)(2,1)S(1)} %shard_map.136), channel_id=1, replica_groups=mesh['zh'=4,'x'=4,'y'=8,'zl'=2,'c'=2] {'zh','y','zl'}, dimensions={0} | all-to-all | bytes 786432 | tf_op jit(solution)/shard_map/all_to_all | solution.py:442
  105.4 0.2 shard_map.137
  105.6 10.8 %all_to_all.22 = bf16[4,192,384]{2,1,0:T(8,128)(2,1)S(1)} all-to-all(bf16[4,192,384]{2,1,0:T(8,128)(2,1)S(1)} %get-tuple-element.63), channel_id=1, replica_groups=mesh['zh'=4,'x'=4,'y'=8,'zl'=2,'c'=2] {'x'}, dimensions={0} | all-to-all | bytes 1179648 | tf_op jit(solution)/shard_map/all_to_all | solution.py:442
  116.4 1.9 %collective-permute-start.6 = (bf16[768,384]{1,0:T(8,128)(2,1)S(1)}, bf16[768,384]{1,0:T(8,128)(2,1)S(1)}, u32[]{:S(2)}, u32[]{:S(2)}) collective-permute-start(bf16[768,384]{1,0:T(8,128)(2,1)S(1)} %bitcast.6), channel_id=1, source_target_pairs={{0,1},{1,0},{2,3},{3,2},{4,5},{5,4},{6,7},{7,6},{8,9},{9,8},{10,11... | collective-permute-start | bytes 1769480 | tf_op jit(solution)/shard_map/ppermute | solution.py:446
  118.3 4.3 %collective-permute-start.7 = (f32[3,384]{1,0:T(4,128)S(1)}, f32[3,384]{1,0:T(4,128)S(1)}, u32[]{:S(2)}, u32[]{:S(2)}) collective-permute-start(f32[3,384]{1,0:T(4,128)S(1)} %get-tuple-element.70), channel_id=1, source_target_pairs={{0,0},{1,256},{2,1},{3,257},{4,2},{5,258},{6,3},{7,259},{8,4},{9,2... | collective-permute-start | bytes 13832 | tf_op jit(solution)/shard_map/ppermute | solution.py:499
  122.6 2.3 %shard_map.138 = bf16[256,384]{1,0:T(8,128)(2,1)} custom-call(f32[256,384]{1,0:T(8,128)S(1)} %get-tuple-element.56.grad_conv, f32[24,384]{1,0:T(8,128)S(1)} %collective-permute-done.3.low, f32[24,384]{1,0:T(8,128)S(1)} %collective-permute-done.4.high, f32[7,7,384]{2,1,0:T(8,128)S(1)} %get-tuple-element.41.taps, bf16[256,384]{1,0:T(8,128)(2,1)S(1)} %bitcast.9), custom_call_target="tpu_custom_call" | custom-call | flops 9633792 | bytes 2097152 | tf_op jit(solution)/shard_map/pallas_call | solution.py:299
  124.9 9.2 %collective-permute-done.7.in_rows = f32[3,384]{1,0:T(4,128)S(1)} collective-permute-done((f32[3,384]{1,0:T(4,128)S(1)}, f32[3,384]{1,0:T(4,128)S(1)}, u32[]{:S(2)}, u32[]{:S(2)}) %collective-permute-start.7) | collective-permute-done | bytes 4640 | tf_op jit(solution)/shard_map/ppermute | solution.py:499
  134.1 1.1 shard_map.139
  (8 shorter events, 0.0 us)
Async XLA Ops:
  7.2 75.6 %reduce-scatter.2.cloned.1.call-start = ((), (), s32[]{:S(2)}) async-start(), calls=%async_computation.5 | async-start | bytes 1474560 | tf_op jit(solution)/shard_map/reduce_scatter | solution.py:491
  8.2 11.0 %collective-permute-start = (bf16[32,384]{1,0:T(8,128)(2,1)S(1)}, bf16[32,384]{1,0:T(8,128)(2,1)S(1)}, u32[]{:S(2)}, u32[]{:S(2)}) collective-permute-start(bf16[32,384]{1,0:T(8,128)(2,1)S(1)} %get-tuple-element.39), channel_id=1, source_target_pairs={{0,4},{4,8},{8,12},{12,16},{16,20},{20,24},{24,28},{28,32},{32,36}... | collective-permute-start | bytes 73736 | tf_op jit(solution)/shard_map/ppermute | solution.py:433
  12.9 6.9 %collective-permute-start.1 = (bf16[32,384]{1,0:T(8,128)(2,1)S(1)}, bf16[32,384]{1,0:T(8,128)(2,1)S(1)}, u32[]{:S(2)}, u32[]{:S(2)}) collective-permute-start(bf16[32,384]{1,0:T(8,128)(2,1)S(1)} %get-tuple-element.40), channel_id=1, source_target_pairs={{4,0},{8,4},{12,8},{16,12},{20,16},{24,20},{28,24},{32,28},{36,32}... | collective-permute-start | bytes 73736 | tf_op jit(solution)/shard_map/ppermute | solution.py:438
  22.8 3.9 %collective-permute-start.2 = (bf16[768,384]{1,0:T(8,128)(2,1)S(1)}, bf16[768,384]{1,0:T(8,128)(2,1)S(1)}, u32[]{:S(2)}, u32[]{:S(2)}) collective-permute-start(bf16[768,384]{1,0:T(8,128)(2,1)S(1)} %get-tuple-element.47), channel_id=1, source_target_pairs={{0,1},{1,0},{2,3},{3,2},{4,5},{5,4},{6,7},{7,6},{8,9},{9,8},{10,11... | collective-permute-start | bytes 1769480 | tf_op jit(solution)/shard_map/ppermute | solution.py:446
  28.6 3.9 %collective-permute-start.5 = (bf16[768,384]{1,0:T(8,128)(2,1)S(1)}, bf16[768,384]{1,0:T(8,128)(2,1)S(1)}, u32[]{:S(2)}, u32[]{:S(2)}) collective-permute-start(bf16[768,384]{1,0:T(8,128)(2,1)S(1)} %get-tuple-element.61), channel_id=1, source_target_pairs={{0,1},{1,0},{2,3},{3,2},{4,5},{5,4},{6,7},{7,6},{8,9},{9,8},{10,11... | collective-permute-start | bytes 1769480 | tf_op jit(solution)/shard_map/ppermute | solution.py:446
  33.6 16.4 %all-to-all-start = ((bf16[4,192,384]{2,1,0:T(8,128)(2,1)}), bf16[4,192,384]{2,1,0:T(8,128)(2,1)S(1)}, u32[]{:S(2)}, u32[]{:S(2)}) async-start(bf16[4,192,384]{2,1,0:T(8,128)(2,1)} %bitcast.3), calls=%async_computation | async-start | bytes 1179648 | tf_op jit(solution)/shard_map/all_to_all | solution.py:442
  38.4 6.5 %collective-permute-start.3 = (f32[24,384]{1,0:T(8,128)S(1)}, f32[24,384]{1,0:T(8,128)S(1)}, u32[]{:S(2)}, u32[]{:S(2)}) collective-permute-start(f32[24,384]{1,0:T(8,128)S(1)} %get-tuple-element.58), channel_id=1, source_target_pairs={{0,4},{4,8},{8,12},{12,16},{16,20},{20,24},{24,28},{28,32},{32,36}... | collective-permute-start | bytes 110600 | tf_op jit(solution)/shard_map/ppermute | solution.py:433
  42.9 7.1 %collective-permute-start.4 = (f32[24,384]{1,0:T(8,128)S(1)}, f32[24,384]{1,0:T(8,128)S(1)}, u32[]{:S(2)}, u32[]{:S(2)}) collective-permute-start(f32[24,384]{1,0:T(8,128)S(1)} %get-tuple-element.59), channel_id=1, source_target_pairs={{4,0},{8,4},{12,8},{16,12},{20,16},{24,20},{28,24},{32,28},{36,32}... | collective-permute-start | bytes 110600 | tf_op jit(solution)/shard_map/ppermute | solution.py:438
  82.7 1.0 copy-start.1
  83.9 38.7 %copy-start = (bf16[1,8,32,384]{3,2,1,0:T(8,128)(2,1)S(1)}, bf16[1,8,32,384]{3,2,1,0:T(8,128)(2,1)}, u32[]{:S(2)}) copy-start(bf16[1,8,32,384]{3,2,1,0:T(8,128)(2,1)} %param.12) | copy-start | bytes 589828
  116.4 17.7 %collective-permute-start.6 = (bf16[768,384]{1,0:T(8,128)(2,1)S(1)}, bf16[768,384]{1,0:T(8,128)(2,1)S(1)}, u32[]{:S(2)}, u32[]{:S(2)}) collective-permute-start(bf16[768,384]{1,0:T(8,128)(2,1)S(1)} %bitcast.6), channel_id=1, source_target_pairs={{0,1},{1,0},{2,3},{3,2},{4,5},{5,4},{6,7},{7,6},{8,9},{9,8},{10,11... | collective-permute-start | bytes 1769480 | tf_op jit(solution)/shard_map/ppermute | solution.py:446
  118.3 15.7 %collective-permute-start.7 = (f32[3,384]{1,0:T(4,128)S(1)}, f32[3,384]{1,0:T(4,128)S(1)}, u32[]{:S(2)}, u32[]{:S(2)}) collective-permute-start(f32[3,384]{1,0:T(4,128)S(1)} %get-tuple-element.70), channel_id=1, source_target_pairs={{0,0},{1,256},{2,1},{3,257},{4,2},{5,258},{6,3},{7,259},{8,4},{9,2... | collective-permute-start | bytes 13832 | tf_op jit(solution)/shard_map/ppermute | solution.py:499
Sparse Core Ops, SparseCore 0:
  33.7 31.9 reduce-scatter.1

commit v5 on v4

--- a/solution.py
+++ b/solution.py
@@ -17,7 +17,7 @@
 ROWS = 3
 EDGE = 4 * SIDE
 EPSILON = 1e-06
-VMEM_LIMIT = 24 * 1024 * 1024
+VMEM_LIMIT = 16 * 1024 * 1024
 NT = (((1,), (1,)), ((), ()))
 
 TILE = ("zh", "x", "y")
@@ -250,17 +250,27 @@
     return summed
 
 
-def turn_kernel(scale, received, in_rows, message, spread, total):
+def lines_kernel(place, kept, received, own, first, second, third):
+    rows = own.shape[0]
+    for d, block in enumerate((own, first, second, third)):
+        part = pl.ds(pl.multiple_of((place[0] ^ d) * rows, rows), rows)
+        block[...] = (kept[part, :] + received[part, :].astype(jnp.float32)).astype(block.dtype)
+
+
+def turn_kernel(scale, received, own, first, second, third, message, spread, total):
     members, places, _ = message.shape
-    blocks = lane_blocks(in_rows.shape[1])
-    summed = add_members(received) * scale
+    blocks = lane_blocks(own.shape[1])
+    finished = add_members(received) * scale
     spread[...] = jnp.zeros_like(spread)
     size = ROWS * len(blocks)
     for place in range(size):
-        row = jnp.broadcast_to(summed[place : place + 1, :], (members, LANES))
+        row = jnp.broadcast_to(finished[place : place + 1, :], (members, LANES))
         spread[pl.ds(place, members, stride=places), :] = row
     for k, lanes in enumerate(blocks):
-        total[k] = in_rows[:, lanes]
+        summed = own[:, lanes]
+        for block in (first, second, third):
+            summed = summed + block[:, lanes].astype(jnp.float32)
+        total[k] = summed
         for r in range(ROWS):
             place = size + r * len(blocks) + k
             part = total[k, pl.ds(r, members, stride=ROWS), :]
@@ -396,15 +406,24 @@
     )[0]
 
 
-def turn(scale, received, in_rows, places):
+def split_lines(place, kept, received, lines):
+    rows, width = kept.shape
+    block = (rows // lines, width)
+    return call(
+        lines_kernel, [(block, F32)] + [(block, B16)] * 3, [], [place], [kept, received],
+        kept.size, 4 * kept.size,
+    )
+
+
+def turn(scale, received, in_blocks, places):
     members = received.shape[0]
-    rows, width = in_rows.shape
+    rows, width = in_blocks[0].shape
     return call(
         functools.partial(turn_kernel, scale),
         [((members, places, LANES), B16)],
         [pltpu.VMEM((members * places, LANES), F32), pltpu.VMEM((width // LANES, rows, LANES), F32)],
         [],
-        [received, in_rows],
+        [received, *in_blocks],
         received.size, 6 * received.size,
     )[0]
 
@@ -485,19 +504,23 @@
     kept, sent, grad_conv, low, high = backward(
         core, grad_pre, w_in_here, normed, standard, inverse, vectors
     )
-    in_total = kept + swap(sent).astype(F32)
+    line = lax.axis_index("x").astype(jnp.int32).reshape(1)
+    own, *others = split_lines(line, kept, swap(sent), lines)
     low, high = from_left(high), from_right(low)
-    out_blocks, low, high, _ = lax.optimization_barrier((out_blocks, low, high, in_total))
-    in_rows = lax.psum_scatter(in_total, "x", scatter_dimension=0, tiled=True)
-
+
+    out_blocks, *_ = lax.optimization_barrier((out_blocks, *others))
+    pairs = [[(i, i ^ d) for i in range(lines)] for d in range(1, lines)]
+    in_blocks = [own] + [lax.ppermute(block, "x", pair) for block, pair in zip(others, pairs)]
     received = exchange(pack(out_blocks, ring, 16), RING)
-    received = exchange(turn(scale, received, in_rows, 24), RING)
+    received, low, high = lax.optimization_barrier((received, low, high))
+    grad_image = to_features(grad_conv, low, high, taps, upstream)
+    received = exchange(turn(scale, received, in_blocks, 24), RING)
+    received, grad_image = lax.optimization_barrier((received, grad_image))
     message, in_rows = unpack(scale, received, lines, out_blocks.shape[1], channels)
     own = exchange(message, "x").reshape(-1, channels)
-    own, in_rows, low, high = lax.optimization_barrier((own, in_rows, low, high))
+    own, in_rows = lax.optimization_barrier((own, in_rows))
     other = swap(own)
     in_rows = lax.ppermute(in_rows, EVERY, owners(sizes))
-    grad_image = to_features(grad_conv, low, high, taps, upstream)
     grad_w_out, grad_w_in = join(core, own, other, in_rows)
     return (grad_image.reshape(1, height, breadth, channels), grad_w_in, grad_w_out)
 

time: 143 us -> 136 us (0.951)
  blocking collectives: 64.8 us -> 10.7 us
  starting transfers between devices: 28.1 us -> 70.1 us
  waiting for transfers between devices: 18 us -> 36.7 us
  between operations: 14.2 us -> 0.85 us
  Pallas kernels: 14 us -> 15.6 us
    all_to_all x3 -> x1, blocking collectives: 64.8 us -> 10.7 us  [exchange(): return lax.all_to_all(blocks, axes, split_axis=0, concat_axis=0, tiled=True)]
    all_to_all x1 -> x3, starting transfers between devices: 4.78 us -> 36.3 us  [exchange(): return lax.all_to_all(blocks, axes, split_axis=0, concat_axis=0, tiled=True)]
    all_to_all x1 -> x3, waiting for transfers between devices: 0.01 us -> 18.2 us  [exchange(): return lax.all_to_all(blocks, axes, split_axis=0, concat_axis=0, tiled=True)]
    ppermute x0 -> x3, starting transfers between devices: none -> 10.6 us  [body(): lax.ppermute(block, 'x', pair)]
    ppermute x1, waiting for transfers between devices: 9.17 us -> 11.5 us  [body(): in_rows = lax.ppermute(in_rows, EVERY, owners(sizes))]
    ppermute x3, waiting for transfers between devices: 3.08 us -> 1.23 us  [swap(): return lax.ppermute(block, 'c', SWAP)]
    pallas_call x10 -> x11, Pallas kernels: 14 us -> 15.6 us  [call(): pl.pallas_call(kernel, out_shape=[jax.ShapeDtypeStruct(shape, kind) for s...]
  transfers between devices with their start and end apart: 10 -> 14, of which waited for: 5 -> 6; matrix products, arithmetic and copies ran while one was open for 0% -> 0% of each run, Pallas kernels for 5% -> 6%
where the time goes in v5:
time: 136 us
  starting transfers between devices  70.1 us (52%)
  waiting for transfers between devices  36.7 us (27%)
  Pallas kernels  15.6 us (11%)
  blocking collectives  10.7 us (8%)
    all_to_all x3, starting transfers between devices, exchange(): return lax.all_to_all(blocks, axes, split_axis=0, concat_axis=0, tiled=True)  36.3 us
    all_to_all x3, waiting for transfers between devices, exchange(): return lax.all_to_all(blocks, axes, split_axis=0, concat_axis=0, tiled=True)  18.2 us
    pallas_call x11, Pallas kernels, call(): pl.pallas_call(kernel, out_shape=[jax.ShapeDtypeStruct(shape, kind) for s...  15.6 us
    ppermute x1, waiting for transfers between devices, body(): in_rows = lax.ppermute(in_rows, EVERY, owners(sizes))  11.5 us
    all_to_all x1, blocking collectives, exchange(): return lax.all_to_all(blocks, axes, split_axis=0, concat_axis=0, tiled=True)  10.7 us
    ppermute x3, starting transfers between devices, body(): lax.ppermute(block, 'x', pair)  10.6 us
    ppermute x2, starting transfers between devices, from_left(): return lax.ppermute(block, TILE, [(i, i + 1) for i in range(count - 1)])  9.28 us
    ppermute x3, starting transfers between devices, swap(): return lax.ppermute(block, 'c', SWAP)  5.88 us
  transfers between devices with their start and end apart: 14, of which 6 were waited for; matrix products, arithmetic and copies ran while one was open for 0% of the time, Pallas kernels for 6%

profile of v5, /device:TPU:30, one launch (start us, length us, event | category | flops | bytes accessed | tf_op | source)
XLA Modules:
  0.0 135.5 jit_solution(5694023553975921812)
XLA Ops:
  0.6 1.0 shard_map.131
  1.6 4.7 %collective-permute-start = (bf16[32,384]{1,0:T(8,128)(2,1)S(1)}, bf16[32,384]{1,0:T(8,128)(2,1)S(1)}, u32[]{:S(2)}, u32[]{:S(2)}) collective-permute-start(bf16[32,384]{1,0:T(8,128)(2,1)S(1)} %get-tuple-element.44), channel_id=1, source_target_pairs={{0,4},{4,8},{8,12},{12,16},{16,20},{20,24},{24,28},{28,32},{32,36}... | collective-permute-start | bytes 73736 | tf_op jit(solution)/shard_map/ppermute | solution.py:452
  6.4 1.9 %collective-permute-start.1 = (bf16[32,384]{1,0:T(8,128)(2,1)S(1)}, bf16[32,384]{1,0:T(8,128)(2,1)S(1)}, u32[]{:S(2)}, u32[]{:S(2)}) collective-permute-start(bf16[32,384]{1,0:T(8,128)(2,1)S(1)} %get-tuple-element.45), channel_id=1, source_target_pairs={{4,0},{8,4},{12,8},{16,12},{20,16},{24,20},{28,24},{32,28},{36,32}... | collective-permute-start | bytes 73736 | tf_op jit(solution)/shard_map/ppermute | solution.py:457
  8.3 4.4 %shard_map.130 = (f32[256,384]{1,0:T(8,128)S(1)}, bf16[256,384]{1,0:T(8,128)(2,1)S(1)}, f32[1536,256]{1,0:T(8,128)S(1)}, bf16[1536,384]{1,0:T(8,128)(2,1)S(1)}, ...) custom-call(s32[1,4]{1,0:T(1,128)} %flags.1, ...), custom_call_target="tpu_custom_call" | custom-call | flops 301989888 | bytes 8388608 | tf_op jit(solution)/shard_map/pallas_call | solution.py:309
  12.7 0.6 collective-permute-done.1.high
  13.3 2.9 %shard_map.132 = (f32[768,384]{1,0:T(8,128)S(1)}, bf16[768,384]{1,0:T(8,128)(2,1)S(1)}, f32[256,384]{1,0:T(8,128)S(1)}, f32[256,128]{1,0:T(8,128)S(1)}, bf16[256...) custom-call(s32[1]{0:T(128)} %bitcast.core, f32[256,384]{1,0:T(8,128)S(1)} %get-tuple-element.43.conv, ...), custom_call_target="tpu_custom_call" | custom-call | flops 603979776 | bytes 8388608 | tf_op jit(solution)/shard_map/pallas_call | solution.py:309
  16.2 1.9 %collective-permute-start.2 = (bf16[768,384]{1,0:T(8,128)(2,1)S(1)}, bf16[768,384]{1,0:T(8,128)(2,1)S(1)}, u32[]{:S(2)}, u32[]{:S(2)}) collective-permute-start(bf16[768,384]{1,0:T(8,128)(2,1)S(1)} %get-tuple-element.52), channel_id=1, source_target_pairs={{0,1},{1,0},{2,3},{3,2},{4,5},{5,4},{6,7},{7,6},{8,9},{9,8},{10,11... | collective-permute-start | bytes 1769480 | tf_op jit(solution)/shard_map/ppermute | solution.py:465
  18.1 0.7 shard_map.133.grad_pre
  18.9 1.2 collective-permute-done.2
  20.1 0.9 add_convert_fusion
  21.0 0.9 shard_map.134
  21.9 2.0 %collective-permute-start.3 = (bf16[768,384]{1,0:T(8,128)(2,1)S(1)}, bf16[768,384]{1,0:T(8,128)(2,1)S(1)}, u32[]{:S(2)}, u32[]{:S(2)}) collective-permute-start(bf16[768,384]{1,0:T(8,128)(2,1)S(1)} %get-tuple-element.63), channel_id=1, source_target_pairs={{0,1},{1,0},{2,3},{3,2},{4,5},{5,4},{6,7},{7,6},{8,9},{9,8},{10,11... | collective-permute-start | bytes 1769480 | tf_op jit(solution)/shard_map/ppermute | solution.py:465
  24.0 4.8 %all-to-all-start = ((bf16[4,192,384]{2,1,0:T(8,128)(2,1)}), bf16[4,192,384]{2,1,0:T(8,128)(2,1)S(1)}, u32[]{:S(2)}, u32[]{:S(2)}) async-start(bf16[4,192,384]{2,1,0:T(8,128)(2,1)} %bitcast.11), calls=%async_computation | async-start | bytes 1179648 | tf_op jit(solution)/shard_map/all_to_all | solution.py:461
  28.9 0.7 copy-done.1
  29.6 7.9 %all-to-all-done.out_blocks = bf16[4,192,384]{2,1,0:T(8,128)(2,1)S(1)} async-done(((bf16[4,192,384]{2,1,0:T(8,128)(2,1)}), bf16[4,192,384]{2,1,0:T(8,128)(2,1)S(1)}, u32[]{:S(2)}, u32[]{:S(2)}) %all-to-all-start) | async-done | bytes 589856 | tf_op jit(solution)/shard_map/all_to_all | solution.py:461
  37.4 0.9 shard_map.136
  38.4 16.6 %all-to-all-start.1 = ((bf16[64,16,128]{2,1,0:T(8,128)(2,1)}), bf16[64,16,128]{2,1,0:T(8,128)(2,1)S(1)}, u32[]{:S(2)}, u32[]{:S(2)}) async-start(bf16[64,16,128]{2,1,0:T(8,128)(2,1)} %shard_map.136), calls=%async_computation.1 | async-start | bytes 524288 | tf_op jit(solution)/shard_map/all_to_all | solution.py:461
  55.0 2.1 %collective-permute-start.6 = (bf16[192,384]{1,0:T(8,128)(2,1)S(1)}, bf16[192,384]{1,0:T(8,128)(2,1)S(1)}, u32[]{:S(2)}, u32[]{:S(2)}) collective-permute-start(bf16[192,384]{1,0:T(8,128)(2,1)S(1)} %copy-done.2), channel_id=1, source_target_pairs={{0,32},{32,0},{64,96},{96,64},{1,33},{33,1},{65,97},{97,65},{2,34}... | collective-permute-start | bytes 442376 | tf_op jit(solution)/shard_map/ppermute | solution.py:513
  57.1 5.4 %collective-permute-start.7 = (bf16[192,384]{1,0:T(8,128)(2,1)S(1)}, bf16[192,384]{1,0:T(8,128)(2,1)S(1)}, u32[]{:S(2)}, u32[]{:S(2)}) collective-permute-start(bf16[192,384]{1,0:T(8,128)(2,1)S(1)} %get-tuple-element.65), channel_id=1, source_target_pairs={{0,64},{32,96},{64,0},{96,32},{1,65},{33,97},{65,1},{97,33},{2,66}... | collective-permute-start | bytes 442376 | tf_op jit(solution)/shard_map/ppermute | solution.py:513
  62.5 3.1 %collective-permute-start.8 = (bf16[192,384]{1,0:T(8,128)(2,1)S(1)}, bf16[192,384]{1,0:T(8,128)(2,1)S(1)}, u32[]{:S(2)}, u32[]{:S(2)}) collective-permute-start(bf16[192,384]{1,0:T(8,128)(2,1)S(1)} %get-tuple-element.66), channel_id=1, source_target_pairs={{0,96},{32,64},{64,32},{96,0},{1,97},{33,65},{65,33},{97,1},{2,98}... | collective-permute-start | bytes 442376 | tf_op jit(solution)/shard_map/ppermute | solution.py:513
  65.6 4.6 %collective-permute-start.4 = (f32[24,384]{1,0:T(8,128)S(1)}, f32[24,384]{1,0:T(8,128)S(1)}, u32[]{:S(2)}, u32[]{:S(2)}) collective-permute-start(f32[24,384]{1,0:T(8,128)S(1)} %get-tuple-element.68), channel_id=1, source_target_pairs={{0,4},{4,8},{8,12},{12,16},{16,20},{20,24},{24,28},{28,32},{32,36}... | collective-permute-start | bytes 110600 | tf_op jit(solution)/shard_map/ppermute | solution.py:452
  70.2 1.9 %collective-permute-start.5 = (f32[24,384]{1,0:T(8,128)S(1)}, f32[24,384]{1,0:T(8,128)S(1)}, u32[]{:S(2)}, u32[]{:S(2)}) collective-permute-start(f32[24,384]{1,0:T(8,128)S(1)} %get-tuple-element.69), channel_id=1, source_target_pairs={{4,0},{8,4},{12,8},{16,12},{20,16},{24,20},{28,24},{32,28},{36,32}... | collective-permute-start | bytes 110600 | tf_op jit(solution)/shard_map/ppermute | solution.py:457
  72.1 5.1 %collective-permute-done.5.high = f32[24,384]{1,0:T(8,128)S(1)} collective-permute-done((f32[24,384]{1,0:T(8,128)S(1)}, f32[24,384]{1,0:T(8,128)S(1)}, u32[]{:S(2)}, u32[]{:S(2)}) %collective-permute-start.5) | collective-permute-done | bytes 36896 | tf_op jit(solution)/shard_map/ppermute | solution.py:457
  77.3 1.1 shard_map.137
  78.3 14.9 %all-to-all-start.2 = ((bf16[64,24,128]{2,1,0:T(8,128)(2,1)}), bf16[64,24,128]{2,1,0:T(8,128)(2,1)S(1)}, u32[]{:S(2)}, u32[]{:S(2)}) async-start(bf16[64,24,128]{2,1,0:T(8,128)(2,1)} %shard_map.137), calls=%async_computation.2 | async-start | bytes 786432 | tf_op jit(solution)/shard_map/all_to_all | solution.py:461
  93.2 2.3 %shard_map.138 = bf16[256,384]{1,0:T(8,128)(2,1)} custom-call(f32[256,384]{1,0:T(8,128)S(1)} %get-tuple-element.72.grad_conv, f32[24,384]{1,0:T(8,128)S(1)} %collective-permute-done.4.low, f32[24,384]{1,0:T(8,128)S(1)} %collective-permute-done.5.high, f32[7,7,384]{2,1,0:T(8,128)S(1)} %get-tuple-element.46.taps, bf16[256,384]{1,0:T(8,128)(2,1)S(1)} %bitcast.10), custom_call_target="tpu_custom_call" | custom-call | flops 9633792 | bytes 2097152 | tf_op jit(solution)/shard_map/pallas_call | solution.py:309
  95.5 10.4 %all-to-all-done.2.received = bf16[64,24,128]{2,1,0:T(8,128)(2,1)S(1)} async-done(((bf16[64,24,128]{2,1,0:T(8,128)(2,1)}), bf16[64,24,128]{2,1,0:T(8,128)(2,1)S(1)}, u32[]{:S(2)}, u32[]{:S(2)}) %all-to-all-start.2) | async-done | bytes 393248 | tf_op jit(solution)/shard_map/all_to_all | solution.py:461
  106.1 10.7 %all_to_all.20 = bf16[4,192,384]{2,1,0:T(8,128)(2,1)S(1)} all-to-all(bf16[4,192,384]{2,1,0:T(8,128)(2,1)S(1)} %get-tuple-element.77), channel_id=1, replica_groups=mesh['zh'=4,'x'=4,'y'=8,'zl'=2,'c'=2] {'x'}, dimensions={0} | all-to-all | bytes 1179648 | tf_op jit(solution)/shard_map/all_to_all | solution.py:461
  116.7 1.9 %collective-permute-start.9 = (bf16[768,384]{1,0:T(8,128)(2,1)S(1)}, bf16[768,384]{1,0:T(8,128)(2,1)S(1)}, u32[]{:S(2)}, u32[]{:S(2)}) collective-permute-start(bf16[768,384]{1,0:T(8,128)(2,1)S(1)} %bitcast.7), channel_id=1, source_target_pairs={{0,1},{1,0},{2,3},{3,2},{4,5},{5,4},{6,7},{7,6},{8,9},{9,8},{10,11... | collective-permute-start | bytes 1769480 | tf_op jit(solution)/shard_map/ppermute | solution.py:465
  118.7 4.2 %collective-permute-start.10 = (f32[3,384]{1,0:T(4,128)S(1)}, f32[3,384]{1,0:T(4,128)S(1)}, u32[]{:S(2)}, u32[]{:S(2)}) collective-permute-start(f32[3,384]{1,0:T(4,128)S(1)} %get-tuple-element.80), channel_id=1, source_target_pairs={{0,0},{1,256},{2,1},{3,257},{4,2},{5,258},{6,3},{7,259},{8,4},{9,2... | collective-permute-start | bytes 13832 | tf_op jit(solution)/shard_map/ppermute | solution.py:523
  122.9 11.5 %collective-permute-done.10.in_rows = f32[3,384]{1,0:T(4,128)S(1)} collective-permute-done((f32[3,384]{1,0:T(4,128)S(1)}, f32[3,384]{1,0:T(4,128)S(1)}, u32[]{:S(2)}, u32[]{:S(2)}) %collective-permute-start.10) | collective-permute-done | bytes 4640 | tf_op jit(solution)/shard_map/ppermute | solution.py:523
  134.4 1.1 shard_map.140
  (15 shorter events, 0.3 us)
Async XLA Ops:
  1.6 11.0 %collective-permute-start = (bf16[32,384]{1,0:T(8,128)(2,1)S(1)}, bf16[32,384]{1,0:T(8,128)(2,1)S(1)}, u32[]{:S(2)}, u32[]{:S(2)}) collective-permute-start(bf16[32,384]{1,0:T(8,128)(2,1)S(1)} %get-tuple-element.44), channel_id=1, source_target_pairs={{0,4},{4,8},{8,12},{12,16},{16,20},{20,24},{24,28},{28,32},{32,36}... | collective-permute-start | bytes 73736 | tf_op jit(solution)/shard_map/ppermute | solution.py:452
  6.4 6.9 %collective-permute-start.1 = (bf16[32,384]{1,0:T(8,128)(2,1)S(1)}, bf16[32,384]{1,0:T(8,128)(2,1)S(1)}, u32[]{:S(2)}, u32[]{:S(2)}) collective-permute-start(bf16[32,384]{1,0:T(8,128)(2,1)S(1)} %get-tuple-element.45), channel_id=1, source_target_pairs={{4,0},{8,4},{12,8},{16,12},{20,16},{24,20},{28,24},{32,28},{36,32}... | collective-permute-start | bytes 73736 | tf_op jit(solution)/shard_map/ppermute | solution.py:457
  16.2 3.9 %collective-permute-start.2 = (bf16[768,384]{1,0:T(8,128)(2,1)S(1)}, bf16[768,384]{1,0:T(8,128)(2,1)S(1)}, u32[]{:S(2)}, u32[]{:S(2)}) collective-permute-start(bf16[768,384]{1,0:T(8,128)(2,1)S(1)} %get-tuple-element.52), channel_id=1, source_target_pairs={{0,1},{1,0},{2,3},{3,2},{4,5},{5,4},{6,7},{7,6},{8,9},{9,8},{10,11... | collective-permute-start | bytes 1769480 | tf_op jit(solution)/shard_map/ppermute | solution.py:465
  21.9 6.9 %collective-permute-start.3 = (bf16[768,384]{1,0:T(8,128)(2,1)S(1)}, bf16[768,384]{1,0:T(8,128)(2,1)S(1)}, u32[]{:S(2)}, u32[]{:S(2)}) collective-permute-start(bf16[768,384]{1,0:T(8,128)(2,1)S(1)} %get-tuple-element.63), channel_id=1, source_target_pairs={{0,1},{1,0},{2,3},{3,2},{4,5},{5,4},{6,7},{7,6},{8,9},{9,8},{10,11... | collective-permute-start | bytes 1769480 | tf_op jit(solution)/shard_map/ppermute | solution.py:465
  24.0 13.4 %all-to-all-start = ((bf16[4,192,384]{2,1,0:T(8,128)(2,1)}), bf16[4,192,384]{2,1,0:T(8,128)(2,1)S(1)}, u32[]{:S(2)}, u32[]{:S(2)}) async-start(bf16[4,192,384]{2,1,0:T(8,128)(2,1)} %bitcast.11), calls=%async_computation | async-start | bytes 1179648 | tf_op jit(solution)/shard_map/all_to_all | solution.py:461
  28.9 0.7 copy-start.1
  37.4 17.6 %copy-start.2 = (bf16[192,384]{1,0:T(8,128)(2,1)S(1)}, bf16[192,384]{1,0:T(8,128)(2,1)}, u32[]{:S(2)}) copy-start(bf16[192,384]{1,0:T(8,128)(2,1)} %copy-done.1) | copy-start | bytes 442372
  38.4 38.9 %all-to-all-start.1 = ((bf16[64,16,128]{2,1,0:T(8,128)(2,1)}), bf16[64,16,128]{2,1,0:T(8,128)(2,1)S(1)}, u32[]{:S(2)}, u32[]{:S(2)}) async-start(bf16[64,16,128]{2,1,0:T(8,128)(2,1)} %shard_map.136), calls=%async_computation.1 | async-start | bytes 524288 | tf_op jit(solution)/shard_map/all_to_all | solution.py:461
  55.0 38.2 %copy-start = (bf16[1,8,32,384]{3,2,1,0:T(8,128)(2,1)S(1)}, bf16[1,8,32,384]{3,2,1,0:T(8,128)(2,1)}, u32[]{:S(2)}) copy-start(bf16[1,8,32,384]{3,2,1,0:T(8,128)(2,1)} %param.12) | copy-start | bytes 589828
  55.0 22.2 %collective-permute-start.6 = (bf16[192,384]{1,0:T(8,128)(2,1)S(1)}, bf16[192,384]{1,0:T(8,128)(2,1)S(1)}, u32[]{:S(2)}, u32[]{:S(2)}) collective-permute-start(bf16[192,384]{1,0:T(8,128)(2,1)S(1)} %copy-done.2), channel_id=1, source_target_pairs={{0,32},{32,0},{64,96},{96,64},{1,33},{33,1},{65,97},{97,65},{2,34}... | collective-permute-start | bytes 442376 | tf_op jit(solution)/shard_map/ppermute | solution.py:513
  57.1 20.2 %collective-permute-start.7 = (bf16[192,384]{1,0:T(8,128)(2,1)S(1)}, bf16[192,384]{1,0:T(8,128)(2,1)S(1)}, u32[]{:S(2)}, u32[]{:S(2)}) collective-permute-start(bf16[192,384]{1,0:T(8,128)(2,1)S(1)} %get-tuple-element.65), channel_id=1, source_target_pairs={{0,64},{32,96},{64,0},{96,32},{1,65},{33,97},{65,1},{97,33},{2,66}... | collective-permute-start | bytes 442376 | tf_op jit(solution)/shard_map/ppermute | solution.py:513
  62.5 14.8 %collective-permute-start.8 = (bf16[192,384]{1,0:T(8,128)(2,1)S(1)}, bf16[192,384]{1,0:T(8,128)(2,1)S(1)}, u32[]{:S(2)}, u32[]{:S(2)}) collective-permute-start(bf16[192,384]{1,0:T(8,128)(2,1)S(1)} %get-tuple-element.66), channel_id=1, source_target_pairs={{0,96},{32,64},{64,32},{96,0},{1,97},{33,65},{65,33},{97,1},{2,98}... | collective-permute-start | bytes 442376 | tf_op jit(solution)/shard_map/ppermute | solution.py:513
  65.6 6.5 %collective-permute-start.4 = (f32[24,384]{1,0:T(8,128)S(1)}, f32[24,384]{1,0:T(8,128)S(1)}, u32[]{:S(2)}, u32[]{:S(2)}) collective-permute-start(f32[24,384]{1,0:T(8,128)S(1)} %get-tuple-element.68), channel_id=1, source_target_pairs={{0,4},{4,8},{8,12},{12,16},{16,20},{20,24},{24,28},{28,32},{32,36}... | collective-permute-start | bytes 110600 | tf_op jit(solution)/shard_map/ppermute | solution.py:452
  70.2 7.1 %collective-permute-start.5 = (f32[24,384]{1,0:T(8,128)S(1)}, f32[24,384]{1,0:T(8,128)S(1)}, u32[]{:S(2)}, u32[]{:S(2)}) collective-permute-start(f32[24,384]{1,0:T(8,128)S(1)} %get-tuple-element.69), channel_id=1, source_target_pairs={{4,0},{8,4},{12,8},{16,12},{20,16},{24,20},{28,24},{32,28},{36,32}... | collective-permute-start | bytes 110600 | tf_op jit(solution)/shard_map/ppermute | solution.py:457
  78.3 27.5 %all-to-all-start.2 = ((bf16[64,24,128]{2,1,0:T(8,128)(2,1)}), bf16[64,24,128]{2,1,0:T(8,128)(2,1)S(1)}, u32[]{:S(2)}, u32[]{:S(2)}) async-start(bf16[64,24,128]{2,1,0:T(8,128)(2,1)} %shard_map.137), calls=%async_computation.2 | async-start | bytes 786432 | tf_op jit(solution)/shard_map/all_to_all | solution.py:461
  116.7 17.7 %collective-permute-start.9 = (bf16[768,384]{1,0:T(8,128)(2,1)S(1)}, bf16[768,384]{1,0:T(8,128)(2,1)S(1)}, u32[]{:S(2)}, u32[]{:S(2)}) collective-permute-start(bf16[768,384]{1,0:T(8,128)(2,1)S(1)} %bitcast.7), channel_id=1, source_target_pairs={{0,1},{1,0},{2,3},{3,2},{4,5},{5,4},{6,7},{7,6},{8,9},{9,8},{10,11... | collective-permute-start | bytes 1769480 | tf_op jit(solution)/shard_map/ppermute | solution.py:465
  118.7 15.7 %collective-permute-start.10 = (f32[3,384]{1,0:T(4,128)S(1)}, f32[3,384]{1,0:T(4,128)S(1)}, u32[]{:S(2)}, u32[]{:S(2)}) collective-permute-start(f32[3,384]{1,0:T(4,128)S(1)} %get-tuple-element.80), channel_id=1, source_target_pairs={{0,0},{1,256},{2,1},{3,257},{4,2},{5,258},{6,3},{7,259},{8,4},{9,2... | collective-permute-start | bytes 13832 | tf_op jit(solution)/shard_map/ppermute | solution.py:523

commit v6 on v4

--- a/solution.py
+++ b/solution.py
@@ -17,12 +17,13 @@
 ROWS = 3
 EDGE = 4 * SIDE
 EPSILON = 1e-06
-VMEM_LIMIT = 24 * 1024 * 1024
+VMEM_LIMIT = 16 * 1024 * 1024
 NT = (((1,), (1,)), ((), ()))
 
-TILE = ("zh", "x", "y")
-RING = ("zh", "y", "zl")
-EVERY = ("zh", "x", "y", "zl", "c")
+TILE = ("zh", "xh", "xl", "yh", "yl")
+CUBE = ("xl", "yl", "zl")
+FAR = ("zh", "xh", "yh")
+EVERY = ("zh", "xh", "xl", "yh", "yl", "zl", "c")
 SWAP = [(0, 1), (1, 0)]
 
 
@@ -136,9 +137,10 @@
         )
 
 
-def second_kernel(
-    core, conv, low, high, taps, vectors, w_in_t, b_cols, out_grad,
-    kept, sent, standard, inverse, normed, preact, cdf, rows, low_wide, high_wide, hidden
+def middle_kernel(
+    core, conv, low, high, taps, vectors, w_in_t, b_cols, out_grad, back, w_in,
+    kept, sent, grad_conv, low_edge, high_edge,
+    rows, low_wide, high_wide, standard, normed, preact, hidden, grad_pre
 ):
     width = conv.shape[1]
     rows[...] = conv[...]
@@ -152,12 +154,12 @@
         for j, total in enumerate(convolve([None] * (2 * HALO) + near, taps, lanes, False)):
             start = (COLS - HALO + j) * SIDE
             rows[start : start + SIDE, lanes] += total
+    gain, bias = vectors[SIDE : SIDE + 1, :], vectors[2 * SIDE : 2 * SIDE + 1, :]
     conv_out = rows[...] + vectors[:1, :]
     centre = conv_out - jnp.mean(conv_out, axis=-1, keepdims=True)
-    scale = lax.rsqrt(jnp.mean(centre * centre, axis=-1, keepdims=True) + EPSILON)
-    inverse[...] = jnp.broadcast_to(scale, inverse.shape)
-    standard[...] = centre * scale
-    normed[...] = (standard[...] * vectors[SIDE : SIDE + 1, :] + vectors[2 * SIDE : 2 * SIDE + 1, :]).astype(jnp.bfloat16)
+    inverse = lax.rsqrt(jnp.mean(centre * centre, axis=-1, keepdims=True) + EPSILON)
+    standard[...] = centre * inverse
+    normed[...] = (standard[...] * gain + bias).astype(jnp.bfloat16)
     preact[...] = matmul(w_in_t[...], normed[...], NT)
 
     def step(i, carry):
@@ -165,50 +167,29 @@
         for lanes in lane_blocks(preact.shape[1]):
             z = preact[part, lanes] + b_cols[part, :]
             below = 0.5 * (1.0 + lax.erf(z * 0.7071067811865476))
-            preact[part, lanes] = z
-            cdf[part, lanes] = below
+            density = jnp.exp(-0.5 * z * z) * 0.3989422804014327
             hidden[part, lanes] = (z * below).astype(jnp.bfloat16)
+            slope = below + z * density
+            grad_pre[part, lanes] = (back[part, lanes] * slope).astype(jnp.bfloat16)
         return carry
 
     lax.fori_loop(0, preact.shape[0] // CHUNK, step, 0, unroll=2)
     half = hidden.shape[0] // 2
     other = pl.ds(pl.multiple_of((1 - core[0]) * half, half), half)
     own = pl.ds(pl.multiple_of(core[0] * half, half), half)
-    sent[...] = matmul(hidden[other, :], out_grad[...]).astype(jnp.bfloat16)
-    kept[...] = matmul(hidden[own, :], out_grad[...])
-
-
-def slope_kernel(back, preact, cdf, grad_pre):
-    def step(i, carry):
-        part = pl.ds(pl.multiple_of(i * CHUNK, CHUNK), CHUNK)
-        for lanes in lane_blocks(preact.shape[1]):
-            z = preact[part, lanes]
-            density = jnp.exp(-0.5 * z * z) * 0.3989422804014327
-            slope = cdf[part, lanes] + z * density
-            grad_pre[part, lanes] = (back[part, lanes] * slope).astype(jnp.bfloat16)
-        return carry
-
-    lax.fori_loop(0, preact.shape[0] // CHUNK, step, 0, unroll=2)
-
-
-def third_kernel(
-    core, grad_pre, w_in, normed, standard, inverse, vectors,
-    kept, sent, grad_conv, low, high
-):
-    grad_std = matmul(w_in[...], grad_pre[...]).T * vectors[SIDE : SIDE + 1, :]
-    half = grad_pre.shape[0] // 2
-    other = pl.ds(pl.multiple_of((1 - core[0]) * half, half), half)
-    own = pl.ds(pl.multiple_of(core[0] * half, half), half)
-    sent[...] = matmul(grad_pre[other, :], normed[...]).astype(jnp.bfloat16)
-    kept[...] = matmul(grad_pre[own, :], normed[...])
+    sent[:half, :] = matmul(hidden[other, :], out_grad[...]).astype(jnp.bfloat16)
+    sent[half:, :] = matmul(grad_pre[other, :], normed[...]).astype(jnp.bfloat16)
+    kept[:half, :] = matmul(hidden[own, :], out_grad[...])
+    kept[half:, :] = matmul(grad_pre[own, :], normed[...])
+    grad_std = matmul(w_in[...], grad_pre[...]).T * gain
     norm = standard[...]
     mean = jnp.mean(grad_std, axis=-1, keepdims=True)
     along = jnp.mean(grad_std * norm, axis=-1, keepdims=True)
-    result = inverse[:, :1] * (grad_std - mean - norm * along)
+    result = inverse * (grad_std - mean - norm * along)
     grad_conv[...] = result
     edge = HALO * SIDE
-    low[...] = result[:edge, :]
-    high[...] = result[result.shape[0] - edge :, :]
+    low_edge[...] = result[:edge, :]
+    high_edge[...] = result[result.shape[0] - edge :, :]
 
 
 def last_kernel(grad_conv, low, high, taps, cotangent, grad_features, wide):
@@ -229,18 +210,15 @@
         grad_features[:, lanes] = result.astype(jnp.bfloat16)
 
 
-def pack_kernel(out_blocks, message, spread):
-    members, places, _ = message.shape
-    blocks = lane_blocks(out_blocks.shape[2])
-    spread[...] = jnp.zeros_like(spread)
-    for r in range(ROWS):
-        part = slice(r * members, (r + 1) * members)
-        for k, lanes in enumerate(blocks):
-            summed = out_blocks[0, part, lanes].astype(jnp.float32)
-            for i in range(1, out_blocks.shape[0]):
-                summed += out_blocks[i, part, lanes].astype(jnp.float32)
-            spread[pl.ds(r * len(blocks) + k, members, stride=places), :] = summed
-    message[...] = spread[...].reshape(message.shape).astype(jnp.bfloat16)
+def cube_kernel(kept, received, message):
+    members, rows, _ = message.shape
+    rows //= 2
+    for m in range(members):
+        for i in range(2):
+            start = (i * members + m) * rows
+            part = slice(start, start + rows)
+            total = kept[part, :] + received[part, :].astype(jnp.float32)
+            message[m, i * rows : (i + 1) * rows, :] = total.astype(jnp.bfloat16)
 
 
 def add_members(received):
@@ -250,25 +228,39 @@
     return summed
 
 
-def turn_kernel(scale, received, in_rows, message, spread, total):
+def far_kernel(received, message, spread, total):
     members, places, _ = message.shape
-    blocks = lane_blocks(in_rows.shape[1])
-    summed = add_members(received) * scale
+    blocks = lane_blocks(received.shape[2])
+    rows = ROWS * members
+    size = ROWS * len(blocks)
     spread[...] = jnp.zeros_like(spread)
+    for k, lanes in enumerate(blocks):
+        summed = received[0, :, lanes].astype(jnp.float32)
+        for i in range(1, received.shape[0]):
+            summed += received[i, :, lanes].astype(jnp.float32)
+        total[k] = summed
+        for r in range(ROWS):
+            place = r * len(blocks) + k
+            part = total[k, r * members : (r + 1) * members, :]
+            spread[pl.ds(place, members, stride=places), :] = part
+            part = total[k, pl.ds(rows + r, members, stride=ROWS), :]
+            spread[pl.ds(size + place, members, stride=places), :] = part
+    message[...] = spread[...].reshape(message.shape).astype(jnp.bfloat16)
+
+
+def turn_kernel(scale, received, message, grad_w_in, sums):
+    sums[...] = add_members(received) * scale
+    width = grad_w_in.shape[1]
+    blocks = lane_blocks(width)
     size = ROWS * len(blocks)
-    for place in range(size):
-        row = jnp.broadcast_to(summed[place : place + 1, :], (members, LANES))
-        spread[pl.ds(place, members, stride=places), :] = row
     for k, lanes in enumerate(blocks):
-        total[k] = in_rows[:, lanes]
-        for r in range(ROWS):
-            place = size + r * len(blocks) + k
-            part = total[k, pl.ds(r, members, stride=ROWS), :]
-            spread[pl.ds(place, members, stride=places), :] = part
-    message[...] = spread[...].reshape(message.shape).astype(jnp.bfloat16)
-
-
-def unpack_kernel(scale, received, message, grad_w_in, spread, sums):
+        grad_w_in[:, lanes] = sums[pl.ds(size + k, ROWS, stride=len(blocks)), :]
+    finished = sums[: message.shape[1], :].astype(jnp.bfloat16)
+    for m in range(message.shape[0]):
+        message[m] = finished
+
+
+def unpack_kernel(received, message, spread):
     members, places, _ = received.shape
     blocks = lane_blocks(message.shape[2])
     spread[...] = received[...].astype(jnp.float32).reshape(spread.shape)
@@ -278,10 +270,6 @@
             part = part.astype(jnp.bfloat16)
             for i in range(message.shape[0]):
                 message[i, r * members : (r + 1) * members, lanes] = part
-    sums[...] = add_members(received)
-    size = ROWS * len(blocks)
-    for k, lanes in enumerate(blocks):
-        grad_w_in[:, lanes] = sums[pl.ds(size + k, ROWS, stride=len(blocks)), :] * scale
 
 
 def join_kernel(core, own, other, in_rows, grad_w_out, grad_w_in):
@@ -340,36 +328,18 @@
     )
 
 
-def forward(core, conv, low, high, taps, vectors, w_in_t, b_cols, out_grad):
+def middle(core, conv, low, high, taps, vectors, w_in_t, b_cols, out_grad, back, w_in):
     rows, width = conv.shape
     hidden = w_in_t.shape[0]
-    halo = pltpu.VMEM((EDGE, width), F32)
-    return call(
-        second_kernel,
-        [((hidden // 2, width), F32), ((hidden // 2, width), B16), ((rows, width), F32), ((rows, LANES), F32),
-         ((rows, width), B16), ((hidden, rows), F32), ((hidden, rows), F32)],
-        [pltpu.VMEM((rows, width), F32), halo, halo, pltpu.VMEM((hidden, rows), B16)],
+    halo, edge = pltpu.VMEM((EDGE, width), F32), (HALO * SIDE, width)
+    return call(
+        middle_kernel,
+        [((hidden, width), F32), ((hidden, width), B16), ((rows, width), F32), (edge, F32), (edge, F32)],
+        [pltpu.VMEM((rows, width), F32), halo, halo, pltpu.VMEM((rows, width), F32), pltpu.VMEM((rows, width), B16),
+         pltpu.VMEM((hidden, rows), F32), pltpu.VMEM((hidden, rows), B16), pltpu.VMEM((hidden, rows), B16)],
         [core],
-        [conv, low, high, taps, vectors, w_in_t, b_cols, out_grad],
-        4 * rows * width * hidden, 8 * 1024 * 1024,
-    )
-
-
-def slopes(back, preact, cdf):
-    return call(slope_kernel, [(back.shape, B16)], [], [], [back, preact, cdf], 10 * back.size, 14 * back.size)[0]
-
-
-def backward(core, grad_pre, w_in, normed, standard, inverse, vectors):
-    rows, width = standard.shape
-    hidden = grad_pre.shape[0]
-    edge = (HALO * SIDE, width)
-    return call(
-        third_kernel,
-        [((hidden // 2, width), F32), ((hidden // 2, width), B16), ((rows, width), F32), (edge, F32), (edge, F32)],
-        [],
-        [core],
-        [grad_pre, w_in, normed, standard, inverse, vectors],
-        4 * rows * width * hidden, 8 * 1024 * 1024,
+        [conv, low, high, taps, vectors, w_in_t, b_cols, out_grad, back, w_in],
+        8 * rows * width * hidden, 12 * 1024 * 1024,
     )
 
 
@@ -385,39 +355,46 @@
     )[0]
 
 
-def pack(out_blocks, members, places):
-    return call(
-        pack_kernel,
-        [((members, places, LANES), B16)],
-        [pltpu.VMEM((members * places, LANES), F32)],
-        [],
-        [out_blocks],
-        out_blocks.size, 3 * out_blocks.size,
+def to_cube(members, kept, received):
+    rows, width = kept.shape
+    return call(
+        cube_kernel, [((members, rows // members, width), B16)], [], [], [kept, received], 2 * kept.size, 8 * kept.size
     )[0]
 
 
-def turn(scale, received, in_rows, places):
-    members = received.shape[0]
-    rows, width = in_rows.shape
+def to_far(received, members):
+    _, rows, width = received.shape
+    return call(
+        far_kernel,
+        [((members, 24, LANES), B16)],
+        [pltpu.VMEM((members * 24, LANES), F32), pltpu.VMEM((width // LANES, rows, LANES), F32)],
+        [],
+        [received],
+        received.size, 3 * received.size,
+    )[0]
+
+
+def turn(scale, received, width):
+    members, places, _ = received.shape
     return call(
         functools.partial(turn_kernel, scale),
-        [((members, places, LANES), B16)],
-        [pltpu.VMEM((members * places, LANES), F32), pltpu.VMEM((width // LANES, rows, LANES), F32)],
-        [],
-        [received, in_rows],
+        [((members, 16, LANES), B16), ((ROWS, width), F32)],
+        [pltpu.VMEM((places, LANES), F32)],
+        [],
+        [received],
+        received.size, 4 * received.size,
+    )
+
+
+def unpack(received, members, width):
+    return call(
+        unpack_kernel,
+        [((members, ROWS * received.shape[0], width), B16)],
+        [pltpu.VMEM((received.shape[0] * received.shape[1], LANES), F32)],
+        [],
+        [received],
         received.size, 6 * received.size,
     )[0]
-
-
-def unpack(scale, received, lines, rows, width):
-    return call(
-        functools.partial(unpack_kernel, scale),
-        [((lines, rows, width), B16), ((ROWS, width), F32)],
-        [pltpu.VMEM((received.shape[0] * received.shape[1], LANES), F32), pltpu.VMEM(received.shape[1:], F32)],
-        [],
-        [received],
-        received.size, 6 * received.size,
-    )
 
 
 def join(core, own, other, in_rows):
@@ -447,14 +424,16 @@
 
 
 def owners(sizes):
-    zh_n, x_n, y_n, zl_n, c_n = sizes
+    count = math.prod(sizes.values())
     pairs = []
-    for source in range(zh_n * x_n * y_n * zl_n * c_n):
-        rest, c = divmod(source, c_n)
-        rest, zl = divmod(rest, zl_n)
-        rest, y = divmod(rest, y_n)
-        zh, x = divmod(rest, x_n)
-        pairs.append((source, (((c * x_n + x) * zh_n + zh) * y_n + y) * zl_n + zl))
+    for source in range(count):
+        rest, at = source, {}
+        for axis in reversed(EVERY):
+            rest, at[axis] = divmod(rest, sizes[axis])
+        target = 0
+        for axis in ("c",) + CUBE + FAR:
+            target = target * sizes[axis] + at[axis]
+        pairs.append((source, target))
     return pairs
 
 
@@ -468,42 +447,35 @@
     low, high = from_left(high), from_right(low)
     upstream = cotangent[0].reshape(-1, channels)
     core = lax.axis_index("c").astype(jnp.int32).reshape(1)
-    sizes = [lax.axis_size(axis) for axis in EVERY]
-    lines, ring = sizes[1], sizes[0] * sizes[2] * sizes[3]
-    scale = 1.0 / math.sqrt(height * breadth * math.prod(sizes))
+    sizes = {axis: lax.axis_size(axis) for axis in EVERY}
+    near = math.prod(sizes[axis] for axis in CUBE)
+    far = math.prod(sizes[axis] for axis in FAR)
+    scale = 1.0 / math.sqrt(height * breadth * math.prod(sizes.values()))
 
     conv, out_grad, back, w_in_t, b_cols, w_in_here, taps, vectors = before_halos(
         tissue, rows, upstream, kernel, conv_bias, ln_gain, ln_bias, w_in, b_in, w_out, layer_scale
     )
-    kept, sent, standard, inverse, normed, preact, cdf = forward(
-        core, conv, low, high, taps, vectors, w_in_t, b_cols, out_grad
-    )
-    grad_pre = slopes(back, preact, cdf)
-    total = (kept + swap(sent).astype(F32)).astype(B16).reshape(lines, -1, channels)
-    total, grad_pre = lax.optimization_barrier((total, grad_pre))
-    out_blocks = exchange(total, "x")
-    kept, sent, grad_conv, low, high = backward(
-        core, grad_pre, w_in_here, normed, standard, inverse, vectors
-    )
-    in_total = kept + swap(sent).astype(F32)
+    kept, sent, grad_conv, low, high = middle(
+        core, conv, low, high, taps, vectors, w_in_t, b_cols, out_grad, back, w_in_here
+    )
+    message = to_cube(near, kept, swap(sent))
+    received = exchange(message, CUBE)
     low, high = from_left(high), from_right(low)
-    out_blocks, low, high, _ = lax.optimization_barrier((out_blocks, low, high, in_total))
-    in_rows = lax.psum_scatter(in_total, "x", scatter_dimension=0, tiled=True)
-
-    received = exchange(pack(out_blocks, ring, 16), RING)
-    received = exchange(turn(scale, received, in_rows, 24), RING)
-    message, in_rows = unpack(scale, received, lines, out_blocks.shape[1], channels)
-    own = exchange(message, "x").reshape(-1, channels)
-    own, in_rows, low, high = lax.optimization_barrier((own, in_rows, low, high))
-    other = swap(own)
+    received, low, high = lax.optimization_barrier((received, low, high))
+    received = exchange(to_far(received, far), FAR)
+    grad_image = to_features(grad_conv, low, high, taps, upstream)
+    received, grad_image = lax.optimization_barrier((received, grad_image))
+    message, in_rows = turn(scale, received, channels)
+    received = exchange(message, FAR)
     in_rows = lax.ppermute(in_rows, EVERY, owners(sizes))
-    grad_image = to_features(grad_conv, low, high, taps, upstream)
-    grad_w_out, grad_w_in = join(core, own, other, in_rows)
+    received, in_rows = lax.optimization_barrier((received, in_rows))
+    own = exchange(unpack(received, near, channels), CUBE).reshape(-1, channels)
+    grad_w_out, grad_w_in = join(core, own, swap(own), in_rows)
     return (grad_image.reshape(1, height, breadth, channels), grad_w_in, grad_w_out)
 
 
 def solution(mesh):
-    fine = jax.sharding.Mesh(mesh.devices.reshape(4, 4, 8, 2, 2), EVERY)
+    fine = jax.sharding.Mesh(mesh.devices.reshape(4, 2, 2, 4, 2, 2, 2), EVERY)
     band = P(("zl", "c"), None, TILE, None)
     placed = (band, band) + (P(),) * 8 + (P(("zl", "c"), TILE),)
     return jax.shard_map(

time: 143 us -> 120 us (0.84)
  the two profiles are of different devices: /device:TPU:30 before, /device:TPU:1 now
where the time goes in v6:
time: 120 us; the launch traced here: 119 us
  starting transfers between devices  59.9 us (50%)
  waiting for transfers between devices  32.3 us (27%)
  Pallas kernels  16 us (13%)
  blocking collectives  10.2 us (8%)
    all_to_all x3, starting transfers between devices, exchange(): return lax.all_to_all(blocks, axes, split_axis=0, concat_axis=0, tiled=True)  26.1 us
    all_to_all x3, waiting for transfers between devices, exchange(): return lax.all_to_all(blocks, axes, split_axis=0, concat_axis=0, tiled=True)  16.9 us
    pallas_call x9, Pallas kernels, call(): pl.pallas_call(kernel, out_shape=[jax.ShapeDtypeStruct(shape, kind) for s...  16 us
    ppermute x2, starting transfers between devices, swap(): return lax.ppermute(block, 'c', SWAP)  13.3 us
    ppermute x1, starting transfers between devices, body(): in_rows = lax.ppermute(in_rows, EVERY, owners(sizes))  10.3 us
    all_to_all x1, blocking collectives, exchange(): return lax.all_to_all(blocks, axes, split_axis=0, concat_axis=0, tiled=True)  10.2 us
    ppermute x2, waiting for transfers between devices, from_left(): return lax.ppermute(block, TILE, [(i, i + 1) for i in range(count - 1)])  10 us
    ppermute x2, starting transfers between devices, from_left(): return lax.ppermute(block, TILE, [(i, i + 1) for i in range(count - 1)])  7.67 us
  transfers between devices with their start and end apart: 10, of which 8 were waited for; matrix products, arithmetic and copies ran while one was open for 0% of the time, Pallas kernels for 6%

profile of v6, /device:TPU:1, one launch (start us, length us, event | category | flops | bytes accessed | tf_op | source)
XLA Modules:
  0.0 119.2 jit_solution(14693444516551338721)
XLA Ops:
  0.6 1.0 shard_map.131
  1.6 4.0 %collective-permute-start = (bf16[32,384]{1,0:T(8,128)(2,1)S(1)}, bf16[32,384]{1,0:T(8,128)(2,1)S(1)}, u32[]{:S(2)}, u32[]{:S(2)}) collective-permute-start(bf16[32,384]{1,0:T(8,128)(2,1)S(1)} %get-tuple-element.30), channel_id=1, source_target_pairs={{0,4},{4,8},{8,12},{12,16},{16,20},{20,24},{24,28},{28,32},{32,36}... | collective-permute-start | bytes 73736 | tf_op jit(solution)/shard_map/ppermute | solution.py:410
  5.7 1.3 %collective-permute-start.1 = (bf16[32,384]{1,0:T(8,128)(2,1)S(1)}, bf16[32,384]{1,0:T(8,128)(2,1)S(1)}, u32[]{:S(2)}, u32[]{:S(2)}) collective-permute-start(bf16[32,384]{1,0:T(8,128)(2,1)S(1)} %get-tuple-element.31), channel_id=1, source_target_pairs={{4,0},{8,4},{12,8},{16,12},{20,16},{24,20},{28,24},{32,28},{36,32}... | collective-permute-start | bytes 73736 | tf_op jit(solution)/shard_map/ppermute | solution.py:415
  7.0 4.4 %shard_map.130 = (f32[256,384]{1,0:T(8,128)S(1)}, bf16[256,384]{1,0:T(8,128)(2,1)S(1)}, f32[1536,256]{1,0:T(8,128)S(1)}, bf16[1536,384]{1,0:T(8,128)(2,1)S(1)}, ...) custom-call(s32[1,4]{1,0:T(1,128)} %flags.1, ...), custom_call_target="tpu_custom_call" | custom-call | flops 301989888 | bytes 8388608 | tf_op jit(solution)/shard_map/pallas_call | solution.py:287
  11.4 0.0 collective-permute-done.low
  11.4 0.0 collective-permute-done.1.high
  11.4 4.2 %shard_map.132 = (f32[1536,384]{1,0:T(8,128)S(1)}, bf16[1536,384]{1,0:T(8,128)(2,1)S(1)}, f32[256,384]{1,0:T(8,128)S(1)}, f32[24,384]{1,0:T(8,128)S(1)}, f32[24,384]{1,0:T(8,128)S(1)}) custom-call(s32[1]{0:T(128)} %bitcast.core, f32[256,384]{1,0:T(8,128)S(1)} %get-tuple-element.29.conv, bf16[32,384]{1,0:T(8,128)(2,1)S(1)} %collective-permute-done.low, ...), custom_call_target="tpu_custom_call" | custom-call | flops 1207959552 | bytes 12582912 | tf_op jit(solution)/shard_map/pallas_call | solution.py:287
  15.6 6.0 %collective-permute-start.2 = (bf16[1536,384]{1,0:T(8,128)(2,1)S(1)}, bf16[1536,384]{1,0:T(8,128)(2,1)S(1)}, u32[]{:S(2)}, u32[]{:S(2)}) collective-permute-start(bf16[1536,384]{1,0:T(8,128)(2,1)S(1)} %get-tuple-element.40), channel_id=1, source_target_pairs={{0,1},{1,0},{2,3},{3,2},{4,5},{5,4},{6,7},{7,6},{8,9},{9,8},{10,11... | collective-permute-start | bytes 3538952 | tf_op jit(solution)/shard_map/ppermute | solution.py:423
  21.7 2.5 %collective-permute-done.2.received = bf16[1536,384]{1,0:T(8,128)(2,1)S(1)} collective-permute-done((bf16[1536,384]{1,0:T(8,128)(2,1)S(1)}, bf16[1536,384]{1,0:T(8,128)(2,1)S(1)}, u32[]{:S(2)}, u32[]{:S(2)}) %collective-permute-start.2) | collective-permute-done | bytes 1179680 | tf_op jit(solution)/shard_map/ppermute | solution.py:423
  24.1 1.3 %shard_map.133 = bf16[8,192,384]{2,1,0:T(8,128)(2,1)} custom-call(f32[1536,384]{1,0:T(8,128)S(1)} %get-tuple-element.39.kept, bf16[1536,384]{1,0:T(8,128)(2,1)S(1)} %collective-permute-done.2.received), custom_call_target="tpu_custom_call" | custom-call | flops 1179648 | bytes 4718592 | tf_op jit(solution)/shard_map/pallas_call | solution.py:287
  25.4 4.3 %all-to-all-start = ((bf16[8,192,384]{2,1,0:T(8,128)(2,1)}), bf16[8,192,384]{2,1,0:T(8,128)(2,1)S(1)}, u32[]{:S(2)}, u32[]{:S(2)}) async-start(bf16[8,192,384]{2,1,0:T(8,128)(2,1)} %shard_map.133), calls=%async_computation | async-start | bytes 2359296 | tf_op jit(solution)/shard_map/all_to_all | solution.py:419
  29.7 0.0 copy-start
  29.7 3.6 %collective-permute-start.3 = (f32[24,384]{1,0:T(8,128)S(1)}, f32[24,384]{1,0:T(8,128)S(1)}, u32[]{:S(2)}, u32[]{:S(2)}) collective-permute-start(f32[24,384]{1,0:T(8,128)S(1)} %get-tuple-element.41), channel_id=1, source_target_pairs={{0,4},{4,8},{8,12},{12,16},{16,20},{20,24},{24,28},{28,32},{32,36}... | collective-permute-start | bytes 110600 | tf_op jit(solution)/shard_map/ppermute | solution.py:410
  33.3 1.3 %collective-permute-start.4 = (f32[24,384]{1,0:T(8,128)S(1)}, f32[24,384]{1,0:T(8,128)S(1)}, u32[]{:S(2)}, u32[]{:S(2)}) collective-permute-start(f32[24,384]{1,0:T(8,128)S(1)} %get-tuple-element.42), channel_id=1, source_target_pairs={{4,0},{8,4},{12,8},{16,12},{20,16},{24,20},{28,24},{32,28},{36,32}... | collective-permute-start | bytes 110600 | tf_op jit(solution)/shard_map/ppermute | solution.py:415
  34.6 10.0 %collective-permute-done.3.low = f32[24,384]{1,0:T(8,128)S(1)} collective-permute-done((f32[24,384]{1,0:T(8,128)S(1)}, f32[24,384]{1,0:T(8,128)S(1)}, u32[]{:S(2)}, u32[]{:S(2)}) %collective-permute-start.3) | collective-permute-done | bytes 36896 | tf_op jit(solution)/shard_map/ppermute | solution.py:410
  44.7 0.6 collective-permute-done.4.high
  45.2 1.5 %all-to-all-done.received = bf16[8,192,384]{2,1,0:T(8,128)(2,1)S(1)} async-done(((bf16[8,192,384]{2,1,0:T(8,128)(2,1)}), bf16[8,192,384]{2,1,0:T(8,128)(2,1)S(1)}, u32[]{:S(2)}, u32[]{:S(2)}) %all-to-all-start) | async-done | bytes 1179680 | tf_op jit(solution)/shard_map/all_to_all | solution.py:419
  46.8 0.9 shard_map.134
  47.7 17.9 %all-to-all-start.1 = ((bf16[32,24,128]{2,1,0:T(8,128)(2,1)}), bf16[32,24,128]{2,1,0:T(8,128)(2,1)S(1)}, u32[]{:S(2)}, u32[]{:S(2)}) async-start(bf16[32,24,128]{2,1,0:T(8,128)(2,1)} %shard_map.134), calls=%async_computation.1 | async-start | bytes 393216 | tf_op jit(solution)/shard_map/all_to_all | solution.py:419
  65.6 0.0 copy-done
  65.6 2.3 %shard_map.135 = bf16[256,384]{1,0:T(8,128)(2,1)} custom-call(f32[256,384]{1,0:T(8,128)S(1)} %get-tuple-element.44.grad_conv, f32[24,384]{1,0:T(8,128)S(1)} %collective-permute-done.3.low, f32[24,384]{1,0:T(8,128)S(1)} %collective-permute-done.4.high, f32[7,7,384]{2,1,0:T(8,128)S(1)} %get-tuple-element.32.taps, bf16[256,384]{1,0:T(8,128)(2,1)S(1)} %bitcast.8), custom_call_target="tpu_custom_call" | custom-call | flops 9633792 | bytes 2097152 | tf_op jit(solution)/shard_map/pallas_call | solution.py:287
  67.9 12.3 %all-to-all-done.1.received = bf16[32,24,128]{2,1,0:T(8,128)(2,1)S(1)} async-done(((bf16[32,24,128]{2,1,0:T(8,128)(2,1)}), bf16[32,24,128]{2,1,0:T(8,128)(2,1)S(1)}, u32[]{:S(2)}, u32[]{:S(2)}) %all-to-all-start.1) | async-done | bytes 196640 | tf_op jit(solution)/shard_map/all_to_all | solution.py:419
  80.2 0.7 shard_map.136
  80.9 3.9 %all-to-all-start.2 = ((bf16[32,16,128]{2,1,0:T(8,128)(2,1)}), bf16[32,16,128]{2,1,0:T(8,128)(2,1)S(1)}, u32[]{:S(2)}, u32[]{:S(2)}) async-start(bf16[32,16,128]{2,1,0:T(8,128)(2,1)} %get-tuple-element.49), calls=%async_computation.2 | async-start | bytes 262144 | tf_op jit(solution)/shard_map/all_to_all | solution.py:419
  84.7 10.3 %collective-permute-start.5 = (f32[3,384]{1,0:T(4,128)S(1)}, f32[3,384]{1,0:T(4,128)S(1)}, u32[]{:S(2)}, u32[]{:S(2)}) collective-permute-start(f32[3,384]{1,0:T(4,128)S(1)} %get-tuple-element.50), channel_id=1, source_target_pairs={{0,0},{1,256},{2,32},{3,288},{4,64},{5,320},{6,96},{7,352},{8,1},{... | collective-permute-start | bytes 13832 | tf_op jit(solution)/shard_map/ppermute | solution.py:470
  95.0 0.8 collective-permute-done.5.in_rows
  95.8 3.1 %all-to-all-done.2.received = bf16[32,16,128]{2,1,0:T(8,128)(2,1)S(1)} async-done(((bf16[32,16,128]{2,1,0:T(8,128)(2,1)}), bf16[32,16,128]{2,1,0:T(8,128)(2,1)S(1)}, u32[]{:S(2)}, u32[]{:S(2)}) %all-to-all-start.2) | async-done | bytes 131104 | tf_op jit(solution)/shard_map/all_to_all | solution.py:419
  98.9 0.1 shard_map.137
  99.0 10.2 %all_to_all.20 = bf16[8,96,384]{2,1,0:T(8,128)(2,1)S(1)} all-to-all(bf16[8,96,384]{2,1,0:T(8,128)(2,1)S(1)} %shard_map.137), channel_id=1, replica_groups=mesh['zh'=4,'xh'=2,'xl'=2,'yh'=4,'yl'=2,'zl'=2,'c'=2] {'xl','yl','zl'}, dimensions={0} | all-to-all | bytes 1179648 | tf_op jit(solution)/shard_map/all_to_all | solution.py:419
  109.2 7.2 %collective-permute-start.6 = (bf16[768,384]{1,0:T(8,128)(2,1)S(1)}, bf16[768,384]{1,0:T(8,128)(2,1)S(1)}, u32[]{:S(2)}, u32[]{:S(2)}) collective-permute-start(bf16[768,384]{1,0:T(8,128)(2,1)S(1)} %bitcast.5), channel_id=1, source_target_pairs={{0,1},{1,0},{2,3},{3,2},{4,5},{5,4},{6,7},{7,6},{8,9},{9,8},{10,11... | collective-permute-start | bytes 1769480 | tf_op jit(solution)/shard_map/ppermute | solution.py:423
  116.5 1.6 %collective-permute-done.6.other = bf16[768,384]{1,0:T(8,128)(2,1)S(1)} collective-permute-done((bf16[768,384]{1,0:T(8,128)(2,1)S(1)}, bf16[768,384]{1,0:T(8,128)(2,1)S(1)}, u32[]{:S(2)}, u32[]{:S(2)}) %collective-permute-start.6) | collective-permute-done | bytes 589856 | tf_op jit(solution)/shard_map/ppermute | solution.py:423
  118.1 1.1 shard_map.138
Async XLA Ops:
  1.6 9.7 %collective-permute-start = (bf16[32,384]{1,0:T(8,128)(2,1)S(1)}, bf16[32,384]{1,0:T(8,128)(2,1)S(1)}, u32[]{:S(2)}, u32[]{:S(2)}) collective-permute-start(bf16[32,384]{1,0:T(8,128)(2,1)S(1)} %get-tuple-element.30), channel_id=1, source_target_pairs={{0,4},{4,8},{8,12},{12,16},{16,20},{20,24},{24,28},{28,32},{32,36}... | collective-permute-start | bytes 73736 | tf_op jit(solution)/shard_map/ppermute | solution.py:410
  5.7 5.7 %collective-permute-start.1 = (bf16[32,384]{1,0:T(8,128)(2,1)S(1)}, bf16[32,384]{1,0:T(8,128)(2,1)S(1)}, u32[]{:S(2)}, u32[]{:S(2)}) collective-permute-start(bf16[32,384]{1,0:T(8,128)(2,1)S(1)} %get-tuple-element.31), channel_id=1, source_target_pairs={{4,0},{8,4},{12,8},{16,12},{20,16},{24,20},{28,24},{32,28},{36,32}... | collective-permute-start | bytes 73736 | tf_op jit(solution)/shard_map/ppermute | solution.py:415
  15.6 8.5 %collective-permute-start.2 = (bf16[1536,384]{1,0:T(8,128)(2,1)S(1)}, bf16[1536,384]{1,0:T(8,128)(2,1)S(1)}, u32[]{:S(2)}, u32[]{:S(2)}) collective-permute-start(bf16[1536,384]{1,0:T(8,128)(2,1)S(1)} %get-tuple-element.40), channel_id=1, source_target_pairs={{0,1},{1,0},{2,3},{3,2},{4,5},{5,4},{6,7},{7,6},{8,9},{9,8},{10,11... | collective-permute-start | bytes 3538952 | tf_op jit(solution)/shard_map/ppermute | solution.py:423
  25.4 21.4 %all-to-all-start = ((bf16[8,192,384]{2,1,0:T(8,128)(2,1)}), bf16[8,192,384]{2,1,0:T(8,128)(2,1)S(1)}, u32[]{:S(2)}, u32[]{:S(2)}) async-start(bf16[8,192,384]{2,1,0:T(8,128)(2,1)} %shard_map.133), calls=%async_computation | async-start | bytes 2359296 | tf_op jit(solution)/shard_map/all_to_all | solution.py:419
  29.7 35.9 %copy-start = (bf16[1,8,32,384]{3,2,1,0:T(8,128)(2,1)S(1)}, bf16[1,8,32,384]{3,2,1,0:T(8,128)(2,1)}, u32[]{:S(2)}) copy-start(bf16[1,8,32,384]{3,2,1,0:T(8,128)(2,1)} %param.12) | copy-start | bytes 589828
  29.7 15.0 %collective-permute-start.3 = (f32[24,384]{1,0:T(8,128)S(1)}, f32[24,384]{1,0:T(8,128)S(1)}, u32[]{:S(2)}, u32[]{:S(2)}) collective-permute-start(f32[24,384]{1,0:T(8,128)S(1)} %get-tuple-element.41), channel_id=1, source_target_pairs={{0,4},{4,8},{8,12},{12,16},{16,20},{20,24},{24,28},{28,32},{32,36}... | collective-permute-start | bytes 110600 | tf_op jit(solution)/shard_map/ppermute | solution.py:410
  33.3 11.9 %collective-permute-start.4 = (f32[24,384]{1,0:T(8,128)S(1)}, f32[24,384]{1,0:T(8,128)S(1)}, u32[]{:S(2)}, u32[]{:S(2)}) collective-permute-start(f32[24,384]{1,0:T(8,128)S(1)} %get-tuple-element.42), channel_id=1, source_target_pairs={{4,0},{8,4},{12,8},{16,12},{20,16},{24,20},{28,24},{32,28},{36,32}... | collective-permute-start | bytes 110600 | tf_op jit(solution)/shard_map/ppermute | solution.py:415
  47.7 32.5 %all-to-all-start.1 = ((bf16[32,24,128]{2,1,0:T(8,128)(2,1)}), bf16[32,24,128]{2,1,0:T(8,128)(2,1)S(1)}, u32[]{:S(2)}, u32[]{:S(2)}) async-start(bf16[32,24,128]{2,1,0:T(8,128)(2,1)} %shard_map.134), calls=%async_computation.1 | async-start | bytes 393216 | tf_op jit(solution)/shard_map/all_to_all | solution.py:419
  80.9 18.0 %all-to-all-start.2 = ((bf16[32,16,128]{2,1,0:T(8,128)(2,1)}), bf16[32,16,128]{2,1,0:T(8,128)(2,1)S(1)}, u32[]{:S(2)}, u32[]{:S(2)}) async-start(bf16[32,16,128]{2,1,0:T(8,128)(2,1)} %get-tuple-element.49), calls=%async_computation.2 | async-start | bytes 262144 | tf_op jit(solution)/shard_map/all_to_all | solution.py:419
  84.7 11.1 %collective-permute-start.5 = (f32[3,384]{1,0:T(4,128)S(1)}, f32[3,384]{1,0:T(4,128)S(1)}, u32[]{:S(2)}, u32[]{:S(2)}) collective-permute-start(f32[3,384]{1,0:T(4,128)S(1)} %get-tuple-element.50), channel_id=1, source_target_pairs={{0,0},{1,256},{2,32},{3,288},{4,64},{5,320},{6,96},{7,352},{8,1},{... | collective-permute-start | bytes 13832 | tf_op jit(solution)/shard_map/ppermute | solution.py:470
  109.2 8.9 %collective-permute-start.6 = (bf16[768,384]{1,0:T(8,128)(2,1)S(1)}, bf16[768,384]{1,0:T(8,128)(2,1)S(1)}, u32[]{:S(2)}, u32[]{:S(2)}) collective-permute-start(bf16[768,384]{1,0:T(8,128)(2,1)S(1)} %bitcast.5), channel_id=1, source_target_pairs={{0,1},{1,0},{2,3},{3,2},{4,5},{5,4},{6,7},{7,6},{8,9},{9,8},{10,11... | collective-permute-start | bytes 1769480 | tf_op jit(solution)/shard_map/ppermute | solution.py:423

commit v7 on v6

--- a/solution.py
+++ b/solution.py
@@ -22,7 +22,8 @@
 
 TILE = ("zh", "xh", "xl", "yh", "yl")
 CUBE = ("xl", "yl", "zl")
-FAR = ("zh", "xh", "yh")
+LINE = ("zh",)
+PLANE = ("xh", "yh")
 EVERY = ("zh", "xh", "xl", "yh", "yl", "zl", "c")
 SWAP = [(0, 1), (1, 0)]
 
@@ -228,48 +229,42 @@
     return summed
 
 
-def far_kernel(received, message, spread, total):
-    members, places, _ = message.shape
-    blocks = lane_blocks(received.shape[2])
-    rows = ROWS * members
-    size = ROWS * len(blocks)
-    spread[...] = jnp.zeros_like(spread)
-    for k, lanes in enumerate(blocks):
-        summed = received[0, :, lanes].astype(jnp.float32)
-        for i in range(1, received.shape[0]):
-            summed += received[i, :, lanes].astype(jnp.float32)
-        total[k] = summed
-        for r in range(ROWS):
-            place = r * len(blocks) + k
-            part = total[k, r * members : (r + 1) * members, :]
-            spread[pl.ds(place, members, stride=places), :] = part
-            part = total[k, pl.ds(rows + r, members, stride=ROWS), :]
-            spread[pl.ds(size + place, members, stride=places), :] = part
-    message[...] = spread[...].reshape(message.shape).astype(jnp.bfloat16)
-
-
-def turn_kernel(scale, received, message, grad_w_in, sums):
-    sums[...] = add_members(received) * scale
-    width = grad_w_in.shape[1]
-    blocks = lane_blocks(width)
-    size = ROWS * len(blocks)
-    for k, lanes in enumerate(blocks):
-        grad_w_in[:, lanes] = sums[pl.ds(size + k, ROWS, stride=len(blocks)), :]
-    finished = sums[: message.shape[1], :].astype(jnp.bfloat16)
+def line_kernel(received, message, total):
+    members, rows, _ = message.shape
+    rows //= 2
+    total[...] = add_members(received)
+    for m in range(members):
+        block = [total[start + m * rows : start + (m + 1) * rows, :] for start in (0, members * rows)]
+        message[m] = jnp.concatenate(block, axis=0).astype(jnp.bfloat16)
+
+
+def plane_kernel(received, message, total, block):
+    rows = total.shape[0] // 2
+    total[...] = add_members(received)
+    block[...] = jnp.zeros_like(block)
+    block[:rows, :] = total[:rows, :]
+    for m in range(message.shape[0]):
+        start = rows + m * ROWS
+        block[rows : rows + ROWS, :] = total[start : start + ROWS, :]
+        message[m] = block[...].astype(jnp.bfloat16)
+
+
+def turn_kernel(scale, received, message, grad_w_in):
+    rows = message.shape[1]
+    total = add_members(received) * scale
+    grad_w_in[...] = total[rows : rows + ROWS, :]
+    finished = total[:rows, :].astype(jnp.bfloat16)
     for m in range(message.shape[0]):
         message[m] = finished
 
 
-def unpack_kernel(received, message, spread):
-    members, places, _ = received.shape
-    blocks = lane_blocks(message.shape[2])
-    spread[...] = received[...].astype(jnp.float32).reshape(spread.shape)
-    for r in range(ROWS):
-        for k, lanes in enumerate(blocks):
-            part = spread[pl.ds(r * len(blocks) + k, members, stride=places), :]
-            part = part.astype(jnp.bfloat16)
-            for i in range(message.shape[0]):
-                message[i, r * members : (r + 1) * members, lanes] = part
+def unpack_kernel(received, message, total):
+    members, rows, _ = received.shape
+    for m in range(members):
+        total[m * rows : (m + 1) * rows, :] = received[m].astype(jnp.float32)
+    whole = total[...].astype(jnp.bfloat16)
+    for m in range(message.shape[0]):
+        message[m] = whole
 
 
 def join_kernel(core, own, other, in_rows, grad_w_out, grad_w_in):
@@ -362,38 +357,40 @@
     )[0]
 
 
-def to_far(received, members):
+def to_line(received, members):
     _, rows, width = received.shape
     return call(
-        far_kernel,
-        [((members, 24, LANES), B16)],
-        [pltpu.VMEM((members * 24, LANES), F32), pltpu.VMEM((width // LANES, rows, LANES), F32)],
-        [],
-        [received],
+        line_kernel, [((members, rows // members, width), B16)], [pltpu.VMEM((rows, width), F32)], [], [received],
         received.size, 3 * received.size,
     )[0]
 
 
-def turn(scale, received, width):
-    members, places, _ = received.shape
-    return call(
-        functools.partial(turn_kernel, scale),
-        [((members, 16, LANES), B16), ((ROWS, width), F32)],
-        [pltpu.VMEM((places, LANES), F32)],
+def to_plane(received, members):
+    _, rows, width = received.shape
+    return call(
+        plane_kernel,
+        [((members, rows // 2 + SIDE, width), B16)],
+        [pltpu.VMEM((rows, width), F32), pltpu.VMEM((rows // 2 + SIDE, width), F32)],
         [],
         [received],
         received.size, 4 * received.size,
-    )
-
-
-def unpack(received, members, width):
-    return call(
-        unpack_kernel,
-        [((members, ROWS * received.shape[0], width), B16)],
-        [pltpu.VMEM((received.shape[0] * received.shape[1], LANES), F32)],
-        [],
-        [received],
-        received.size, 6 * received.size,
+    )[0]
+
+
+def turn(scale, received, members):
+    _, rows, width = received.shape
+    return call(
+        functools.partial(turn_kernel, scale),
+        [((members, rows - SIDE, width), B16), ((ROWS, width), F32)], [], [], [received],
+        received.size, 4 * received.size,
+    )
+
+
+def unpack(received, members):
+    count, rows, width = received.shape
+    return call(
+        unpack_kernel, [((members, count * rows, width), B16)], [pltpu.VMEM((count * rows, width), F32)], [], [received],
+        received.size, 10 * received.size,
     )[0]
 
 
@@ -431,7 +428,7 @@
         for axis in reversed(EVERY):
             rest, at[axis] = divmod(rest, sizes[axis])
         target = 0
-        for axis in ("c",) + CUBE + FAR:
+        for axis in ("c",) + CUBE + LINE + PLANE:
             target = target * sizes[axis] + at[axis]
         pairs.append((source, target))
     return pairs
@@ -448,8 +445,7 @@
     upstream = cotangent[0].reshape(-1, channels)
     core = lax.axis_index("c").astype(jnp.int32).reshape(1)
     sizes = {axis: lax.axis_size(axis) for axis in EVERY}
-    near = math.prod(sizes[axis] for axis in CUBE)
-    far = math.prod(sizes[axis] for axis in FAR)
+    cube, line, plane = (math.prod(sizes[axis] for axis in axes) for axes in (CUBE, LINE, PLANE))
     scale = 1.0 / math.sqrt(height * breadth * math.prod(sizes.values()))
 
     conv, out_grad, back, w_in_t, b_cols, w_in_here, taps, vectors = before_halos(
@@ -458,18 +454,19 @@
     kept, sent, grad_conv, low, high = middle(
         core, conv, low, high, taps, vectors, w_in_t, b_cols, out_grad, back, w_in_here
     )
-    message = to_cube(near, kept, swap(sent))
+    message = to_cube(cube, kept, swap(sent))
     received = exchange(message, CUBE)
     low, high = from_left(high), from_right(low)
     received, low, high = lax.optimization_barrier((received, low, high))
-    received = exchange(to_far(received, far), FAR)
+    received = exchange(to_line(received, line), LINE)
+    received = exchange(to_plane(received, plane), PLANE)
+    message, in_rows = turn(scale, received, line)
+    received = exchange(message, LINE)
+    received, in_rows, low, high = lax.optimization_barrier((received, in_rows, low, high))
+    own = exchange(unpack(received, cube), CUBE).reshape(-1, channels)
+    in_rows = lax.ppermute(in_rows, EVERY, owners(sizes))
     grad_image = to_features(grad_conv, low, high, taps, upstream)
-    received, grad_image = lax.optimization_barrier((received, grad_image))
-    message, in_rows = turn(scale, received, channels)
-    received = exchange(message, FAR)
-    in_rows = lax.ppermute(in_rows, EVERY, owners(sizes))
-    received, in_rows = lax.optimization_barrier((received, in_rows))
-    own = exchange(unpack(received, near, channels), CUBE).reshape(-1, channels)
+    own, in_rows, grad_image = lax.optimization_barrier((own, in_rows, grad_image))
     grad_w_out, grad_w_in = join(core, own, swap(own), in_rows)
     return (grad_image.reshape(1, height, breadth, channels), grad_w_in, grad_w_out)
 

time: 120 us -> 120 us (level)
  the two profiles are of different devices: /device:TPU:1 before, /device:TPU:41 now
where the time goes in v7:
time: 120 us; the launch traced here: 119 us
  starting transfers between devices  45.9 us (38%)
  blocking collectives  40.8 us (34%)
  waiting for transfers between devices  16.5 us (14%)
  Pallas kernels  15.4 us (13%)
    all_to_all x3, blocking collectives, exchange(): return lax.all_to_all(blocks, axes, split_axis=0, concat_axis=0, tiled=True)  40.8 us
    pallas_call x10, Pallas kernels, call(): pl.pallas_call(kernel, out_shape=[jax.ShapeDtypeStruct(shape, kind) for s...  15.4 us
    all_to_all x2, starting transfers between devices, exchange(): return lax.all_to_all(blocks, axes, split_axis=0, concat_axis=0, tiled=True)  11.9 us
    ppermute x2, starting transfers between devices, swap(): return lax.ppermute(block, 'c', SWAP)  11.9 us
    ppermute x1, starting transfers between devices, body(): in_rows = lax.ppermute(in_rows, EVERY, owners(sizes))  11.5 us
    ppermute x2, waiting for transfers between devices, from_left(): return lax.ppermute(block, TILE, [(i, i + 1) for i in range(count - 1)])  10.4 us
    ppermute x2, starting transfers between devices, from_right(): return lax.ppermute(block, TILE, [(i + 1, i) for i in range(count - 1)])  6.34 us
    ppermute x2, starting transfers between devices, from_left(): return lax.ppermute(block, TILE, [(i, i + 1) for i in range(count - 1)])  4.21 us
  transfers between devices with their start and end apart: 9, of which 5 were waited for; matrix products, arithmetic and copies ran while one was open for 0% of the time, Pallas kernels for 6%

profile of v7, /device:TPU:41, one launch (start us, length us, event | category | flops | bytes accessed | tf_op | source)
XLA Modules:
  0.0 119.3 jit_solution(15409782909343678522)
XLA Ops:
  0.6 1.0 shard_map.131
  1.6 2.3 %collective-permute-start = (bf16[32,384]{1,0:T(8,128)(2,1)S(1)}, bf16[32,384]{1,0:T(8,128)(2,1)S(1)}, u32[]{:S(2)}, u32[]{:S(2)}) collective-permute-start(bf16[32,384]{1,0:T(8,128)(2,1)S(1)} %get-tuple-element.33), channel_id=1, source_target_pairs={{0,4},{4,8},{8,12},{12,16},{16,20},{20,24},{24,28},{28,32},{32,36}... | collective-permute-start | bytes 73736 | tf_op jit(solution)/shard_map/ppermute | solution.py:407
  4.0 3.0 %collective-permute-start.1 = (bf16[32,384]{1,0:T(8,128)(2,1)S(1)}, bf16[32,384]{1,0:T(8,128)(2,1)S(1)}, u32[]{:S(2)}, u32[]{:S(2)}) collective-permute-start(bf16[32,384]{1,0:T(8,128)(2,1)S(1)} %get-tuple-element.34), channel_id=1, source_target_pairs={{4,0},{8,4},{12,8},{16,12},{20,16},{24,20},{28,24},{32,28},{36,32}... | collective-permute-start | bytes 73736 | tf_op jit(solution)/shard_map/ppermute | solution.py:412
  7.0 4.4 %shard_map.130 = (f32[256,384]{1,0:T(8,128)S(1)}, bf16[256,384]{1,0:T(8,128)(2,1)S(1)}, f32[1536,256]{1,0:T(8,128)S(1)}, bf16[1536,384]{1,0:T(8,128)(2,1)S(1)}, ...) custom-call(s32[1,4]{1,0:T(1,128)} %flags.1, ...), custom_call_target="tpu_custom_call" | custom-call | flops 301989888 | bytes 8388608 | tf_op jit(solution)/shard_map/pallas_call | solution.py:282
  11.3 0.0 collective-permute-done.low
  11.4 0.0 collective-permute-done.1.high
  11.4 4.2 %shard_map.132 = (f32[1536,384]{1,0:T(8,128)S(1)}, bf16[1536,384]{1,0:T(8,128)(2,1)S(1)}, f32[256,384]{1,0:T(8,128)S(1)}, f32[24,384]{1,0:T(8,128)S(1)}, f32[24,384]{1,0:T(8,128)S(1)}) custom-call(s32[1]{0:T(128)} %bitcast.core, f32[256,384]{1,0:T(8,128)S(1)} %get-tuple-element.32.conv, bf16[32,384]{1,0:T(8,128)(2,1)S(1)} %collective-permute-done.low, ...), custom_call_target="tpu_custom_call" | custom-call | flops 1207959552 | bytes 12582912 | tf_op jit(solution)/shard_map/pallas_call | solution.py:282
  15.6 3.1 %collective-permute-start.2 = (bf16[1536,384]{1,0:T(8,128)(2,1)S(1)}, bf16[1536,384]{1,0:T(8,128)(2,1)S(1)}, u32[]{:S(2)}, u32[]{:S(2)}) collective-permute-start(bf16[1536,384]{1,0:T(8,128)(2,1)S(1)} %get-tuple-element.43), channel_id=1, source_target_pairs={{0,1},{1,0},{2,3},{3,2},{4,5},{5,4},{6,7},{7,6},{8,9},{9,8},{10,11... | collective-permute-start | bytes 3538952 | tf_op jit(solution)/shard_map/ppermute | solution.py:420
  18.7 2.5 %collective-permute-done.2.received = bf16[1536,384]{1,0:T(8,128)(2,1)S(1)} collective-permute-done((bf16[1536,384]{1,0:T(8,128)(2,1)S(1)}, bf16[1536,384]{1,0:T(8,128)(2,1)S(1)}, u32[]{:S(2)}, u32[]{:S(2)}) %collective-permute-start.2) | collective-permute-done | bytes 1179680 | tf_op jit(solution)/shard_map/ppermute | solution.py:420
  21.2 1.3 %shard_map.133 = bf16[8,192,384]{2,1,0:T(8,128)(2,1)} custom-call(f32[1536,384]{1,0:T(8,128)S(1)} %get-tuple-element.42.kept, bf16[1536,384]{1,0:T(8,128)(2,1)S(1)} %collective-permute-done.2.received), custom_call_target="tpu_custom_call" | custom-call | flops 1179648 | bytes 4718592 | tf_op jit(solution)/shard_map/pallas_call | solution.py:282
  22.4 6.6 %all-to-all-start = ((bf16[8,192,384]{2,1,0:T(8,128)(2,1)}), bf16[8,192,384]{2,1,0:T(8,128)(2,1)S(1)}, u32[]{:S(2)}, u32[]{:S(2)}) async-start(bf16[8,192,384]{2,1,0:T(8,128)(2,1)} %shard_map.133), calls=%async_computation | async-start | bytes 2359296 | tf_op jit(solution)/shard_map/all_to_all | solution.py:416
  29.0 1.9 %collective-permute-start.3 = (f32[24,384]{1,0:T(8,128)S(1)}, f32[24,384]{1,0:T(8,128)S(1)}, u32[]{:S(2)}, u32[]{:S(2)}) collective-permute-start(f32[24,384]{1,0:T(8,128)S(1)} %get-tuple-element.44), channel_id=1, source_target_pairs={{0,4},{4,8},{8,12},{12,16},{16,20},{20,24},{24,28},{28,32},{32,36}... | collective-permute-start | bytes 110600 | tf_op jit(solution)/shard_map/ppermute | solution.py:407
  30.9 3.4 %collective-permute-start.4 = (f32[24,384]{1,0:T(8,128)S(1)}, f32[24,384]{1,0:T(8,128)S(1)}, u32[]{:S(2)}, u32[]{:S(2)}) collective-permute-start(f32[24,384]{1,0:T(8,128)S(1)} %get-tuple-element.45), channel_id=1, source_target_pairs={{4,0},{8,4},{12,8},{16,12},{20,16},{24,20},{28,24},{32,28},{36,32}... | collective-permute-start | bytes 110600 | tf_op jit(solution)/shard_map/ppermute | solution.py:412
  34.3 10.4 %collective-permute-done.3.low = f32[24,384]{1,0:T(8,128)S(1)} collective-permute-done((f32[24,384]{1,0:T(8,128)S(1)}, f32[24,384]{1,0:T(8,128)S(1)}, u32[]{:S(2)}, u32[]{:S(2)}) %collective-permute-start.3) | collective-permute-done | bytes 36896 | tf_op jit(solution)/shard_map/ppermute | solution.py:407
  44.7 0.0 collective-permute-done.4.high
  44.7 0.6 all-to-all-done.received
  45.4 0.2 shard_map.134
  45.5 16.5 %all_to_all.25.received = bf16[4,48,384]{2,1,0:T(8,128)(2,1)S(1)} all-to-all(bf16[4,48,384]{2,1,0:T(8,128)(2,1)S(1)} %shard_map.134), channel_id=1, replica_groups=mesh['zh'=4,'xh'=2,'xl'=2,'yh'=4,'yl'=2,'zl'=2,'c'=2] {'zh'}, dimensions={0} | all-to-all | bytes 294912 | tf_op jit(solution)/shard_map/all_to_all | solution.py:416
  62.0 0.1 shard_map.135
  62.1 14.9 %all_to_all.26.received = bf16[8,32,384]{2,1,0:T(8,128)(2,1)S(1)} all-to-all(bf16[8,32,384]{2,1,0:T(8,128)(2,1)S(1)} %shard_map.135), channel_id=1, replica_groups=mesh['zh'=4,'xh'=2,'xl'=2,'yh'=4,'yl'=2,'zl'=2,'c'=2] {'xh','yh'}, dimensions={0} | all-to-all | bytes 393216 | tf_op jit(solution)/shard_map/all_to_all | solution.py:416
  76.9 0.0 copy-start
  77.0 9.4 %all_to_all.27.received = bf16[4,24,384]{2,1,0:T(8,128)(2,1)S(1)} all-to-all(bf16[4,24,384]{2,1,0:T(8,128)(2,1)S(1)} %get-tuple-element.47), channel_id=1, replica_groups=mesh['zh'=4,'xh'=2,'xl'=2,'yh'=4,'yl'=2,'zl'=2,'c'=2] {'zh'}, dimensions={0} | all-to-all | bytes 147456 | tf_op jit(solution)/shard_map/all_to_all | solution.py:416
  86.4 0.9 shard_map.137
  87.3 5.4 %all-to-all-start.4 = ((bf16[8,96,384]{2,1,0:T(8,128)(2,1)}), bf16[8,96,384]{2,1,0:T(8,128)(2,1)S(1)}, u32[]{:S(2)}, u32[]{:S(2)}) async-start(bf16[8,96,384]{2,1,0:T(8,128)(2,1)} %shard_map.137), calls=%async_computation.4 | async-start | bytes 1179648 | tf_op jit(solution)/shard_map/all_to_all | solution.py:416
  92.7 11.5 %collective-permute-start.5 = (f32[3,384]{1,0:T(4,128)S(1)}, f32[3,384]{1,0:T(4,128)S(1)}, u32[]{:S(2)}, u32[]{:S(2)}) collective-permute-start(f32[3,384]{1,0:T(4,128)S(1)} %get-tuple-element.52), channel_id=1, source_target_pairs={{0,0},{1,256},{2,32},{3,288},{4,64},{5,320},{6,96},{7,352},{8,1},{... | collective-permute-start | bytes 13832 | tf_op jit(solution)/shard_map/ppermute | solution.py:467
  104.1 0.0 copy-done
  104.1 2.3 %shard_map.138 = bf16[256,384]{1,0:T(8,128)(2,1)} custom-call(f32[256,384]{1,0:T(8,128)S(1)} %get-tuple-element.53.grad_conv, f32[24,384]{1,0:T(8,128)S(1)} %collective-permute-done.3.low, f32[24,384]{1,0:T(8,128)S(1)} %collective-permute-done.4.high, f32[7,7,384]{2,1,0:T(8,128)S(1)} %get-tuple-element.35.taps, bf16[256,384]{1,0:T(8,128)(2,1)S(1)} %bitcast.8), custom_call_target="tpu_custom_call" | custom-call | flops 9633792 | bytes 2097152 | tf_op jit(solution)/shard_map/pallas_call | solution.py:282
  106.4 1.4 %collective-permute-done.5.in_rows = f32[3,384]{1,0:T(4,128)S(1)} collective-permute-done((f32[3,384]{1,0:T(4,128)S(1)}, f32[3,384]{1,0:T(4,128)S(1)}, u32[]{:S(2)}, u32[]{:S(2)}) %collective-permute-start.5) | collective-permute-done | bytes 4640 | tf_op jit(solution)/shard_map/ppermute | solution.py:467
  107.8 0.0 all-to-all-done.4
  107.8 8.8 %collective-permute-start.6 = (bf16[768,384]{1,0:T(8,128)(2,1)S(1)}, bf16[768,384]{1,0:T(8,128)(2,1)S(1)}, u32[]{:S(2)}, u32[]{:S(2)}) collective-permute-start(bf16[768,384]{1,0:T(8,128)(2,1)S(1)} %bitcast.5), channel_id=1, source_target_pairs={{0,1},{1,0},{2,3},{3,2},{4,5},{5,4},{6,7},{7,6},{8,9},{9,8},{10,11... | collective-permute-start | bytes 1769480 | tf_op jit(solution)/shard_map/ppermute | solution.py:420
  116.6 1.6 %collective-permute-done.6.other = bf16[768,384]{1,0:T(8,128)(2,1)S(1)} collective-permute-done((bf16[768,384]{1,0:T(8,128)(2,1)S(1)}, bf16[768,384]{1,0:T(8,128)(2,1)S(1)}, u32[]{:S(2)}, u32[]{:S(2)}) %collective-permute-start.6) | collective-permute-done | bytes 589856 | tf_op jit(solution)/shard_map/ppermute | solution.py:420
  118.2 1.1 shard_map.139
  (1 shorter events, 0.0 us)
Async XLA Ops:
  1.6 9.7 %collective-permute-start = (bf16[32,384]{1,0:T(8,128)(2,1)S(1)}, bf16[32,384]{1,0:T(8,128)(2,1)S(1)}, u32[]{:S(2)}, u32[]{:S(2)}) collective-permute-start(bf16[32,384]{1,0:T(8,128)(2,1)S(1)} %get-tuple-element.33), channel_id=1, source_target_pairs={{0,4},{4,8},{8,12},{12,16},{16,20},{20,24},{24,28},{28,32},{32,36}... | collective-permute-start | bytes 73736 | tf_op jit(solution)/shard_map/ppermute | solution.py:407
  4.0 7.4 %collective-permute-start.1 = (bf16[32,384]{1,0:T(8,128)(2,1)S(1)}, bf16[32,384]{1,0:T(8,128)(2,1)S(1)}, u32[]{:S(2)}, u32[]{:S(2)}) collective-permute-start(bf16[32,384]{1,0:T(8,128)(2,1)S(1)} %get-tuple-element.34), channel_id=1, source_target_pairs={{4,0},{8,4},{12,8},{16,12},{20,16},{24,20},{28,24},{32,28},{36,32}... | collective-permute-start | bytes 73736 | tf_op jit(solution)/shard_map/ppermute | solution.py:412
  15.6 5.6 %collective-permute-start.2 = (bf16[1536,384]{1,0:T(8,128)(2,1)S(1)}, bf16[1536,384]{1,0:T(8,128)(2,1)S(1)}, u32[]{:S(2)}, u32[]{:S(2)}) collective-permute-start(bf16[1536,384]{1,0:T(8,128)(2,1)S(1)} %get-tuple-element.43), channel_id=1, source_target_pairs={{0,1},{1,0},{2,3},{3,2},{4,5},{5,4},{6,7},{7,6},{8,9},{9,8},{10,11... | collective-permute-start | bytes 3538952 | tf_op jit(solution)/shard_map/ppermute | solution.py:420
  22.4 22.9 %all-to-all-start = ((bf16[8,192,384]{2,1,0:T(8,128)(2,1)}), bf16[8,192,384]{2,1,0:T(8,128)(2,1)S(1)}, u32[]{:S(2)}, u32[]{:S(2)}) async-start(bf16[8,192,384]{2,1,0:T(8,128)(2,1)} %shard_map.133), calls=%async_computation | async-start | bytes 2359296 | tf_op jit(solution)/shard_map/all_to_all | solution.py:416
  29.0 15.7 %collective-permute-start.3 = (f32[24,384]{1,0:T(8,128)S(1)}, f32[24,384]{1,0:T(8,128)S(1)}, u32[]{:S(2)}, u32[]{:S(2)}) collective-permute-start(f32[24,384]{1,0:T(8,128)S(1)} %get-tuple-element.44), channel_id=1, source_target_pairs={{0,4},{4,8},{8,12},{12,16},{16,20},{20,24},{24,28},{28,32},{32,36}... | collective-permute-start | bytes 110600 | tf_op jit(solution)/shard_map/ppermute | solution.py:407
  30.9 13.8 %collective-permute-start.4 = (f32[24,384]{1,0:T(8,128)S(1)}, f32[24,384]{1,0:T(8,128)S(1)}, u32[]{:S(2)}, u32[]{:S(2)}) collective-permute-start(f32[24,384]{1,0:T(8,128)S(1)} %get-tuple-element.45), channel_id=1, source_target_pairs={{4,0},{8,4},{12,8},{16,12},{20,16},{24,20},{28,24},{32,28},{36,32}... | collective-permute-start | bytes 110600 | tf_op jit(solution)/shard_map/ppermute | solution.py:412
  76.9 27.2 %copy-start = (bf16[1,8,32,384]{3,2,1,0:T(8,128)(2,1)S(1)}, bf16[1,8,32,384]{3,2,1,0:T(8,128)(2,1)}, u32[]{:S(2)}) copy-start(bf16[1,8,32,384]{3,2,1,0:T(8,128)(2,1)} %param.12) | copy-start | bytes 589828
  87.3 20.5 %all-to-all-start.4 = ((bf16[8,96,384]{2,1,0:T(8,128)(2,1)}), bf16[8,96,384]{2,1,0:T(8,128)(2,1)S(1)}, u32[]{:S(2)}, u32[]{:S(2)}) async-start(bf16[8,96,384]{2,1,0:T(8,128)(2,1)} %shard_map.137), calls=%async_computation.4 | async-start | bytes 1179648 | tf_op jit(solution)/shard_map/all_to_all | solution.py:416
  92.7 15.2 %collective-permute-start.5 = (f32[3,384]{1,0:T(4,128)S(1)}, f32[3,384]{1,0:T(4,128)S(1)}, u32[]{:S(2)}, u32[]{:S(2)}) collective-permute-start(f32[3,384]{1,0:T(4,128)S(1)} %get-tuple-element.52), channel_id=1, source_target_pairs={{0,0},{1,256},{2,32},{3,288},{4,64},{5,320},{6,96},{7,352},{8,1},{... | collective-permute-start | bytes 13832 | tf_op jit(solution)/shard_map/ppermute | solution.py:467
  107.8 10.4 %collective-permute-start.6 = (bf16[768,384]{1,0:T(8,128)(2,1)S(1)}, bf16[768,384]{1,0:T(8,128)(2,1)S(1)}, u32[]{:S(2)}, u32[]{:S(2)}) collective-permute-start(bf16[768,384]{1,0:T(8,128)(2,1)S(1)} %bitcast.5), channel_id=1, source_target_pairs={{0,1},{1,0},{2,3},{3,2},{4,5},{5,4},{6,7},{7,6},{8,9},{9,8},{10,11... | collective-permute-start | bytes 1769480 | tf_op jit(solution)/shard_map/ppermute | solution.py:420

commit v8 on v7

--- a/solution.py
+++ b/solution.py
@@ -1,4 +1,5 @@
 import functools
+import itertools
 import math
 
 import jax
@@ -16,6 +17,7 @@
 CHUNK = 32
 ROWS = 3
 EDGE = 4 * SIDE
+TAIL = 16
 EPSILON = 1e-06
 VMEM_LIMIT = 16 * 1024 * 1024
 NT = (((1,), (1,)), ((), ()))
@@ -139,7 +141,7 @@
 
 
 def middle_kernel(
-    core, conv, low, high, taps, vectors, w_in_t, b_cols, out_grad, back, w_in,
+    device, conv, low, high, taps, vectors, w_in_t, b_cols, out_grad, back, w_in,
     kept, sent, grad_conv, low_edge, high_edge,
     rows, low_wide, high_wide, standard, normed, preact, hidden, grad_pre
 ):
@@ -176,8 +178,9 @@
 
     lax.fori_loop(0, preact.shape[0] // CHUNK, step, 0, unroll=2)
     half = hidden.shape[0] // 2
-    other = pl.ds(pl.multiple_of((1 - core[0]) * half, half), half)
-    own = pl.ds(pl.multiple_of(core[0] * half, half), half)
+    core = device[0] & 1
+    other = pl.ds(pl.multiple_of((1 - core) * half, half), half)
+    own = pl.ds(pl.multiple_of(core * half, half), half)
     sent[:half, :] = matmul(hidden[other, :], out_grad[...]).astype(jnp.bfloat16)
     sent[half:, :] = matmul(grad_pre[other, :], normed[...]).astype(jnp.bfloat16)
     kept[:half, :] = matmul(hidden[own, :], out_grad[...])
@@ -214,12 +217,21 @@
 def cube_kernel(kept, received, message):
     members, rows, _ = message.shape
     rows //= 2
+    half = members * rows
     for m in range(members):
-        for i in range(2):
-            start = (i * members + m) * rows
-            part = slice(start, start + rows)
-            total = kept[part, :] + received[part, :].astype(jnp.float32)
-            message[m, i * rows : (i + 1) * rows, :] = total.astype(jnp.bfloat16)
+        part = slice(m * rows, (m + 1) * rows)
+        total = kept[part, :] + received[part, :].astype(jnp.float32)
+        message[m, :rows, :] = total.astype(jnp.bfloat16)
+    run = 4 * ROWS
+    for bit7, bit6, bit5 in itertools.product(range(2), repeat=3):
+        start = half + (bit7 * 4 + bit6 * 2 + bit5) * rows
+        total = kept[start : start + rows, :] + received[start : start + rows, :].astype(jnp.float32)
+        for bit2 in range(2):
+            runs = [total[(2 * i + bit2) * run : (2 * i + bit2 + 1) * run, :] for i in range(4)]
+            place = rows + bit6 * 4 * run
+            message[bit5 * 4 + bit2 * 2 + bit7, place : place + 4 * run, :] = jnp.concatenate(
+                runs, axis=0
+            ).astype(jnp.bfloat16)
 
 
 def add_members(received):
@@ -230,48 +242,69 @@
 
 
 def line_kernel(received, message, total):
-    members, rows, _ = message.shape
+    members, rows, width = message.shape
     rows //= 2
-    total[...] = add_members(received)
+    summed = add_members(received)
+    for k, lanes in enumerate(lane_blocks(width)):
+        total[k] = summed[:, lanes]
+        for m in range(members):
+            parts = [total[k, m * rows : (m + 1) * rows, :]]
+            for r in range(ROWS):
+                start = members * rows + m * ROWS + r
+                parts.append(total[k, pl.ds(start, SIDE, stride=members * ROWS), :])
+            message[m, :, lanes] = jnp.concatenate(parts, axis=0).astype(jnp.bfloat16)
+
+
+def plane_kernel(received, message, total, block):
+    rows = received.shape[1] // 2
+    members = message.shape[0]
+    summed = add_members(received)
+    for k, lanes in enumerate(lane_blocks(received.shape[2])):
+        total[k] = summed[:, lanes]
+    block[...] = jnp.zeros_like(block)
     for m in range(members):
-        block = [total[start + m * rows : start + (m + 1) * rows, :] for start in (0, members * rows)]
-        message[m] = jnp.concatenate(block, axis=0).astype(jnp.bfloat16)
-
-
-def plane_kernel(received, message, total, block):
-    rows = total.shape[0] // 2
-    total[...] = add_members(received)
-    block[...] = jnp.zeros_like(block)
-    block[:rows, :] = total[:rows, :]
-    for m in range(message.shape[0]):
-        start = rows + m * ROWS
-        block[rows : rows + ROWS, :] = total[start : start + ROWS, :]
+        for k, lanes in enumerate(lane_blocks(received.shape[2])):
+            block[:rows, lanes] = total[k, :rows, :]
+            block[rows : rows + ROWS, lanes] = total[k, pl.ds(rows + m, ROWS, stride=members), :]
         message[m] = block[...].astype(jnp.bfloat16)
 
 
-def turn_kernel(scale, received, message, grad_w_in):
-    rows = message.shape[1]
-    total = add_members(received) * scale
-    grad_w_in[...] = total[rows : rows + ROWS, :]
-    finished = total[:rows, :].astype(jnp.bfloat16)
+def turn_kernel(scale, received, message):
+    finished = (add_members(received) * scale).astype(jnp.bfloat16)
     for m in range(message.shape[0]):
         message[m] = finished
 
 
-def unpack_kernel(received, message, total):
-    members, rows, _ = received.shape
-    for m in range(members):
-        total[m * rows : (m + 1) * rows, :] = received[m].astype(jnp.float32)
-    whole = total[...].astype(jnp.bfloat16)
-    for m in range(message.shape[0]):
-        message[m] = whole
-
-
-def join_kernel(core, own, other, in_rows, grad_w_out, grad_w_in):
-    half = own.shape[0]
-    grad_w_out[pl.ds(pl.multiple_of(core[0] * half, half), half), :] = own[...]
-    grad_w_out[pl.ds(pl.multiple_of((1 - core[0]) * half, half), half), :] = other[...]
-    grad_w_in[...] = in_rows[...]
+def unpack_kernel(received, message, block):
+    rows = received.shape[1] - SIDE
+    count = received.shape[0] * rows
+    parts = [received[m].astype(jnp.float32) for m in range(received.shape[0])]
+    block[count:, :] = jnp.zeros_like(block[count:, :])
+    for m, part in enumerate(parts):
+        block[m * rows : (m + 1) * rows, :] = part[:rows, :]
+    for bit1 in range(2):
+        for bit0 in range(2):
+            start = count + bit0 * ROWS
+            block[start : start + ROWS, :] = parts[2 * bit1 + bit0][rows : rows + ROWS, :]
+        whole = block[...].astype(jnp.bfloat16)
+        for m in range(bit1, message.shape[0], 2):
+            message[m] = whole
+
+
+def join_kernel(device, own, other, grad_w_out, grad_w_in):
+    number = device[0]
+    here = number & 1
+    source = ((number >> 5) & 1) * 4 + ((number >> 2) & 1) * 2 + ((number >> 7) & 1)
+    members, rows, width = own.shape
+    count = rows - TAIL
+    half = members * count
+    for core, blocks in ((here, own), (1 - here, other)):
+        for m in range(members):
+            start = pl.multiple_of(core * half + m * count, count)
+            grad_w_out[pl.ds(start, count), :] = blocks[m, :count, :]
+    tails = [blocks[source, count:, :].astype(jnp.float32) for blocks in (own, other)]
+    tail = jnp.where(number >> 8 == here, tails[0], tails[1])
+    grad_w_in[...] = jnp.where(here == 0, tail[:ROWS, :], tail[ROWS : 2 * ROWS, :])
 
 
 def call(kernel, outs, scratch, scalars, arrays, flops, nbytes, space=pltpu.VMEM):
@@ -323,7 +356,7 @@
     )
 
 
-def middle(core, conv, low, high, taps, vectors, w_in_t, b_cols, out_grad, back, w_in):
+def middle(device, conv, low, high, taps, vectors, w_in_t, b_cols, out_grad, back, w_in):
     rows, width = conv.shape
     hidden = w_in_t.shape[0]
     halo, edge = pltpu.VMEM((EDGE, width), F32), (HALO * SIDE, width)
@@ -332,7 +365,7 @@
         [((hidden, width), F32), ((hidden, width), B16), ((rows, width), F32), (edge, F32), (edge, F32)],
         [pltpu.VMEM((rows, width), F32), halo, halo, pltpu.VMEM((rows, width), F32), pltpu.VMEM((rows, width), B16),
          pltpu.VMEM((hidden, rows), F32), pltpu.VMEM((hidden, rows), B16), pltpu.VMEM((hidden, rows), B16)],
-        [core],
+        [device],
         [conv, low, high, taps, vectors, w_in_t, b_cols, out_grad, back, w_in],
         8 * rows * width * hidden, 12 * 1024 * 1024,
     )
@@ -360,7 +393,8 @@
 def to_line(received, members):
     _, rows, width = received.shape
     return call(
-        line_kernel, [((members, rows // members, width), B16)], [pltpu.VMEM((rows, width), F32)], [], [received],
+        line_kernel, [((members, rows // members, width), B16)],
+        [pltpu.VMEM((width // LANES, rows, LANES), F32)], [], [received],
         received.size, 3 * received.size,
     )[0]
 
@@ -370,7 +404,7 @@
     return call(
         plane_kernel,
         [((members, rows // 2 + SIDE, width), B16)],
-        [pltpu.VMEM((rows, width), F32), pltpu.VMEM((rows // 2 + SIDE, width), F32)],
+        [pltpu.VMEM((width // LANES, rows, LANES), F32), pltpu.VMEM((rows // 2 + SIDE, width), F32)],
         [],
         [received],
         received.size, 4 * received.size,
@@ -380,24 +414,24 @@
 def turn(scale, received, members):
     _, rows, width = received.shape
     return call(
-        functools.partial(turn_kernel, scale),
-        [((members, rows - SIDE, width), B16), ((ROWS, width), F32)], [], [], [received],
+        functools.partial(turn_kernel, scale), [((members, rows, width), B16)], [], [], [received],
         received.size, 4 * received.size,
-    )
+    )[0]
 
 
 def unpack(received, members):
     count, rows, width = received.shape
-    return call(
-        unpack_kernel, [((members, count * rows, width), B16)], [pltpu.VMEM((count * rows, width), F32)], [], [received],
+    rows = count * (rows - SIDE) + TAIL
+    return call(
+        unpack_kernel, [((members, rows, width), B16)], [pltpu.VMEM((rows, width), F32)], [], [received],
         received.size, 10 * received.size,
     )[0]
 
 
-def join(core, own, other, in_rows):
-    rows, width = own.shape
-    return call(
-        join_kernel, [((2 * rows, width), B16), (in_rows.shape, F32)], [], [core], [own, other, in_rows],
+def join(device, own, other):
+    members, rows, width = own.shape
+    return call(
+        join_kernel, [((2 * members * (rows - TAIL), width), B16), ((ROWS, width), F32)], [], [device], [own, other],
         own.size, 8 * own.size,
     )
 
@@ -418,20 +452,6 @@
 
 def swap(block):
     return lax.ppermute(block, "c", SWAP)
-
-
-def owners(sizes):
-    count = math.prod(sizes.values())
-    pairs = []
-    for source in range(count):
-        rest, at = source, {}
-        for axis in reversed(EVERY):
-            rest, at[axis] = divmod(rest, sizes[axis])
-        target = 0
-        for axis in ("c",) + CUBE + LINE + PLANE:
-            target = target * sizes[axis] + at[axis]
-        pairs.append((source, target))
-    return pairs
 
 
 def body(
@@ -443,7 +463,7 @@
     low, high = edges(rows)
     low, high = from_left(high), from_right(low)
     upstream = cotangent[0].reshape(-1, channels)
-    core = lax.axis_index("c").astype(jnp.int32).reshape(1)
+    device = lax.axis_index(EVERY).astype(jnp.int32).reshape(1)
     sizes = {axis: lax.axis_size(axis) for axis in EVERY}
     cube, line, plane = (math.prod(sizes[axis] for axis in axes) for axes in (CUBE, LINE, PLANE))
     scale = 1.0 / math.sqrt(height * breadth * math.prod(sizes.values()))
@@ -452,7 +472,7 @@
         tissue, rows, upstream, kernel, conv_bias, ln_gain, ln_bias, w_in, b_in, w_out, layer_scale
     )
     kept, sent, grad_conv, low, high = middle(
-        core, conv, low, high, taps, vectors, w_in_t, b_cols, out_grad, back, w_in_here
+        device, conv, low, high, taps, vectors, w_in_t, b_cols, out_grad, back, w_in_here
     )
     message = to_cube(cube, kept, swap(sent))
     received = exchange(message, CUBE)
@@ -460,14 +480,12 @@
     received, low, high = lax.optimization_barrier((received, low, high))
     received = exchange(to_line(received, line), LINE)
     received = exchange(to_plane(received, plane), PLANE)
-    message, in_rows = turn(scale, received, line)
-    received = exchange(message, LINE)
-    received, in_rows, low, high = lax.optimization_barrier((received, in_rows, low, high))
-    own = exchange(unpack(received, cube), CUBE).reshape(-1, channels)
-    in_rows = lax.ppermute(in_rows, EVERY, owners(sizes))
+    received = exchange(turn(scale, received, line), LINE)
+    received, low, high = lax.optimization_barrier((received, low, high))
+    own = exchange(unpack(received, cube), CUBE)
     grad_image = to_features(grad_conv, low, high, taps, upstream)
-    own, in_rows, grad_image = lax.optimization_barrier((own, in_rows, grad_image))
-    grad_w_out, grad_w_in = join(core, own, swap(own), in_rows)
+    own, grad_image = lax.optimization_barrier((own, grad_image))
+    grad_w_out, grad_w_in = join(device, own, swap(own))
     return (grad_image.reshape(1, height, breadth, channels), grad_w_in, grad_w_out)
 
 

time: 120 us -> 118 us (0.983)
  the two profiles are of different devices: /device:TPU:41 before, /device:TPU:1 now
where the time goes in v8:
time: 118 us; the launch traced here: 117 us
  blocking collectives  45.1 us (38%)
  starting transfers between devices  33.5 us (28%)
  waiting for transfers between devices  22.3 us (19%)
  Pallas kernels  15.6 us (13%)
    all_to_all x3, blocking collectives, exchange(): return lax.all_to_all(blocks, axes, split_axis=0, concat_axis=0, tiled=True)  45.1 us
    ppermute x2, starting transfers between devices, swap(): return lax.ppermute(block, 'c', SWAP)  15.6 us
    pallas_call x10, Pallas kernels, call(): pl.pallas_call(kernel, out_shape=[jax.ShapeDtypeStruct(shape, kind) for s...  15.6 us
    ppermute x2, waiting for transfers between devices, from_left(): return lax.ppermute(block, TILE, [(i, i + 1) for i in range(count - 1)])  10.2 us
    all_to_all x2, starting transfers between devices, exchange(): return lax.all_to_all(blocks, axes, split_axis=0, concat_axis=0, tiled=True)  7.83 us
    ppermute x2, starting transfers between devices, from_left(): return lax.ppermute(block, TILE, [(i, i + 1) for i in range(count - 1)])  7.53 us
    all_to_all x2, waiting for transfers between devices, exchange(): return lax.all_to_all(blocks, axes, split_axis=0, concat_axis=0, tiled=True)  7.4 us
    ppermute x2, waiting for transfers between devices, swap(): return lax.ppermute(block, 'c', SWAP)  4.2 us
  transfers between devices with their start and end apart: 8, of which 6 were waited for; matrix products, arithmetic and copies ran while one was open for 0% of the time, Pallas kernels for 6%

profile of v8, /device:TPU:1, one launch (start us, length us, event | category | flops | bytes accessed | tf_op | source)
XLA Modules:
  0.0 117.3 jit_solution(16135227430289307392)
XLA Ops:
  0.6 1.0 shard_map.131
  1.6 4.0 %collective-permute-start = (bf16[32,384]{1,0:T(8,128)(2,1)S(1)}, bf16[32,384]{1,0:T(8,128)(2,1)S(1)}, u32[]{:S(2)}, u32[]{:S(2)}) collective-permute-start(bf16[32,384]{1,0:T(8,128)(2,1)S(1)} %get-tuple-element.29), channel_id=1, source_target_pairs={{0,4},{4,8},{8,12},{12,16},{16,20},{20,24},{24,28},{28,32},{32,36}... | collective-permute-start | bytes 73736 | tf_op jit(solution)/shard_map/ppermute | solution.py:441
  5.7 1.3 %collective-permute-start.1 = (bf16[32,384]{1,0:T(8,128)(2,1)S(1)}, bf16[32,384]{1,0:T(8,128)(2,1)S(1)}, u32[]{:S(2)}, u32[]{:S(2)}) collective-permute-start(bf16[32,384]{1,0:T(8,128)(2,1)S(1)} %get-tuple-element.30), channel_id=1, source_target_pairs={{4,0},{8,4},{12,8},{16,12},{20,16},{24,20},{28,24},{32,28},{36,32}... | collective-permute-start | bytes 73736 | tf_op jit(solution)/shard_map/ppermute | solution.py:446
  7.0 4.4 %shard_map.130 = (f32[256,384]{1,0:T(8,128)S(1)}, bf16[256,384]{1,0:T(8,128)(2,1)S(1)}, f32[1536,256]{1,0:T(8,128)S(1)}, bf16[1536,384]{1,0:T(8,128)(2,1)S(1)}, ...) custom-call(s32[1,4]{1,0:T(1,128)} %flags.1, ...), custom_call_target="tpu_custom_call" | custom-call | flops 301989888 | bytes 8388608 | tf_op jit(solution)/shard_map/pallas_call | solution.py:315
  11.4 0.0 collective-permute-done.low
  11.4 0.0 collective-permute-done.1.high
  11.4 4.2 %shard_map.132 = (f32[1536,384]{1,0:T(8,128)S(1)}, bf16[1536,384]{1,0:T(8,128)(2,1)S(1)}, f32[256,384]{1,0:T(8,128)S(1)}, f32[24,384]{1,0:T(8,128)S(1)}, f32[24,384]{1,0:T(8,128)S(1)}) custom-call(s32[1]{0:T(128)} %bitcast.device, f32[256,384]{1,0:T(8,128)S(1)} %get-tuple-element.28.conv, bf16[32,384]{1,0:T(8,128)(2,1)S(1)} %collective-permute-done.low, ...), custom_call_target="tpu_custom_call" | custom-call | flops 1207959552 | bytes 12582912 | tf_op jit(solution)/shard_map/pallas_call | solution.py:315
  15.6 6.0 %collective-permute-start.2 = (bf16[1536,384]{1,0:T(8,128)(2,1)S(1)}, bf16[1536,384]{1,0:T(8,128)(2,1)S(1)}, u32[]{:S(2)}, u32[]{:S(2)}) collective-permute-start(bf16[1536,384]{1,0:T(8,128)(2,1)S(1)} %get-tuple-element.39), channel_id=1, source_target_pairs={{0,1},{1,0},{2,3},{3,2},{4,5},{5,4},{6,7},{7,6},{8,9},{9,8},{10,11... | collective-permute-start | bytes 3538952 | tf_op jit(solution)/shard_map/ppermute | solution.py:454
  21.7 2.5 %collective-permute-done.2.received = bf16[1536,384]{1,0:T(8,128)(2,1)S(1)} collective-permute-done((bf16[1536,384]{1,0:T(8,128)(2,1)S(1)}, bf16[1536,384]{1,0:T(8,128)(2,1)S(1)}, u32[]{:S(2)}, u32[]{:S(2)}) %collective-permute-start.2) | collective-permute-done | bytes 1179680 | tf_op jit(solution)/shard_map/ppermute | solution.py:454
  24.1 1.3 %shard_map.133 = bf16[8,192,384]{2,1,0:T(8,128)(2,1)} custom-call(f32[1536,384]{1,0:T(8,128)S(1)} %get-tuple-element.38.kept, bf16[1536,384]{1,0:T(8,128)(2,1)S(1)} %collective-permute-done.2.received), custom_call_target="tpu_custom_call" | custom-call | flops 1179648 | bytes 4718592 | tf_op jit(solution)/shard_map/pallas_call | solution.py:315
  25.4 4.3 %all-to-all-start = ((bf16[8,192,384]{2,1,0:T(8,128)(2,1)}), bf16[8,192,384]{2,1,0:T(8,128)(2,1)S(1)}, u32[]{:S(2)}, u32[]{:S(2)}) async-start(bf16[8,192,384]{2,1,0:T(8,128)(2,1)} %shard_map.133), calls=%async_computation | async-start | bytes 2359296 | tf_op jit(solution)/shard_map/all_to_all | solution.py:450
  29.7 3.5 %collective-permute-start.3 = (f32[24,384]{1,0:T(8,128)S(1)}, f32[24,384]{1,0:T(8,128)S(1)}, u32[]{:S(2)}, u32[]{:S(2)}) collective-permute-start(f32[24,384]{1,0:T(8,128)S(1)} %get-tuple-element.40), channel_id=1, source_target_pairs={{0,4},{4,8},{8,12},{12,16},{16,20},{20,24},{24,28},{28,32},{32,36}... | collective-permute-start | bytes 110600 | tf_op jit(solution)/shard_map/ppermute | solution.py:441
  33.2 1.3 %collective-permute-start.4 = (f32[24,384]{1,0:T(8,128)S(1)}, f32[24,384]{1,0:T(8,128)S(1)}, u32[]{:S(2)}, u32[]{:S(2)}) collective-permute-start(f32[24,384]{1,0:T(8,128)S(1)} %get-tuple-element.41), channel_id=1, source_target_pairs={{4,0},{8,4},{12,8},{16,12},{20,16},{24,20},{28,24},{32,28},{36,32}... | collective-permute-start | bytes 110600 | tf_op jit(solution)/shard_map/ppermute | solution.py:446
  34.5 10.2 %collective-permute-done.3.low = f32[24,384]{1,0:T(8,128)S(1)} collective-permute-done((f32[24,384]{1,0:T(8,128)S(1)}, f32[24,384]{1,0:T(8,128)S(1)}, u32[]{:S(2)}, u32[]{:S(2)}) %collective-permute-start.3) | collective-permute-done | bytes 36896 | tf_op jit(solution)/shard_map/ppermute | solution.py:441
  44.7 0.6 collective-permute-done.4.high
  45.3 1.5 %all-to-all-done.received = bf16[8,192,384]{2,1,0:T(8,128)(2,1)S(1)} async-done(((bf16[8,192,384]{2,1,0:T(8,128)(2,1)}), bf16[8,192,384]{2,1,0:T(8,128)(2,1)S(1)}, u32[]{:S(2)}, u32[]{:S(2)}) %all-to-all-start) | async-done | bytes 1179680 | tf_op jit(solution)/shard_map/all_to_all | solution.py:450
  46.8 0.2 shard_map.134
  47.1 22.0 %all_to_all.25.received = bf16[4,48,384]{2,1,0:T(8,128)(2,1)S(1)} all-to-all(bf16[4,48,384]{2,1,0:T(8,128)(2,1)S(1)} %shard_map.134), channel_id=1, replica_groups=mesh['zh'=4,'xh'=2,'xl'=2,'yh'=4,'yl'=2,'zl'=2,'c'=2] {'zh'}, dimensions={0} | all-to-all | bytes 294912 | tf_op jit(solution)/shard_map/all_to_all | solution.py:450
  69.1 0.1 shard_map.135
  69.1 13.6 %all_to_all.26.received = bf16[8,32,384]{2,1,0:T(8,128)(2,1)S(1)} all-to-all(bf16[8,32,384]{2,1,0:T(8,128)(2,1)S(1)} %shard_map.135), channel_id=1, replica_groups=mesh['zh'=4,'xh'=2,'xl'=2,'yh'=4,'yl'=2,'zl'=2,'c'=2] {'xh','yh'}, dimensions={0} | all-to-all | bytes 393216 | tf_op jit(solution)/shard_map/all_to_all | solution.py:450
  82.8 0.0 copy-start
  82.8 9.6 %all_to_all.27.received = bf16[4,32,384]{2,1,0:T(8,128)(2,1)S(1)} all-to-all(bf16[4,32,384]{2,1,0:T(8,128)(2,1)S(1)} %shard_map.136), channel_id=1, replica_groups=mesh['zh'=4,'xh'=2,'xl'=2,'yh'=4,'yl'=2,'zl'=2,'c'=2] {'zh'}, dimensions={0} | all-to-all | bytes 196608 | tf_op jit(solution)/shard_map/all_to_all | solution.py:450
  92.3 0.9 shard_map.137
  93.3 3.5 %all-to-all-start.4 = ((bf16[8,112,384]{2,1,0:T(8,128)(2,1)}), bf16[8,112,384]{2,1,0:T(8,128)(2,1)S(1)}, u32[]{:S(2)}, u32[]{:S(2)}) async-start(bf16[8,112,384]{2,1,0:T(8,128)(2,1)} %shard_map.137), calls=%async_computation.4 | async-start | bytes 1376256 | tf_op jit(solution)/shard_map/all_to_all | solution.py:450
  96.8 0.0 copy-done
  96.8 2.3 %shard_map.138 = bf16[256,384]{1,0:T(8,128)(2,1)} custom-call(f32[256,384]{1,0:T(8,128)S(1)} %get-tuple-element.46.grad_conv, f32[24,384]{1,0:T(8,128)S(1)} %collective-permute-done.3.low, f32[24,384]{1,0:T(8,128)S(1)} %collective-permute-done.4.high, f32[7,7,384]{2,1,0:T(8,128)S(1)} %get-tuple-element.31.taps, bf16[256,384]{1,0:T(8,128)(2,1)S(1)} %bitcast.5), custom_call_target="tpu_custom_call" | custom-call | flops 9633792 | bytes 2097152 | tf_op jit(solution)/shard_map/pallas_call | solution.py:315
  99.1 5.8 %all-to-all-done.4.own = bf16[8,112,384]{2,1,0:T(8,128)(2,1)S(1)} async-done(((bf16[8,112,384]{2,1,0:T(8,128)(2,1)}), bf16[8,112,384]{2,1,0:T(8,128)(2,1)S(1)}, u32[]{:S(2)}, u32[]{:S(2)}) %all-to-all-start.4) | async-done | bytes 688160 | tf_op jit(solution)/shard_map/all_to_all | solution.py:450
  104.9 9.5 %collective-permute-start.5 = (bf16[8,112,384]{2,1,0:T(8,128)(2,1)S(1)}, bf16[8,112,384]{2,1,0:T(8,128)(2,1)S(1)}, u32[]{:S(2)}, u32[]{:S(2)}) collective-permute-start(bf16[8,112,384]{2,1,0:T(8,128)(2,1)S(1)} %all-to-all-done.4.own), channel_id=1, source_target_pairs={{0,1},{1,0},{2,3},{3,2},{4,5},{5,4},{6,7},{7,6},{8,9},{9,8},{10,11... | collective-permute-start | bytes 2064392 | tf_op jit(solution)/shard_map/ppermute | solution.py:454
  114.5 1.7 %collective-permute-done.5.other = bf16[8,112,384]{2,1,0:T(8,128)(2,1)S(1)} collective-permute-done((bf16[8,112,384]{2,1,0:T(8,128)(2,1)S(1)}, bf16[8,112,384]{2,1,0:T(8,128)(2,1)S(1)}, u32[]{:S(2)}, u32[]{:S(2)}) %collective-permute-start.5) | collective-permute-done | bytes 688160 | tf_op jit(solution)/shard_map/ppermute | solution.py:454
  116.2 1.1 shard_map.139
  (1 shorter events, 0.0 us)
Async XLA Ops:
  1.6 9.8 %collective-permute-start = (bf16[32,384]{1,0:T(8,128)(2,1)S(1)}, bf16[32,384]{1,0:T(8,128)(2,1)S(1)}, u32[]{:S(2)}, u32[]{:S(2)}) collective-permute-start(bf16[32,384]{1,0:T(8,128)(2,1)S(1)} %get-tuple-element.29), channel_id=1, source_target_pairs={{0,4},{4,8},{8,12},{12,16},{16,20},{20,24},{24,28},{28,32},{32,36}... | collective-permute-start | bytes 73736 | tf_op jit(solution)/shard_map/ppermute | solution.py:441
  5.7 5.7 %collective-permute-start.1 = (bf16[32,384]{1,0:T(8,128)(2,1)S(1)}, bf16[32,384]{1,0:T(8,128)(2,1)S(1)}, u32[]{:S(2)}, u32[]{:S(2)}) collective-permute-start(bf16[32,384]{1,0:T(8,128)(2,1)S(1)} %get-tuple-element.30), channel_id=1, source_target_pairs={{4,0},{8,4},{12,8},{16,12},{20,16},{24,20},{28,24},{32,28},{36,32}... | collective-permute-start | bytes 73736 | tf_op jit(solution)/shard_map/ppermute | solution.py:446
  15.6 8.5 %collective-permute-start.2 = (bf16[1536,384]{1,0:T(8,128)(2,1)S(1)}, bf16[1536,384]{1,0:T(8,128)(2,1)S(1)}, u32[]{:S(2)}, u32[]{:S(2)}) collective-permute-start(bf16[1536,384]{1,0:T(8,128)(2,1)S(1)} %get-tuple-element.39), channel_id=1, source_target_pairs={{0,1},{1,0},{2,3},{3,2},{4,5},{5,4},{6,7},{7,6},{8,9},{9,8},{10,11... | collective-permute-start | bytes 3538952 | tf_op jit(solution)/shard_map/ppermute | solution.py:454
  25.4 21.4 %all-to-all-start = ((bf16[8,192,384]{2,1,0:T(8,128)(2,1)}), bf16[8,192,384]{2,1,0:T(8,128)(2,1)S(1)}, u32[]{:S(2)}, u32[]{:S(2)}) async-start(bf16[8,192,384]{2,1,0:T(8,128)(2,1)} %shard_map.133), calls=%async_computation | async-start | bytes 2359296 | tf_op jit(solution)/shard_map/all_to_all | solution.py:450
  29.7 15.0 %collective-permute-start.3 = (f32[24,384]{1,0:T(8,128)S(1)}, f32[24,384]{1,0:T(8,128)S(1)}, u32[]{:S(2)}, u32[]{:S(2)}) collective-permute-start(f32[24,384]{1,0:T(8,128)S(1)} %get-tuple-element.40), channel_id=1, source_target_pairs={{0,4},{4,8},{8,12},{12,16},{16,20},{20,24},{24,28},{28,32},{32,36}... | collective-permute-start | bytes 110600 | tf_op jit(solution)/shard_map/ppermute | solution.py:441
  33.2 12.0 %collective-permute-start.4 = (f32[24,384]{1,0:T(8,128)S(1)}, f32[24,384]{1,0:T(8,128)S(1)}, u32[]{:S(2)}, u32[]{:S(2)}) collective-permute-start(f32[24,384]{1,0:T(8,128)S(1)} %get-tuple-element.41), channel_id=1, source_target_pairs={{4,0},{8,4},{12,8},{16,12},{20,16},{24,20},{28,24},{32,28},{36,32}... | collective-permute-start | bytes 110600 | tf_op jit(solution)/shard_map/ppermute | solution.py:446
  82.8 14.0 %copy-start = (bf16[1,8,32,384]{3,2,1,0:T(8,128)(2,1)S(1)}, bf16[1,8,32,384]{3,2,1,0:T(8,128)(2,1)}, u32[]{:S(2)}) copy-start(bf16[1,8,32,384]{3,2,1,0:T(8,128)(2,1)} %param.12) | copy-start | bytes 589828
  93.3 11.7 %all-to-all-start.4 = ((bf16[8,112,384]{2,1,0:T(8,128)(2,1)}), bf16[8,112,384]{2,1,0:T(8,128)(2,1)S(1)}, u32[]{:S(2)}, u32[]{:S(2)}) async-start(bf16[8,112,384]{2,1,0:T(8,128)(2,1)} %shard_map.137), calls=%async_computation.4 | async-start | bytes 1376256 | tf_op jit(solution)/shard_map/all_to_all | solution.py:450
  104.9 11.3 %collective-permute-start.5 = (bf16[8,112,384]{2,1,0:T(8,128)(2,1)S(1)}, bf16[8,112,384]{2,1,0:T(8,128)(2,1)S(1)}, u32[]{:S(2)}, u32[]{:S(2)}) collective-permute-start(bf16[8,112,384]{2,1,0:T(8,128)(2,1)S(1)} %all-to-all-done.4.own), channel_id=1, source_target_pairs={{0,1},{1,0},{2,3},{3,2},{4,5},{5,4},{6,7},{7,6},{8,9},{9,8},{10,11... | collective-permute-start | bytes 2064392 | tf_op jit(solution)/shard_map/ppermute | solution.py:454

commit v9 on v8

--- a/solution.py
+++ b/solution.py
@@ -73,21 +73,9 @@
         wide[k] = source[:, lanes].astype(jnp.float32)
 
 
-def edge_kernel(features, low, high, image, wide, sem):
-    copy = pltpu.make_async_copy(features, image, sem)
-    copy.start()
-    copy.wait()
-    widen(image, wide)
-    count = EDGE // SIDE
-    for k, lanes in enumerate(lane_blocks(features.shape[1])):
-        for first, edge in ((0, low), (COLS - count, high)):
-            columns = [wide[k, pl.ds(first + j, SIDE, stride=COLS), :] for j in range(count)]
-            edge[:, lanes] = jnp.concatenate(columns, axis=0).astype(jnp.bfloat16)
-
-
 def first_kernel(
     flags, features, cotangent, w_out, w_in, b_in, taps, scale, conv_bias, gain, bias,
-    conv, out_grad, back, w_in_t, b_cols, w_in_here, taps_here, vectors,
+    low_edge, high_edge, conv, out_grad, back, w_in_t, b_cols, w_in_here, taps_here, vectors,
     wide, flags_here, image, upstream, w_out_here, b_here, scale_here, conv_bias_here, gain_here, bias_here, sems
 ):
     width = features.shape[1]
@@ -117,7 +105,11 @@
     copies[4].wait()
     copies[5].wait()
     widen(image, wide)
+    count = EDGE // SIDE
     for k, lanes in enumerate(lane_blocks(width)):
+        for first, edge in ((0, low_edge), (COLS - count, high_edge)):
+            columns = [wide[k, pl.ds(first + j, SIDE, stride=COLS), :] for j in range(count)]
+            edge[:, lanes] = jnp.concatenate(columns, axis=0).astype(jnp.bfloat16)
         for t in range(COLS // SIDE):
             columns = []
             for j in range(t * SIDE - HALO, (t + 1) * SIDE + HALO):
@@ -141,9 +133,9 @@
 
 
 def middle_kernel(
-    device, conv, low, high, taps, vectors, w_in_t, b_cols, out_grad, back, w_in,
-    kept, sent, grad_conv, low_edge, high_edge,
-    rows, low_wide, high_wide, standard, normed, preact, hidden, grad_pre
+    device, conv, low, high, taps, vectors, w_in_t, b_cols, out_grad, back,
+    kept, sent, standard, inverse, grad_pre,
+    rows, low_wide, high_wide, normed, preact, hidden
 ):
     width = conv.shape[1]
     rows[...] = conv[...]
@@ -160,8 +152,9 @@
     gain, bias = vectors[SIDE : SIDE + 1, :], vectors[2 * SIDE : 2 * SIDE + 1, :]
     conv_out = rows[...] + vectors[:1, :]
     centre = conv_out - jnp.mean(conv_out, axis=-1, keepdims=True)
-    inverse = lax.rsqrt(jnp.mean(centre * centre, axis=-1, keepdims=True) + EPSILON)
-    standard[...] = centre * inverse
+    scale = lax.rsqrt(jnp.mean(centre * centre, axis=-1, keepdims=True) + EPSILON)
+    inverse[...] = jnp.broadcast_to(scale, inverse.shape)
+    standard[...] = centre * scale
     normed[...] = (standard[...] * gain + bias).astype(jnp.bfloat16)
     preact[...] = matmul(w_in_t[...], normed[...], NT)
 
@@ -185,11 +178,14 @@
     sent[half:, :] = matmul(grad_pre[other, :], normed[...]).astype(jnp.bfloat16)
     kept[:half, :] = matmul(hidden[own, :], out_grad[...])
     kept[half:, :] = matmul(grad_pre[own, :], normed[...])
-    grad_std = matmul(w_in[...], grad_pre[...]).T * gain
+
+
+def back_kernel(grad_pre, w_in, standard, inverse, vectors, grad_conv, low_edge, high_edge):
+    grad_std = matmul(w_in[...], grad_pre[...]).T * vectors[SIDE : SIDE + 1, :]
     norm = standard[...]
     mean = jnp.mean(grad_std, axis=-1, keepdims=True)
     along = jnp.mean(grad_std * norm, axis=-1, keepdims=True)
-    result = inverse * (grad_std - mean - norm * along)
+    result = inverse[:, :1] * (grad_std - mean - norm * along)
     grad_conv[...] = result
     edge = HALO * SIDE
     low_edge[...] = result[:edge, :]
@@ -241,51 +237,49 @@
     return summed
 
 
-def line_kernel(received, message, total):
+def plane_kernel(received, message, total):
     members, rows, width = message.shape
     rows //= 2
     summed = add_members(received)
     for k, lanes in enumerate(lane_blocks(width)):
         total[k] = summed[:, lanes]
         for m in range(members):
-            parts = [total[k, m * rows : (m + 1) * rows, :]]
-            for r in range(ROWS):
-                start = members * rows + m * ROWS + r
-                parts.append(total[k, pl.ds(start, SIDE, stride=members * ROWS), :])
+            start = (members + m) * rows
+            parts = [total[k, pl.ds(m, rows, stride=members), :], total[k, start : start + rows, :]]
             message[m, :, lanes] = jnp.concatenate(parts, axis=0).astype(jnp.bfloat16)
 
 
-def plane_kernel(received, message, total, block):
-    rows = received.shape[1] // 2
-    members = message.shape[0]
-    summed = add_members(received)
-    for k, lanes in enumerate(lane_blocks(received.shape[2])):
-        total[k] = summed[:, lanes]
+def line_kernel(received, message):
+    summed = add_members(received).astype(jnp.bfloat16)
+    for m in range(message.shape[0]):
+        message[m] = summed
+
+
+def turn_kernel(scale, received, message, in_rows, block):
+    finished = add_members(received) * scale
+    rows = finished.shape[0] // 2
     block[...] = jnp.zeros_like(block)
+    block[:rows, :] = finished[:rows, :]
+    in_rows[...] = jnp.zeros_like(in_rows)
+    in_rows[:rows, :] = finished[rows:, :]
+    whole = block[...].astype(jnp.bfloat16)
+    for m in range(message.shape[0]):
+        message[m] = whole
+
+
+def unpack_kernel(received, in_rows, message, spread, block):
+    members, _, width = received.shape
+    rows = 4 * ROWS
+    count = members * rows
+    block[count:, :] = jnp.zeros_like(block[count:, :])
     for m in range(members):
-        for k, lanes in enumerate(lane_blocks(received.shape[2])):
-            block[:rows, lanes] = total[k, :rows, :]
-            block[rows : rows + ROWS, lanes] = total[k, pl.ds(rows + m, ROWS, stride=members), :]
-        message[m] = block[...].astype(jnp.bfloat16)
-
-
-def turn_kernel(scale, received, message):
-    finished = (add_members(received) * scale).astype(jnp.bfloat16)
-    for m in range(message.shape[0]):
-        message[m] = finished
-
-
-def unpack_kernel(received, message, block):
-    rows = received.shape[1] - SIDE
-    count = received.shape[0] * rows
-    parts = [received[m].astype(jnp.float32) for m in range(received.shape[0])]
-    block[count:, :] = jnp.zeros_like(block[count:, :])
-    for m, part in enumerate(parts):
-        block[m * rows : (m + 1) * rows, :] = part[:rows, :]
+        part = received[m].astype(jnp.float32)
+        for k, lanes in enumerate(lane_blocks(width)):
+            spread[k, pl.ds(m, rows, stride=members), :] = part[:rows, lanes]
+    for k, lanes in enumerate(lane_blocks(width)):
+        block[:count, lanes] = spread[k]
     for bit1 in range(2):
-        for bit0 in range(2):
-            start = count + bit0 * ROWS
-            block[start : start + ROWS, :] = parts[2 * bit1 + bit0][rows : rows + ROWS, :]
+        block[count : count + 2 * ROWS, :] = in_rows[bit1 * 2 * ROWS : (bit1 + 1) * 2 * ROWS, :]
         whole = block[...].astype(jnp.bfloat16)
         for m in range(bit1, message.shape[0], 2):
             message[m] = whole
@@ -326,24 +320,12 @@
 F32, B16 = jnp.float32, jnp.bfloat16
 
 
-def edges(features):
-    rows, width = features.shape
-    return call(
-        edge_kernel,
-        [((EDGE, width), B16), ((EDGE, width), B16)],
-        [pltpu.VMEM((rows, width), B16), pltpu.VMEM((width // LANES, rows, LANES), F32), pltpu.SemaphoreType.DMA],
-        [],
-        [features],
-        features.size, 2 * features.size, pltpu.HBM,
-    )
-
-
 def before_halos(flags, features, cotangent, kernel, conv_bias, gain, bias, w_in, b_in, w_out, layer_scale):
     rows, width = features.shape
     hidden = w_out.shape[0]
     return call(
         first_kernel,
-        [((rows, width), F32), ((rows, width), B16), ((hidden, rows), F32), ((hidden, width), B16),
+        [((EDGE, width), B16), ((EDGE, width), B16), ((rows, width), F32), ((rows, width), B16), ((hidden, rows), F32), ((hidden, width), B16),
          ((hidden, LANES), F32), (w_in.shape, B16), (kernel.shape, F32), ((3 * SIDE, width), F32)],
         [pltpu.VMEM((width // LANES, rows, LANES), F32), pltpu.SMEM(flags.shape, jnp.int32),
          pltpu.VMEM((rows, width), B16), pltpu.VMEM((rows, width), B16), pltpu.VMEM(w_out.shape, B16),
@@ -356,18 +338,28 @@
     )
 
 
-def middle(device, conv, low, high, taps, vectors, w_in_t, b_cols, out_grad, back, w_in):
+def middle(device, conv, low, high, taps, vectors, w_in_t, b_cols, out_grad, back):
     rows, width = conv.shape
     hidden = w_in_t.shape[0]
-    halo, edge = pltpu.VMEM((EDGE, width), F32), (HALO * SIDE, width)
+    halo = pltpu.VMEM((EDGE, width), F32)
     return call(
         middle_kernel,
-        [((hidden, width), F32), ((hidden, width), B16), ((rows, width), F32), (edge, F32), (edge, F32)],
-        [pltpu.VMEM((rows, width), F32), halo, halo, pltpu.VMEM((rows, width), F32), pltpu.VMEM((rows, width), B16),
-         pltpu.VMEM((hidden, rows), F32), pltpu.VMEM((hidden, rows), B16), pltpu.VMEM((hidden, rows), B16)],
+        [((hidden, width), F32), ((hidden, width), B16), ((rows, width), F32), ((rows, LANES), F32), ((hidden, rows), B16)],
+        [pltpu.VMEM((rows, width), F32), halo, halo, pltpu.VMEM((rows, width), B16),
+         pltpu.VMEM((hidden, rows), F32), pltpu.VMEM((hidden, rows), B16)],
         [device],
-        [conv, low, high, taps, vectors, w_in_t, b_cols, out_grad, back, w_in],
-        8 * rows * width * hidden, 12 * 1024 * 1024,
+        [conv, low, high, taps, vectors, w_in_t, b_cols, out_grad, back],
+        6 * rows * width * hidden, 12 * 1024 * 1024,
+    )
+
+
+def to_conv(grad_pre, w_in, standard, inverse, vectors):
+    rows, width = standard.shape
+    edge = (HALO * SIDE, width)
+    return call(
+        back_kernel, [((rows, width), F32), (edge, F32), (edge, F32)], [], [],
+        [grad_pre, w_in, standard, inverse, vectors],
+        2 * grad_pre.size * width, 4 * grad_pre.size,
     )
 
 
@@ -390,40 +382,37 @@
     )[0]
 
 
-def to_line(received, members):
+def to_plane(received, members):
     _, rows, width = received.shape
     return call(
-        line_kernel, [((members, rows // members, width), B16)],
+        plane_kernel, [((members, rows // members, width), B16)],
         [pltpu.VMEM((width // LANES, rows, LANES), F32)], [], [received],
         received.size, 3 * received.size,
     )[0]
 
 
-def to_plane(received, members):
+def to_line(received, members):
     _, rows, width = received.shape
     return call(
-        plane_kernel,
-        [((members, rows // 2 + SIDE, width), B16)],
-        [pltpu.VMEM((width // LANES, rows, LANES), F32), pltpu.VMEM((rows // 2 + SIDE, width), F32)],
-        [],
-        [received],
-        received.size, 4 * received.size,
+        line_kernel, [((members, rows, width), B16)], [], [], [received], received.size, 4 * received.size
     )[0]
 
 
 def turn(scale, received, members):
-    _, rows, width = received.shape
-    return call(
-        functools.partial(turn_kernel, scale), [((members, rows, width), B16)], [], [], [received],
-        received.size, 4 * received.size,
-    )[0]
-
-
-def unpack(received, members):
-    count, rows, width = received.shape
-    rows = count * (rows - SIDE) + TAIL
-    return call(
-        unpack_kernel, [((members, rows, width), B16)], [pltpu.VMEM((rows, width), F32)], [], [received],
+    width = received.shape[2]
+    return call(
+        functools.partial(turn_kernel, scale),
+        [((members, 16, width), B16), ((16, width), F32)], [pltpu.VMEM((16, width), F32)], [], [received],
+        received.size, 6 * received.size,
+    )
+
+
+def unpack(received, in_rows, members):
+    count, _, width = received.shape
+    count *= 4 * ROWS
+    return call(
+        unpack_kernel, [((members, count + TAIL, width), B16)],
+        [pltpu.VMEM((width // LANES, count, LANES), F32), pltpu.VMEM((count + TAIL, width), F32)], [], [received, in_rows],
         received.size, 10 * received.size,
     )[0]
 
@@ -460,29 +449,31 @@
     image = features[0]
     height, breadth, channels = image.shape
     rows = image.reshape(-1, channels)
-    low, high = edges(rows)
-    low, high = from_left(high), from_right(low)
     upstream = cotangent[0].reshape(-1, channels)
     device = lax.axis_index(EVERY).astype(jnp.int32).reshape(1)
     sizes = {axis: lax.axis_size(axis) for axis in EVERY}
     cube, line, plane = (math.prod(sizes[axis] for axis in axes) for axes in (CUBE, LINE, PLANE))
     scale = 1.0 / math.sqrt(height * breadth * math.prod(sizes.values()))
 
-    conv, out_grad, back, w_in_t, b_cols, w_in_here, taps, vectors = before_halos(
+    device, rows = lax.optimization_barrier((device, rows))
+    low, high, conv, out_grad, back, w_in_t, b_cols, w_in_here, taps, vectors = before_halos(
         tissue, rows, upstream, kernel, conv_bias, ln_gain, ln_bias, w_in, b_in, w_out, layer_scale
     )
-    kept, sent, grad_conv, low, high = middle(
-        device, conv, low, high, taps, vectors, w_in_t, b_cols, out_grad, back, w_in_here
-    )
-    message = to_cube(cube, kept, swap(sent))
-    received = exchange(message, CUBE)
+    low, high = from_left(high), from_right(low)
+    kept, sent, standard, inverse, grad_pre = middle(
+        device, conv, low, high, taps, vectors, w_in_t, b_cols, out_grad, back
+    )
+    grad_conv, low, high = to_conv(grad_pre, w_in_here, standard, inverse, vectors)
+    kept, low, high = lax.optimization_barrier((kept, low, high))
+    received = exchange(to_cube(cube, kept, swap(sent)), CUBE)
     low, high = from_left(high), from_right(low)
     received, low, high = lax.optimization_barrier((received, low, high))
+    received = exchange(to_plane(received, plane), PLANE)
     received = exchange(to_line(received, line), LINE)
-    received = exchange(to_plane(received, plane), PLANE)
-    received = exchange(turn(scale, received, line), LINE)
+    message, in_rows = turn(scale, received, plane)
+    received = exchange(message, PLANE)
     received, low, high = lax.optimization_barrier((received, low, high))
-    own = exchange(unpack(received, cube), CUBE)
+    own = exchange(unpack(received, in_rows, cube), CUBE)
     grad_image = to_features(grad_conv, low, high, taps, upstream)
     own, grad_image = lax.optimization_barrier((own, grad_image))
     grad_w_out, grad_w_in = join(device, own, swap(own))

time: 118 us -> 122 us (1.034)
  waiting for transfers between devices: 22.3 us -> 26.6 us
    ppermute x2, waiting for transfers between devices: 0.57 us -> 3.3 us  [from_right(): return lax.ppermute(block, TILE, [(i + 1, i) for i in range(count - 1)])]
    all_to_all x2, waiting for transfers between devices: 7.4 us -> 8.79 us  [exchange(): return lax.all_to_all(blocks, axes, split_axis=0, concat_axis=0, tiled=True)]
  transfers between devices with their start and end apart: 8 -> 8, of which waited for: 6 -> 6; matrix products, arithmetic and copies ran while one was open for 0% -> 0% of each run, Pallas kernels for 6% -> 2%
where the time goes in v9:
time: 122 us
  blocking collectives  45.8 us (38%)
  starting transfers between devices  33.7 us (28%)
  waiting for transfers between devices  26.6 us (22%)
  Pallas kernels  14.7 us (12%)
    all_to_all x3, blocking collectives, exchange(): return lax.all_to_all(blocks, axes, split_axis=0, concat_axis=0, tiled=True)  45.8 us
    ppermute x2, starting transfers between devices, swap(): return lax.ppermute(block, 'c', SWAP)  16.2 us
    pallas_call x10, Pallas kernels, call(): pl.pallas_call(kernel, out_shape=[jax.ShapeDtypeStruct(shape, kind) for s...  14.7 us
    ppermute x2, waiting for transfers between devices, from_left(): return lax.ppermute(block, TILE, [(i, i + 1) for i in range(count - 1)])  11 us
    all_to_all x2, waiting for transfers between devices, exchange(): return lax.all_to_all(blocks, axes, split_axis=0, concat_axis=0, tiled=True)  8.79 us
    all_to_all x2, starting transfers between devices, exchange(): return lax.all_to_all(blocks, axes, split_axis=0, concat_axis=0, tiled=True)  7.69 us
    ppermute x2, starting transfers between devices, from_left(): return lax.ppermute(block, TILE, [(i, i + 1) for i in range(count - 1)])  7.29 us
    ppermute x2, waiting for transfers between devices, swap(): return lax.ppermute(block, 'c', SWAP)  3.52 us
  transfers between devices with their start and end apart: 8, of which 6 were waited for; matrix products, arithmetic and copies ran while one was open for 0% of the time, Pallas kernels for 2%

profile of v9, /device:TPU:1, one launch (start us, length us, event | category | flops | bytes accessed | tf_op | source)
XLA Modules:
  0.0 121.6 jit_solution(18384868163122706411)
XLA Ops:
  0.7 4.4 %shard_map.130 = (bf16[32,384]{1,0:T(8,128)(2,1)S(1)}, bf16[32,384]{1,0:T(8,128)(2,1)S(1)}, f32[256,384]{1,0:T(8,128)S(1)}, bf16[256,384]{1,0:T(8,128)(2,1)S(1)}...) custom-call(s32[1,4]{1,0:T(1,128)} %flags.1, ...), custom_call_target="tpu_custom_call" | custom-call | flops 301989888 | bytes 8388608 | tf_op jit(solution)/shard_map/pallas_call | solution.py:309
  5.1 4.0 %collective-permute-start = (bf16[32,384]{1,0:T(8,128)(2,1)S(1)}, bf16[32,384]{1,0:T(8,128)(2,1)S(1)}, u32[]{:S(2)}, u32[]{:S(2)}) collective-permute-start(bf16[32,384]{1,0:T(8,128)(2,1)S(1)} %get-tuple-element.41), channel_id=1, source_target_pairs={{0,4},{4,8},{8,12},{12,16},{16,20},{20,24},{24,28},{28,32},{32,36}... | collective-permute-start | bytes 73736 | tf_op jit(solution)/shard_map/ppermute | solution.py:430
  9.1 1.3 %collective-permute-start.1 = (bf16[32,384]{1,0:T(8,128)(2,1)S(1)}, bf16[32,384]{1,0:T(8,128)(2,1)S(1)}, u32[]{:S(2)}, u32[]{:S(2)}) collective-permute-start(bf16[32,384]{1,0:T(8,128)(2,1)S(1)} %get-tuple-element.42), channel_id=1, source_target_pairs={{4,0},{8,4},{12,8},{16,12},{20,16},{24,20},{28,24},{32,28},{36,32}... | collective-permute-start | bytes 73736 | tf_op jit(solution)/shard_map/ppermute | solution.py:435
  10.4 0.0 collective-permute-done.low
  10.4 3.3 %collective-permute-done.1.high = bf16[32,384]{1,0:T(8,128)(2,1)S(1)} collective-permute-done((bf16[32,384]{1,0:T(8,128)(2,1)S(1)}, bf16[32,384]{1,0:T(8,128)(2,1)S(1)}, u32[]{:S(2)}, u32[]{:S(2)}) %collective-permute-start.1) | collective-permute-done | bytes 24608 | tf_op jit(solution)/shard_map/ppermute | solution.py:435
  13.7 3.7 %shard_map.131 = (f32[1536,384]{1,0:T(8,128)S(1)}, bf16[1536,384]{1,0:T(8,128)(2,1)S(1)}, f32[256,384]{1,0:T(8,128)S(1)}, f32[256,128]{1,0:T(8,128)S(1)}, bf16[1536,256]{1,0:T(8,128)(2,1)S(1)}) custom-call(s32[1]{0:T(128)} %bitcast.device, f32[256,384]{1,0:T(8,128)S(1)} %get-tuple-element.40.conv, bf16[32,384]{1,0:T(8,128)(2,1)S(1)} %collective-permute-done.low, ...), custom_call_target="tpu_custom_call" | custom-call | flops 905969664 | bytes 12582912 | tf_op jit(solution)/shard_map/pallas_call | solution.py:309
  17.4 7.2 %collective-permute-start.2 = (bf16[1536,384]{1,0:T(8,128)(2,1)S(1)}, bf16[1536,384]{1,0:T(8,128)(2,1)S(1)}, u32[]{:S(2)}, u32[]{:S(2)}) collective-permute-start(bf16[1536,384]{1,0:T(8,128)(2,1)S(1)} %get-tuple-element.57), channel_id=1, source_target_pairs={{0,1},{1,0},{2,3},{3,2},{4,5},{5,4},{6,7},{7,6},{8,9},{9,8},{10,11... | collective-permute-start | bytes 3538952 | tf_op jit(solution)/shard_map/ppermute | solution.py:443
  24.6 0.7 shard_map.132
  25.3 1.8 %collective-permute-done.2.received = bf16[1536,384]{1,0:T(8,128)(2,1)S(1)} collective-permute-done((bf16[1536,384]{1,0:T(8,128)(2,1)S(1)}, bf16[1536,384]{1,0:T(8,128)(2,1)S(1)}, u32[]{:S(2)}, u32[]{:S(2)}) %collective-permute-start.2) | collective-permute-done | bytes 1179680 | tf_op jit(solution)/shard_map/ppermute | solution.py:443
  27.0 1.3 %shard_map.133 = bf16[8,192,384]{2,1,0:T(8,128)(2,1)} custom-call(f32[1536,384]{1,0:T(8,128)S(1)} %get-tuple-element.56.kept, bf16[1536,384]{1,0:T(8,128)(2,1)S(1)} %collective-permute-done.2.received), custom_call_target="tpu_custom_call" | custom-call | flops 1179648 | bytes 4718592 | tf_op jit(solution)/shard_map/pallas_call | solution.py:309
  28.4 3.6 %all-to-all-start = ((bf16[8,192,384]{2,1,0:T(8,128)(2,1)}), bf16[8,192,384]{2,1,0:T(8,128)(2,1)S(1)}, u32[]{:S(2)}, u32[]{:S(2)}) async-start(bf16[8,192,384]{2,1,0:T(8,128)(2,1)} %shard_map.133), calls=%async_computation | async-start | bytes 2359296 | tf_op jit(solution)/shard_map/all_to_all | solution.py:439
  31.9 3.3 %collective-permute-start.3 = (f32[24,384]{1,0:T(8,128)S(1)}, f32[24,384]{1,0:T(8,128)S(1)}, u32[]{:S(2)}, u32[]{:S(2)}) collective-permute-start(f32[24,384]{1,0:T(8,128)S(1)} %get-tuple-element.58), channel_id=1, source_target_pairs={{0,4},{4,8},{8,12},{12,16},{16,20},{20,24},{24,28},{28,32},{32,36}... | collective-permute-start | bytes 110600 | tf_op jit(solution)/shard_map/ppermute | solution.py:430
  35.2 1.3 %collective-permute-start.4 = (f32[24,384]{1,0:T(8,128)S(1)}, f32[24,384]{1,0:T(8,128)S(1)}, u32[]{:S(2)}, u32[]{:S(2)}) collective-permute-start(f32[24,384]{1,0:T(8,128)S(1)} %get-tuple-element.59), channel_id=1, source_target_pairs={{4,0},{8,4},{12,8},{16,12},{20,16},{24,20},{28,24},{32,28},{36,32}... | collective-permute-start | bytes 110600 | tf_op jit(solution)/shard_map/ppermute | solution.py:435
  36.5 11.0 %collective-permute-done.3.low = f32[24,384]{1,0:T(8,128)S(1)} collective-permute-done((f32[24,384]{1,0:T(8,128)S(1)}, f32[24,384]{1,0:T(8,128)S(1)}, u32[]{:S(2)}, u32[]{:S(2)}) %collective-permute-start.3) | collective-permute-done | bytes 36896 | tf_op jit(solution)/shard_map/ppermute | solution.py:430
  47.5 0.0 collective-permute-done.4.high
  47.5 2.9 %all-to-all-done.received = bf16[8,192,384]{2,1,0:T(8,128)(2,1)S(1)} async-done(((bf16[8,192,384]{2,1,0:T(8,128)(2,1)}), bf16[8,192,384]{2,1,0:T(8,128)(2,1)S(1)}, u32[]{:S(2)}, u32[]{:S(2)}) %all-to-all-start) | async-done | bytes 1179680 | tf_op jit(solution)/shard_map/all_to_all | solution.py:439
  50.4 0.2 shard_map.134
  50.7 19.9 %all_to_all.25.received = bf16[8,24,384]{2,1,0:T(8,128)(2,1)S(1)} all-to-all(bf16[8,24,384]{2,1,0:T(8,128)(2,1)S(1)} %shard_map.134), channel_id=1, replica_groups=mesh['zh'=4,'xh'=2,'xl'=2,'yh'=4,'yl'=2,'zl'=2,'c'=2] {'xh','yh'}, dimensions={0} | all-to-all | bytes 294912 | tf_op jit(solution)/shard_map/all_to_all | solution.py:439
  70.6 14.1 %all_to_all.26.received = bf16[4,24,384]{2,1,0:T(8,128)(2,1)S(1)} all-to-all(bf16[4,24,384]{2,1,0:T(8,128)(2,1)S(1)} %shard_map.135), channel_id=1, replica_groups=mesh['zh'=4,'xh'=2,'xl'=2,'yh'=4,'yl'=2,'zl'=2,'c'=2] {'zh'}, dimensions={0} | all-to-all | bytes 147456 | tf_op jit(solution)/shard_map/all_to_all | solution.py:439
  84.7 0.0 copy-start
  84.7 11.8 %all_to_all.27.received = bf16[8,16,384]{2,1,0:T(8,128)(2,1)S(1)} all-to-all(bf16[8,16,384]{2,1,0:T(8,128)(2,1)S(1)} %get-tuple-element.61), channel_id=1, replica_groups=mesh['zh'=4,'xh'=2,'xl'=2,'yh'=4,'yl'=2,'zl'=2,'c'=2] {'xh','yh'}, dimensions={0} | all-to-all | bytes 196608 | tf_op jit(solution)/shard_map/all_to_all | solution.py:439
  96.5 0.9 shard_map.137
  97.5 4.1 %all-to-all-start.4 = ((bf16[8,112,384]{2,1,0:T(8,128)(2,1)}), bf16[8,112,384]{2,1,0:T(8,128)(2,1)S(1)}, u32[]{:S(2)}, u32[]{:S(2)}) async-start(bf16[8,112,384]{2,1,0:T(8,128)(2,1)} %shard_map.137), calls=%async_computation.4 | async-start | bytes 1376256 | tf_op jit(solution)/shard_map/all_to_all | solution.py:439
  101.6 0.0 copy-done
  101.6 2.3 %shard_map.138 = bf16[256,384]{1,0:T(8,128)(2,1)} custom-call(f32[256,384]{1,0:T(8,128)S(1)} %get-tuple-element.66.grad_conv, f32[24,384]{1,0:T(8,128)S(1)} %collective-permute-done.3.low, f32[24,384]{1,0:T(8,128)S(1)} %collective-permute-done.4.high, f32[7,7,384]{2,1,0:T(8,128)S(1)} %get-tuple-element.43.taps, bf16[256,384]{1,0:T(8,128)(2,1)S(1)} %bitcast.5), custom_call_target="tpu_custom_call" | custom-call | flops 9633792 | bytes 2097152 | tf_op jit(solution)/shard_map/pallas_call | solution.py:309
  103.9 5.9 %all-to-all-done.4.own = bf16[8,112,384]{2,1,0:T(8,128)(2,1)S(1)} async-done(((bf16[8,112,384]{2,1,0:T(8,128)(2,1)}), bf16[8,112,384]{2,1,0:T(8,128)(2,1)S(1)}, u32[]{:S(2)}, u32[]{:S(2)}) %all-to-all-start.4) | async-done | bytes 688160 | tf_op jit(solution)/shard_map/all_to_all | solution.py:439
  109.8 9.0 %collective-permute-start.5 = (bf16[8,112,384]{2,1,0:T(8,128)(2,1)S(1)}, bf16[8,112,384]{2,1,0:T(8,128)(2,1)S(1)}, u32[]{:S(2)}, u32[]{:S(2)}) collective-permute-start(bf16[8,112,384]{2,1,0:T(8,128)(2,1)S(1)} %all-to-all-done.4.own), channel_id=1, source_target_pairs={{0,1},{1,0},{2,3},{3,2},{4,5},{5,4},{6,7},{7,6},{8,9},{9,8},{10,11... | collective-permute-start | bytes 2064392 | tf_op jit(solution)/shard_map/ppermute | solution.py:443
  118.7 1.7 %collective-permute-done.5.other = bf16[8,112,384]{2,1,0:T(8,128)(2,1)S(1)} collective-permute-done((bf16[8,112,384]{2,1,0:T(8,128)(2,1)S(1)}, bf16[8,112,384]{2,1,0:T(8,128)(2,1)S(1)}, u32[]{:S(2)}, u32[]{:S(2)}) %collective-permute-start.5) | collective-permute-done | bytes 688160 | tf_op jit(solution)/shard_map/ppermute | solution.py:443
  120.5 1.1 shard_map.139
  (2 shorter events, 0.0 us)
Async XLA Ops:
  5.1 5.3 %collective-permute-start = (bf16[32,384]{1,0:T(8,128)(2,1)S(1)}, bf16[32,384]{1,0:T(8,128)(2,1)S(1)}, u32[]{:S(2)}, u32[]{:S(2)}) collective-permute-start(bf16[32,384]{1,0:T(8,128)(2,1)S(1)} %get-tuple-element.41), channel_id=1, source_target_pairs={{0,4},{4,8},{8,12},{12,16},{16,20},{20,24},{24,28},{28,32},{32,36}... | collective-permute-start | bytes 73736 | tf_op jit(solution)/shard_map/ppermute | solution.py:430
  9.1 4.6 %collective-permute-start.1 = (bf16[32,384]{1,0:T(8,128)(2,1)S(1)}, bf16[32,384]{1,0:T(8,128)(2,1)S(1)}, u32[]{:S(2)}, u32[]{:S(2)}) collective-permute-start(bf16[32,384]{1,0:T(8,128)(2,1)S(1)} %get-tuple-element.42), channel_id=1, source_target_pairs={{4,0},{8,4},{12,8},{16,12},{20,16},{24,20},{28,24},{32,28},{36,32}... | collective-permute-start | bytes 73736 | tf_op jit(solution)/shard_map/ppermute | solution.py:435
  17.4 9.7 %collective-permute-start.2 = (bf16[1536,384]{1,0:T(8,128)(2,1)S(1)}, bf16[1536,384]{1,0:T(8,128)(2,1)S(1)}, u32[]{:S(2)}, u32[]{:S(2)}) collective-permute-start(bf16[1536,384]{1,0:T(8,128)(2,1)S(1)} %get-tuple-element.57), channel_id=1, source_target_pairs={{0,1},{1,0},{2,3},{3,2},{4,5},{5,4},{6,7},{7,6},{8,9},{9,8},{10,11... | collective-permute-start | bytes 3538952 | tf_op jit(solution)/shard_map/ppermute | solution.py:443
  28.4 22.1 %all-to-all-start = ((bf16[8,192,384]{2,1,0:T(8,128)(2,1)}), bf16[8,192,384]{2,1,0:T(8,128)(2,1)S(1)}, u32[]{:S(2)}, u32[]{:S(2)}) async-start(bf16[8,192,384]{2,1,0:T(8,128)(2,1)} %shard_map.133), calls=%async_computation | async-start | bytes 2359296 | tf_op jit(solution)/shard_map/all_to_all | solution.py:439
  31.9 15.6 %collective-permute-start.3 = (f32[24,384]{1,0:T(8,128)S(1)}, f32[24,384]{1,0:T(8,128)S(1)}, u32[]{:S(2)}, u32[]{:S(2)}) collective-permute-start(f32[24,384]{1,0:T(8,128)S(1)} %get-tuple-element.58), channel_id=1, source_target_pairs={{0,4},{4,8},{8,12},{12,16},{16,20},{20,24},{24,28},{28,32},{32,36}... | collective-permute-start | bytes 110600 | tf_op jit(solution)/shard_map/ppermute | solution.py:430
  35.2 12.3 %collective-permute-start.4 = (f32[24,384]{1,0:T(8,128)S(1)}, f32[24,384]{1,0:T(8,128)S(1)}, u32[]{:S(2)}, u32[]{:S(2)}) collective-permute-start(f32[24,384]{1,0:T(8,128)S(1)} %get-tuple-element.59), channel_id=1, source_target_pairs={{4,0},{8,4},{12,8},{16,12},{20,16},{24,20},{28,24},{32,28},{36,32}... | collective-permute-start | bytes 110600 | tf_op jit(solution)/shard_map/ppermute | solution.py:435
  84.7 16.9 %copy-start = (bf16[1,8,32,384]{3,2,1,0:T(8,128)(2,1)S(1)}, bf16[1,8,32,384]{3,2,1,0:T(8,128)(2,1)}, u32[]{:S(2)}) copy-start(bf16[1,8,32,384]{3,2,1,0:T(8,128)(2,1)} %param.12) | copy-start | bytes 589828
  97.5 12.3 %all-to-all-start.4 = ((bf16[8,112,384]{2,1,0:T(8,128)(2,1)}), bf16[8,112,384]{2,1,0:T(8,128)(2,1)S(1)}, u32[]{:S(2)}, u32[]{:S(2)}) async-start(bf16[8,112,384]{2,1,0:T(8,128)(2,1)} %shard_map.137), calls=%async_computation.4 | async-start | bytes 1376256 | tf_op jit(solution)/shard_map/all_to_all | solution.py:439
  109.8 10.7 %collective-permute-start.5 = (bf16[8,112,384]{2,1,0:T(8,128)(2,1)S(1)}, bf16[8,112,384]{2,1,0:T(8,128)(2,1)S(1)}, u32[]{:S(2)}, u32[]{:S(2)}) collective-permute-start(bf16[8,112,384]{2,1,0:T(8,128)(2,1)S(1)} %all-to-all-done.4.own), channel_id=1, source_target_pairs={{0,1},{1,0},{2,3},{3,2},{4,5},{5,4},{6,7},{7,6},{8,9},{9,8},{10,11... | collective-permute-start | bytes 2064392 | tf_op jit(solution)/shard_map/ppermute | solution.py:443

commit v10 on v8

--- a/solution.py
+++ b/solution.py
@@ -141,9 +141,9 @@
 
 
 def middle_kernel(
-    device, conv, low, high, taps, vectors, w_in_t, b_cols, out_grad, back, w_in,
-    kept, sent, grad_conv, low_edge, high_edge,
-    rows, low_wide, high_wide, standard, normed, preact, hidden, grad_pre
+    device, conv, low, high, taps, vectors, w_in_t, b_cols, out_grad, back,
+    kept, sent, standard, inverse, grad_pre,
+    rows, low_wide, high_wide, normed, preact, hidden
 ):
     width = conv.shape[1]
     rows[...] = conv[...]
@@ -160,8 +160,9 @@
     gain, bias = vectors[SIDE : SIDE + 1, :], vectors[2 * SIDE : 2 * SIDE + 1, :]
     conv_out = rows[...] + vectors[:1, :]
     centre = conv_out - jnp.mean(conv_out, axis=-1, keepdims=True)
-    inverse = lax.rsqrt(jnp.mean(centre * centre, axis=-1, keepdims=True) + EPSILON)
-    standard[...] = centre * inverse
+    scale = lax.rsqrt(jnp.mean(centre * centre, axis=-1, keepdims=True) + EPSILON)
+    inverse[...] = jnp.broadcast_to(scale, inverse.shape)
+    standard[...] = centre * scale
     normed[...] = (standard[...] * gain + bias).astype(jnp.bfloat16)
     preact[...] = matmul(w_in_t[...], normed[...], NT)
 
@@ -185,11 +186,14 @@
     sent[half:, :] = matmul(grad_pre[other, :], normed[...]).astype(jnp.bfloat16)
     kept[:half, :] = matmul(hidden[own, :], out_grad[...])
     kept[half:, :] = matmul(grad_pre[own, :], normed[...])
-    grad_std = matmul(w_in[...], grad_pre[...]).T * gain
+
+
+def back_kernel(grad_pre, w_in, standard, inverse, vectors, grad_conv, low_edge, high_edge):
+    grad_std = matmul(w_in[...], grad_pre[...]).T * vectors[SIDE : SIDE + 1, :]
     norm = standard[...]
     mean = jnp.mean(grad_std, axis=-1, keepdims=True)
     along = jnp.mean(grad_std * norm, axis=-1, keepdims=True)
-    result = inverse * (grad_std - mean - norm * along)
+    result = inverse[:, :1] * (grad_std - mean - norm * along)
     grad_conv[...] = result
     edge = HALO * SIDE
     low_edge[...] = result[:edge, :]
@@ -356,18 +360,28 @@
     )
 
 
-def middle(device, conv, low, high, taps, vectors, w_in_t, b_cols, out_grad, back, w_in):
+def middle(device, conv, low, high, taps, vectors, w_in_t, b_cols, out_grad, back):
     rows, width = conv.shape
     hidden = w_in_t.shape[0]
-    halo, edge = pltpu.VMEM((EDGE, width), F32), (HALO * SIDE, width)
+    halo = pltpu.VMEM((EDGE, width), F32)
     return call(
         middle_kernel,
-        [((hidden, width), F32), ((hidden, width), B16), ((rows, width), F32), (edge, F32), (edge, F32)],
-        [pltpu.VMEM((rows, width), F32), halo, halo, pltpu.VMEM((rows, width), F32), pltpu.VMEM((rows, width), B16),
-         pltpu.VMEM((hidden, rows), F32), pltpu.VMEM((hidden, rows), B16), pltpu.VMEM((hidden, rows), B16)],
+        [((hidden, width), F32), ((hidden, width), B16), ((rows, width), F32), ((rows, LANES), F32), ((hidden, rows), B16)],
+        [pltpu.VMEM((rows, width), F32), halo, halo, pltpu.VMEM((rows, width), B16),
+         pltpu.VMEM((hidden, rows), F32), pltpu.VMEM((hidden, rows), B16)],
         [device],
-        [conv, low, high, taps, vectors, w_in_t, b_cols, out_grad, back, w_in],
-        8 * rows * width * hidden, 12 * 1024 * 1024,
+        [conv, low, high, taps, vectors, w_in_t, b_cols, out_grad, back],
+        6 * rows * width * hidden, 12 * 1024 * 1024,
+    )
+
+
+def to_conv(grad_pre, w_in, standard, inverse, vectors):
+    rows, width = standard.shape
+    edge = (HALO * SIDE, width)
+    return call(
+        back_kernel, [((rows, width), F32), (edge, F32), (edge, F32)], [], [],
+        [grad_pre, w_in, standard, inverse, vectors],
+        2 * grad_pre.size * width, 4 * grad_pre.size,
     )
 
 
@@ -471,17 +485,17 @@
     conv, out_grad, back, w_in_t, b_cols, w_in_here, taps, vectors = before_halos(
         tissue, rows, upstream, kernel, conv_bias, ln_gain, ln_bias, w_in, b_in, w_out, layer_scale
     )
-    kept, sent, grad_conv, low, high = middle(
-        device, conv, low, high, taps, vectors, w_in_t, b_cols, out_grad, back, w_in_here
-    )
-    message = to_cube(cube, kept, swap(sent))
-    received = exchange(message, CUBE)
-    low, high = from_left(high), from_right(low)
-    received, low, high = lax.optimization_barrier((received, low, high))
+    kept, sent, standard, inverse, grad_pre = middle(
+        device, conv, low, high, taps, vectors, w_in_t, b_cols, out_grad, back
+    )
+    grad_conv, low, high = to_conv(grad_pre, w_in_here, standard, inverse, vectors)
+    kept, low, high = lax.optimization_barrier((kept, low, high))
+    received = exchange(to_cube(cube, kept, swap(sent)), CUBE)
     received = exchange(to_line(received, line), LINE)
     received = exchange(to_plane(received, plane), PLANE)
     received = exchange(turn(scale, received, line), LINE)
     received, low, high = lax.optimization_barrier((received, low, high))
+    low, high = from_left(high), from_right(low)
     own = exchange(unpack(received, cube), CUBE)
     grad_image = to_features(grad_conv, low, high, taps, upstream)
     own, grad_image = lax.optimization_barrier((own, grad_image))

time: 118 us -> 118 us (level); the launches traced: 117 us -> 116 us
  blocking collectives: 45.1 us -> 64.5 us
  waiting for transfers between devices: 22.3 us -> 6.93 us
  starting transfers between devices: 33.5 us -> 29.2 us
    all_to_all x3 -> x4, blocking collectives: 45.1 us -> 64.5 us  [exchange(): return lax.all_to_all(blocks, axes, split_axis=0, concat_axis=0, tiled=True)]
    ppermute x2, waiting for transfers between devices: 10.2 us -> 0.15 us  [from_left(): return lax.ppermute(block, TILE, [(i, i + 1) for i in range(count - 1)])]
    all_to_all x2 -> x1, waiting for transfers between devices: 7.4 us -> 0.01 us  [exchange(): return lax.all_to_all(blocks, axes, split_axis=0, concat_axis=0, tiled=True)]
    all_to_all x2 -> x1, starting transfers between devices: 7.83 us -> 4.24 us  [exchange(): return lax.all_to_all(blocks, axes, split_axis=0, concat_axis=0, tiled=True)]
    ppermute x2, waiting for transfers between devices: 0.57 us -> 3.26 us  [from_right(): return lax.ppermute(block, TILE, [(i + 1, i) for i in range(count - 1)])]
    pallas_call x10 -> x11, Pallas kernels: 15.6 us -> 14.7 us  [call(): pl.pallas_call(kernel, out_shape=[jax.ShapeDtypeStruct(shape, kind) for s...]
  transfers between devices with their start and end apart: 8 -> 7, of which waited for: 6 -> 4; matrix products, arithmetic and copies ran while one was open for 0% -> 0% of each run, Pallas kernels for 6% -> 6%
where the time goes in v10:
time: 118 us; the launch traced here: 116 us
  blocking collectives  64.5 us (55%)
  starting transfers between devices  29.2 us (25%)
  Pallas kernels  14.7 us (12%)
  waiting for transfers between devices  6.93 us (6%)
    all_to_all x4, blocking collectives, exchange(): return lax.all_to_all(blocks, axes, split_axis=0, concat_axis=0, tiled=True)  64.5 us
    ppermute x2, starting transfers between devices, swap(): return lax.ppermute(block, 'c', SWAP)  15 us
    pallas_call x11, Pallas kernels, call(): pl.pallas_call(kernel, out_shape=[jax.ShapeDtypeStruct(shape, kind) for s...  14.7 us
    ppermute x2, starting transfers between devices, from_left(): return lax.ppermute(block, TILE, [(i, i + 1) for i in range(count - 1)])  7.39 us
    all_to_all x1, starting transfers between devices, exchange(): return lax.all_to_all(blocks, axes, split_axis=0, concat_axis=0, tiled=True)  4.24 us
    ppermute x2, waiting for transfers between devices, swap(): return lax.ppermute(block, 'c', SWAP)  3.52 us
    ppermute x2, waiting for transfers between devices, from_right(): return lax.ppermute(block, TILE, [(i + 1, i) for i in range(count - 1)])  3.26 us
    ppermute x2, starting transfers between devices, from_right(): return lax.ppermute(block, TILE, [(i + 1, i) for i in range(count - 1)])  2.58 us
  transfers between devices with their start and end apart: 7, of which 4 were waited for; matrix products, arithmetic and copies ran while one was open for 0% of the time, Pallas kernels for 6%

profile of v10, /device:TPU:1, one launch (start us, length us, event | category | flops | bytes accessed | tf_op | source)
XLA Modules:
  0.0 116.1 jit_solution(160183171933777803)
XLA Ops:
  0.6 1.0 shard_map.131
  1.6 4.0 %collective-permute-start = (bf16[32,384]{1,0:T(8,128)(2,1)S(1)}, bf16[32,384]{1,0:T(8,128)(2,1)S(1)}, u32[]{:S(2)}, u32[]{:S(2)}) collective-permute-start(bf16[32,384]{1,0:T(8,128)(2,1)S(1)} %get-tuple-element.32), channel_id=1, source_target_pairs={{0,4},{4,8},{8,12},{12,16},{16,20},{20,24},{24,28},{28,32},{32,36}... | collective-permute-start | bytes 73736 | tf_op jit(solution)/shard_map/ppermute | solution.py:455
  5.7 1.3 %collective-permute-start.1 = (bf16[32,384]{1,0:T(8,128)(2,1)S(1)}, bf16[32,384]{1,0:T(8,128)(2,1)S(1)}, u32[]{:S(2)}, u32[]{:S(2)}) collective-permute-start(bf16[32,384]{1,0:T(8,128)(2,1)S(1)} %get-tuple-element.33), channel_id=1, source_target_pairs={{4,0},{8,4},{12,8},{16,12},{20,16},{24,20},{28,24},{32,28},{36,32}... | collective-permute-start | bytes 73736 | tf_op jit(solution)/shard_map/ppermute | solution.py:460
  7.0 4.4 %shard_map.130 = (f32[256,384]{1,0:T(8,128)S(1)}, bf16[256,384]{1,0:T(8,128)(2,1)S(1)}, f32[1536,256]{1,0:T(8,128)S(1)}, bf16[1536,384]{1,0:T(8,128)(2,1)S(1)}, ...) custom-call(s32[1,4]{1,0:T(1,128)} %flags.1, ...), custom_call_target="tpu_custom_call" | custom-call | flops 301989888 | bytes 8388608 | tf_op jit(solution)/shard_map/pallas_call | solution.py:319
  11.4 0.0 collective-permute-done.low
  11.4 0.0 collective-permute-done.1.high
  11.4 3.7 %shard_map.132 = (f32[1536,384]{1,0:T(8,128)S(1)}, bf16[1536,384]{1,0:T(8,128)(2,1)S(1)}, f32[256,384]{1,0:T(8,128)S(1)}, f32[256,128]{1,0:T(8,128)S(1)}, bf16[1536,256]{1,0:T(8,128)(2,1)S(1)}) custom-call(s32[1]{0:T(128)} %bitcast.device, f32[256,384]{1,0:T(8,128)S(1)} %get-tuple-element.31.conv, bf16[32,384]{1,0:T(8,128)(2,1)S(1)} %collective-permute-done.low, ...), custom_call_target="tpu_custom_call" | custom-call | flops 905969664 | bytes 12582912 | tf_op jit(solution)/shard_map/pallas_call | solution.py:319
  15.1 6.0 %collective-permute-start.2 = (bf16[1536,384]{1,0:T(8,128)(2,1)S(1)}, bf16[1536,384]{1,0:T(8,128)(2,1)S(1)}, u32[]{:S(2)}, u32[]{:S(2)}) collective-permute-start(bf16[1536,384]{1,0:T(8,128)(2,1)S(1)} %get-tuple-element.48), channel_id=1, source_target_pairs={{0,1},{1,0},{2,3},{3,2},{4,5},{5,4},{6,7},{7,6},{8,9},{9,8},{10,11... | collective-permute-start | bytes 3538952 | tf_op jit(solution)/shard_map/ppermute | solution.py:468
  21.2 0.7 shard_map.133
  21.9 1.8 %collective-permute-done.2.received = bf16[1536,384]{1,0:T(8,128)(2,1)S(1)} collective-permute-done((bf16[1536,384]{1,0:T(8,128)(2,1)S(1)}, bf16[1536,384]{1,0:T(8,128)(2,1)S(1)}, u32[]{:S(2)}, u32[]{:S(2)}) %collective-permute-start.2) | collective-permute-done | bytes 1179680 | tf_op jit(solution)/shard_map/ppermute | solution.py:468
  23.6 0.3 shard_map.134
  23.9 20.0 %all_to_all.25.received = bf16[8,192,384]{2,1,0:T(8,128)(2,1)S(1)} all-to-all(bf16[8,192,384]{2,1,0:T(8,128)(2,1)S(1)} %shard_map.134), channel_id=1, replica_groups=mesh['zh'=4,'xh'=2,'xl'=2,'yh'=4,'yl'=2,'zl'=2,'c'=2] {'xl','yl','zl'}, dimensions={0} | all-to-all | bytes 2359296 | tf_op jit(solution)/shard_map/all_to_all | solution.py:464
  43.9 0.2 shard_map.135
  44.2 20.2 %all_to_all.26.received = bf16[4,48,384]{2,1,0:T(8,128)(2,1)S(1)} all-to-all(bf16[4,48,384]{2,1,0:T(8,128)(2,1)S(1)} %shard_map.135), channel_id=1, replica_groups=mesh['zh'=4,'xh'=2,'xl'=2,'yh'=4,'yl'=2,'zl'=2,'c'=2] {'zh'}, dimensions={0} | all-to-all | bytes 294912 | tf_op jit(solution)/shard_map/all_to_all | solution.py:464
  64.3 0.1 shard_map.136
  64.4 14.7 %all_to_all.27.received = bf16[8,32,384]{2,1,0:T(8,128)(2,1)S(1)} all-to-all(bf16[8,32,384]{2,1,0:T(8,128)(2,1)S(1)} %shard_map.136), channel_id=1, replica_groups=mesh['zh'=4,'xh'=2,'xl'=2,'yh'=4,'yl'=2,'zl'=2,'c'=2] {'xh','yh'}, dimensions={0} | all-to-all | bytes 393216 | tf_op jit(solution)/shard_map/all_to_all | solution.py:464
  79.2 0.0 copy-start
  79.2 9.6 %all_to_all.28.received = bf16[4,32,384]{2,1,0:T(8,128)(2,1)S(1)} all-to-all(bf16[4,32,384]{2,1,0:T(8,128)(2,1)S(1)} %shard_map.137), channel_id=1, replica_groups=mesh['zh'=4,'xh'=2,'xl'=2,'yh'=4,'yl'=2,'zl'=2,'c'=2] {'zh'}, dimensions={0} | all-to-all | bytes 196608 | tf_op jit(solution)/shard_map/all_to_all | solution.py:464
  88.8 0.9 shard_map.138
  89.7 4.2 %all-to-all-start.4 = ((bf16[8,112,384]{2,1,0:T(8,128)(2,1)}), bf16[8,112,384]{2,1,0:T(8,128)(2,1)S(1)}, u32[]{:S(2)}, u32[]{:S(2)}) async-start(bf16[8,112,384]{2,1,0:T(8,128)(2,1)} %shard_map.138), calls=%async_computation.4 | async-start | bytes 1376256 | tf_op jit(solution)/shard_map/all_to_all | solution.py:464
  93.9 3.4 %collective-permute-start.3 = (f32[24,384]{1,0:T(8,128)S(1)}, f32[24,384]{1,0:T(8,128)S(1)}, u32[]{:S(2)}, u32[]{:S(2)}) collective-permute-start(f32[24,384]{1,0:T(8,128)S(1)} %get-tuple-element.53), channel_id=1, source_target_pairs={{0,4},{4,8},{8,12},{12,16},{16,20},{20,24},{24,28},{28,32},{32,36}... | collective-permute-start | bytes 110600 | tf_op jit(solution)/shard_map/ppermute | solution.py:455
  97.3 1.3 %collective-permute-start.4 = (f32[24,384]{1,0:T(8,128)S(1)}, f32[24,384]{1,0:T(8,128)S(1)}, u32[]{:S(2)}, u32[]{:S(2)}) collective-permute-start(f32[24,384]{1,0:T(8,128)S(1)} %get-tuple-element.54), channel_id=1, source_target_pairs={{4,0},{8,4},{12,8},{16,12},{20,16},{24,20},{28,24},{32,28},{36,32}... | collective-permute-start | bytes 110600 | tf_op jit(solution)/shard_map/ppermute | solution.py:460
  98.6 0.1 collective-permute-done.3.low
  98.7 3.3 %collective-permute-done.4.high = f32[24,384]{1,0:T(8,128)S(1)} collective-permute-done((f32[24,384]{1,0:T(8,128)S(1)}, f32[24,384]{1,0:T(8,128)S(1)}, u32[]{:S(2)}, u32[]{:S(2)}) %collective-permute-start.4) | collective-permute-done | bytes 36896 | tf_op jit(solution)/shard_map/ppermute | solution.py:460
  102.0 0.0 copy-done
  102.0 2.3 %shard_map.139 = bf16[256,384]{1,0:T(8,128)(2,1)} custom-call(f32[256,384]{1,0:T(8,128)S(1)} %get-tuple-element.52.grad_conv, f32[24,384]{1,0:T(8,128)S(1)} %collective-permute-done.3.low, f32[24,384]{1,0:T(8,128)S(1)} %collective-permute-done.4.high, f32[7,7,384]{2,1,0:T(8,128)S(1)} %get-tuple-element.34.taps, bf16[256,384]{1,0:T(8,128)(2,1)S(1)} %bitcast.5), custom_call_target="tpu_custom_call" | custom-call | flops 9633792 | bytes 2097152 | tf_op jit(solution)/shard_map/pallas_call | solution.py:319
  104.3 0.0 all-to-all-done.4.own
  104.3 8.9 %collective-permute-start.5 = (bf16[8,112,384]{2,1,0:T(8,128)(2,1)S(1)}, bf16[8,112,384]{2,1,0:T(8,128)(2,1)S(1)}, u32[]{:S(2)}, u32[]{:S(2)}) collective-permute-start(bf16[8,112,384]{2,1,0:T(8,128)(2,1)S(1)} %all-to-all-done.4.own), channel_id=1, source_target_pairs={{0,1},{1,0},{2,3},{3,2},{4,5},{5,4},{6,7},{7,6},{8,9},{9,8},{10,11... | collective-permute-start | bytes 2064392 | tf_op jit(solution)/shard_map/ppermute | solution.py:468
  113.2 1.7 %collective-permute-done.5.other = bf16[8,112,384]{2,1,0:T(8,128)(2,1)S(1)} collective-permute-done((bf16[8,112,384]{2,1,0:T(8,128)(2,1)S(1)}, bf16[8,112,384]{2,1,0:T(8,128)(2,1)S(1)}, u32[]{:S(2)}, u32[]{:S(2)}) %collective-permute-start.5) | collective-permute-done | bytes 688160 | tf_op jit(solution)/shard_map/ppermute | solution.py:468
  114.9 1.1 shard_map.140
  (1 shorter events, 0.0 us)
Async XLA Ops:
  1.6 9.8 %collective-permute-start = (bf16[32,384]{1,0:T(8,128)(2,1)S(1)}, bf16[32,384]{1,0:T(8,128)(2,1)S(1)}, u32[]{:S(2)}, u32[]{:S(2)}) collective-permute-start(bf16[32,384]{1,0:T(8,128)(2,1)S(1)} %get-tuple-element.32), channel_id=1, source_target_pairs={{0,4},{4,8},{8,12},{12,16},{16,20},{20,24},{24,28},{28,32},{32,36}... | collective-permute-start | bytes 73736 | tf_op jit(solution)/shard_map/ppermute | solution.py:455
  5.7 5.7 %collective-permute-start.1 = (bf16[32,384]{1,0:T(8,128)(2,1)S(1)}, bf16[32,384]{1,0:T(8,128)(2,1)S(1)}, u32[]{:S(2)}, u32[]{:S(2)}) collective-permute-start(bf16[32,384]{1,0:T(8,128)(2,1)S(1)} %get-tuple-element.33), channel_id=1, source_target_pairs={{4,0},{8,4},{12,8},{16,12},{20,16},{24,20},{28,24},{32,28},{36,32}... | collective-permute-start | bytes 73736 | tf_op jit(solution)/shard_map/ppermute | solution.py:460
  15.1 8.5 %collective-permute-start.2 = (bf16[1536,384]{1,0:T(8,128)(2,1)S(1)}, bf16[1536,384]{1,0:T(8,128)(2,1)S(1)}, u32[]{:S(2)}, u32[]{:S(2)}) collective-permute-start(bf16[1536,384]{1,0:T(8,128)(2,1)S(1)} %get-tuple-element.48), channel_id=1, source_target_pairs={{0,1},{1,0},{2,3},{3,2},{4,5},{5,4},{6,7},{7,6},{8,9},{9,8},{10,11... | collective-permute-start | bytes 3538952 | tf_op jit(solution)/shard_map/ppermute | solution.py:468
  79.2 22.8 %copy-start = (bf16[1,8,32,384]{3,2,1,0:T(8,128)(2,1)S(1)}, bf16[1,8,32,384]{3,2,1,0:T(8,128)(2,1)}, u32[]{:S(2)}) copy-start(bf16[1,8,32,384]{3,2,1,0:T(8,128)(2,1)} %param.12) | copy-start | bytes 589828
  89.7 14.6 %all-to-all-start.4 = ((bf16[8,112,384]{2,1,0:T(8,128)(2,1)}), bf16[8,112,384]{2,1,0:T(8,128)(2,1)S(1)}, u32[]{:S(2)}, u32[]{:S(2)}) async-start(bf16[8,112,384]{2,1,0:T(8,128)(2,1)} %shard_map.138), calls=%async_computation.4 | async-start | bytes 1376256 | tf_op jit(solution)/shard_map/all_to_all | solution.py:464
  93.9 4.8 %collective-permute-start.3 = (f32[24,384]{1,0:T(8,128)S(1)}, f32[24,384]{1,0:T(8,128)S(1)}, u32[]{:S(2)}, u32[]{:S(2)}) collective-permute-start(f32[24,384]{1,0:T(8,128)S(1)} %get-tuple-element.53), channel_id=1, source_target_pairs={{0,4},{4,8},{8,12},{12,16},{16,20},{20,24},{24,28},{28,32},{32,36}... | collective-permute-start | bytes 110600 | tf_op jit(solution)/shard_map/ppermute | solution.py:455
  97.3 4.7 %collective-permute-start.4 = (f32[24,384]{1,0:T(8,128)S(1)}, f32[24,384]{1,0:T(8,128)S(1)}, u32[]{:S(2)}, u32[]{:S(2)}) collective-permute-start(f32[24,384]{1,0:T(8,128)S(1)} %get-tuple-element.54), channel_id=1, source_target_pairs={{4,0},{8,4},{12,8},{16,12},{20,16},{24,20},{28,24},{32,28},{36,32}... | collective-permute-start | bytes 110600 | tf_op jit(solution)/shard_map/ppermute | solution.py:460
  104.3 10.7 %collective-permute-start.5 = (bf16[8,112,384]{2,1,0:T(8,128)(2,1)S(1)}, bf16[8,112,384]{2,1,0:T(8,128)(2,1)S(1)}, u32[]{:S(2)}, u32[]{:S(2)}) collective-permute-start(bf16[8,112,384]{2,1,0:T(8,128)(2,1)S(1)} %all-to-all-done.4.own), channel_id=1, source_target_pairs={{0,1},{1,0},{2,3},{3,2},{4,5},{5,4},{6,7},{7,6},{8,9},{9,8},{10,11... | collective-permute-start | bytes 2064392 | tf_op jit(solution)/shard_map/ppermute | solution.py:468

commit v11 on v10

--- a/solution.py
+++ b/solution.py
@@ -17,16 +17,15 @@
 CHUNK = 32
 ROWS = 3
 EDGE = 4 * SIDE
-TAIL = 16
 EPSILON = 1e-06
 VMEM_LIMIT = 16 * 1024 * 1024
 NT = (((1,), (1,)), ((), ()))
 
-TILE = ("zh", "xh", "xl", "yh", "yl")
+TILE = ("zh", "xh", "xl", "y2", "y1", "yl")
 CUBE = ("xl", "yl", "zl")
-LINE = ("zh",)
-PLANE = ("xh", "yh")
-EVERY = ("zh", "xh", "xl", "yh", "yl", "zl", "c")
+FOUR = ("xh", "y1")
+EIGHT = ("zh", "y2")
+EVERY = ("zh", "xh", "xl", "y2", "y1", "yl", "zl", "c")
 SWAP = [(0, 1), (1, 0)]
 
 
@@ -183,9 +182,14 @@
     other = pl.ds(pl.multiple_of((1 - core) * half, half), half)
     own = pl.ds(pl.multiple_of(core * half, half), half)
     sent[:half, :] = matmul(hidden[other, :], out_grad[...]).astype(jnp.bfloat16)
-    sent[half:, :] = matmul(grad_pre[other, :], normed[...]).astype(jnp.bfloat16)
     kept[:half, :] = matmul(hidden[own, :], out_grad[...])
-    kept[half:, :] = matmul(grad_pre[own, :], normed[...])
+    run = 64 * ROWS
+    for i in range(half // run):
+        place = half + i * run
+        start = pl.multiple_of((2 * i + 1 - core) * run, run)
+        sent[place : place + run, :] = matmul(grad_pre[pl.ds(start, run), :], normed[...]).astype(jnp.bfloat16)
+        start = pl.multiple_of((2 * i + core) * run, run)
+        kept[place : place + run, :] = matmul(grad_pre[pl.ds(start, run), :], normed[...])
 
 
 def back_kernel(grad_pre, w_in, standard, inverse, vectors, grad_conv, low_edge, high_edge):
@@ -226,16 +230,18 @@
         part = slice(m * rows, (m + 1) * rows)
         total = kept[part, :] + received[part, :].astype(jnp.float32)
         message[m, :rows, :] = total.astype(jnp.bfloat16)
-    run = 4 * ROWS
-    for bit7, bit6, bit5 in itertools.product(range(2), repeat=3):
-        start = half + (bit7 * 4 + bit6 * 2 + bit5) * rows
-        total = kept[start : start + rows, :] + received[start : start + rows, :].astype(jnp.float32)
-        for bit2 in range(2):
-            runs = [total[(2 * i + bit2) * run : (2 * i + bit2 + 1) * run, :] for i in range(4)]
-            place = rows + bit6 * 4 * run
-            message[bit5 * 4 + bit2 * 2 + bit7, place : place + 4 * run, :] = jnp.concatenate(
-                runs, axis=0
-            ).astype(jnp.bfloat16)
+    run = 2 * ROWS
+    for top, bit5 in itertools.product(range(2), repeat=2):
+        totals = []
+        for i in (2 * top, 2 * top + 1):
+            start = half + (2 * i + bit5) * rows
+            totals.append(kept[start : start + rows, :] + received[start : start + rows, :].astype(jnp.float32))
+        for low in range(4):
+            runs = [
+                total[(4 * i + low) * run : (4 * i + low + 1) * run, :] for total in totals for i in range(4)
+            ]
+            place = rows + top * 8 * run
+            message[bit5 * 4 + low, place : place + 8 * run, :] = jnp.concatenate(runs, axis=0).astype(jnp.bfloat16)
 
 
 def add_members(received):
@@ -245,7 +251,7 @@
     return summed
 
 
-def line_kernel(received, message, total):
+def four_kernel(received, message, total):
     members, rows, width = message.shape
     rows //= 2
     summed = add_members(received)
@@ -254,61 +260,43 @@
         for m in range(members):
             parts = [total[k, m * rows : (m + 1) * rows, :]]
             for r in range(ROWS):
-                start = members * rows + m * ROWS + r
+                start = members * rows + (m % 2) * 2 * ROWS + (m // 2) * ROWS + r
                 parts.append(total[k, pl.ds(start, SIDE, stride=members * ROWS), :])
             message[m, :, lanes] = jnp.concatenate(parts, axis=0).astype(jnp.bfloat16)
 
 
-def plane_kernel(received, message, total, block):
+def eight_kernel(received, message, total, block):
     rows = received.shape[1] // 2
     members = message.shape[0]
     summed = add_members(received)
     for k, lanes in enumerate(lane_blocks(received.shape[2])):
         total[k] = summed[:, lanes]
     block[...] = jnp.zeros_like(block)
+    block[:rows, :] = summed[:rows, :]
     for m in range(members):
         for k, lanes in enumerate(lane_blocks(received.shape[2])):
-            block[:rows, lanes] = total[k, :rows, :]
             block[rows : rows + ROWS, lanes] = total[k, pl.ds(rows + m, ROWS, stride=members), :]
         message[m] = block[...].astype(jnp.bfloat16)
 
 
-def turn_kernel(scale, received, message):
-    finished = (add_members(received) * scale).astype(jnp.bfloat16)
+def turn_kernel(scale, received, message, grad_w_in):
+    finished = add_members(received) * scale
+    rows = message.shape[1]
+    grad_w_in[...] = finished[rows : rows + ROWS, :]
+    whole = finished[:rows, :].astype(jnp.bfloat16)
     for m in range(message.shape[0]):
-        message[m] = finished
-
-
-def unpack_kernel(received, message, block):
-    rows = received.shape[1] - SIDE
-    count = received.shape[0] * rows
-    parts = [received[m].astype(jnp.float32) for m in range(received.shape[0])]
-    block[count:, :] = jnp.zeros_like(block[count:, :])
-    for m, part in enumerate(parts):
-        block[m * rows : (m + 1) * rows, :] = part[:rows, :]
-    for bit1 in range(2):
-        for bit0 in range(2):
-            start = count + bit0 * ROWS
-            block[start : start + ROWS, :] = parts[2 * bit1 + bit0][rows : rows + ROWS, :]
-        whole = block[...].astype(jnp.bfloat16)
-        for m in range(bit1, message.shape[0], 2):
-            message[m] = whole
-
-
-def join_kernel(device, own, other, grad_w_out, grad_w_in):
-    number = device[0]
-    here = number & 1
-    source = ((number >> 5) & 1) * 4 + ((number >> 2) & 1) * 2 + ((number >> 7) & 1)
-    members, rows, width = own.shape
-    count = rows - TAIL
-    half = members * count
-    for core, blocks in ((here, own), (1 - here, other)):
-        for m in range(members):
-            start = pl.multiple_of(core * half + m * count, count)
-            grad_w_out[pl.ds(start, count), :] = blocks[m, :count, :]
-    tails = [blocks[source, count:, :].astype(jnp.float32) for blocks in (own, other)]
-    tail = jnp.where(number >> 8 == here, tails[0], tails[1])
-    grad_w_in[...] = jnp.where(here == 0, tail[:ROWS, :], tail[ROWS : 2 * ROWS, :])
+        message[m] = whole
+
+
+def join_kernel(device, own, other, in_rows, grad_w_out, grad_w_in):
+    core = device[0] & 1
+    grad_w_in[...] = in_rows[...]
+    members, rows, _ = own.shape
+    for place, blocks in ((core, own), (1 - core, other)):
+        for m in range(0, members, 2):
+            pair = [blocks[i].astype(jnp.float32) for i in (m, m + 1)]
+            start = pl.multiple_of((place * members + m) * rows, 2 * rows)
+            grad_w_out[pl.ds(start, 2 * rows), :] = jnp.concatenate(pair, axis=0).astype(jnp.bfloat16)
 
 
 def call(kernel, outs, scratch, scalars, arrays, flops, nbytes, space=pltpu.VMEM):
@@ -404,19 +392,19 @@
     )[0]
 
 
-def to_line(received, members):
+def to_four(received, members):
     _, rows, width = received.shape
     return call(
-        line_kernel, [((members, rows // members, width), B16)],
+        four_kernel, [((members, rows // members, width), B16)],
         [pltpu.VMEM((width // LANES, rows, LANES), F32)], [], [received],
         received.size, 3 * received.size,
     )[0]
 
 
-def to_plane(received, members):
+def to_eight(received, members):
     _, rows, width = received.shape
     return call(
-        plane_kernel,
+        eight_kernel,
         [((members, rows // 2 + SIDE, width), B16)],
         [pltpu.VMEM((width // LANES, rows, LANES), F32), pltpu.VMEM((rows // 2 + SIDE, width), F32)],
         [],
@@ -428,24 +416,16 @@
 def turn(scale, received, members):
     _, rows, width = received.shape
     return call(
-        functools.partial(turn_kernel, scale), [((members, rows, width), B16)], [], [], [received],
+        functools.partial(turn_kernel, scale),
+        [((members, rows - SIDE, width), B16), ((ROWS, width), F32)], [], [], [received],
         received.size, 4 * received.size,
-    )[0]
-
-
-def unpack(received, members):
-    count, rows, width = received.shape
-    rows = count * (rows - SIDE) + TAIL
-    return call(
-        unpack_kernel, [((members, rows, width), B16)], [pltpu.VMEM((rows, width), F32)], [], [received],
-        received.size, 10 * received.size,
-    )[0]
-
-
-def join(device, own, other):
+    )
+
+
+def join(device, own, other, in_rows):
     members, rows, width = own.shape
     return call(
-        join_kernel, [((2 * members * (rows - TAIL), width), B16), ((ROWS, width), F32)], [], [device], [own, other],
+        join_kernel, [((2 * members * rows, width), B16), (in_rows.shape, F32)], [], [device], [own, other, in_rows],
         own.size, 8 * own.size,
     )
 
@@ -479,7 +459,7 @@
     upstream = cotangent[0].reshape(-1, channels)
     device = lax.axis_index(EVERY).astype(jnp.int32).reshape(1)
     sizes = {axis: lax.axis_size(axis) for axis in EVERY}
-    cube, line, plane = (math.prod(sizes[axis] for axis in axes) for axes in (CUBE, LINE, PLANE))
+    cube, four, eight = (math.prod(sizes[axis] for axis in axes) for axes in (CUBE, FOUR, EIGHT))
     scale = 1.0 / math.sqrt(height * breadth * math.prod(sizes.values()))
 
     conv, out_grad, back, w_in_t, b_cols, w_in_here, taps, vectors = before_halos(
@@ -491,20 +471,23 @@
     grad_conv, low, high = to_conv(grad_pre, w_in_here, standard, inverse, vectors)
     kept, low, high = lax.optimization_barrier((kept, low, high))
     received = exchange(to_cube(cube, kept, swap(sent)), CUBE)
-    received = exchange(to_line(received, line), LINE)
-    received = exchange(to_plane(received, plane), PLANE)
-    received = exchange(turn(scale, received, line), LINE)
+    low, high = from_left(high), from_right(low)
     received, low, high = lax.optimization_barrier((received, low, high))
-    low, high = from_left(high), from_right(low)
-    own = exchange(unpack(received, cube), CUBE)
+    received = exchange(to_four(received, four), FOUR)
+    received = exchange(to_eight(received, eight), EIGHT)
+    message, in_rows = turn(scale, received, cube * four)
+    own = exchange(message, CUBE + FOUR)
+    pairs = [(2 * xh + c, 2 * c + xh) for xh in range(2) for c in range(2)]
+    in_rows = lax.ppermute(in_rows, ("xh", "c"), pairs)
+    message, low, high = lax.optimization_barrier((message, low, high))
     grad_image = to_features(grad_conv, low, high, taps, upstream)
-    own, grad_image = lax.optimization_barrier((own, grad_image))
-    grad_w_out, grad_w_in = join(device, own, swap(own))
+    own, in_rows, grad_image = lax.optimization_barrier((own, in_rows, grad_image))
+    grad_w_out, grad_w_in = join(device, own, swap(own), in_rows)
     return (grad_image.reshape(1, height, breadth, channels), grad_w_in, grad_w_out)
 
 
 def solution(mesh):
-    fine = jax.sharding.Mesh(mesh.devices.reshape(4, 2, 2, 4, 2, 2, 2), EVERY)
+    fine = jax.sharding.Mesh(mesh.devices.reshape(4, 2, 2, 2, 2, 2, 2, 2), EVERY)
     band = P(("zl", "c"), None, TILE, None)
     placed = (band, band) + (P(),) * 8 + (P(("zl", "c"), TILE),)
     return jax.shard_map(

time: 118 us -> 115 us (0.975)
  blocking collectives: 64.5 us -> 39.6 us
  starting transfers between devices: 29.2 us -> 42.2 us
  waiting for transfers between devices: 6.93 us -> 15.7 us
    all_to_all x4 -> x2, blocking collectives: 64.5 us -> 39.6 us  [exchange(): return lax.all_to_all(blocks, axes, split_axis=0, concat_axis=0, tiled=True)]
    ppermute x2, waiting for transfers between devices: 0.15 us -> 10.2 us  [from_left(): return lax.ppermute(block, TILE, [(i, i + 1) for i in range(count - 1)])]
    ppermute x0 -> x1, starting transfers between devices: none -> 9.69 us  [body(): in_rows = lax.ppermute(in_rows, ('xh', 'c'), pairs)]
    all_to_all x1 -> x2, starting transfers between devices: 4.24 us -> 8.19 us  [exchange(): return lax.all_to_all(blocks, axes, split_axis=0, concat_axis=0, tiled=True)]
    ppermute x2, waiting for transfers between devices: 3.26 us -> 0.55 us  [from_right(): return lax.ppermute(block, TILE, [(i + 1, i) for i in range(count - 1)])]
    all_to_all x1 -> x2, waiting for transfers between devices: 0.01 us -> 1.58 us  [exchange(): return lax.all_to_all(blocks, axes, split_axis=0, concat_axis=0, tiled=True)]
    pallas_call x11 -> x10, Pallas kernels: 14.7 us -> 15.7 us  [call(): pl.pallas_call(kernel, out_shape=[jax.ShapeDtypeStruct(shape, kind) for s...]
  transfers between devices with their start and end apart: 7 -> 9, of which waited for: 4 -> 5; matrix products, arithmetic and copies ran while one was open for 0% -> 0% of each run, Pallas kernels for 6% -> 6%
where the time goes in v11:
time: 115 us; the launch traced here: 114 us
  starting transfers between devices  42.2 us (37%)
  blocking collectives  39.6 us (34%)
  Pallas kernels  15.7 us (14%)
  waiting for transfers between devices  15.7 us (14%)
    all_to_all x2, blocking collectives, exchange(): return lax.all_to_all(blocks, axes, split_axis=0, concat_axis=0, tiled=True)  39.6 us
    pallas_call x10, Pallas kernels, call(): pl.pallas_call(kernel, out_shape=[jax.ShapeDtypeStruct(shape, kind) for s...  15.7 us
    ppermute x2, starting transfers between devices, swap(): return lax.ppermute(block, 'c', SWAP)  14.2 us
    ppermute x2, waiting for transfers between devices, from_left(): return lax.ppermute(block, TILE, [(i, i + 1) for i in range(count - 1)])  10.2 us
    ppermute x1, starting transfers between devices, body(): in_rows = lax.ppermute(in_rows, ('xh', 'c'), pairs)  9.69 us
    all_to_all x2, starting transfers between devices, exchange(): return lax.all_to_all(blocks, axes, split_axis=0, concat_axis=0, tiled=True)  8.19 us
    ppermute x2, starting transfers between devices, from_left(): return lax.ppermute(block, TILE, [(i, i + 1) for i in range(count - 1)])  7.53 us
    ppermute x2, waiting for transfers between devices, swap(): return lax.ppermute(block, 'c', SWAP)  3.38 us
  transfers between devices with their start and end apart: 9, of which 5 were waited for; matrix products, arithmetic and copies ran while one was open for 0% of the time, Pallas kernels for 6%

profile of v11, /device:TPU:1, one launch (start us, length us, event | category | flops | bytes accessed | tf_op | source)
XLA Modules:
  0.0 114.0 jit_solution(16797610978591855165)
XLA Ops:
  0.6 1.0 shard_map.131
  1.6 4.0 %collective-permute-start = (bf16[32,384]{1,0:T(8,128)(2,1)S(1)}, bf16[32,384]{1,0:T(8,128)(2,1)S(1)}, u32[]{:S(2)}, u32[]{:S(2)}) collective-permute-start(bf16[32,384]{1,0:T(8,128)(2,1)S(1)} %get-tuple-element.37), channel_id=1, source_target_pairs={{0,4},{4,8},{8,12},{12,16},{16,20},{20,24},{24,28},{28,32},{32,36}... | collective-permute-start | bytes 73736 | tf_op jit(solution)/shard_map/ppermute | solution.py:435
  5.7 1.3 %collective-permute-start.1 = (bf16[32,384]{1,0:T(8,128)(2,1)S(1)}, bf16[32,384]{1,0:T(8,128)(2,1)S(1)}, u32[]{:S(2)}, u32[]{:S(2)}) collective-permute-start(bf16[32,384]{1,0:T(8,128)(2,1)S(1)} %get-tuple-element.38), channel_id=1, source_target_pairs={{4,0},{8,4},{12,8},{16,12},{20,16},{24,20},{28,24},{32,28},{36,32}... | collective-permute-start | bytes 73736 | tf_op jit(solution)/shard_map/ppermute | solution.py:440
  7.0 4.4 %shard_map.130 = (f32[256,384]{1,0:T(8,128)S(1)}, bf16[256,384]{1,0:T(8,128)(2,1)S(1)}, f32[1536,256]{1,0:T(8,128)S(1)}, bf16[1536,384]{1,0:T(8,128)(2,1)S(1)}, ...) custom-call(s32[1,4]{1,0:T(1,128)} %flags.1, ...), custom_call_target="tpu_custom_call" | custom-call | flops 301989888 | bytes 8388608 | tf_op jit(solution)/shard_map/pallas_call | solution.py:307
  11.4 0.0 collective-permute-done.low
  11.4 0.0 collective-permute-done.1.high
  11.4 3.7 %shard_map.132 = (f32[1536,384]{1,0:T(8,128)S(1)}, bf16[1536,384]{1,0:T(8,128)(2,1)S(1)}, f32[256,384]{1,0:T(8,128)S(1)}, f32[256,128]{1,0:T(8,128)S(1)}, bf16[1536,256]{1,0:T(8,128)(2,1)S(1)}) custom-call(s32[1]{0:T(128)} %bitcast.device, f32[256,384]{1,0:T(8,128)S(1)} %get-tuple-element.36.conv, bf16[32,384]{1,0:T(8,128)(2,1)S(1)} %collective-permute-done.low, ...), custom_call_target="tpu_custom_call" | custom-call | flops 905969664 | bytes 12582912 | tf_op jit(solution)/shard_map/pallas_call | solution.py:307
  15.1 6.1 %collective-permute-start.2 = (bf16[1536,384]{1,0:T(8,128)(2,1)S(1)}, bf16[1536,384]{1,0:T(8,128)(2,1)S(1)}, u32[]{:S(2)}, u32[]{:S(2)}) collective-permute-start(bf16[1536,384]{1,0:T(8,128)(2,1)S(1)} %get-tuple-element.53), channel_id=1, source_target_pairs={{0,1},{1,0},{2,3},{3,2},{4,5},{5,4},{6,7},{7,6},{8,9},{9,8},{10,11... | collective-permute-start | bytes 3538952 | tf_op jit(solution)/shard_map/ppermute | solution.py:448
  21.2 0.7 shard_map.133
  21.9 1.8 %collective-permute-done.2.received = bf16[1536,384]{1,0:T(8,128)(2,1)S(1)} collective-permute-done((bf16[1536,384]{1,0:T(8,128)(2,1)S(1)}, bf16[1536,384]{1,0:T(8,128)(2,1)S(1)}, u32[]{:S(2)}, u32[]{:S(2)}) %collective-permute-start.2) | collective-permute-done | bytes 1179680 | tf_op jit(solution)/shard_map/ppermute | solution.py:448
  23.6 1.4 %shard_map.134 = bf16[8,192,384]{2,1,0:T(8,128)(2,1)} custom-call(f32[1536,384]{1,0:T(8,128)S(1)} %get-tuple-element.52.kept, bf16[1536,384]{1,0:T(8,128)(2,1)S(1)} %collective-permute-done.2.received), custom_call_target="tpu_custom_call" | custom-call | flops 1179648 | bytes 4718592 | tf_op jit(solution)/shard_map/pallas_call | solution.py:307
  25.0 4.3 %all-to-all-start = ((bf16[8,192,384]{2,1,0:T(8,128)(2,1)}), bf16[8,192,384]{2,1,0:T(8,128)(2,1)S(1)}, u32[]{:S(2)}, u32[]{:S(2)}) async-start(bf16[8,192,384]{2,1,0:T(8,128)(2,1)} %shard_map.134), calls=%async_computation | async-start | bytes 2359296 | tf_op jit(solution)/shard_map/all_to_all | solution.py:444
  29.3 3.5 %collective-permute-start.3 = (f32[24,384]{1,0:T(8,128)S(1)}, f32[24,384]{1,0:T(8,128)S(1)}, u32[]{:S(2)}, u32[]{:S(2)}) collective-permute-start(f32[24,384]{1,0:T(8,128)S(1)} %get-tuple-element.54), channel_id=1, source_target_pairs={{0,4},{4,8},{8,12},{12,16},{16,20},{20,24},{24,28},{28,32},{32,36}... | collective-permute-start | bytes 110600 | tf_op jit(solution)/shard_map/ppermute | solution.py:435
  32.8 1.3 %collective-permute-start.4 = (f32[24,384]{1,0:T(8,128)S(1)}, f32[24,384]{1,0:T(8,128)S(1)}, u32[]{:S(2)}, u32[]{:S(2)}) collective-permute-start(f32[24,384]{1,0:T(8,128)S(1)} %get-tuple-element.55), channel_id=1, source_target_pairs={{4,0},{8,4},{12,8},{16,12},{20,16},{24,20},{28,24},{32,28},{36,32}... | collective-permute-start | bytes 110600 | tf_op jit(solution)/shard_map/ppermute | solution.py:440
  34.1 10.2 %collective-permute-done.3.low = f32[24,384]{1,0:T(8,128)S(1)} collective-permute-done((f32[24,384]{1,0:T(8,128)S(1)}, f32[24,384]{1,0:T(8,128)S(1)}, u32[]{:S(2)}, u32[]{:S(2)}) %collective-permute-start.3) | collective-permute-done | bytes 36896 | tf_op jit(solution)/shard_map/ppermute | solution.py:435
  44.3 0.5 collective-permute-done.4.high
  44.8 1.6 %all-to-all-done.received = bf16[8,192,384]{2,1,0:T(8,128)(2,1)S(1)} async-done(((bf16[8,192,384]{2,1,0:T(8,128)(2,1)}), bf16[8,192,384]{2,1,0:T(8,128)(2,1)S(1)}, u32[]{:S(2)}, u32[]{:S(2)}) %all-to-all-start) | async-done | bytes 1179680 | tf_op jit(solution)/shard_map/all_to_all | solution.py:444
  46.4 0.2 shard_map.135
  46.6 0.0 copy-start
  46.6 13.5 %all_to_all.20.received = bf16[4,48,384]{2,1,0:T(8,128)(2,1)S(1)} all-to-all(bf16[4,48,384]{2,1,0:T(8,128)(2,1)S(1)} %shard_map.135), channel_id=1, replica_groups=mesh['zh'=4,'xh'=2,'xl'=2,'y2'=2,'y1'=2,'yl'=2,'zl'=2,'c'=2] {'xh','y1'}, dimensions={0} | all-to-all | bytes 294912 | tf_op jit(solution)/shard_map/all_to_all | solution.py:444
  60.1 0.1 shard_map.136
  60.2 26.2 %all_to_all.21.received = bf16[8,32,384]{2,1,0:T(8,128)(2,1)S(1)} all-to-all(bf16[8,32,384]{2,1,0:T(8,128)(2,1)S(1)} %shard_map.136), channel_id=1, replica_groups=mesh['zh'=4,'xh'=2,'xl'=2,'y2'=2,'y1'=2,'yl'=2,'zl'=2,'c'=2] {'zh','y2'}, dimensions={0} | all-to-all | bytes 393216 | tf_op jit(solution)/shard_map/all_to_all | solution.py:444
  86.4 0.9 shard_map.137
  87.2 3.9 %all-to-all-start.3 = ((bf16[32,24,384]{2,1,0:T(8,128)(2,1)}), bf16[32,24,384]{2,1,0:T(8,128)(2,1)S(1)}, u32[]{:S(2)}, u32[]{:S(2)}) async-start(bf16[32,24,384]{2,1,0:T(8,128)(2,1)} %get-tuple-element.57), calls=%async_computation.3 | async-start | bytes 1179648 | tf_op jit(solution)/shard_map/all_to_all | solution.py:444
  91.1 9.7 %collective-permute-start.5 = (f32[3,384]{1,0:T(4,128)S(1)}, f32[3,384]{1,0:T(4,128)S(1)}, u32[]{:S(2)}, u32[]{:S(2)}) collective-permute-start(f32[3,384]{1,0:T(4,128)S(1)} %get-tuple-element.58), channel_id=1, source_target_pairs={{0,0},{1,64},{64,1},{65,65},{2,2},{3,66},{66,3},{67,67},{4,4},{5,6... | collective-permute-start | bytes 13832 | tf_op jit(solution)/shard_map/ppermute | solution.py:481
  100.8 0.0 copy-done
  100.8 2.3 %shard_map.138 = bf16[256,384]{1,0:T(8,128)(2,1)} custom-call(f32[256,384]{1,0:T(8,128)S(1)} %get-tuple-element.59.grad_conv, f32[24,384]{1,0:T(8,128)S(1)} %collective-permute-done.3.low, f32[24,384]{1,0:T(8,128)S(1)} %collective-permute-done.4.high, f32[7,7,384]{2,1,0:T(8,128)S(1)} %get-tuple-element.39.taps, bf16[256,384]{1,0:T(8,128)(2,1)S(1)} %bitcast.5), custom_call_target="tpu_custom_call" | custom-call | flops 9633792 | bytes 2097152 | tf_op jit(solution)/shard_map/pallas_call | solution.py:307
  103.1 0.0 collective-permute-done.5.in_rows
  103.1 0.0 all-to-all-done.3.own
  103.1 8.1 %collective-permute-start.6 = (bf16[32,24,384]{2,1,0:T(8,128)(2,1)S(1)}, bf16[32,24,384]{2,1,0:T(8,128)(2,1)S(1)}, u32[]{:S(2)}, u32[]{:S(2)}) collective-permute-start(bf16[32,24,384]{2,1,0:T(8,128)(2,1)S(1)} %all-to-all-done.3.own), channel_id=1, source_target_pairs={{0,1},{1,0},{2,3},{3,2},{4,5},{5,4},{6,7},{7,6},{8,9},{9,8},{10,11... | collective-permute-start | bytes 1769480 | tf_op jit(solution)/shard_map/ppermute | solution.py:448
  111.3 1.6 %collective-permute-done.6.other = bf16[32,24,384]{2,1,0:T(8,128)(2,1)S(1)} collective-permute-done((bf16[32,24,384]{2,1,0:T(8,128)(2,1)S(1)}, bf16[32,24,384]{2,1,0:T(8,128)(2,1)S(1)}, u32[]{:S(2)}, u32[]{:S(2)}) %collective-permute-start.6) | collective-permute-done | bytes 589856 | tf_op jit(solution)/shard_map/ppermute | solution.py:448
  112.9 1.1 shard_map.139
Async XLA Ops:
  1.6 9.8 %collective-permute-start = (bf16[32,384]{1,0:T(8,128)(2,1)S(1)}, bf16[32,384]{1,0:T(8,128)(2,1)S(1)}, u32[]{:S(2)}, u32[]{:S(2)}) collective-permute-start(bf16[32,384]{1,0:T(8,128)(2,1)S(1)} %get-tuple-element.37), channel_id=1, source_target_pairs={{0,4},{4,8},{8,12},{12,16},{16,20},{20,24},{24,28},{28,32},{32,36}... | collective-permute-start | bytes 73736 | tf_op jit(solution)/shard_map/ppermute | solution.py:435
  5.7 5.7 %collective-permute-start.1 = (bf16[32,384]{1,0:T(8,128)(2,1)S(1)}, bf16[32,384]{1,0:T(8,128)(2,1)S(1)}, u32[]{:S(2)}, u32[]{:S(2)}) collective-permute-start(bf16[32,384]{1,0:T(8,128)(2,1)S(1)} %get-tuple-element.38), channel_id=1, source_target_pairs={{4,0},{8,4},{12,8},{16,12},{20,16},{24,20},{28,24},{32,28},{36,32}... | collective-permute-start | bytes 73736 | tf_op jit(solution)/shard_map/ppermute | solution.py:440
  15.1 8.5 %collective-permute-start.2 = (bf16[1536,384]{1,0:T(8,128)(2,1)S(1)}, bf16[1536,384]{1,0:T(8,128)(2,1)S(1)}, u32[]{:S(2)}, u32[]{:S(2)}) collective-permute-start(bf16[1536,384]{1,0:T(8,128)(2,1)S(1)} %get-tuple-element.53), channel_id=1, source_target_pairs={{0,1},{1,0},{2,3},{3,2},{4,5},{5,4},{6,7},{7,6},{8,9},{9,8},{10,11... | collective-permute-start | bytes 3538952 | tf_op jit(solution)/shard_map/ppermute | solution.py:448
  25.0 21.4 %all-to-all-start = ((bf16[8,192,384]{2,1,0:T(8,128)(2,1)}), bf16[8,192,384]{2,1,0:T(8,128)(2,1)S(1)}, u32[]{:S(2)}, u32[]{:S(2)}) async-start(bf16[8,192,384]{2,1,0:T(8,128)(2,1)} %shard_map.134), calls=%async_computation | async-start | bytes 2359296 | tf_op jit(solution)/shard_map/all_to_all | solution.py:444
  29.3 15.0 %collective-permute-start.3 = (f32[24,384]{1,0:T(8,128)S(1)}, f32[24,384]{1,0:T(8,128)S(1)}, u32[]{:S(2)}, u32[]{:S(2)}) collective-permute-start(f32[24,384]{1,0:T(8,128)S(1)} %get-tuple-element.54), channel_id=1, source_target_pairs={{0,4},{4,8},{8,12},{12,16},{16,20},{20,24},{24,28},{28,32},{32,36}... | collective-permute-start | bytes 110600 | tf_op jit(solution)/shard_map/ppermute | solution.py:435
  32.8 12.0 %collective-permute-start.4 = (f32[24,384]{1,0:T(8,128)S(1)}, f32[24,384]{1,0:T(8,128)S(1)}, u32[]{:S(2)}, u32[]{:S(2)}) collective-permute-start(f32[24,384]{1,0:T(8,128)S(1)} %get-tuple-element.55), channel_id=1, source_target_pairs={{4,0},{8,4},{12,8},{16,12},{20,16},{24,20},{28,24},{32,28},{36,32}... | collective-permute-start | bytes 110600 | tf_op jit(solution)/shard_map/ppermute | solution.py:440
  46.6 54.2 %copy-start = (bf16[1,8,32,384]{3,2,1,0:T(8,128)(2,1)S(1)}, bf16[1,8,32,384]{3,2,1,0:T(8,128)(2,1)}, u32[]{:S(2)}) copy-start(bf16[1,8,32,384]{3,2,1,0:T(8,128)(2,1)} %param.12) | copy-start | bytes 589828
  87.2 15.9 %all-to-all-start.3 = ((bf16[32,24,384]{2,1,0:T(8,128)(2,1)}), bf16[32,24,384]{2,1,0:T(8,128)(2,1)S(1)}, u32[]{:S(2)}, u32[]{:S(2)}) async-start(bf16[32,24,384]{2,1,0:T(8,128)(2,1)} %get-tuple-element.57), calls=%async_computation.3 | async-start | bytes 1179648 | tf_op jit(solution)/shard_map/all_to_all | solution.py:444
  91.1 12.0 %collective-permute-start.5 = (f32[3,384]{1,0:T(4,128)S(1)}, f32[3,384]{1,0:T(4,128)S(1)}, u32[]{:S(2)}, u32[]{:S(2)}) collective-permute-start(f32[3,384]{1,0:T(4,128)S(1)} %get-tuple-element.58), channel_id=1, source_target_pairs={{0,0},{1,64},{64,1},{65,65},{2,2},{3,66},{66,3},{67,67},{4,4},{5,6... | collective-permute-start | bytes 13832 | tf_op jit(solution)/shard_map/ppermute | solution.py:481
  103.1 9.8 %collective-permute-start.6 = (bf16[32,24,384]{2,1,0:T(8,128)(2,1)S(1)}, bf16[32,24,384]{2,1,0:T(8,128)(2,1)S(1)}, u32[]{:S(2)}, u32[]{:S(2)}) collective-permute-start(bf16[32,24,384]{2,1,0:T(8,128)(2,1)S(1)} %all-to-all-done.3.own), channel_id=1, source_target_pairs={{0,1},{1,0},{2,3},{3,2},{4,5},{5,4},{6,7},{7,6},{8,9},{9,8},{10,11... | collective-permute-start | bytes 1769480 | tf_op jit(solution)/shard_map/ppermute | solution.py:448

commit v12 on v11

--- a/solution.py
+++ b/solution.py
@@ -116,8 +116,8 @@
     copies[4].wait()
     copies[5].wait()
     widen(image, wide)
-    for k, lanes in enumerate(lane_blocks(width)):
-        for t in range(COLS // SIDE):
+    def convolve_tile(t):
+        for k, lanes in enumerate(lane_blocks(width)):
             columns = []
             for j in range(t * SIDE - HALO, (t + 1) * SIDE + HALO):
                 inside = 0 <= j < COLS
@@ -125,6 +125,15 @@
             for j, total in enumerate(convolve(columns, taps_here, lanes, False)):
                 start = (t * SIDE + j) * SIDE
                 conv[start : start + SIDE, lanes] = total
+
+    for t in range(COLS // SIDE):
+        tissue = flags_here[0, t] != 0
+        pl.when(tissue)(functools.partial(convolve_tile, t))
+
+        @pl.when(jnp.logical_not(tissue))
+        def _(t=t):
+            conv[t * rows : (t + 1) * rows, :] = jnp.zeros((rows, width), jnp.float32)
+
     for copy in copies[6:]:
         copy.wait()
     hidden = w_in.shape[1]
@@ -471,10 +480,11 @@
     grad_conv, low, high = to_conv(grad_pre, w_in_here, standard, inverse, vectors)
     kept, low, high = lax.optimization_barrier((kept, low, high))
     received = exchange(to_cube(cube, kept, swap(sent)), CUBE)
+    received = exchange(to_four(received, four), FOUR)
+    received, low, high = lax.optimization_barrier((received, low, high))
+    received = exchange(to_eight(received, eight), EIGHT)
     low, high = from_left(high), from_right(low)
     received, low, high = lax.optimization_barrier((received, low, high))
-    received = exchange(to_four(received, four), FOUR)
-    received = exchange(to_eight(received, eight), EIGHT)
     message, in_rows = turn(scale, received, cube * four)
     own = exchange(message, CUBE + FOUR)
     pairs = [(2 * xh + c, 2 * c + xh) for xh in range(2) for c in range(2)]

time: 115 us -> 116 us (level)
  the two profiles are of different devices: /device:TPU:1 before, /device:TPU:177 now
where the time goes in v12:
time: 116 us; the launch traced here: 115 us
  starting transfers between devices  55.3 us (48%)
  blocking collectives  38.2 us (33%)
  Pallas kernels  14.7 us (13%)
  waiting for transfers between devices  6.17 us (5%)
    all_to_all x2, blocking collectives, exchange(): return lax.all_to_all(blocks, axes, split_axis=0, concat_axis=0, tiled=True)  38.2 us
    all_to_all x2, starting transfers between devices, exchange(): return lax.all_to_all(blocks, axes, split_axis=0, concat_axis=0, tiled=True)  24 us
    pallas_call x10, Pallas kernels, call(): pl.pallas_call(kernel, out_shape=[jax.ShapeDtypeStruct(shape, kind) for s...  14.7 us
    ppermute x2, starting transfers between devices, swap(): return lax.ppermute(block, 'c', SWAP)  10.4 us
    ppermute x1, starting transfers between devices, body(): in_rows = lax.ppermute(in_rows, ('xh', 'c'), pairs)  10.4 us
    ppermute x2, starting transfers between devices, from_right(): return lax.ppermute(block, TILE, [(i + 1, i) for i in range(count - 1)])  6.12 us
    ppermute x2, starting transfers between devices, from_left(): return lax.ppermute(block, TILE, [(i, i + 1) for i in range(count - 1)])  4.43 us
    ppermute x2, waiting for transfers between devices, swap(): return lax.ppermute(block, 'c', SWAP)  3.38 us
  transfers between devices with their start and end apart: 9, of which 4 were waited for; matrix products, arithmetic and copies ran while one was open for 0% of the time, Pallas kernels for 6%

profile of v12, /device:TPU:177, one launch (start us, length us, event | category | flops | bytes accessed | tf_op | source)
XLA Modules:
  0.0 115.1 jit_solution(7939404604597864226)
XLA Ops:
  0.6 1.0 shard_map.131
  1.6 2.3 %collective-permute-start = (bf16[32,384]{1,0:T(8,128)(2,1)S(1)}, bf16[32,384]{1,0:T(8,128)(2,1)S(1)}, u32[]{:S(2)}, u32[]{:S(2)}) collective-permute-start(bf16[32,384]{1,0:T(8,128)(2,1)S(1)} %get-tuple-element.40), channel_id=1, source_target_pairs={{0,4},{4,8},{8,12},{12,16},{16,20},{20,24},{24,28},{28,32},{32,36}... | collective-permute-start | bytes 73736 | tf_op jit(solution)/shard_map/ppermute | solution.py:444
  4.0 3.0 %collective-permute-start.1 = (bf16[32,384]{1,0:T(8,128)(2,1)S(1)}, bf16[32,384]{1,0:T(8,128)(2,1)S(1)}, u32[]{:S(2)}, u32[]{:S(2)}) collective-permute-start(bf16[32,384]{1,0:T(8,128)(2,1)S(1)} %get-tuple-element.41), channel_id=1, source_target_pairs={{4,0},{8,4},{12,8},{16,12},{20,16},{24,20},{28,24},{32,28},{36,32}... | collective-permute-start | bytes 73736 | tf_op jit(solution)/shard_map/ppermute | solution.py:449
  7.0 3.6 %shard_map.130 = (f32[256,384]{1,0:T(8,128)S(1)}, bf16[256,384]{1,0:T(8,128)(2,1)S(1)}, f32[1536,256]{1,0:T(8,128)S(1)}, bf16[1536,384]{1,0:T(8,128)(2,1)S(1)}, ...) custom-call(s32[1,4]{1,0:T(1,128)} %flags.1, ...), custom_call_target="tpu_custom_call" | custom-call | flops 301989888 | bytes 8388608 | tf_op jit(solution)/shard_map/pallas_call | solution.py:316
  10.6 0.0 collective-permute-done.low
  10.6 0.0 collective-permute-done.1.high
  10.6 3.7 %shard_map.132 = (f32[1536,384]{1,0:T(8,128)S(1)}, bf16[1536,384]{1,0:T(8,128)(2,1)S(1)}, f32[256,384]{1,0:T(8,128)S(1)}, f32[256,128]{1,0:T(8,128)S(1)}, bf16[1536,256]{1,0:T(8,128)(2,1)S(1)}) custom-call(s32[1]{0:T(128)} %bitcast.device, f32[256,384]{1,0:T(8,128)S(1)} %get-tuple-element.39.conv, bf16[32,384]{1,0:T(8,128)(2,1)S(1)} %collective-permute-done.low, ...), custom_call_target="tpu_custom_call" | custom-call | flops 905969664 | bytes 12582912 | tf_op jit(solution)/shard_map/pallas_call | solution.py:316
  14.3 3.5 %collective-permute-start.2 = (bf16[1536,384]{1,0:T(8,128)(2,1)S(1)}, bf16[1536,384]{1,0:T(8,128)(2,1)S(1)}, u32[]{:S(2)}, u32[]{:S(2)}) collective-permute-start(bf16[1536,384]{1,0:T(8,128)(2,1)S(1)} %get-tuple-element.56), channel_id=1, source_target_pairs={{0,1},{1,0},{2,3},{3,2},{4,5},{5,4},{6,7},{7,6},{8,9},{9,8},{10,11... | collective-permute-start | bytes 3538952 | tf_op jit(solution)/shard_map/ppermute | solution.py:457
  17.9 0.7 shard_map.133
  18.5 1.8 %collective-permute-done.2.received = bf16[1536,384]{1,0:T(8,128)(2,1)S(1)} collective-permute-done((bf16[1536,384]{1,0:T(8,128)(2,1)S(1)}, bf16[1536,384]{1,0:T(8,128)(2,1)S(1)}, u32[]{:S(2)}, u32[]{:S(2)}) %collective-permute-start.2) | collective-permute-done | bytes 1179680 | tf_op jit(solution)/shard_map/ppermute | solution.py:457
  20.3 0.4 shard_map.134
  20.7 20.7 %all_to_all.20.received = bf16[8,192,384]{2,1,0:T(8,128)(2,1)S(1)} all-to-all(bf16[8,192,384]{2,1,0:T(8,128)(2,1)S(1)} %shard_map.134), channel_id=1, replica_groups=mesh['zh'=4,'xh'=2,'xl'=2,'y2'=2,'y1'=2,'yl'=2,'zl'=2,'c'=2] {'xl','yl',..., dimensions={0} | all-to-all | bytes 2359296 | tf_op jit(solution)/shard_map/all_to_all | solution.py:453
  41.3 0.2 shard_map.135
  41.6 0.0 copy-start
  41.6 17.5 %all_to_all.21.received = bf16[4,48,384]{2,1,0:T(8,128)(2,1)S(1)} all-to-all(bf16[4,48,384]{2,1,0:T(8,128)(2,1)S(1)} %shard_map.135), channel_id=1, replica_groups=mesh['zh'=4,'xh'=2,'xl'=2,'y2'=2,'y1'=2,'yl'=2,'zl'=2,'c'=2] {'xh','y1'}, dimensions={0} | all-to-all | bytes 294912 | tf_op jit(solution)/shard_map/all_to_all | solution.py:453
  59.1 0.8 shard_map.136
  59.8 9.1 %all-to-all-start.2 = ((bf16[8,32,384]{2,1,0:T(8,128)(2,1)}), bf16[8,32,384]{2,1,0:T(8,128)(2,1)S(1)}, u32[]{:S(2)}, u32[]{:S(2)}) async-start(bf16[8,32,384]{2,1,0:T(8,128)(2,1)} %shard_map.136), calls=%async_computation.2 | async-start | bytes 393216 | tf_op jit(solution)/shard_map/all_to_all | solution.py:453
  68.9 2.1 %collective-permute-start.3 = (f32[24,384]{1,0:T(8,128)S(1)}, f32[24,384]{1,0:T(8,128)S(1)}, u32[]{:S(2)}, u32[]{:S(2)}) collective-permute-start(f32[24,384]{1,0:T(8,128)S(1)} %get-tuple-element.60), channel_id=1, source_target_pairs={{0,4},{4,8},{8,12},{12,16},{16,20},{20,24},{24,28},{28,32},{32,36}... | collective-permute-start | bytes 110600 | tf_op jit(solution)/shard_map/ppermute | solution.py:444
  71.0 3.1 %collective-permute-start.4 = (f32[24,384]{1,0:T(8,128)S(1)}, f32[24,384]{1,0:T(8,128)S(1)}, u32[]{:S(2)}, u32[]{:S(2)}) collective-permute-start(f32[24,384]{1,0:T(8,128)S(1)} %get-tuple-element.61), channel_id=1, source_target_pairs={{4,0},{8,4},{12,8},{16,12},{20,16},{24,20},{28,24},{32,28},{36,32}... | collective-permute-start | bytes 110600 | tf_op jit(solution)/shard_map/ppermute | solution.py:449
  74.2 0.4 collective-permute-done.3.low
  74.6 2.4 %collective-permute-done.4.high = f32[24,384]{1,0:T(8,128)S(1)} collective-permute-done((f32[24,384]{1,0:T(8,128)S(1)}, f32[24,384]{1,0:T(8,128)S(1)}, u32[]{:S(2)}, u32[]{:S(2)}) %collective-permute-start.4) | collective-permute-done | bytes 36896 | tf_op jit(solution)/shard_map/ppermute | solution.py:449
  76.9 0.0 all-to-all-done.2.received
  76.9 0.9 shard_map.137
  77.8 14.9 %all-to-all-start.3 = ((bf16[32,24,384]{2,1,0:T(8,128)(2,1)}), bf16[32,24,384]{2,1,0:T(8,128)(2,1)S(1)}, u32[]{:S(2)}, u32[]{:S(2)}) async-start(bf16[32,24,384]{2,1,0:T(8,128)(2,1)} %get-tuple-element.63), calls=%async_computation.3 | async-start | bytes 1179648 | tf_op jit(solution)/shard_map/all_to_all | solution.py:453
  92.8 10.4 %collective-permute-start.5 = (f32[3,384]{1,0:T(4,128)S(1)}, f32[3,384]{1,0:T(4,128)S(1)}, u32[]{:S(2)}, u32[]{:S(2)}) collective-permute-start(f32[3,384]{1,0:T(4,128)S(1)} %get-tuple-element.64), channel_id=1, source_target_pairs={{0,0},{1,64},{64,1},{65,65},{2,2},{3,66},{66,3},{67,67},{4,4},{5,6... | collective-permute-start | bytes 13832 | tf_op jit(solution)/shard_map/ppermute | solution.py:491
  103.2 0.0 copy-done
  103.2 2.3 %shard_map.138 = bf16[256,384]{1,0:T(8,128)(2,1)} custom-call(f32[256,384]{1,0:T(8,128)S(1)} %get-tuple-element.65.grad_conv, f32[24,384]{1,0:T(8,128)S(1)} %collective-permute-done.3.low, f32[24,384]{1,0:T(8,128)S(1)} %collective-permute-done.4.high, f32[7,7,384]{2,1,0:T(8,128)S(1)} %get-tuple-element.42.taps, bf16[256,384]{1,0:T(8,128)(2,1)S(1)} %bitcast.5), custom_call_target="tpu_custom_call" | custom-call | flops 9633792 | bytes 2097152 | tf_op jit(solution)/shard_map/pallas_call | solution.py:316
  105.4 0.0 collective-permute-done.5.in_rows
  105.4 0.0 all-to-all-done.3.own
  105.4 6.9 %collective-permute-start.6 = (bf16[32,24,384]{2,1,0:T(8,128)(2,1)S(1)}, bf16[32,24,384]{2,1,0:T(8,128)(2,1)S(1)}, u32[]{:S(2)}, u32[]{:S(2)}) collective-permute-start(bf16[32,24,384]{2,1,0:T(8,128)(2,1)S(1)} %all-to-all-done.3.own), channel_id=1, source_target_pairs={{0,1},{1,0},{2,3},{3,2},{4,5},{5,4},{6,7},{7,6},{8,9},{9,8},{10,11... | collective-permute-start | bytes 1769480 | tf_op jit(solution)/shard_map/ppermute | solution.py:457
  112.4 1.6 %collective-permute-done.6.other = bf16[32,24,384]{2,1,0:T(8,128)(2,1)S(1)} collective-permute-done((bf16[32,24,384]{2,1,0:T(8,128)(2,1)S(1)}, bf16[32,24,384]{2,1,0:T(8,128)(2,1)S(1)}, u32[]{:S(2)}, u32[]{:S(2)}) %collective-permute-start.6) | collective-permute-done | bytes 589856 | tf_op jit(solution)/shard_map/ppermute | solution.py:457
  114.0 1.1 shard_map.139
Async XLA Ops:
  1.6 9.0 %collective-permute-start = (bf16[32,384]{1,0:T(8,128)(2,1)S(1)}, bf16[32,384]{1,0:T(8,128)(2,1)S(1)}, u32[]{:S(2)}, u32[]{:S(2)}) collective-permute-start(bf16[32,384]{1,0:T(8,128)(2,1)S(1)} %get-tuple-element.40), channel_id=1, source_target_pairs={{0,4},{4,8},{8,12},{12,16},{16,20},{20,24},{24,28},{28,32},{32,36}... | collective-permute-start | bytes 73736 | tf_op jit(solution)/shard_map/ppermute | solution.py:444
  4.0 6.7 %collective-permute-start.1 = (bf16[32,384]{1,0:T(8,128)(2,1)S(1)}, bf16[32,384]{1,0:T(8,128)(2,1)S(1)}, u32[]{:S(2)}, u32[]{:S(2)}) collective-permute-start(bf16[32,384]{1,0:T(8,128)(2,1)S(1)} %get-tuple-element.41), channel_id=1, source_target_pairs={{4,0},{8,4},{12,8},{16,12},{20,16},{24,20},{28,24},{32,28},{36,32}... | collective-permute-start | bytes 73736 | tf_op jit(solution)/shard_map/ppermute | solution.py:449
  14.3 6.0 %collective-permute-start.2 = (bf16[1536,384]{1,0:T(8,128)(2,1)S(1)}, bf16[1536,384]{1,0:T(8,128)(2,1)S(1)}, u32[]{:S(2)}, u32[]{:S(2)}) collective-permute-start(bf16[1536,384]{1,0:T(8,128)(2,1)S(1)} %get-tuple-element.56), channel_id=1, source_target_pairs={{0,1},{1,0},{2,3},{3,2},{4,5},{5,4},{6,7},{7,6},{8,9},{9,8},{10,11... | collective-permute-start | bytes 3538952 | tf_op jit(solution)/shard_map/ppermute | solution.py:457
  41.6 61.6 %copy-start = (bf16[1,8,32,384]{3,2,1,0:T(8,128)(2,1)S(1)}, bf16[1,8,32,384]{3,2,1,0:T(8,128)(2,1)}, u32[]{:S(2)}) copy-start(bf16[1,8,32,384]{3,2,1,0:T(8,128)(2,1)} %param.12) | copy-start | bytes 589828
  59.8 17.1 %all-to-all-start.2 = ((bf16[8,32,384]{2,1,0:T(8,128)(2,1)}), bf16[8,32,384]{2,1,0:T(8,128)(2,1)S(1)}, u32[]{:S(2)}, u32[]{:S(2)}) async-start(bf16[8,32,384]{2,1,0:T(8,128)(2,1)} %shard_map.136), calls=%async_computation.2 | async-start | bytes 393216 | tf_op jit(solution)/shard_map/all_to_all | solution.py:453
  68.9 5.7 %collective-permute-start.3 = (f32[24,384]{1,0:T(8,128)S(1)}, f32[24,384]{1,0:T(8,128)S(1)}, u32[]{:S(2)}, u32[]{:S(2)}) collective-permute-start(f32[24,384]{1,0:T(8,128)S(1)} %get-tuple-element.60), channel_id=1, source_target_pairs={{0,4},{4,8},{8,12},{12,16},{16,20},{20,24},{24,28},{28,32},{32,36}... | collective-permute-start | bytes 110600 | tf_op jit(solution)/shard_map/ppermute | solution.py:444
  71.0 5.9 %collective-permute-start.4 = (f32[24,384]{1,0:T(8,128)S(1)}, f32[24,384]{1,0:T(8,128)S(1)}, u32[]{:S(2)}, u32[]{:S(2)}) collective-permute-start(f32[24,384]{1,0:T(8,128)S(1)} %get-tuple-element.61), channel_id=1, source_target_pairs={{4,0},{8,4},{12,8},{16,12},{20,16},{24,20},{28,24},{32,28},{36,32}... | collective-permute-start | bytes 110600 | tf_op jit(solution)/shard_map/ppermute | solution.py:449
  77.8 27.6 %all-to-all-start.3 = ((bf16[32,24,384]{2,1,0:T(8,128)(2,1)}), bf16[32,24,384]{2,1,0:T(8,128)(2,1)S(1)}, u32[]{:S(2)}, u32[]{:S(2)}) async-start(bf16[32,24,384]{2,1,0:T(8,128)(2,1)} %get-tuple-element.63), calls=%async_computation.3 | async-start | bytes 1179648 | tf_op jit(solution)/shard_map/all_to_all | solution.py:453
  92.8 12.7 %collective-permute-start.5 = (f32[3,384]{1,0:T(4,128)S(1)}, f32[3,384]{1,0:T(4,128)S(1)}, u32[]{:S(2)}, u32[]{:S(2)}) collective-permute-start(f32[3,384]{1,0:T(4,128)S(1)} %get-tuple-element.64), channel_id=1, source_target_pairs={{0,0},{1,64},{64,1},{65,65},{2,2},{3,66},{66,3},{67,67},{4,4},{5,6... | collective-permute-start | bytes 13832 | tf_op jit(solution)/shard_map/ppermute | solution.py:491
  105.4 8.5 %collective-permute-start.6 = (bf16[32,24,384]{2,1,0:T(8,128)(2,1)S(1)}, bf16[32,24,384]{2,1,0:T(8,128)(2,1)S(1)}, u32[]{:S(2)}, u32[]{:S(2)}) collective-permute-start(bf16[32,24,384]{2,1,0:T(8,128)(2,1)S(1)} %all-to-all-done.3.own), channel_id=1, source_target_pairs={{0,1},{1,0},{2,3},{3,2},{4,5},{5,4},{6,7},{7,6},{8,9},{9,8},{10,11... | collective-permute-start | bytes 1769480 | tf_op jit(solution)/shard_map/ppermute | solution.py:457

commit v13 on v12

--- a/solution.py
+++ b/solution.py
@@ -16,7 +16,7 @@
 LANES = 128
 CHUNK = 32
 ROWS = 3
-EDGE = 4 * SIDE
+EDGE = 10 * SIDE
 EPSILON = 1e-06
 VMEM_LIMIT = 16 * 1024 * 1024
 NT = (((1,), (1,)), ((), ()))
@@ -72,22 +72,33 @@
         wide[k] = source[:, lanes].astype(jnp.float32)
 
 
-def edge_kernel(features, low, high, image, wide, sem):
-    copy = pltpu.make_async_copy(features, image, sem)
-    copy.start()
-    copy.wait()
+def edge_kernel(
+    flags, features, cotangent, scale, low, high, flags_here, image, upstream, scale_here, wide, wide_grad, sems
+):
+    pairs = [(features, image), (cotangent, upstream), (scale, scale_here), (flags, flags_here)]
+    copies = [pltpu.make_async_copy(src, dst, sems.at[i]) for i, (src, dst) in enumerate(pairs)]
+    for copy in copies:
+        copy.start()
+    for copy in copies:
+        copy.wait()
     widen(image, wide)
-    count = EDGE // SIDE
+    widen(upstream, wide_grad)
+    by_lane = scale_here[...].reshape(1, features.shape[1])
     for k, lanes in enumerate(lane_blocks(features.shape[1])):
-        for first, edge in ((0, low), (COLS - count, high)):
-            columns = [wide[k, pl.ds(first + j, SIDE, stride=COLS), :] for j in range(count)]
+        for first, first_grad, edge in ((0, 0, low), (COLS - 2 * HALO, COLS - HALO, high)):
+            columns = [wide[k, pl.ds(first + j, SIDE, stride=COLS), :] for j in range(2 * HALO)]
+            gate = flags_here[0, first_grad // SIDE].astype(jnp.float32)
+            for j in range(HALO):
+                column = wide_grad[k, pl.ds(first_grad + j, SIDE, stride=COLS), :]
+                columns.append(column * by_lane[:, lanes] * gate)
+            columns.append(jnp.zeros((SIDE, LANES), jnp.float32))
             edge[:, lanes] = jnp.concatenate(columns, axis=0).astype(jnp.bfloat16)
 
 
 def first_kernel(
     flags, features, cotangent, w_out, w_in, b_in, taps, scale, conv_bias, gain, bias,
-    conv, out_grad, back, w_in_t, b_cols, w_in_here, taps_here, vectors,
-    wide, flags_here, image, upstream, w_out_here, b_here, scale_here, conv_bias_here, gain_here, bias_here, sems
+    conv, out_grad, back, w_in_t, b_cols, w_in_here, w_out_here, taps_here, vectors,
+    wide, flags_here, image, upstream, b_here, scale_here, conv_bias_here, gain_here, bias_here, sems
 ):
     width = features.shape[1]
     pairs = [
@@ -158,7 +169,7 @@
     low_wide[...] = low[...].astype(jnp.float32)
     high_wide[...] = high[...].astype(jnp.float32)
     for lanes in lane_blocks(width):
-        near = [low_wide[(j + 1) * SIDE : (j + 2) * SIDE, lanes] for j in range(HALO)]
+        near = [low_wide[(HALO + j) * SIDE : (HALO + j + 1) * SIDE, lanes] for j in range(HALO)]
         for j, total in enumerate(convolve(near + [None] * (2 * HALO), taps, lanes, False)):
             rows[j * SIDE : (j + 1) * SIDE, lanes] += total
         near = [high_wide[j * SIDE : (j + 1) * SIDE, lanes] for j in range(HALO)]
@@ -201,16 +212,56 @@
         kept[place : place + run, :] = matmul(grad_pre[pl.ds(start, run), :], normed[...])
 
 
-def back_kernel(grad_pre, w_in, standard, inverse, vectors, grad_conv, low_edge, high_edge):
-    grad_std = matmul(w_in[...], grad_pre[...]).T * vectors[SIDE : SIDE + 1, :]
-    norm = standard[...]
+def through_norm(grad_std, standard, inverse):
     mean = jnp.mean(grad_std, axis=-1, keepdims=True)
-    along = jnp.mean(grad_std * norm, axis=-1, keepdims=True)
-    result = inverse[:, :1] * (grad_std - mean - norm * along)
-    grad_conv[...] = result
+    along = jnp.mean(grad_std * standard, axis=-1, keepdims=True)
+    return inverse * (grad_std - mean - standard * along)
+
+
+def back_kernel(
+    grad_pre, w_in, standard, inverse, vectors, w_out, w_in_t, b_cols, taps, own_low, own_high, low, high,
+    grad_conv, low_conv, high_conv,
+    rows, out_grad, preact, back, halo_pre
+):
+    conv_bias, gain, bias = (vectors[i * SIDE : i * SIDE + 1, :] for i in range(3))
+    grad_std = matmul(w_in[...], grad_pre[...]).T * gain
+    grad_conv[...] = through_norm(grad_std, standard[...], inverse[:, :1])
+
     edge = HALO * SIDE
-    low_edge[...] = result[:edge, :]
-    high_edge[...] = result[result.shape[0] - edge :, :]
+    rows[...] = jnp.zeros_like(rows)
+    for lanes in lane_blocks(rows.shape[1]):
+        near, far = ([x[:, lanes].astype(jnp.float32) for x in pair] for pair in ((own_low, own_high), (low, high)))
+        for i in range(2):
+            column = lambda block, j: block[j * SIDE : (j + 1) * SIDE, :]
+            beyond = [column(far[i], j) for j in range(2 * HALO)]
+            inside = [column(near[i], j + i * HALO) for j in range(HALO)]
+            columns = inside + beyond if i else beyond + inside
+            for j, total in enumerate(convolve(columns, taps, lanes, False)):
+                start = i * edge + j * SIDE
+                rows[start : start + SIDE, lanes] = total
+        grads = [block[2 * edge : 3 * edge, :] for block in far]
+        grads.append(jnp.zeros((rows.shape[0] - 2 * edge, LANES), jnp.float32))
+        out_grad[:, lanes] = jnp.concatenate(grads, axis=0).astype(jnp.bfloat16)
+    conv_out = rows[...] + conv_bias
+    centre = conv_out - jnp.mean(conv_out, axis=-1, keepdims=True)
+    scale = lax.rsqrt(jnp.mean(centre * centre, axis=-1, keepdims=True) + EPSILON)
+    norm = centre * scale
+    preact[...] = matmul(w_in_t[...], (norm * gain + bias).astype(jnp.bfloat16), NT)
+    back[...] = matmul(w_out[...], out_grad[...], NT)
+
+    def step(i, carry):
+        part = pl.ds(pl.multiple_of(i * CHUNK, CHUNK), CHUNK)
+        z = preact[part, :] + b_cols[part, :]
+        below = 0.5 * (1.0 + lax.erf(z * 0.7071067811865476))
+        density = jnp.exp(-0.5 * z * z) * 0.3989422804014327
+        halo_pre[part, :] = (back[part, :] * (below + z * density)).astype(jnp.bfloat16)
+        return carry
+
+    lax.fori_loop(0, preact.shape[0] // CHUNK, step, 0, unroll=4)
+    grad_std = matmul(w_in[...], halo_pre[...]).T * gain
+    result = through_norm(grad_std, norm, scale)
+    low_conv[...] = result[:edge, :]
+    high_conv[...] = result[edge : 2 * edge, :]
 
 
 def last_kernel(grad_conv, low, high, taps, cotangent, grad_features, wide):
@@ -327,15 +378,17 @@
 F32, B16 = jnp.float32, jnp.bfloat16
 
 
-def edges(features):
+def edges(flags, features, cotangent, layer_scale):
     rows, width = features.shape
+    wide = pltpu.VMEM((width // LANES, rows, LANES), F32)
     return call(
         edge_kernel,
         [((EDGE, width), B16), ((EDGE, width), B16)],
-        [pltpu.VMEM((rows, width), B16), pltpu.VMEM((width // LANES, rows, LANES), F32), pltpu.SemaphoreType.DMA],
+        [pltpu.SMEM(flags.shape, jnp.int32), pltpu.VMEM((rows, width), B16), pltpu.VMEM((rows, width), B16),
+         pltpu.VMEM((width,), F32), wide, wide, pltpu.SemaphoreType.DMA((4,))],
         [],
-        [features],
-        features.size, 2 * features.size, pltpu.HBM,
+        [flags, features, cotangent, layer_scale],
+        features.size, 4 * features.size, pltpu.HBM,
     )
 
 
@@ -345,9 +398,9 @@
     return call(
         first_kernel,
         [((rows, width), F32), ((rows, width), B16), ((hidden, rows), F32), ((hidden, width), B16),
-         ((hidden, LANES), F32), (w_in.shape, B16), (kernel.shape, F32), ((3 * SIDE, width), F32)],
+         ((hidden, LANES), F32), (w_in.shape, B16), (w_out.shape, B16), (kernel.shape, F32), ((3 * SIDE, width), F32)],
         [pltpu.VMEM((width // LANES, rows, LANES), F32), pltpu.SMEM(flags.shape, jnp.int32),
-         pltpu.VMEM((rows, width), B16), pltpu.VMEM((rows, width), B16), pltpu.VMEM(w_out.shape, B16),
+         pltpu.VMEM((rows, width), B16), pltpu.VMEM((rows, width), B16),
          pltpu.VMEM(b_in.shape, F32), pltpu.VMEM((width,), F32), pltpu.VMEM((width,), F32),
          pltpu.VMEM((width,), F32), pltpu.VMEM((width,), F32),
          pltpu.SemaphoreType.DMA((11,))],
@@ -372,12 +425,16 @@
     )
 
 
-def to_conv(grad_pre, w_in, standard, inverse, vectors):
+def to_conv(grad_pre, w_in, standard, inverse, vectors, *more):
     rows, width = standard.shape
+    hidden = grad_pre.shape[0]
     edge = (HALO * SIDE, width)
     return call(
-        back_kernel, [((rows, width), F32), (edge, F32), (edge, F32)], [], [],
-        [grad_pre, w_in, standard, inverse, vectors],
+        back_kernel, [((rows, width), F32), (edge, F32), (edge, F32)],
+        [pltpu.VMEM((LANES, width), F32), pltpu.VMEM((LANES, width), B16), pltpu.VMEM((hidden, LANES), F32),
+         pltpu.VMEM((hidden, LANES), F32), pltpu.VMEM((hidden, LANES), B16)],
+        [],
+        [grad_pre, w_in, standard, inverse, vectors, *more],
         2 * grad_pre.size * width, 4 * grad_pre.size,
     )
 
@@ -463,28 +520,28 @@
     image = features[0]
     height, breadth, channels = image.shape
     rows = image.reshape(-1, channels)
-    low, high = edges(rows)
-    low, high = from_left(high), from_right(low)
     upstream = cotangent[0].reshape(-1, channels)
+    own_low, own_high = edges(tissue, rows, upstream, layer_scale)
+    low, high = from_left(own_high), from_right(own_low)
     device = lax.axis_index(EVERY).astype(jnp.int32).reshape(1)
     sizes = {axis: lax.axis_size(axis) for axis in EVERY}
     cube, four, eight = (math.prod(sizes[axis] for axis in axes) for axes in (CUBE, FOUR, EIGHT))
     scale = 1.0 / math.sqrt(height * breadth * math.prod(sizes.values()))
 
-    conv, out_grad, back, w_in_t, b_cols, w_in_here, taps, vectors = before_halos(
+    conv, out_grad, back, w_in_t, b_cols, w_in_here, w_out_here, taps, vectors = before_halos(
         tissue, rows, upstream, kernel, conv_bias, ln_gain, ln_bias, w_in, b_in, w_out, layer_scale
     )
     kept, sent, standard, inverse, grad_pre = middle(
         device, conv, low, high, taps, vectors, w_in_t, b_cols, out_grad, back
     )
-    grad_conv, low, high = to_conv(grad_pre, w_in_here, standard, inverse, vectors)
+    grad_conv, low, high = to_conv(
+        grad_pre, w_in_here, standard, inverse, vectors,
+        w_out_here, w_in_t, b_cols, taps, own_low, own_high, low, high,
+    )
     kept, low, high = lax.optimization_barrier((kept, low, high))
     received = exchange(to_cube(cube, kept, swap(sent)), CUBE)
     received = exchange(to_four(received, four), FOUR)
-    received, low, high = lax.optimization_barrier((received, low, high))
     received = exchange(to_eight(received, eight), EIGHT)
-    low, high = from_left(high), from_right(low)
-    received, low, high = lax.optimization_barrier((received, low, high))
     message, in_rows = turn(scale, received, cube * four)
     own = exchange(message, CUBE + FOUR)
     pairs = [(2 * xh + c, 2 * c + xh) for xh in range(2) for c in range(2)]

time: 116 us -> 113 us (0.974)
  the two profiles are of different devices: /device:TPU:177 before, /device:TPU:1 now
where the time goes in v13:
time: 113 us
  blocking collectives  59.7 us (53%)
  starting transfers between devices  31.9 us (28%)
  Pallas kernels  16.8 us (15%)
  waiting for transfers between devices  3.72 us (3%)
    all_to_all x3, blocking collectives, exchange(): return lax.all_to_all(blocks, axes, split_axis=0, concat_axis=0, tiled=True)  59.7 us
    pallas_call x10, Pallas kernels, call(): pl.pallas_call(kernel, out_shape=[jax.ShapeDtypeStruct(shape, kind) for s...  16.8 us
    ppermute x2, starting transfers between devices, swap(): return lax.ppermute(block, 'c', SWAP)  13.6 us
    ppermute x1, starting transfers between devices, body(): in_rows = lax.ppermute(in_rows, ('xh', 'c'), pairs)  9.05 us
    ppermute x1, starting transfers between devices, from_left(): return lax.ppermute(block, TILE, [(i, i + 1) for i in range(count - 1)])  4.03 us
    all_to_all x1, starting transfers between devices, exchange(): return lax.all_to_all(blocks, axes, split_axis=0, concat_axis=0, tiled=True)  3.9 us
  transfers between devices with their start and end apart: 6, of which 2 were waited for; matrix products, arithmetic and copies ran while one was open for 0% of the time, Pallas kernels for 8%

profile of v13, /device:TPU:1, one launch (start us, length us, event | category | flops | bytes accessed | tf_op | source)
XLA Modules:
  0.0 112.9 jit_solution(14661448287900674178)
XLA Ops:
  0.6 1.2 %shard_map.131 = (bf16[80,384]{1,0:T(8,128)(2,1)S(1)}, bf16[80,384]{1,0:T(8,128)(2,1)S(1)}) custom-call(s32[1,4]{1,0:T(1,128)} %flags.3, bf16[256,384]{1,0:T(8,128)(2,1)} %bitcast.7, bf16[256,384]{1,0:T(8,128)(2,1)} %bitcast.4, f32[384]{0:T(512)} %scale.3), custom_call_target="tpu_custom_call" | custom-call | flops 98304 | bytes 393216 | tf_op jit(solution)/shard_map/pallas_call | solution.py:367
  1.9 4.0 %collective-permute-start = (bf16[80,384]{1,0:T(8,128)(2,1)S(1)}, bf16[80,384]{1,0:T(8,128)(2,1)S(1)}, u32[]{:S(2)}, u32[]{:S(2)}) collective-permute-start(bf16[80,384]{1,0:T(8,128)(2,1)S(1)} %get-tuple-element.35.own_high), channel_id=1, source_target_pairs={{0,4},{4,8},{8,12},{12,16},{16,20},{20,24},{24,28},{28,32},{32,36}... | collective-permute-start | bytes 184328 | tf_op jit(solution)/shard_map/ppermute | solution.py:501
  5.9 1.3 %collective-permute-start.1 = (bf16[80,384]{1,0:T(8,128)(2,1)S(1)}, bf16[80,384]{1,0:T(8,128)(2,1)S(1)}, u32[]{:S(2)}, u32[]{:S(2)}) collective-permute-start(bf16[80,384]{1,0:T(8,128)(2,1)S(1)} %get-tuple-element.36.own_low), channel_id=1, source_target_pairs={{4,0},{8,4},{12,8},{16,12},{20,16},{24,20},{28,24},{32,28},{36,32}... | collective-permute-start | bytes 184328 | tf_op jit(solution)/shard_map/ppermute | solution.py:506
  7.2 4.0 %shard_map.130 = (f32[256,384]{1,0:T(8,128)S(1)}, bf16[256,384]{1,0:T(8,128)(2,1)S(1)}, f32[1536,256]{1,0:T(8,128)S(1)}, bf16[1536,384]{1,0:T(8,128)(2,1)S(1)}, ...) custom-call(s32[1,4]{1,0:T(1,128)} %flags.3, ...), custom_call_target="tpu_custom_call" | custom-call | flops 301989888 | bytes 8388608 | tf_op jit(solution)/shard_map/pallas_call | solution.py:367
  11.2 0.0 collective-permute-done.low
  11.2 0.0 collective-permute-done.1.high
  11.3 3.7 %shard_map.132 = (f32[1536,384]{1,0:T(8,128)S(1)}, bf16[1536,384]{1,0:T(8,128)(2,1)S(1)}, f32[256,384]{1,0:T(8,128)S(1)}, f32[256,128]{1,0:T(8,128)S(1)}, bf16[1536,256]{1,0:T(8,128)(2,1)S(1)}) custom-call(s32[1]{0:T(128)} %bitcast.device, f32[256,384]{1,0:T(8,128)S(1)} %get-tuple-element.34.conv, bf16[80,384]{1,0:T(8,128)(2,1)S(1)} %collective-permute-done.low, ...), custom_call_target="tpu_custom_call" | custom-call | flops 905969664 | bytes 12582912 | tf_op jit(solution)/shard_map/pallas_call | solution.py:367
  15.0 6.8 %collective-permute-start.2 = (bf16[1536,384]{1,0:T(8,128)(2,1)S(1)}, bf16[1536,384]{1,0:T(8,128)(2,1)S(1)}, u32[]{:S(2)}, u32[]{:S(2)}) collective-permute-start(bf16[1536,384]{1,0:T(8,128)(2,1)S(1)} %get-tuple-element.52), channel_id=1, source_target_pairs={{0,1},{1,0},{2,3},{3,2},{4,5},{5,4},{6,7},{7,6},{8,9},{9,8},{10,11... | collective-permute-start | bytes 3538952 | tf_op jit(solution)/shard_map/ppermute | solution.py:514
  21.8 2.9 %shard_map.133 = (f32[256,384]{1,0:T(8,128)S(1)}, f32[24,384]{1,0:T(8,128)S(1)}, f32[24,384]{1,0:T(8,128)S(1)}) custom-call(bf16[1536,256]{1,0:T(8,128)(2,1)S(1)} %get-tuple-element.44.grad_pre, bf16[384,1536]{1,0:T(8,128)(2,1)S(1)} %get-tuple-element.45.w_in, f32[256,384]{1,0:T(8,128)S(1)} %get-tuple-element.46.standard, ...), custom_call_target="tpu_custom_call" | custom-call | flops 301989888 | bytes 1572864 | tf_op jit(solution)/shard_map/pallas_call | solution.py:367
  24.7 0.0 collective-permute-done.2.received
  24.7 0.4 shard_map.134
  25.1 19.3 %all_to_all.20.received = bf16[8,192,384]{2,1,0:T(8,128)(2,1)S(1)} all-to-all(bf16[8,192,384]{2,1,0:T(8,128)(2,1)S(1)} %shard_map.134), channel_id=1, replica_groups=mesh['zh'=4,'xh'=2,'xl'=2,'y2'=2,'y1'=2,'yl'=2,'zl'=2,'c'=2] {'xl','yl',..., dimensions={0} | all-to-all | bytes 2359296 | tf_op jit(solution)/shard_map/all_to_all | solution.py:510
  44.4 0.2 shard_map.135
  44.6 0.0 copy-start
  44.7 14.2 %all_to_all.21.received = bf16[4,48,384]{2,1,0:T(8,128)(2,1)S(1)} all-to-all(bf16[4,48,384]{2,1,0:T(8,128)(2,1)S(1)} %shard_map.135), channel_id=1, replica_groups=mesh['zh'=4,'xh'=2,'xl'=2,'y2'=2,'y1'=2,'yl'=2,'zl'=2,'c'=2] {'xh','y1'}, dimensions={0} | all-to-all | bytes 294912 | tf_op jit(solution)/shard_map/all_to_all | solution.py:510
  58.9 0.1 shard_map.136
  59.0 26.1 %all_to_all.22.received = bf16[8,32,384]{2,1,0:T(8,128)(2,1)S(1)} all-to-all(bf16[8,32,384]{2,1,0:T(8,128)(2,1)S(1)} %shard_map.136), channel_id=1, replica_groups=mesh['zh'=4,'xh'=2,'xl'=2,'y2'=2,'y1'=2,'yl'=2,'zl'=2,'c'=2] {'zh','y2'}, dimensions={0} | all-to-all | bytes 393216 | tf_op jit(solution)/shard_map/all_to_all | solution.py:510
  85.1 0.9 shard_map.137
  86.0 3.9 %all-to-all-start.3 = ((bf16[32,24,384]{2,1,0:T(8,128)(2,1)}), bf16[32,24,384]{2,1,0:T(8,128)(2,1)S(1)}, u32[]{:S(2)}, u32[]{:S(2)}) async-start(bf16[32,24,384]{2,1,0:T(8,128)(2,1)} %get-tuple-element.53), calls=%async_computation.3 | async-start | bytes 1179648 | tf_op jit(solution)/shard_map/all_to_all | solution.py:510
  89.9 9.1 %collective-permute-start.3 = (f32[3,384]{1,0:T(4,128)S(1)}, f32[3,384]{1,0:T(4,128)S(1)}, u32[]{:S(2)}, u32[]{:S(2)}) collective-permute-start(f32[3,384]{1,0:T(4,128)S(1)} %get-tuple-element.54), channel_id=1, source_target_pairs={{0,0},{1,64},{64,1},{65,65},{2,2},{3,66},{66,3},{67,67},{4,4},{5,6... | collective-permute-start | bytes 13832 | tf_op jit(solution)/shard_map/ppermute | solution.py:548
  98.9 0.0 copy-done
  98.9 2.3 %shard_map.138 = bf16[256,384]{1,0:T(8,128)(2,1)} custom-call(f32[256,384]{1,0:T(8,128)S(1)} %get-tuple-element.55.grad_conv, f32[24,384]{1,0:T(8,128)S(1)} %get-tuple-element.58.low, f32[24,384]{1,0:T(8,128)S(1)} %get-tuple-element.59.high, f32[7,7,384]{2,1,0:T(8,128)S(1)} %get-tuple-element.37.taps, bf16[256,384]{1,0:T(8,128)(2,1)S(1)} %bitcast.6), custom_call_target="tpu_custom_call" | custom-call | flops 9633792 | bytes 2097152 | tf_op jit(solution)/shard_map/pallas_call | solution.py:367
  101.2 0.0 collective-permute-done.3.in_rows
  101.2 2.1 %all-to-all-done.3.own = bf16[32,24,384]{2,1,0:T(8,128)(2,1)S(1)} async-done(((bf16[32,24,384]{2,1,0:T(8,128)(2,1)}), bf16[32,24,384]{2,1,0:T(8,128)(2,1)S(1)}, u32[]{:S(2)}, u32[]{:S(2)}) %all-to-all-start.3) | async-done | bytes 589856 | tf_op jit(solution)/shard_map/all_to_all | solution.py:510
  103.3 6.8 %collective-permute-start.4 = (bf16[32,24,384]{2,1,0:T(8,128)(2,1)S(1)}, bf16[32,24,384]{2,1,0:T(8,128)(2,1)S(1)}, u32[]{:S(2)}, u32[]{:S(2)}) collective-permute-start(bf16[32,24,384]{2,1,0:T(8,128)(2,1)S(1)} %all-to-all-done.3.own), channel_id=1, source_target_pairs={{0,1},{1,0},{2,3},{3,2},{4,5},{5,4},{6,7},{7,6},{8,9},{9,8},{10,11... | collective-permute-start | bytes 1769480 | tf_op jit(solution)/shard_map/ppermute | solution.py:514
  110.1 1.6 %collective-permute-done.4.other = bf16[32,24,384]{2,1,0:T(8,128)(2,1)S(1)} collective-permute-done((bf16[32,24,384]{2,1,0:T(8,128)(2,1)S(1)}, bf16[32,24,384]{2,1,0:T(8,128)(2,1)S(1)}, u32[]{:S(2)}, u32[]{:S(2)}) %collective-permute-start.4) | collective-permute-done | bytes 589856 | tf_op jit(solution)/shard_map/ppermute | solution.py:514
  111.7 1.1 %shard_map.139 = (bf16[1536,384]{1,0:T(8,128)(2,1)}, f32[3,384]{1,0:T(4,128)}) custom-call(s32[1]{0:T(128)} %bitcast.device, bf16[32,24,384]{2,1,0:T(8,128)(2,1)S(1)} %all-to-all-done.3.own, bf16[32,24,384]{2,1,0:T(8,128)(2,1)S(1)} %collective-permute-done.4.other, f32[3,384]{1,0:T(4,128)S(1)} %collective-permute-done.3.in_rows), custom_call_target="tpu_custom_call" | custom-call | flops 294912 | bytes 2359296 | tf_op jit(solution)/shard_map/pallas_call | solution.py:367
Async XLA Ops:
  1.9 9.4 %collective-permute-start = (bf16[80,384]{1,0:T(8,128)(2,1)S(1)}, bf16[80,384]{1,0:T(8,128)(2,1)S(1)}, u32[]{:S(2)}, u32[]{:S(2)}) collective-permute-start(bf16[80,384]{1,0:T(8,128)(2,1)S(1)} %get-tuple-element.35.own_high), channel_id=1, source_target_pairs={{0,4},{4,8},{8,12},{12,16},{16,20},{20,24},{24,28},{28,32},{32,36}... | collective-permute-start | bytes 184328 | tf_op jit(solution)/shard_map/ppermute | solution.py:501
  5.9 5.3 %collective-permute-start.1 = (bf16[80,384]{1,0:T(8,128)(2,1)S(1)}, bf16[80,384]{1,0:T(8,128)(2,1)S(1)}, u32[]{:S(2)}, u32[]{:S(2)}) collective-permute-start(bf16[80,384]{1,0:T(8,128)(2,1)S(1)} %get-tuple-element.36.own_low), channel_id=1, source_target_pairs={{4,0},{8,4},{12,8},{16,12},{20,16},{24,20},{28,24},{32,28},{36,32}... | collective-permute-start | bytes 184328 | tf_op jit(solution)/shard_map/ppermute | solution.py:506
  15.0 9.8 %collective-permute-start.2 = (bf16[1536,384]{1,0:T(8,128)(2,1)S(1)}, bf16[1536,384]{1,0:T(8,128)(2,1)S(1)}, u32[]{:S(2)}, u32[]{:S(2)}) collective-permute-start(bf16[1536,384]{1,0:T(8,128)(2,1)S(1)} %get-tuple-element.52), channel_id=1, source_target_pairs={{0,1},{1,0},{2,3},{3,2},{4,5},{5,4},{6,7},{7,6},{8,9},{9,8},{10,11... | collective-permute-start | bytes 3538952 | tf_op jit(solution)/shard_map/ppermute | solution.py:514
  44.6 54.3 %copy-start = (bf16[1,8,32,384]{3,2,1,0:T(8,128)(2,1)S(1)}, bf16[1,8,32,384]{3,2,1,0:T(8,128)(2,1)}, u32[]{:S(2)}) copy-start(bf16[1,8,32,384]{3,2,1,0:T(8,128)(2,1)} %param.12) | copy-start | bytes 589828
  86.0 17.4 %all-to-all-start.3 = ((bf16[32,24,384]{2,1,0:T(8,128)(2,1)}), bf16[32,24,384]{2,1,0:T(8,128)(2,1)S(1)}, u32[]{:S(2)}, u32[]{:S(2)}) async-start(bf16[32,24,384]{2,1,0:T(8,128)(2,1)} %get-tuple-element.53), calls=%async_computation.3 | async-start | bytes 1179648 | tf_op jit(solution)/shard_map/all_to_all | solution.py:510
  89.9 11.4 %collective-permute-start.3 = (f32[3,384]{1,0:T(4,128)S(1)}, f32[3,384]{1,0:T(4,128)S(1)}, u32[]{:S(2)}, u32[]{:S(2)}) collective-permute-start(f32[3,384]{1,0:T(4,128)S(1)} %get-tuple-element.54), channel_id=1, source_target_pairs={{0,0},{1,64},{64,1},{65,65},{2,2},{3,66},{66,3},{67,67},{4,4},{5,6... | collective-permute-start | bytes 13832 | tf_op jit(solution)/shard_map/ppermute | solution.py:548
  103.3 8.4 %collective-permute-start.4 = (bf16[32,24,384]{2,1,0:T(8,128)(2,1)S(1)}, bf16[32,24,384]{2,1,0:T(8,128)(2,1)S(1)}, u32[]{:S(2)}, u32[]{:S(2)}) collective-permute-start(bf16[32,24,384]{2,1,0:T(8,128)(2,1)S(1)} %all-to-all-done.3.own), channel_id=1, source_target_pairs={{0,1},{1,0},{2,3},{3,2},{4,5},{5,4},{6,7},{7,6},{8,9},{9,8},{10,11... | collective-permute-start | bytes 1769480 | tf_op jit(solution)/shard_map/ppermute | solution.py:514

commit v14 on v13

--- a/solution.py
+++ b/solution.py
@@ -541,14 +541,15 @@
     kept, low, high = lax.optimization_barrier((kept, low, high))
     received = exchange(to_cube(cube, kept, swap(sent)), CUBE)
     received = exchange(to_four(received, four), FOUR)
+    received, low, high = lax.optimization_barrier((received, low, high))
+    grad_image = to_features(grad_conv, low, high, taps, upstream)
     received = exchange(to_eight(received, eight), EIGHT)
+    received, grad_image = lax.optimization_barrier((received, grad_image))
     message, in_rows = turn(scale, received, cube * four)
     own = exchange(message, CUBE + FOUR)
+    own, in_rows = lax.optimization_barrier((own, in_rows))
     pairs = [(2 * xh + c, 2 * c + xh) for xh in range(2) for c in range(2)]
     in_rows = lax.ppermute(in_rows, ("xh", "c"), pairs)
-    message, low, high = lax.optimization_barrier((message, low, high))
-    grad_image = to_features(grad_conv, low, high, taps, upstream)
-    own, in_rows, grad_image = lax.optimization_barrier((own, in_rows, grad_image))
     grad_w_out, grad_w_in = join(device, own, swap(own), in_rows)
     return (grad_image.reshape(1, height, breadth, channels), grad_w_in, grad_w_out)
 

time: 113 us -> 118 us (1.044)
  waiting for transfers between devices: 3.72 us -> 13.1 us
  blocking collectives: 59.7 us -> 50.5 us
  starting transfers between devices: 31.9 us -> 36.4 us
    all_to_all x1, starting transfers between devices: 3.9 us -> 14.3 us  [exchange(): return lax.all_to_all(blocks, axes, split_axis=0, concat_axis=0, tiled=True)]
    all_to_all x3, blocking collectives: 59.7 us -> 50.5 us  [exchange(): return lax.all_to_all(blocks, axes, split_axis=0, concat_axis=0, tiled=True)]
    all_to_all x1, waiting for transfers between devices: 2.1 us -> 9.75 us  [exchange(): return lax.all_to_all(blocks, axes, split_axis=0, concat_axis=0, tiled=True)]
    ppermute x1, starting transfers between devices: 9.05 us -> 3.1 us  [body(): in_rows = lax.ppermute(in_rows, ('xh', 'c'), pairs)]
    ppermute x1, waiting for transfers between devices: 0.01 us -> 3.35 us  [body(): in_rows = lax.ppermute(in_rows, ('xh', 'c'), pairs)]
    ppermute x2, waiting for transfers between devices: 1.61 us -> 0.01 us  [swap(): return lax.ppermute(block, 'c', SWAP)]
where the time goes in v14:
time: 118 us; the launch traced here: 117 us
  blocking collectives  50.5 us (43%)
  starting transfers between devices  36.4 us (31%)
  Pallas kernels  16.7 us (14%)
  waiting for transfers between devices  13.1 us (11%)
    all_to_all x3, blocking collectives, exchange(): return lax.all_to_all(blocks, axes, split_axis=0, concat_axis=0, tiled=True)  50.5 us
    pallas_call x10, Pallas kernels, call(): pl.pallas_call(kernel, out_shape=[jax.ShapeDtypeStruct(shape, kind) for s...  16.7 us
    all_to_all x1, starting transfers between devices, exchange(): return lax.all_to_all(blocks, axes, split_axis=0, concat_axis=0, tiled=True)  14.3 us
    ppermute x2, starting transfers between devices, swap(): return lax.ppermute(block, 'c', SWAP)  13.7 us
    all_to_all x1, waiting for transfers between devices, exchange(): return lax.all_to_all(blocks, axes, split_axis=0, concat_axis=0, tiled=True)  9.75 us
    ppermute x1, starting transfers between devices, from_left(): return lax.ppermute(block, TILE, [(i, i + 1) for i in range(count - 1)])  4.03 us
    ppermute x1, waiting for transfers between devices, body(): in_rows = lax.ppermute(in_rows, ('xh', 'c'), pairs)  3.35 us
    ppermute x1, starting transfers between devices, body(): in_rows = lax.ppermute(in_rows, ('xh', 'c'), pairs)  3.1 us
  transfers between devices with their start and end apart: 6, of which 2 were waited for; matrix products, arithmetic and copies ran while one was open for 0% of the time, Pallas kernels for 8%

profile of v14, /device:TPU:1, one launch (start us, length us, event | category | flops | bytes accessed | tf_op | source)
XLA Modules:
  0.0 117.4 jit_solution(14544142777164129096)
XLA Ops:
  0.6 1.2 %shard_map.131 = (bf16[80,384]{1,0:T(8,128)(2,1)S(1)}, bf16[80,384]{1,0:T(8,128)(2,1)S(1)}) custom-call(s32[1,4]{1,0:T(1,128)} %flags.3, bf16[256,384]{1,0:T(8,128)(2,1)} %bitcast.7, bf16[256,384]{1,0:T(8,128)(2,1)} %bitcast.4, f32[384]{0:T(512)} %scale.3), custom_call_target="tpu_custom_call" | custom-call | flops 98304 | bytes 393216 | tf_op jit(solution)/shard_map/pallas_call | solution.py:367
  1.9 4.0 %collective-permute-start = (bf16[80,384]{1,0:T(8,128)(2,1)S(1)}, bf16[80,384]{1,0:T(8,128)(2,1)S(1)}, u32[]{:S(2)}, u32[]{:S(2)}) collective-permute-start(bf16[80,384]{1,0:T(8,128)(2,1)S(1)} %get-tuple-element.37.own_high), channel_id=1, source_target_pairs={{0,4},{4,8},{8,12},{12,16},{16,20},{20,24},{24,28},{28,32},{32,36}... | collective-permute-start | bytes 184328 | tf_op jit(solution)/shard_map/ppermute | solution.py:501
  5.9 1.3 %collective-permute-start.1 = (bf16[80,384]{1,0:T(8,128)(2,1)S(1)}, bf16[80,384]{1,0:T(8,128)(2,1)S(1)}, u32[]{:S(2)}, u32[]{:S(2)}) collective-permute-start(bf16[80,384]{1,0:T(8,128)(2,1)S(1)} %get-tuple-element.38.own_low), channel_id=1, source_target_pairs={{4,0},{8,4},{12,8},{16,12},{20,16},{24,20},{28,24},{32,28},{36,32}... | collective-permute-start | bytes 184328 | tf_op jit(solution)/shard_map/ppermute | solution.py:506
  7.2 4.0 %shard_map.130 = (f32[256,384]{1,0:T(8,128)S(1)}, bf16[256,384]{1,0:T(8,128)(2,1)S(1)}, f32[1536,256]{1,0:T(8,128)S(1)}, bf16[1536,384]{1,0:T(8,128)(2,1)S(1)}, ...) custom-call(s32[1,4]{1,0:T(1,128)} %flags.3, ...), custom_call_target="tpu_custom_call" | custom-call | flops 301989888 | bytes 8388608 | tf_op jit(solution)/shard_map/pallas_call | solution.py:367
  11.2 0.0 collective-permute-done.low
  11.2 0.0 collective-permute-done.1.high
  11.3 3.7 %shard_map.132 = (f32[1536,384]{1,0:T(8,128)S(1)}, bf16[1536,384]{1,0:T(8,128)(2,1)S(1)}, f32[256,384]{1,0:T(8,128)S(1)}, f32[256,128]{1,0:T(8,128)S(1)}, bf16[1536,256]{1,0:T(8,128)(2,1)S(1)}) custom-call(s32[1]{0:T(128)} %bitcast.device, f32[256,384]{1,0:T(8,128)S(1)} %get-tuple-element.36.conv, bf16[80,384]{1,0:T(8,128)(2,1)S(1)} %collective-permute-done.low, ...), custom_call_target="tpu_custom_call" | custom-call | flops 905969664 | bytes 12582912 | tf_op jit(solution)/shard_map/pallas_call | solution.py:367
  15.0 6.8 %collective-permute-start.2 = (bf16[1536,384]{1,0:T(8,128)(2,1)S(1)}, bf16[1536,384]{1,0:T(8,128)(2,1)S(1)}, u32[]{:S(2)}, u32[]{:S(2)}) collective-permute-start(bf16[1536,384]{1,0:T(8,128)(2,1)S(1)} %get-tuple-element.54), channel_id=1, source_target_pairs={{0,1},{1,0},{2,3},{3,2},{4,5},{5,4},{6,7},{7,6},{8,9},{9,8},{10,11... | collective-permute-start | bytes 3538952 | tf_op jit(solution)/shard_map/ppermute | solution.py:514
  21.8 2.9 %shard_map.133 = (f32[256,384]{1,0:T(8,128)S(1)}, f32[24,384]{1,0:T(8,128)S(1)}, f32[24,384]{1,0:T(8,128)S(1)}) custom-call(bf16[1536,256]{1,0:T(8,128)(2,1)S(1)} %get-tuple-element.46.grad_pre, bf16[384,1536]{1,0:T(8,128)(2,1)S(1)} %get-tuple-element.47.w_in, f32[256,384]{1,0:T(8,128)S(1)} %get-tuple-element.48.standard, ...), custom_call_target="tpu_custom_call" | custom-call | flops 301989888 | bytes 1572864 | tf_op jit(solution)/shard_map/pallas_call | solution.py:367
  24.7 0.0 collective-permute-done.2.received
  24.7 0.4 shard_map.134
  25.1 20.0 %all_to_all.20.received = bf16[8,192,384]{2,1,0:T(8,128)(2,1)S(1)} all-to-all(bf16[8,192,384]{2,1,0:T(8,128)(2,1)S(1)} %shard_map.134), channel_id=1, replica_groups=mesh['zh'=4,'xh'=2,'xl'=2,'y2'=2,'y1'=2,'yl'=2,'zl'=2,'c'=2] {'xl','yl',..., dimensions={0} | all-to-all | bytes 2359296 | tf_op jit(solution)/shard_map/all_to_all | solution.py:510
  45.1 0.0 copy-start
  45.1 0.2 shard_map.135
  45.3 13.5 %all_to_all.21.received = bf16[4,48,384]{2,1,0:T(8,128)(2,1)S(1)} all-to-all(bf16[4,48,384]{2,1,0:T(8,128)(2,1)S(1)} %shard_map.135), channel_id=1, replica_groups=mesh['zh'=4,'xh'=2,'xl'=2,'y2'=2,'y1'=2,'yl'=2,'zl'=2,'c'=2] {'xh','y1'}, dimensions={0} | all-to-all | bytes 294912 | tf_op jit(solution)/shard_map/all_to_all | solution.py:510
  58.8 0.8 shard_map.136
  59.5 14.3 %all-to-all-start.2 = ((bf16[8,32,384]{2,1,0:T(8,128)(2,1)}), bf16[8,32,384]{2,1,0:T(8,128)(2,1)S(1)}, u32[]{:S(2)}, u32[]{:S(2)}) async-start(bf16[8,32,384]{2,1,0:T(8,128)(2,1)} %shard_map.136), calls=%async_computation.2 | async-start | bytes 393216 | tf_op jit(solution)/shard_map/all_to_all | solution.py:510
  73.8 0.0 copy-done
  73.8 2.3 %shard_map.137 = bf16[256,384]{1,0:T(8,128)(2,1)} custom-call(f32[256,384]{1,0:T(8,128)S(1)} %get-tuple-element.58.grad_conv, f32[24,384]{1,0:T(8,128)S(1)} %get-tuple-element.59.low, f32[24,384]{1,0:T(8,128)S(1)} %get-tuple-element.60.high, f32[7,7,384]{2,1,0:T(8,128)S(1)} %get-tuple-element.39.taps, bf16[256,384]{1,0:T(8,128)(2,1)S(1)} %bitcast.6), custom_call_target="tpu_custom_call" | custom-call | flops 9633792 | bytes 2097152 | tf_op jit(solution)/shard_map/pallas_call | solution.py:367
  76.1 9.7 %all-to-all-done.2.received = bf16[8,32,384]{2,1,0:T(8,128)(2,1)S(1)} async-done(((bf16[8,32,384]{2,1,0:T(8,128)(2,1)}), bf16[8,32,384]{2,1,0:T(8,128)(2,1)S(1)}, u32[]{:S(2)}, u32[]{:S(2)}) %all-to-all-start.2) | async-done | bytes 196640 | tf_op jit(solution)/shard_map/all_to_all | solution.py:510
  85.8 0.1 shard_map.138
  85.9 17.0 %all_to_all.22.own = bf16[32,24,384]{2,1,0:T(8,128)(2,1)S(1)} all-to-all(bf16[32,24,384]{2,1,0:T(8,128)(2,1)S(1)} %get-tuple-element.63), channel_id=1, replica_groups=mesh['zh'=4,'xh'=2,'xl'=2,'y2'=2,'y1'=2,'yl'=2,'zl'=2,'c'=2] {'xl','yl',..., dimensions={0} | all-to-all | bytes 1179648 | tf_op jit(solution)/shard_map/all_to_all | solution.py:510
  102.9 6.9 %collective-permute-start.3 = (bf16[32,24,384]{2,1,0:T(8,128)(2,1)S(1)}, bf16[32,24,384]{2,1,0:T(8,128)(2,1)S(1)}, u32[]{:S(2)}, u32[]{:S(2)}) collective-permute-start(bf16[32,24,384]{2,1,0:T(8,128)(2,1)S(1)} %all_to_all.22.own), channel_id=1, source_target_pairs={{0,1},{1,0},{2,3},{3,2},{4,5},{5,4},{6,7},{7,6},{8,9},{9,8},{10,11... | collective-permute-start | bytes 1769480 | tf_op jit(solution)/shard_map/ppermute | solution.py:514
  109.8 3.1 %collective-permute-start.4 = (f32[3,384]{1,0:T(4,128)S(1)}, f32[3,384]{1,0:T(4,128)S(1)}, u32[]{:S(2)}, u32[]{:S(2)}) collective-permute-start(f32[3,384]{1,0:T(4,128)S(1)} %get-tuple-element.66), channel_id=1, source_target_pairs={{0,0},{1,64},{64,1},{65,65},{2,2},{3,66},{66,3},{67,67},{4,4},{5,6... | collective-permute-start | bytes 13832 | tf_op jit(solution)/shard_map/ppermute | solution.py:552
  112.9 3.3 %collective-permute-done.4.in_rows = f32[3,384]{1,0:T(4,128)S(1)} collective-permute-done((f32[3,384]{1,0:T(4,128)S(1)}, f32[3,384]{1,0:T(4,128)S(1)}, u32[]{:S(2)}, u32[]{:S(2)}) %collective-permute-start.4) | collective-permute-done | bytes 4640 | tf_op jit(solution)/shard_map/ppermute | solution.py:552
  116.3 0.0 collective-permute-done.3.other
  116.3 1.1 shard_map.139
Async XLA Ops:
  1.9 9.4 %collective-permute-start = (bf16[80,384]{1,0:T(8,128)(2,1)S(1)}, bf16[80,384]{1,0:T(8,128)(2,1)S(1)}, u32[]{:S(2)}, u32[]{:S(2)}) collective-permute-start(bf16[80,384]{1,0:T(8,128)(2,1)S(1)} %get-tuple-element.37.own_high), channel_id=1, source_target_pairs={{0,4},{4,8},{8,12},{12,16},{16,20},{20,24},{24,28},{28,32},{32,36}... | collective-permute-start | bytes 184328 | tf_op jit(solution)/shard_map/ppermute | solution.py:501
  5.9 5.3 %collective-permute-start.1 = (bf16[80,384]{1,0:T(8,128)(2,1)S(1)}, bf16[80,384]{1,0:T(8,128)(2,1)S(1)}, u32[]{:S(2)}, u32[]{:S(2)}) collective-permute-start(bf16[80,384]{1,0:T(8,128)(2,1)S(1)} %get-tuple-element.38.own_low), channel_id=1, source_target_pairs={{4,0},{8,4},{12,8},{16,12},{20,16},{24,20},{28,24},{32,28},{36,32}... | collective-permute-start | bytes 184328 | tf_op jit(solution)/shard_map/ppermute | solution.py:506
  15.0 9.8 %collective-permute-start.2 = (bf16[1536,384]{1,0:T(8,128)(2,1)S(1)}, bf16[1536,384]{1,0:T(8,128)(2,1)S(1)}, u32[]{:S(2)}, u32[]{:S(2)}) collective-permute-start(bf16[1536,384]{1,0:T(8,128)(2,1)S(1)} %get-tuple-element.54), channel_id=1, source_target_pairs={{0,1},{1,0},{2,3},{3,2},{4,5},{5,4},{6,7},{7,6},{8,9},{9,8},{10,11... | collective-permute-start | bytes 3538952 | tf_op jit(solution)/shard_map/ppermute | solution.py:514
  45.1 28.8 %copy-start = (bf16[1,8,32,384]{3,2,1,0:T(8,128)(2,1)S(1)}, bf16[1,8,32,384]{3,2,1,0:T(8,128)(2,1)}, u32[]{:S(2)}) copy-start(bf16[1,8,32,384]{3,2,1,0:T(8,128)(2,1)} %param.12) | copy-start | bytes 589828
  59.5 26.3 %all-to-all-start.2 = ((bf16[8,32,384]{2,1,0:T(8,128)(2,1)}), bf16[8,32,384]{2,1,0:T(8,128)(2,1)S(1)}, u32[]{:S(2)}, u32[]{:S(2)}) async-start(bf16[8,32,384]{2,1,0:T(8,128)(2,1)} %shard_map.136), calls=%async_computation.2 | async-start | bytes 393216 | tf_op jit(solution)/shard_map/all_to_all | solution.py:510
  102.9 13.3 %collective-permute-start.3 = (bf16[32,24,384]{2,1,0:T(8,128)(2,1)S(1)}, bf16[32,24,384]{2,1,0:T(8,128)(2,1)S(1)}, u32[]{:S(2)}, u32[]{:S(2)}) collective-permute-start(bf16[32,24,384]{2,1,0:T(8,128)(2,1)S(1)} %all_to_all.22.own), channel_id=1, source_target_pairs={{0,1},{1,0},{2,3},{3,2},{4,5},{5,4},{6,7},{7,6},{8,9},{9,8},{10,11... | collective-permute-start | bytes 1769480 | tf_op jit(solution)/shard_map/ppermute | solution.py:514
  109.8 6.5 %collective-permute-start.4 = (f32[3,384]{1,0:T(4,128)S(1)}, f32[3,384]{1,0:T(4,128)S(1)}, u32[]{:S(2)}, u32[]{:S(2)}) collective-permute-start(f32[3,384]{1,0:T(4,128)S(1)} %get-tuple-element.66), channel_id=1, source_target_pairs={{0,0},{1,64},{64,1},{65,65},{2,2},{3,66},{66,3},{67,67},{4,4},{5,6... | collective-permute-start | bytes 13832 | tf_op jit(solution)/shard_map/ppermute | solution.py:552

commit v15 on v14

--- a/solution.py
+++ b/solution.py
@@ -547,9 +547,9 @@
     received, grad_image = lax.optimization_barrier((received, grad_image))
     message, in_rows = turn(scale, received, cube * four)
     own = exchange(message, CUBE + FOUR)
-    own, in_rows = lax.optimization_barrier((own, in_rows))
     pairs = [(2 * xh + c, 2 * c + xh) for xh in range(2) for c in range(2)]
     in_rows = lax.ppermute(in_rows, ("xh", "c"), pairs)
+    own, in_rows = lax.optimization_barrier((own, in_rows))
     grad_w_out, grad_w_in = join(device, own, swap(own), in_rows)
     return (grad_image.reshape(1, height, breadth, channels), grad_w_in, grad_w_out)
 

time: 118 us -> 114 us (0.966)
  blocking collectives: 50.5 us -> 33.4 us
  starting transfers between devices: 36.4 us -> 46.5 us
  waiting for transfers between devices: 13.1 us -> 16.1 us
    all_to_all x3 -> x2, blocking collectives: 50.5 us -> 33.4 us  [exchange(): return lax.all_to_all(blocks, axes, split_axis=0, concat_axis=0, tiled=True)]
    ppermute x1, starting transfers between devices: 3.1 us -> 9.05 us  [body(): in_rows = lax.ppermute(in_rows, ('xh', 'c'), pairs)]
    all_to_all x1 -> x2, starting transfers between devices: 14.3 us -> 18.2 us  [exchange(): return lax.all_to_all(blocks, axes, split_axis=0, concat_axis=0, tiled=True)]
    all_to_all x1 -> x2, waiting for transfers between devices: 9.75 us -> 12.2 us  [exchange(): return lax.all_to_all(blocks, axes, split_axis=0, concat_axis=0, tiled=True)]
    ppermute x2, waiting for transfers between devices: 0.01 us -> 1.61 us  [swap(): return lax.ppermute(block, 'c', SWAP)]
    ppermute x1, waiting for transfers between devices: 3.35 us -> 1.96 us  [body(): in_rows = lax.ppermute(in_rows, ('xh', 'c'), pairs)]
  transfers between devices with their start and end apart: 6 -> 7, of which waited for: 2 -> 5; matrix products, arithmetic and copies ran while one was open for 0% -> 0% of each run, Pallas kernels for 8% -> 7%
where the time goes in v15:
time: 114 us
  starting transfers between devices  46.5 us (41%)
  blocking collectives  33.4 us (29%)
  Pallas kernels  16.7 us (15%)
  waiting for transfers between devices  16.1 us (14%)
    all_to_all x2, blocking collectives, exchange(): return lax.all_to_all(blocks, axes, split_axis=0, concat_axis=0, tiled=True)  33.4 us
    all_to_all x2, starting transfers between devices, exchange(): return lax.all_to_all(blocks, axes, split_axis=0, concat_axis=0, tiled=True)  18.2 us
    pallas_call x10, Pallas kernels, call(): pl.pallas_call(kernel, out_shape=[jax.ShapeDtypeStruct(shape, kind) for s...  16.7 us
    ppermute x2, starting transfers between devices, swap(): return lax.ppermute(block, 'c', SWAP)  14 us
    all_to_all x2, waiting for transfers between devices, exchange(): return lax.all_to_all(blocks, axes, split_axis=0, concat_axis=0, tiled=True)  12.2 us
    ppermute x1, starting transfers between devices, body(): in_rows = lax.ppermute(in_rows, ('xh', 'c'), pairs)  9.05 us
    ppermute x1, starting transfers between devices, from_left(): return lax.ppermute(block, TILE, [(i, i + 1) for i in range(count - 1)])  4.03 us
  transfers between devices with their start and end apart: 7, of which 5 were waited for; matrix products, arithmetic and copies ran while one was open for 0% of the time, Pallas kernels for 7%

profile of v15, /device:TPU:1, one launch (start us, length us, event | category | flops | bytes accessed | tf_op | source)
XLA Modules:
  0.0 113.6 jit_solution(16915779474114528906)
XLA Ops:
  0.6 1.2 %shard_map.131 = (bf16[80,384]{1,0:T(8,128)(2,1)S(1)}, bf16[80,384]{1,0:T(8,128)(2,1)S(1)}) custom-call(s32[1,4]{1,0:T(1,128)} %flags.3, bf16[256,384]{1,0:T(8,128)(2,1)} %bitcast.7, bf16[256,384]{1,0:T(8,128)(2,1)} %bitcast.4, f32[384]{0:T(512)} %scale.3), custom_call_target="tpu_custom_call" | custom-call | flops 98304 | bytes 393216 | tf_op jit(solution)/shard_map/pallas_call | solution.py:367
  1.9 4.0 %collective-permute-start = (bf16[80,384]{1,0:T(8,128)(2,1)S(1)}, bf16[80,384]{1,0:T(8,128)(2,1)S(1)}, u32[]{:S(2)}, u32[]{:S(2)}) collective-permute-start(bf16[80,384]{1,0:T(8,128)(2,1)S(1)} %get-tuple-element.37.own_high), channel_id=1, source_target_pairs={{0,4},{4,8},{8,12},{12,16},{16,20},{20,24},{24,28},{28,32},{32,36}... | collective-permute-start | bytes 184328 | tf_op jit(solution)/shard_map/ppermute | solution.py:501
  5.9 1.3 %collective-permute-start.1 = (bf16[80,384]{1,0:T(8,128)(2,1)S(1)}, bf16[80,384]{1,0:T(8,128)(2,1)S(1)}, u32[]{:S(2)}, u32[]{:S(2)}) collective-permute-start(bf16[80,384]{1,0:T(8,128)(2,1)S(1)} %get-tuple-element.38.own_low), channel_id=1, source_target_pairs={{4,0},{8,4},{12,8},{16,12},{20,16},{24,20},{28,24},{32,28},{36,32}... | collective-permute-start | bytes 184328 | tf_op jit(solution)/shard_map/ppermute | solution.py:506
  7.2 3.2 %shard_map.130 = (f32[256,384]{1,0:T(8,128)S(1)}, bf16[256,384]{1,0:T(8,128)(2,1)S(1)}, f32[1536,256]{1,0:T(8,128)S(1)}, bf16[1536,384]{1,0:T(8,128)(2,1)S(1)}, ...) custom-call(s32[1,4]{1,0:T(1,128)} %flags.3, ...), custom_call_target="tpu_custom_call" | custom-call | flops 301989888 | bytes 8388608 | tf_op jit(solution)/shard_map/pallas_call | solution.py:367
  10.5 0.0 collective-permute-done.low
  10.5 0.4 collective-permute-done.1.high
  10.9 3.7 %shard_map.132 = (f32[1536,384]{1,0:T(8,128)S(1)}, bf16[1536,384]{1,0:T(8,128)(2,1)S(1)}, f32[256,384]{1,0:T(8,128)S(1)}, f32[256,128]{1,0:T(8,128)S(1)}, bf16[1536,256]{1,0:T(8,128)(2,1)S(1)}) custom-call(s32[1]{0:T(128)} %bitcast.device, f32[256,384]{1,0:T(8,128)S(1)} %get-tuple-element.36.conv, bf16[80,384]{1,0:T(8,128)(2,1)S(1)} %collective-permute-done.low, ...), custom_call_target="tpu_custom_call" | custom-call | flops 905969664 | bytes 12582912 | tf_op jit(solution)/shard_map/pallas_call | solution.py:367
  14.6 7.2 %collective-permute-start.2 = (bf16[1536,384]{1,0:T(8,128)(2,1)S(1)}, bf16[1536,384]{1,0:T(8,128)(2,1)S(1)}, u32[]{:S(2)}, u32[]{:S(2)}) collective-permute-start(bf16[1536,384]{1,0:T(8,128)(2,1)S(1)} %get-tuple-element.54), channel_id=1, source_target_pairs={{0,1},{1,0},{2,3},{3,2},{4,5},{5,4},{6,7},{7,6},{8,9},{9,8},{10,11... | collective-permute-start | bytes 3538952 | tf_op jit(solution)/shard_map/ppermute | solution.py:514
  21.8 2.9 %shard_map.133 = (f32[256,384]{1,0:T(8,128)S(1)}, f32[24,384]{1,0:T(8,128)S(1)}, f32[24,384]{1,0:T(8,128)S(1)}) custom-call(bf16[1536,256]{1,0:T(8,128)(2,1)S(1)} %get-tuple-element.46.grad_pre, bf16[384,1536]{1,0:T(8,128)(2,1)S(1)} %get-tuple-element.47.w_in, f32[256,384]{1,0:T(8,128)S(1)} %get-tuple-element.48.standard, ...), custom_call_target="tpu_custom_call" | custom-call | flops 301989888 | bytes 1572864 | tf_op jit(solution)/shard_map/pallas_call | solution.py:367
  24.7 0.0 collective-permute-done.2.received
  24.7 0.4 shard_map.134
  25.1 20.0 %all_to_all.20.received = bf16[8,192,384]{2,1,0:T(8,128)(2,1)S(1)} all-to-all(bf16[8,192,384]{2,1,0:T(8,128)(2,1)S(1)} %shard_map.134), channel_id=1, replica_groups=mesh['zh'=4,'xh'=2,'xl'=2,'y2'=2,'y1'=2,'yl'=2,'zl'=2,'c'=2] {'xl','yl',..., dimensions={0} | all-to-all | bytes 2359296 | tf_op jit(solution)/shard_map/all_to_all | solution.py:510
  45.1 0.0 copy-start
  45.1 0.2 shard_map.135
  45.3 13.4 %all_to_all.21.received = bf16[4,48,384]{2,1,0:T(8,128)(2,1)S(1)} all-to-all(bf16[4,48,384]{2,1,0:T(8,128)(2,1)S(1)} %shard_map.135), channel_id=1, replica_groups=mesh['zh'=4,'xh'=2,'xl'=2,'y2'=2,'y1'=2,'yl'=2,'zl'=2,'c'=2] {'xh','y1'}, dimensions={0} | all-to-all | bytes 294912 | tf_op jit(solution)/shard_map/all_to_all | solution.py:510
  58.8 0.8 shard_map.136
  59.5 14.3 %all-to-all-start.2 = ((bf16[8,32,384]{2,1,0:T(8,128)(2,1)}), bf16[8,32,384]{2,1,0:T(8,128)(2,1)S(1)}, u32[]{:S(2)}, u32[]{:S(2)}) async-start(bf16[8,32,384]{2,1,0:T(8,128)(2,1)} %shard_map.136), calls=%async_computation.2 | async-start | bytes 393216 | tf_op jit(solution)/shard_map/all_to_all | solution.py:510
  73.8 0.0 copy-done
  73.8 2.3 %shard_map.137 = bf16[256,384]{1,0:T(8,128)(2,1)} custom-call(f32[256,384]{1,0:T(8,128)S(1)} %get-tuple-element.58.grad_conv, f32[24,384]{1,0:T(8,128)S(1)} %get-tuple-element.59.low, f32[24,384]{1,0:T(8,128)S(1)} %get-tuple-element.60.high, f32[7,7,384]{2,1,0:T(8,128)S(1)} %get-tuple-element.39.taps, bf16[256,384]{1,0:T(8,128)(2,1)S(1)} %bitcast.6), custom_call_target="tpu_custom_call" | custom-call | flops 9633792 | bytes 2097152 | tf_op jit(solution)/shard_map/pallas_call | solution.py:367
  76.1 9.7 %all-to-all-done.2.received = bf16[8,32,384]{2,1,0:T(8,128)(2,1)S(1)} async-done(((bf16[8,32,384]{2,1,0:T(8,128)(2,1)}), bf16[8,32,384]{2,1,0:T(8,128)(2,1)S(1)}, u32[]{:S(2)}, u32[]{:S(2)}) %all-to-all-start.2) | async-done | bytes 196640 | tf_op jit(solution)/shard_map/all_to_all | solution.py:510
  85.8 0.9 shard_map.138
  86.7 3.9 %all-to-all-start.3 = ((bf16[32,24,384]{2,1,0:T(8,128)(2,1)}), bf16[32,24,384]{2,1,0:T(8,128)(2,1)S(1)}, u32[]{:S(2)}, u32[]{:S(2)}) async-start(bf16[32,24,384]{2,1,0:T(8,128)(2,1)} %get-tuple-element.63), calls=%async_computation.3 | async-start | bytes 1179648 | tf_op jit(solution)/shard_map/all_to_all | solution.py:510
  90.6 9.1 %collective-permute-start.3 = (f32[3,384]{1,0:T(4,128)S(1)}, f32[3,384]{1,0:T(4,128)S(1)}, u32[]{:S(2)}, u32[]{:S(2)}) collective-permute-start(f32[3,384]{1,0:T(4,128)S(1)} %get-tuple-element.64), channel_id=1, source_target_pairs={{0,0},{1,64},{64,1},{65,65},{2,2},{3,66},{66,3},{67,67},{4,4},{5,6... | collective-permute-start | bytes 13832 | tf_op jit(solution)/shard_map/ppermute | solution.py:551
  99.7 2.0 %collective-permute-done.3.in_rows = f32[3,384]{1,0:T(4,128)S(1)} collective-permute-done((f32[3,384]{1,0:T(4,128)S(1)}, f32[3,384]{1,0:T(4,128)S(1)}, u32[]{:S(2)}, u32[]{:S(2)}) %collective-permute-start.3) | collective-permute-done | bytes 4640 | tf_op jit(solution)/shard_map/ppermute | solution.py:551
  101.6 2.4 %all-to-all-done.3.own = bf16[32,24,384]{2,1,0:T(8,128)(2,1)S(1)} async-done(((bf16[32,24,384]{2,1,0:T(8,128)(2,1)}), bf16[32,24,384]{2,1,0:T(8,128)(2,1)S(1)}, u32[]{:S(2)}, u32[]{:S(2)}) %all-to-all-start.3) | async-done | bytes 589856 | tf_op jit(solution)/shard_map/all_to_all | solution.py:510
  104.1 6.8 %collective-permute-start.4 = (bf16[32,24,384]{2,1,0:T(8,128)(2,1)S(1)}, bf16[32,24,384]{2,1,0:T(8,128)(2,1)S(1)}, u32[]{:S(2)}, u32[]{:S(2)}) collective-permute-start(bf16[32,24,384]{2,1,0:T(8,128)(2,1)S(1)} %all-to-all-done.3.own), channel_id=1, source_target_pairs={{0,1},{1,0},{2,3},{3,2},{4,5},{5,4},{6,7},{7,6},{8,9},{9,8},{10,11... | collective-permute-start | bytes 1769480 | tf_op jit(solution)/shard_map/ppermute | solution.py:514
  110.9 1.6 %collective-permute-done.4.other = bf16[32,24,384]{2,1,0:T(8,128)(2,1)S(1)} collective-permute-done((bf16[32,24,384]{2,1,0:T(8,128)(2,1)S(1)}, bf16[32,24,384]{2,1,0:T(8,128)(2,1)S(1)}, u32[]{:S(2)}, u32[]{:S(2)}) %collective-permute-start.4) | collective-permute-done | bytes 589856 | tf_op jit(solution)/shard_map/ppermute | solution.py:514
  112.5 1.1 shard_map.139
Async XLA Ops:
  1.9 8.6 %collective-permute-start = (bf16[80,384]{1,0:T(8,128)(2,1)S(1)}, bf16[80,384]{1,0:T(8,128)(2,1)S(1)}, u32[]{:S(2)}, u32[]{:S(2)}) collective-permute-start(bf16[80,384]{1,0:T(8,128)(2,1)S(1)} %get-tuple-element.37.own_high), channel_id=1, source_target_pairs={{0,4},{4,8},{8,12},{12,16},{16,20},{20,24},{24,28},{28,32},{32,36}... | collective-permute-start | bytes 184328 | tf_op jit(solution)/shard_map/ppermute | solution.py:501
  5.9 5.0 %collective-permute-start.1 = (bf16[80,384]{1,0:T(8,128)(2,1)S(1)}, bf16[80,384]{1,0:T(8,128)(2,1)S(1)}, u32[]{:S(2)}, u32[]{:S(2)}) collective-permute-start(bf16[80,384]{1,0:T(8,128)(2,1)S(1)} %get-tuple-element.38.own_low), channel_id=1, source_target_pairs={{4,0},{8,4},{12,8},{16,12},{20,16},{24,20},{28,24},{32,28},{36,32}... | collective-permute-start | bytes 184328 | tf_op jit(solution)/shard_map/ppermute | solution.py:506
  14.6 10.2 %collective-permute-start.2 = (bf16[1536,384]{1,0:T(8,128)(2,1)S(1)}, bf16[1536,384]{1,0:T(8,128)(2,1)S(1)}, u32[]{:S(2)}, u32[]{:S(2)}) collective-permute-start(bf16[1536,384]{1,0:T(8,128)(2,1)S(1)} %get-tuple-element.54), channel_id=1, source_target_pairs={{0,1},{1,0},{2,3},{3,2},{4,5},{5,4},{6,7},{7,6},{8,9},{9,8},{10,11... | collective-permute-start | bytes 3538952 | tf_op jit(solution)/shard_map/ppermute | solution.py:514
  45.1 28.7 %copy-start = (bf16[1,8,32,384]{3,2,1,0:T(8,128)(2,1)S(1)}, bf16[1,8,32,384]{3,2,1,0:T(8,128)(2,1)}, u32[]{:S(2)}) copy-start(bf16[1,8,32,384]{3,2,1,0:T(8,128)(2,1)} %param.12) | copy-start | bytes 589828
  59.5 26.3 %all-to-all-start.2 = ((bf16[8,32,384]{2,1,0:T(8,128)(2,1)}), bf16[8,32,384]{2,1,0:T(8,128)(2,1)S(1)}, u32[]{:S(2)}, u32[]{:S(2)}) async-start(bf16[8,32,384]{2,1,0:T(8,128)(2,1)} %shard_map.136), calls=%async_computation.2 | async-start | bytes 393216 | tf_op jit(solution)/shard_map/all_to_all | solution.py:510
  86.7 17.4 %all-to-all-start.3 = ((bf16[32,24,384]{2,1,0:T(8,128)(2,1)}), bf16[32,24,384]{2,1,0:T(8,128)(2,1)S(1)}, u32[]{:S(2)}, u32[]{:S(2)}) async-start(bf16[32,24,384]{2,1,0:T(8,128)(2,1)} %get-tuple-element.63), calls=%async_computation.3 | async-start | bytes 1179648 | tf_op jit(solution)/shard_map/all_to_all | solution.py:510
  90.6 11.0 %collective-permute-start.3 = (f32[3,384]{1,0:T(4,128)S(1)}, f32[3,384]{1,0:T(4,128)S(1)}, u32[]{:S(2)}, u32[]{:S(2)}) collective-permute-start(f32[3,384]{1,0:T(4,128)S(1)} %get-tuple-element.64), channel_id=1, source_target_pairs={{0,0},{1,64},{64,1},{65,65},{2,2},{3,66},{66,3},{67,67},{4,4},{5,6... | collective-permute-start | bytes 13832 | tf_op jit(solution)/shard_map/ppermute | solution.py:551
  104.1 8.4 %collective-permute-start.4 = (bf16[32,24,384]{2,1,0:T(8,128)(2,1)S(1)}, bf16[32,24,384]{2,1,0:T(8,128)(2,1)S(1)}, u32[]{:S(2)}, u32[]{:S(2)}) collective-permute-start(bf16[32,24,384]{2,1,0:T(8,128)(2,1)S(1)} %all-to-all-done.3.own), channel_id=1, source_target_pairs={{0,1},{1,0},{2,3},{3,2},{4,5},{5,4},{6,7},{7,6},{8,9},{9,8},{10,11... | collective-permute-start | bytes 1769480 | tf_op jit(solution)/shard_map/ppermute | solution.py:514

commit v16 on v13

--- a/solution.py
+++ b/solution.py
@@ -354,9 +354,9 @@
     members, rows, _ = own.shape
     for place, blocks in ((core, own), (1 - core, other)):
         for m in range(0, members, 2):
-            pair = [blocks[i].astype(jnp.float32) for i in (m, m + 1)]
             start = pl.multiple_of((place * members + m) * rows, 2 * rows)
-            grad_w_out[pl.ds(start, 2 * rows), :] = jnp.concatenate(pair, axis=0).astype(jnp.bfloat16)
+            pair = jnp.concatenate([blocks[m], blocks[m + 1]], axis=0)
+            grad_w_out[pl.ds(start, 2 * rows), :] = pair
 
 
 def call(kernel, outs, scratch, scalars, arrays, flops, nbytes, space=pltpu.VMEM):

time: 113 us -> 113 us (level)
  no operation moved by 1% of the time
where the time goes in v16:
time: 113 us
  blocking collectives  59.7 us (53%)
  starting transfers between devices  31.8 us (28%)
  Pallas kernels  16.9 us (15%)
  waiting for transfers between devices  3.72 us (3%)
    all_to_all x3, blocking collectives, exchange(): return lax.all_to_all(blocks, axes, split_axis=0, concat_axis=0, tiled=True)  59.7 us
    pallas_call x10, Pallas kernels, call(): pl.pallas_call(kernel, out_shape=[jax.ShapeDtypeStruct(shape, kind) for s...  16.9 us
    ppermute x2, starting transfers between devices, swap(): return lax.ppermute(block, 'c', SWAP)  13.6 us
    ppermute x1, starting transfers between devices, body(): in_rows = lax.ppermute(in_rows, ('xh', 'c'), pairs)  9.05 us
    ppermute x1, starting transfers between devices, from_left(): return lax.ppermute(block, TILE, [(i, i + 1) for i in range(count - 1)])  4.03 us
    all_to_all x1, starting transfers between devices, exchange(): return lax.all_to_all(blocks, axes, split_axis=0, concat_axis=0, tiled=True)  3.9 us
  transfers between devices with their start and end apart: 6, of which 2 were waited for; matrix products, arithmetic and copies ran while one was open for 0% of the time, Pallas kernels for 8%

profile of v16, /device:TPU:1, one launch (start us, length us, event | category | flops | bytes accessed | tf_op | source)
XLA Modules:
  0.0 112.9 jit_solution(3325084977327948028)
XLA Ops:
  0.6 1.2 %shard_map.131 = (bf16[80,384]{1,0:T(8,128)(2,1)S(1)}, bf16[80,384]{1,0:T(8,128)(2,1)S(1)}) custom-call(s32[1,4]{1,0:T(1,128)} %flags.3, bf16[256,384]{1,0:T(8,128)(2,1)} %bitcast.7, bf16[256,384]{1,0:T(8,128)(2,1)} %bitcast.4, f32[384]{0:T(512)} %scale.3), custom_call_target="tpu_custom_call" | custom-call | flops 98304 | bytes 393216 | tf_op jit(solution)/shard_map/pallas_call | solution.py:367
  1.9 4.0 %collective-permute-start = (bf16[80,384]{1,0:T(8,128)(2,1)S(1)}, bf16[80,384]{1,0:T(8,128)(2,1)S(1)}, u32[]{:S(2)}, u32[]{:S(2)}) collective-permute-start(bf16[80,384]{1,0:T(8,128)(2,1)S(1)} %get-tuple-element.35.own_high), channel_id=1, source_target_pairs={{0,4},{4,8},{8,12},{12,16},{16,20},{20,24},{24,28},{28,32},{32,36}... | collective-permute-start | bytes 184328 | tf_op jit(solution)/shard_map/ppermute | solution.py:501
  5.9 1.3 %collective-permute-start.1 = (bf16[80,384]{1,0:T(8,128)(2,1)S(1)}, bf16[80,384]{1,0:T(8,128)(2,1)S(1)}, u32[]{:S(2)}, u32[]{:S(2)}) collective-permute-start(bf16[80,384]{1,0:T(8,128)(2,1)S(1)} %get-tuple-element.36.own_low), channel_id=1, source_target_pairs={{4,0},{8,4},{12,8},{16,12},{20,16},{24,20},{28,24},{32,28},{36,32}... | collective-permute-start | bytes 184328 | tf_op jit(solution)/shard_map/ppermute | solution.py:506
  7.2 4.0 %shard_map.130 = (f32[256,384]{1,0:T(8,128)S(1)}, bf16[256,384]{1,0:T(8,128)(2,1)S(1)}, f32[1536,256]{1,0:T(8,128)S(1)}, bf16[1536,384]{1,0:T(8,128)(2,1)S(1)}, ...) custom-call(s32[1,4]{1,0:T(1,128)} %flags.3, ...), custom_call_target="tpu_custom_call" | custom-call | flops 301989888 | bytes 8388608 | tf_op jit(solution)/shard_map/pallas_call | solution.py:367
  11.3 0.0 collective-permute-done.low
  11.3 0.0 collective-permute-done.1.high
  11.3 3.7 %shard_map.132 = (f32[1536,384]{1,0:T(8,128)S(1)}, bf16[1536,384]{1,0:T(8,128)(2,1)S(1)}, f32[256,384]{1,0:T(8,128)S(1)}, f32[256,128]{1,0:T(8,128)S(1)}, bf16[1536,256]{1,0:T(8,128)(2,1)S(1)}) custom-call(s32[1]{0:T(128)} %bitcast.device, f32[256,384]{1,0:T(8,128)S(1)} %get-tuple-element.34.conv, bf16[80,384]{1,0:T(8,128)(2,1)S(1)} %collective-permute-done.low, ...), custom_call_target="tpu_custom_call" | custom-call | flops 905969664 | bytes 12582912 | tf_op jit(solution)/shard_map/pallas_call | solution.py:367
  15.0 6.8 %collective-permute-start.2 = (bf16[1536,384]{1,0:T(8,128)(2,1)S(1)}, bf16[1536,384]{1,0:T(8,128)(2,1)S(1)}, u32[]{:S(2)}, u32[]{:S(2)}) collective-permute-start(bf16[1536,384]{1,0:T(8,128)(2,1)S(1)} %get-tuple-element.52), channel_id=1, source_target_pairs={{0,1},{1,0},{2,3},{3,2},{4,5},{5,4},{6,7},{7,6},{8,9},{9,8},{10,11... | collective-permute-start | bytes 3538952 | tf_op jit(solution)/shard_map/ppermute | solution.py:514
  21.8 2.9 %shard_map.133 = (f32[256,384]{1,0:T(8,128)S(1)}, f32[24,384]{1,0:T(8,128)S(1)}, f32[24,384]{1,0:T(8,128)S(1)}) custom-call(bf16[1536,256]{1,0:T(8,128)(2,1)S(1)} %get-tuple-element.44.grad_pre, bf16[384,1536]{1,0:T(8,128)(2,1)S(1)} %get-tuple-element.45.w_in, f32[256,384]{1,0:T(8,128)S(1)} %get-tuple-element.46.standard, ...), custom_call_target="tpu_custom_call" | custom-call | flops 301989888 | bytes 1572864 | tf_op jit(solution)/shard_map/pallas_call | solution.py:367
  24.7 0.0 collective-permute-done.2.received
  24.7 0.4 shard_map.134
  25.1 20.0 %all_to_all.20.received = bf16[8,192,384]{2,1,0:T(8,128)(2,1)S(1)} all-to-all(bf16[8,192,384]{2,1,0:T(8,128)(2,1)S(1)} %shard_map.134), channel_id=1, replica_groups=mesh['zh'=4,'xh'=2,'xl'=2,'y2'=2,'y1'=2,'yl'=2,'zl'=2,'c'=2] {'xl','yl',..., dimensions={0} | all-to-all | bytes 2359296 | tf_op jit(solution)/shard_map/all_to_all | solution.py:510
  45.1 0.2 shard_map.135
  45.3 0.0 copy-start
  45.3 13.6 %all_to_all.21.received = bf16[4,48,384]{2,1,0:T(8,128)(2,1)S(1)} all-to-all(bf16[4,48,384]{2,1,0:T(8,128)(2,1)S(1)} %shard_map.135), channel_id=1, replica_groups=mesh['zh'=4,'xh'=2,'xl'=2,'y2'=2,'y1'=2,'yl'=2,'zl'=2,'c'=2] {'xh','y1'}, dimensions={0} | all-to-all | bytes 294912 | tf_op jit(solution)/shard_map/all_to_all | solution.py:510
  58.9 0.1 shard_map.136
  59.0 26.1 %all_to_all.22.received = bf16[8,32,384]{2,1,0:T(8,128)(2,1)S(1)} all-to-all(bf16[8,32,384]{2,1,0:T(8,128)(2,1)S(1)} %shard_map.136), channel_id=1, replica_groups=mesh['zh'=4,'xh'=2,'xl'=2,'y2'=2,'y1'=2,'yl'=2,'zl'=2,'c'=2] {'zh','y2'}, dimensions={0} | all-to-all | bytes 393216 | tf_op jit(solution)/shard_map/all_to_all | solution.py:510
  85.1 0.9 shard_map.137
  86.0 3.9 %all-to-all-start.3 = ((bf16[32,24,384]{2,1,0:T(8,128)(2,1)}), bf16[32,24,384]{2,1,0:T(8,128)(2,1)S(1)}, u32[]{:S(2)}, u32[]{:S(2)}) async-start(bf16[32,24,384]{2,1,0:T(8,128)(2,1)} %get-tuple-element.53), calls=%async_computation.3 | async-start | bytes 1179648 | tf_op jit(solution)/shard_map/all_to_all | solution.py:510
  89.9 9.1 %collective-permute-start.3 = (f32[3,384]{1,0:T(4,128)S(1)}, f32[3,384]{1,0:T(4,128)S(1)}, u32[]{:S(2)}, u32[]{:S(2)}) collective-permute-start(f32[3,384]{1,0:T(4,128)S(1)} %get-tuple-element.54), channel_id=1, source_target_pairs={{0,0},{1,64},{64,1},{65,65},{2,2},{3,66},{66,3},{67,67},{4,4},{5,6... | collective-permute-start | bytes 13832 | tf_op jit(solution)/shard_map/ppermute | solution.py:548
  98.9 0.0 copy-done
  98.9 2.3 %shard_map.138 = bf16[256,384]{1,0:T(8,128)(2,1)} custom-call(f32[256,384]{1,0:T(8,128)S(1)} %get-tuple-element.55.grad_conv, f32[24,384]{1,0:T(8,128)S(1)} %get-tuple-element.58.low, f32[24,384]{1,0:T(8,128)S(1)} %get-tuple-element.59.high, f32[7,7,384]{2,1,0:T(8,128)S(1)} %get-tuple-element.37.taps, bf16[256,384]{1,0:T(8,128)(2,1)S(1)} %bitcast.6), custom_call_target="tpu_custom_call" | custom-call | flops 9633792 | bytes 2097152 | tf_op jit(solution)/shard_map/pallas_call | solution.py:367
  101.2 0.0 collective-permute-done.3.in_rows
  101.2 2.1 %all-to-all-done.3.own = bf16[32,24,384]{2,1,0:T(8,128)(2,1)S(1)} async-done(((bf16[32,24,384]{2,1,0:T(8,128)(2,1)}), bf16[32,24,384]{2,1,0:T(8,128)(2,1)S(1)}, u32[]{:S(2)}, u32[]{:S(2)}) %all-to-all-start.3) | async-done | bytes 589856 | tf_op jit(solution)/shard_map/all_to_all | solution.py:510
  103.3 6.8 %collective-permute-start.4 = (bf16[32,24,384]{2,1,0:T(8,128)(2,1)S(1)}, bf16[32,24,384]{2,1,0:T(8,128)(2,1)S(1)}, u32[]{:S(2)}, u32[]{:S(2)}) collective-permute-start(bf16[32,24,384]{2,1,0:T(8,128)(2,1)S(1)} %all-to-all-done.3.own), channel_id=1, source_target_pairs={{0,1},{1,0},{2,3},{3,2},{4,5},{5,4},{6,7},{7,6},{8,9},{9,8},{10,11... | collective-permute-start | bytes 1769480 | tf_op jit(solution)/shard_map/ppermute | solution.py:514
  110.1 1.6 %collective-permute-done.4.other = bf16[32,24,384]{2,1,0:T(8,128)(2,1)S(1)} collective-permute-done((bf16[32,24,384]{2,1,0:T(8,128)(2,1)S(1)}, bf16[32,24,384]{2,1,0:T(8,128)(2,1)S(1)}, u32[]{:S(2)}, u32[]{:S(2)}) %collective-permute-start.4) | collective-permute-done | bytes 589856 | tf_op jit(solution)/shard_map/ppermute | solution.py:514
  111.7 1.1 %shard_map.139 = (bf16[1536,384]{1,0:T(8,128)(2,1)}, f32[3,384]{1,0:T(4,128)}) custom-call(s32[1]{0:T(128)} %bitcast.device, bf16[32,24,384]{2,1,0:T(8,128)(2,1)S(1)} %all-to-all-done.3.own, bf16[32,24,384]{2,1,0:T(8,128)(2,1)S(1)} %collective-permute-done.4.other, f32[3,384]{1,0:T(4,128)S(1)} %collective-permute-done.3.in_rows), custom_call_target="tpu_custom_call" | custom-call | flops 294912 | bytes 2359296 | tf_op jit(solution)/shard_map/pallas_call | solution.py:367
Async XLA Ops:
  1.9 9.4 %collective-permute-start = (bf16[80,384]{1,0:T(8,128)(2,1)S(1)}, bf16[80,384]{1,0:T(8,128)(2,1)S(1)}, u32[]{:S(2)}, u32[]{:S(2)}) collective-permute-start(bf16[80,384]{1,0:T(8,128)(2,1)S(1)} %get-tuple-element.35.own_high), channel_id=1, source_target_pairs={{0,4},{4,8},{8,12},{12,16},{16,20},{20,24},{24,28},{28,32},{32,36}... | collective-permute-start | bytes 184328 | tf_op jit(solution)/shard_map/ppermute | solution.py:501
  5.9 5.4 %collective-permute-start.1 = (bf16[80,384]{1,0:T(8,128)(2,1)S(1)}, bf16[80,384]{1,0:T(8,128)(2,1)S(1)}, u32[]{:S(2)}, u32[]{:S(2)}) collective-permute-start(bf16[80,384]{1,0:T(8,128)(2,1)S(1)} %get-tuple-element.36.own_low), channel_id=1, source_target_pairs={{4,0},{8,4},{12,8},{16,12},{20,16},{24,20},{28,24},{32,28},{36,32}... | collective-permute-start | bytes 184328 | tf_op jit(solution)/shard_map/ppermute | solution.py:506
  15.0 9.7 %collective-permute-start.2 = (bf16[1536,384]{1,0:T(8,128)(2,1)S(1)}, bf16[1536,384]{1,0:T(8,128)(2,1)S(1)}, u32[]{:S(2)}, u32[]{:S(2)}) collective-permute-start(bf16[1536,384]{1,0:T(8,128)(2,1)S(1)} %get-tuple-element.52), channel_id=1, source_target_pairs={{0,1},{1,0},{2,3},{3,2},{4,5},{5,4},{6,7},{7,6},{8,9},{9,8},{10,11... | collective-permute-start | bytes 3538952 | tf_op jit(solution)/shard_map/ppermute | solution.py:514
  45.3 53.6 %copy-start = (bf16[1,8,32,384]{3,2,1,0:T(8,128)(2,1)S(1)}, bf16[1,8,32,384]{3,2,1,0:T(8,128)(2,1)}, u32[]{:S(2)}) copy-start(bf16[1,8,32,384]{3,2,1,0:T(8,128)(2,1)} %param.12) | copy-start | bytes 589828
  86.0 17.4 %all-to-all-start.3 = ((bf16[32,24,384]{2,1,0:T(8,128)(2,1)}), bf16[32,24,384]{2,1,0:T(8,128)(2,1)S(1)}, u32[]{:S(2)}, u32[]{:S(2)}) async-start(bf16[32,24,384]{2,1,0:T(8,128)(2,1)} %get-tuple-element.53), calls=%async_computation.3 | async-start | bytes 1179648 | tf_op jit(solution)/shard_map/all_to_all | solution.py:510
  89.9 11.4 %collective-permute-start.3 = (f32[3,384]{1,0:T(4,128)S(1)}, f32[3,384]{1,0:T(4,128)S(1)}, u32[]{:S(2)}, u32[]{:S(2)}) collective-permute-start(f32[3,384]{1,0:T(4,128)S(1)} %get-tuple-element.54), channel_id=1, source_target_pairs={{0,0},{1,64},{64,1},{65,65},{2,2},{3,66},{66,3},{67,67},{4,4},{5,6... | collective-permute-start | bytes 13832 | tf_op jit(solution)/shard_map/ppermute | solution.py:548
  103.3 8.4 %collective-permute-start.4 = (bf16[32,24,384]{2,1,0:T(8,128)(2,1)S(1)}, bf16[32,24,384]{2,1,0:T(8,128)(2,1)S(1)}, u32[]{:S(2)}, u32[]{:S(2)}) collective-permute-start(bf16[32,24,384]{2,1,0:T(8,128)(2,1)S(1)} %all-to-all-done.3.own), channel_id=1, source_target_pairs={{0,1},{1,0},{2,3},{3,2},{4,5},{5,4},{6,7},{7,6},{8,9},{9,8},{10,11... | collective-permute-start | bytes 1769480 | tf_op jit(solution)/shard_map/ppermute | solution.py:514
